TPU v7x, 32 devices: a whole 2x2x4 slice. The times are simulated.
32 devices in a mesh: tile: 8 (over y, x, core), view: 4 (over z).
Axes of the slice: x: 2, y: 2, z: 4, core: 2. Of those that a mesh axis runs over, the one named last changes fastest.
Arguments:
- estimate: float32 [64, 64, 256], P('tile'), may hold values from 0.5 to 2
- measured: float32 [4, 64, 64, 256], P('view', 'tile'), may hold values from 0.3 to 3
- kernels: float32 [4, 3, 15], P('view'), may hold values from 0.1 to 1
- labels: int32 [64, 64, 256], P('tile'), may hold values from 0 to 15
- label_owner: int32 [8, 16, 1], P('tile'), may hold values from 0 to 7; in each aligned block of 16 rows (0 to 15, 16 to 31, ..., all dimensions but the last counted through in order) at most 5 rows name the same one
- label_index: int32 [8, 16], P('tile'), may hold values from 0 to 127
Outputs:
- new_estimate: float32 [64, 64, 256], P('tile')
- nucleus_moments: float32 [10, 1024], P(None, 'tile')
Inputs may be any that keep to these rules, and one draw needn't show every extreme that they name: `label_owner`: among the 16 slots of one slab at most 5 name the same owner, a bound that some block reaches.
All inputs are finite; a program needn't handle non-finite values.
Results may differ from a plain program's by a relative error of at most 0.0003.
Values sent between devices are 32-bit elements; how exact they have to be, the bound alone decides.
No kernel may reach another device: no remote copies, remote signals or barrier semaphores. Data moves between devices by JAX's collectives and lax.ppermute only.
A program may use at most 64 MiB of HBM per device.

v0:
```python
import math

import jax
import jax.numpy as jnp
from jax import lax
from jax.sharding import PartitionSpec as P

MOM = 10
CAP = 5
NUC_DEV = 128


def with_halo(cells, sides, width):
    for axis, dim in sides:
        count = lax.axis_size(axis)
        ends = count - 1
        head = lax.slice_in_dim(cells, 0, width, axis=dim)
        tail = lax.slice_in_dim(cells, cells.shape[dim] - width, cells.shape[dim], axis=dim)
        cells = jnp.concatenate(
            [
                lax.ppermute(tail, axis, [(i, (i + 1) % count) for i in range(ends)]),
                cells,
                lax.ppermute(head, axis, [((i + 1) % count, i) for i in range(ends)]),
            ],
            axis=dim,
        )
    return cells


def band_matrix(taps, count):
    radius = (taps.shape[0] - 1) // 2
    rows = lax.broadcasted_iota(jnp.int32, (count, count), 0)
    cols = lax.broadcasted_iota(jnp.int32, (count, count), 1)
    offset = rows - cols + radius
    steps = jnp.arange(taps.shape[0], dtype=jnp.int32)[:, None, None]
    return jnp.sum(taps[:, None, None] * (offset[None] == steps).astype(jnp.float32), axis=0)


def plane_blur(field, taps_y, taps_x, flipped):
    matrix_y = band_matrix(taps_y, field.shape[1])
    matrix_x = band_matrix(taps_x, field.shape[2])
    if flipped:
        matrix_y = matrix_y.T
        matrix_x = matrix_x.T
    result = jnp.einsum("zyx,xw->zyw", field, matrix_x, precision=lax.Precision.HIGHEST)
    return jnp.einsum("zyx,yw->zwx", result, matrix_y, precision=lax.Precision.HIGHEST)


def depth_blur(padded, taps, flipped, count):
    radius = (taps.shape[0] - 1) // 2
    result = jnp.zeros((count,) + padded.shape[1:], jnp.float32)
    for step in range(taps.shape[0]):
        offset = 2 * radius - step if flipped else step
        result = result + taps[step] * padded[offset : offset + count]
    return result


def slot_table(part, label_part, plane_start, slab_planes, slot_count):
    tiles = lax.axis_size("tile")
    depth_total = slab_planes * tiles
    first = lax.axis_index("tile") * slab_planes + plane_start
    planes, height_count, across_count = part.shape
    area = height_count * across_count
    block = math.gcd(32768, area)
    per_plane = area // block
    count = planes * per_plane
    slots = jnp.arange(slot_count, dtype=jnp.int32)

    def add_block(totals, inputs):
        values, slot_ids, number = inputs
        position = number % per_plane * block + jnp.arange(block, dtype=jnp.int32)
        height = ((position // across_count).astype(jnp.float32) + 0.5) / height_count
        across = ((position % across_count).astype(jnp.float32) + 0.5) / across_count
        depth = ((first + number // per_plane).astype(jnp.float32) + 0.5) / depth_total
        features = jnp.stack(
            [
                values,
                values * height,
                values * across,
                values * (height * height),
                values * (across * across),
                values * (height * across),
            ]
        )
        upper = lax.optimization_barrier(features.astype(jnp.bfloat16))
        lower = (features - upper.astype(jnp.float32)).astype(jnp.bfloat16)
        onehot = (slot_ids[:, None] == slots[None, :]).astype(jnp.bfloat16)
        both = jnp.dot(
            jnp.concatenate([upper, lower], axis=0), onehot, preferred_element_type=jnp.float32
        )
        plane_sums = both[:6] + both[6:]
        terms = jnp.stack(
            [
                plane_sums[0],
                depth * plane_sums[0],
                plane_sums[1],
                plane_sums[2],
                depth * depth * plane_sums[0],
                plane_sums[3],
                plane_sums[4],
                depth * plane_sums[1],
                depth * plane_sums[2],
                plane_sums[5],
            ]
        )
        return (totals + terms, None)

    start_totals = jnp.zeros((MOM, slot_count), jnp.float32)
    totals, _ = lax.scan(
        add_block,
        start_totals,
        (
            part.reshape(count, block),
            label_part.reshape(count, block),
            jnp.arange(count, dtype=jnp.int32),
        ),
    )
    return totals


def owner_table(part, label_part, plane_start, slab_planes, label_owner, label_index):
    tiles = lax.axis_size("tile")
    slot_count = label_index.shape[1]
    slot_sums = slot_table(part, label_part, plane_start, slab_planes, slot_count)
    owners = label_owner[0, :, 0]
    member = (owners[:, None] == jnp.arange(tiles, dtype=jnp.int32)[None, :]).astype(jnp.int32)
    running = jnp.cumsum(member, axis=0)
    rank = jnp.sum(member * running, axis=1) - 1
    column = owners * CAP + rank
    send_rows = jnp.zeros((MOM, tiles * CAP), jnp.float32).at[:, column].set(slot_sums)
    send_ids = (
        jnp.zeros((1, tiles * CAP), jnp.float32)
        .at[0, column]
        .set(label_index[0].astype(jnp.float32))
    )
    got_rows, got_ids = (
        lax.all_to_all(send_rows, "tile", split_axis=1, concat_axis=1, tiled=True),
        lax.all_to_all(send_ids, "tile", split_axis=1, concat_axis=1, tiled=True),
    )
    nucleus = got_ids[0].astype(jnp.int32)
    return jax.vmap(lambda values: jax.ops.segment_sum(values, nucleus, num_segments=NUC_DEV))(
        got_rows
    )


def on_device(estimate, measured, kernels, labels, label_owner, label_index):
    weights = kernels[0] / jnp.sum(kernels[0], axis=-1, keepdims=True)
    radius = (weights.shape[1] - 1) // 2
    slab_planes = estimate.shape[0]
    plane = plane_blur(estimate, weights[1], weights[2], False)
    rimmed = with_halo(plane, (("tile", 0),), radius)
    forward = depth_blur(rimmed, weights[0], False, slab_planes)
    ratio = measured[0] / forward
    back_plane = plane_blur(ratio, weights[1], weights[2], True)
    back_rimmed = with_halo(back_plane, (("tile", 0),), radius)
    correction = depth_blur(back_rimmed, weights[0], True, slab_planes)
    views = lax.axis_size("view")
    total = lax.psum(correction, "view")
    new_estimate = estimate * total / views
    table = owner_table(new_estimate, labels, 0, slab_planes, label_owner, label_index)
    mass = table[0]
    slot_count = label_index.shape[1]
    scaled = mass * (slot_count / (slab_planes * estimate.shape[1] * estimate.shape[2]))
    shape_part = table[1:] / jnp.maximum(mass, 1.0)[None, :]
    return (new_estimate, jnp.concatenate([scaled[None, :], shape_part], axis=0))


def solution(mesh):
    placed = (
        P("tile", None, None),
        P("view", "tile", None, None),
        P("view", None, None),
        P("tile", None, None),
        P("tile", None, None),
        P("tile", None),
    )
    return jax.shard_map(
        on_device,
        mesh=mesh,
        in_specs=placed,
        out_specs=(P("tile", None, None), P(None, "tile")),
        check_vma=False,
    )
```

profile of v0, /device:TPU:0, one launch (start us, length us, event | category | flops | bytes accessed | tf_op | source)
XLA Modules:
  0.0 150.4 jit_solution(9110536026624168763)
XLA Ops:
  7.3 0.8 reduce_sum.35
  8.1 0.8 bitcast_divide_fusion
  10.8 2.5 %collective-permute-start = (f32[7,64,256]{2,1,0:T(8,128)S(1)}, f32[7,64,256]{2,1,0:T(8,128)S(1)}, u32[]{:S(2)}, u32[]{:S(2)}) collective-permute-start(f32[7,64,256]{2,1,0:T(8,128)S(1)} %get-tuple-element.188), channel_id=1, source_target_pairs={{0,4},{4,8},{8,12},{12,16},{16,20},{20,24},{24,28},{1,5},{5,9},{9,... | collective-permute-start | bytes 1376264 | tf_op jit(solution)/shard_map/ppermute | solution.py:21
  13.4 1.3 collective-permute-start.1
  14.7 0.7 fusion.132
  15.4 3.8 %collective-permute-done.1 = f32[7,64,256]{2,1,0:T(8,128)S(1)} collective-permute-done((f32[7,64,256]{2,1,0:T(8,128)S(1)}, f32[7,64,256]{2,1,0:T(8,128)S(1)}, u32[]{:S(2)}, u32[]{:S(2)}) %collective-permute-start.1) | collective-permute-done | bytes 458784 | tf_op jit(solution)/shard_map/ppermute | solution.py:23
  19.1 10.8 %fusion.97 = f32[8,64,256]{2,1,0:T(8,128)S(1)} fusion(f32[8,64,256]{2,1,0:T(8,128)S(1)} %convolution_bitcast_fusion.1, f32[7,64,256]{2,1,0:T(8,128)S(1)} %collective-permute-done.1, f32[7,64,256]{2,1,0:T(8,128)S(1)} %collective-permute-done, f32[1,8,64,256]{3,2,1,0:T(8,128)S(1)} %copy-done.4, f32[256,256]{1,0:T(8,128)S(1)} %select_reduce_fusion, ...), kind=kOutput, calls=%fused_computation.175 | convolution fusion | flops 408420352 | bytes 2752572 | tf_op jit(solution)/shard_map/zyx,xw->zyw/dot_general | solution.py:45
  30.7 1.3 collective-permute-start.2
  32.0 11.3 %collective-permute-start.3 = (f32[7,64,256]{2,1,0:T(8,128)S(1)}, f32[7,64,256]{2,1,0:T(8,128)S(1)}, u32[]{:S(2)}, u32[]{:S(2)}) collective-permute-start(f32[7,64,256]{2,1,0:T(8,128)S(1)} %get-tuple-element.187), channel_id=1, source_target_pairs={{0,4},{4,8},{8,12},{12,16},{16,20},{20,24},{24,28},{1,5},{5,9},{9,... | collective-permute-start | bytes 1376264 | tf_op jit(solution)/shard_map/ppermute | solution.py:21
  43.4 1.3 collective-permute-done.3
  44.7 10.7 %fusion.19 = f32[8,64,256]{2,1,0:T(8,128)} fusion(f32[8,64,256]{2,1,0:T(8,128)S(1)} %convolution_bitcast_fusion, f32[7,64,256]{2,1,0:T(8,128)S(1)} %collective-permute-done.3, f32[7,64,256]{2,1,0:T(8,128)S(1)} %collective-permute-done.2, f32[]{:T(128)} %bitcast.22, f32[]{:T(128)} %bitcast.21, f32[]{:T(128)} %bitcast.20, f32[]{:T(128)} %bitcast.19, ...), kind=kLoop, calls=%fused_computation.92 | loop fusion | flops 5636096 | bytes 1966140 | tf_op jit(solution)/shard_map/add | solution.py:54
  56.6 0.7 all_to_all.14
  57.3 12.8 %all-to-all-start = ((f32[1,8,5]{2,0,1:T(1,128)}), f32[1,8,5]{2,0,1:T(1,128)S(1)}, u32[]{:S(2)}, u32[]{:S(2)}) async-start(f32[1,8,5]{2,0,1:T(1,128)} %bitcast.29), calls=%async_computation | async-start | bytes 8192 | tf_op jit(solution)/shard_map/all_to_all | solution.py:138
  70.5 33.7 %all-reduce.3.cloned.1.call-done = f32[8,64,256]{2,1,0:T(8,128)} async-done(((f32[8,64,256]{2,1,0:T(8,128)}), f32[8,64,256]{2,1,0:T(8,128)}) %all-reduce.3.cloned.1.call-update) | async-done | bytes 524304 | tf_op jit(solution)/shard_map/psum | solution.py:158
  104.2 1.1 multiply_multiply_fusion.3
  106.1 26.0 %while.14 = (s32[]{:T(128)}, f32[10,16]{1,0:T(8,128)S(1)}, f32[8,16384]{1,0:T(8,128)S(1)}, s32[8,16384]{1,0:T(8,128)S(1)}, s32[8]{0:T(128)S(1)}, /*index=5*/s32[...) while((s32[]{:T(128)}, f32[10,16]{1,0:T(8,128)S(1)}, ...), condition=%wide.region_8.9_spmd.clone, body=%wide.region_7.8_spmd.clone.sunk | while | flops 8454633 | bytes 3283287 | solution.py:109
  107.9 0.7 dynamic_slice.33
  109.8 0.6 stack.29
  111.1 0.7 dynamic_slice.33
  114.4 0.7 dynamic_slice.33
  116.3 0.6 stack.29
  117.6 0.7 dynamic_slice.33
  119.6 0.6 stack.29
  120.9 0.7 dynamic_slice.33
  124.1 0.7 dynamic_slice.33
  126.1 0.6 stack.29
  127.4 0.7 dynamic_slice.33
  129.3 0.6 stack.29
  130.6 0.7 dynamic_slice.33
  133.4 3.7 %all-to-all-start.1 = ((f32[10,8,5]{0,2,1:T(8,128)}), f32[10,8,5]{0,2,1:T(8,128)S(1)}, u32[]{:S(2)}, u32[]{:S(2)}) async-start(f32[10,8,5]{0,2,1:T(8,128)} %reshape.234), calls=%async_computation.1 | async-start | bytes 65536 | tf_op jit(solution)/shard_map/all_to_all | solution.py:137
  137.1 4.7 %all-to-all-done.1 = f32[10,8,5]{0,2,1:T(8,128)S(1)} async-done(((f32[10,8,5]{0,2,1:T(8,128)}), f32[10,8,5]{0,2,1:T(8,128)S(1)}, u32[]{:S(2)}, u32[]{:S(2)}) %all-to-all-start.1) | async-done | bytes 1632 | tf_op jit(solution)/shard_map/all_to_all | solution.py:137
  141.9 0.8 scatter_custom_fusion.2
  (140 shorter events, 18.7 us)
Async XLA Ops:
  7.2 2.2 %copy-start = (f32[8,64,256]{2,1,0:T(8,128)S(1)}, f32[8,64,256]{2,1,0:T(8,128)}, u32[]{:S(2)}) copy-start(f32[8,64,256]{2,1,0:T(8,128)} %param.8) | copy-start | bytes 1572868
  7.2 97.0 %all-reduce.3.cloned.1.call-start = ((), (), s32[]{:S(2)}) async-start(), calls=%async_computation.2 | async-start | bytes 1048576 | tf_op jit(solution)/shard_map/psum | solution.py:158
  10.7 8.4 %copy-start.4 = (f32[1,8,64,256]{3,2,1,0:T(8,128)S(1)}, f32[1,8,64,256]{3,2,1,0:T(8,128)}, u32[]{:S(2)}) copy-start(f32[1,8,64,256]{3,2,1,0:T(8,128)} %param.9) | copy-start | bytes 1572868
  10.8 4.5 %collective-permute-start = (f32[7,64,256]{2,1,0:T(8,128)S(1)}, f32[7,64,256]{2,1,0:T(8,128)S(1)}, u32[]{:S(2)}, u32[]{:S(2)}) collective-permute-start(f32[7,64,256]{2,1,0:T(8,128)S(1)} %get-tuple-element.188), channel_id=1, source_target_pairs={{0,4},{4,8},{8,12},{12,16},{16,20},{20,24},{24,28},{1,5},{5,9},{9,... | collective-permute-start | bytes 1376264 | tf_op jit(solution)/shard_map/ppermute | solution.py:21
  13.4 5.8 %collective-permute-start.1 = (f32[7,64,256]{2,1,0:T(8,128)S(1)}, f32[7,64,256]{2,1,0:T(8,128)S(1)}, u32[]{:S(2)}, u32[]{:S(2)}) collective-permute-start(f32[7,64,256]{2,1,0:T(8,128)S(1)} %get-tuple-element.189), channel_id=1, source_target_pairs={{4,0},{8,4},{12,8},{16,12},{20,16},{24,20},{28,24},{5,1},{9,5},{13... | collective-permute-start | bytes 1376264 | tf_op jit(solution)/shard_map/ppermute | solution.py:23
  30.6 12.7 %copy-start.3 = (s32[1,16,1]{1,2,0:T(1,128)S(1)}, s32[1,16,1]{1,2,0:T(1,128)}, u32[]{:S(2)}) copy-start(s32[1,16,1]{1,2,0:T(1,128)} %param.12) | copy-start | bytes 196
  30.7 12.8 %collective-permute-start.2 = (f32[7,64,256]{2,1,0:T(8,128)S(1)}, f32[7,64,256]{2,1,0:T(8,128)S(1)}, u32[]{:S(2)}, u32[]{:S(2)}) collective-permute-start(f32[7,64,256]{2,1,0:T(8,128)S(1)} %get-tuple-element.186), channel_id=1, source_target_pairs={{4,0},{8,4},{12,8},{16,12},{20,16},{24,20},{28,24},{5,1},{9,5},{13... | collective-permute-start | bytes 1376264 | tf_op jit(solution)/shard_map/ppermute | solution.py:23
  32.0 12.7 %collective-permute-start.3 = (f32[7,64,256]{2,1,0:T(8,128)S(1)}, f32[7,64,256]{2,1,0:T(8,128)S(1)}, u32[]{:S(2)}, u32[]{:S(2)}) collective-permute-start(f32[7,64,256]{2,1,0:T(8,128)S(1)} %get-tuple-element.187), channel_id=1, source_target_pairs={{0,4},{4,8},{8,12},{12,16},{16,20},{20,24},{24,28},{1,5},{5,9},{9,... | collective-permute-start | bytes 1376264 | tf_op jit(solution)/shard_map/ppermute | solution.py:21
  55.4 0.7 copy-start.5
  55.4 14.8 %copy-start.2 = (s32[8,64,256]{2,1,0:T(8,128)S(1)}, s32[8,64,256]{2,1,0:T(8,128)}, u32[]{:S(2)}) copy-start(s32[8,64,256]{2,1,0:T(8,128)} %param.11) | copy-start | bytes 1572868
  57.3 76.1 %all-to-all-start = ((f32[1,8,5]{2,0,1:T(1,128)}), f32[1,8,5]{2,0,1:T(1,128)S(1)}, u32[]{:S(2)}, u32[]{:S(2)}) async-start(f32[1,8,5]{2,0,1:T(1,128)} %bitcast.29), calls=%async_computation | async-start | bytes 8192 | tf_op jit(solution)/shard_map/all_to_all | solution.py:138
  105.3 0.8 copy-start.1
  133.4 8.5 %all-to-all-start.1 = ((f32[10,8,5]{0,2,1:T(8,128)}), f32[10,8,5]{0,2,1:T(8,128)S(1)}, u32[]{:S(2)}, u32[]{:S(2)}) async-start(f32[10,8,5]{0,2,1:T(8,128)} %reshape.234), calls=%async_computation.1 | async-start | bytes 65536 | tf_op jit(solution)/shard_map/all_to_all | solution.py:137
Sparse Core Ops, SparseCore 0:
  55.5 48.6 all-reduce.2
where the time goes:
time: 151 us; the launch traced here: 150 us
  waiting for transfers between devices  43.5 us (29%)
  starting transfers between devices  32.9 us (22%)
  other arithmetic  20.8 us (14%)
  local copies, waits for them, and re-layouts  16.7 us (11%)
  matrix products  16.1 us (11%)
  between operations  14.3 us (9%)
  loops' own time  6.1 us (4%)
    psum x1, waiting for transfers between devices, on_device(): total = lax.psum(correction, 'view')  33.7 us
    ppermute x2, starting transfers between devices, with_halo(): lax.ppermute(tail, axis, [(i, (i + 1) % count) for i in range(ends)])  13.8 us
    all_to_all x1, starting transfers between devices, owner_table(): lax.all_to_all(send_ids, 'tile', split_axis=1, concat_axis=1, tiled=True)  12.8 us
    dot_general x2, matrix products, plane_blur(): jnp.einsum('zyx,xw->zyw', field, matrix_x, precision=lax.Precision.HIGHEST)  11.4 us
    add x1, other arithmetic, depth_blur(): result = result + taps[step] * padded[offset:offset + count]  10.7 us
    another operation x1, loops' own time, slot_table(): lax.scan(add_block, start_totals, (part.reshape(count, block), label_part...  6.1 us
    dynamic_slice x16, local copies, waits for them, and re-layouts, slot_table(): lax.scan(add_block, start_totals, (part.reshape(count, block), label_part...  5.78 us
    another operation x8, local copies, waits for them, and re-layouts, add_block(): jnp.stack([values, values * height, values * across, values * (height * h...  5.13 us
  transfers between devices with their start and end apart: 7, of which 4 were waited for; matrix products, arithmetic and copies ran while one was open for 16% of the time, Pallas kernels for 0%

commit v1 on v0

v1 whole, which is shorter than its diff:
```python
import functools

import jax
import jax.numpy as jnp
from jax import lax
from jax.experimental import pallas as pl
from jax.experimental.pallas import tpu as pltpu
from jax.sharding import PartitionSpec as P

MOM = 10
ROWS = 8
NUC_DEV = 128
LANES = 128
F32 = jnp.float32
BF16 = jnp.bfloat16
ANY = pl.BlockSpec(memory_space=pl.ANY)
VMEM = pl.BlockSpec(memory_space=pltpu.VMEM)
SMEM = pl.BlockSpec(memory_space=pltpu.SMEM)
LIMIT = 32 * 1024 * 1024


def half_of(view):
    return (view ^ (view >> 1)) & 1


def split(value):
    upper = value.astype(BF16)
    return upper, (value - upper.astype(F32)).astype(BF16)


def band(taps, shape, offset):
    rows = lax.broadcasted_iota(jnp.int32, shape, 0)
    cols = lax.broadcasted_iota(jnp.int32, shape, 1)
    place = cols - rows + offset
    result = jnp.zeros(shape, F32)
    for step in range(taps.shape[1]):
        result = jnp.where(place == step, taps[:, step : step + 1], result)
    return result


def bands_kernel(core, taps_own, taps_other, wide, tall, back):
    half = half_of(lax.axis_index("view"))
    across = wide.shape[-1]
    rows, keep = tall.shape[1], back.shape[1]
    for which, ref in enumerate((taps_own, taps_other)):
        raw = ref[0]
        taps = raw / jnp.sum(raw, axis=-1, keepdims=True)
        taps_y, taps_x = taps[1:2], taps[2:3]
        radius = (raw.shape[1] - 1) // 2
        flipped_x = jnp.concatenate([taps_x[:, t : t + 1] for t in reversed(range(raw.shape[1]))], axis=1)
        flipped_y = jnp.concatenate([taps_y[:, t : t + 1] for t in reversed(range(raw.shape[1]))], axis=1)
        upper, lower = split(band(flipped_x, (across, across), radius))
        wide[which, 0, 0] = upper
        wide[which, 0, 1] = lower
        upper, lower = split(band(taps_x, (across, across), radius))
        wide[which, 1, 0] = upper
        wide[which, 1, 1] = lower
        upper, lower = split(band(taps_y, (rows, rows), radius))
        tall[which] = jnp.concatenate([upper, upper, lower], axis=1)
        shift = (2 * keep - rows) * half
        upper, lower = split(band(flipped_y, (keep, rows), radius + shift - keep * half))
        back[which] = jnp.concatenate([upper, upper, lower], axis=1)


def make_bands(core, taps_own, taps_other, across, rows, keep):
    return pl.pallas_call(
        functools.partial(bands_kernel, core),
        out_shape=(
            jax.ShapeDtypeStruct((2, 2, 2, across, across), BF16),
            jax.ShapeDtypeStruct((2, rows, 3 * rows), BF16),
            jax.ShapeDtypeStruct((2, keep, 3 * rows), BF16),
        ),
        in_specs=[VMEM, VMEM],
        out_specs=(VMEM, VMEM, VMEM),
        compiler_params=pltpu.CompilerParams(vmem_limit_bytes=LIMIT),
        name="bands",
    )(taps_own, taps_other)


def depth_sum(source, weights, planes, flipped, lead, row_at, rows, lane_at, lanes):
    taps = len(weights)
    totals = [None] * planes
    for place in range(planes + taps - 1):
        block = source(place)
        for plane in range(planes):
            step = plane + taps - 1 - place if flipped else place - plane
            if 0 <= step < taps:
                term = weights[step] * block
                totals[plane] = term if totals[plane] is None else totals[plane] + term
    return totals


def load_rims(parity, radius, planes, near, far, place, sems):
    @pl.when(parity == 0)
    def _():
        pltpu.make_async_copy(far, place(0, radius), sems.at[0]).start()
        pltpu.make_async_copy(near, place(radius + planes, radius), sems.at[1]).start()

    @pl.when(parity == 1)
    def _():
        pltpu.make_async_copy(near, place(0, radius), sems.at[0]).start()
        pltpu.make_async_copy(far, place(radius + planes, radius), sems.at[1]).start()

    return [
        pltpu.make_async_copy(far, place(0, radius), sems.at[0]),
        pltpu.make_async_copy(near, place(radius + planes, radius), sems.at[1]),
    ]


def forward_kernel(
    weights, estimate, near, far, measured, swapped, wide, tall, back,
    field, send_near, send_far,
    padded, seen, blur_hi, blur_lo, plane_hi, plane_lo, result, sems, out_sems,
):
    planes, radius = estimate.shape[0], near.shape[0]
    rows, across = near.shape[1], near.shape[2]
    keep = result.shape[2]
    taps = 2 * radius + 1
    parity = lax.axis_index("tile") % 2
    half = half_of(lax.axis_index("view"))
    start = pl.multiple_of((estimate.shape[1] - rows) * half, 16)
    own = pltpu.make_async_copy(
        estimate.at[:, pl.ds(start, rows)], padded.at[pl.ds(radius, planes)], sems.at[2]
    )
    own.start()
    rims = load_rims(
        parity, radius, planes, near, far, lambda at, count: padded.at[pl.ds(at, count)], sems
    )
    views = [
        pltpu.make_async_copy(measured.at[0, :, pl.ds(start, rows)], seen.at[0], sems.at[3]),
        pltpu.make_async_copy(swapped, seen.at[1], sems.at[4]),
    ]
    for copy in views:
        copy.start()
    own.wait()
    for copy in rims:
        copy.wait()
    for which in range(2):
        factors = [weights[which, 0, step] for step in range(taps)]
        for row in range(0, rows, 16):
            for lane in range(0, across, LANES):
                blocks = depth_sum(
                    lambda place: padded[place, row : row + 16, lane : lane + LANES],
                    factors, planes, False, None, row, 16, lane, LANES,
                )
                for plane, block in enumerate(blocks):
                    upper, lower = split(block)
                    at = plane * rows + row
                    blur_hi[which, at : at + 16, lane : lane + LANES] = upper
                    blur_lo[which, at : at + 16, lane : lane + LANES] = lower
    for copy in views:
        copy.wait()
    for which in range(2):
        upper, lower = wide[which, 0, 0], wide[which, 0, 1]
        lines = jnp.dot(blur_hi[which], upper, preferred_element_type=F32)
        lines += jnp.dot(blur_lo[which], upper, preferred_element_type=F32)
        lines += jnp.dot(blur_hi[which], lower, preferred_element_type=F32)
        for plane in range(planes):
            hi, lo = split(lines[plane * rows : (plane + 1) * rows])
            forward = jnp.dot(
                tall[which], jnp.concatenate([hi, lo, hi], axis=0), preferred_element_type=F32
            )
            ratio = seen[which, plane] / forward
            hi, lo = split(ratio)
            turned = jnp.dot(
                back[which], jnp.concatenate([hi, lo, hi], axis=0), preferred_element_type=F32
            )
            hi, lo = split(turned)
            plane_hi[which, plane * keep : (plane + 1) * keep] = hi
            plane_lo[which, plane * keep : (plane + 1) * keep] = lo
        upper, lower = wide[which, 1, 0], wide[which, 1, 1]
        lines = jnp.dot(plane_hi[which], upper, preferred_element_type=F32)
        lines += jnp.dot(plane_lo[which], upper, preferred_element_type=F32)
        lines += jnp.dot(plane_hi[which], lower, preferred_element_type=F32)
        result[which] = lines.reshape(planes, keep, across)
    outs = [
        pltpu.make_async_copy(result.at[:, pl.ds(parity, radius)], send_far, out_sems.at[0]),
        pltpu.make_async_copy(result.at[:, pl.ds(1 - parity, radius)], send_near, out_sems.at[1]),
        pltpu.make_async_copy(result, field, out_sems.at[2]),
    ]
    for copy in outs:
        copy.start()
    for copy in outs:
        copy.wait()


def ratio_fields(weights, estimate, near, far, measured, swapped, wide, tall, back):
    planes, radius, rows, across = estimate.shape[0], near.shape[0], near.shape[1], near.shape[2]
    keep = back.shape[1]
    return pl.pallas_call(
        forward_kernel,
        out_shape=(
            jax.ShapeDtypeStruct((2, planes, keep, across), F32),
            jax.ShapeDtypeStruct((2, radius, keep, across), F32),
            jax.ShapeDtypeStruct((2, radius, keep, across), F32),
        ),
        in_specs=[SMEM, ANY, ANY, ANY, ANY, ANY, VMEM, VMEM, VMEM],
        out_specs=(ANY, ANY, ANY),
        scratch_shapes=[
            pltpu.VMEM((planes + 2 * radius, rows, across), F32),
            pltpu.VMEM((2, planes, rows, across), F32),
            pltpu.VMEM((2, planes * rows, across), BF16),
            pltpu.VMEM((2, planes * rows, across), BF16),
            pltpu.VMEM((2, planes * keep, across), BF16),
            pltpu.VMEM((2, planes * keep, across), BF16),
            pltpu.VMEM((2, planes, keep, across), F32),
            pltpu.SemaphoreType.DMA((5,)),
            pltpu.SemaphoreType.DMA((3,)),
        ],
        compiler_params=pltpu.CompilerParams(vmem_limit_bytes=LIMIT),
        name="ratio_fields",
    )(weights, estimate, near, far, measured, swapped, wide, tall, back)


def backward_kernel(weights, field, near, far, correction, padded, sems):
    planes, radius, keep, across = field.shape[1], near.shape[1], field.shape[2], field.shape[3]
    taps = 2 * radius + 1
    parity = lax.axis_index("tile") % 2
    own = pltpu.make_async_copy(field, padded.at[:, pl.ds(radius, planes)], sems.at[2])
    own.start()
    rims = load_rims(
        parity, radius, planes, near, far, lambda at, count: padded.at[:, pl.ds(at, count)], sems
    )
    own.wait()
    for copy in rims:
        copy.wait()
    for row in range(0, keep, 16):
        for lane in range(0, across, LANES):
            totals = None
            for which in range(2):
                factors = [weights[which, 0, step] for step in range(taps)]
                blocks = depth_sum(
                    lambda place: padded[which, place, row : row + 16, lane : lane + LANES],
                    factors, planes, True, None, row, 16, lane, LANES,
                )
                totals = blocks if totals is None else [a + b for a, b in zip(totals, blocks)]
            for plane, block in enumerate(totals):
                correction[plane, row : row + 16, lane : lane + LANES] = block


def pair_correction(weights, field, near, far):
    _, planes, keep, across = field.shape
    radius = near.shape[1]
    return pl.pallas_call(
        backward_kernel,
        out_shape=jax.ShapeDtypeStruct((planes, keep, across), F32),
        in_specs=[SMEM, ANY, ANY, ANY],
        out_specs=VMEM,
        scratch_shapes=[
            pltpu.VMEM((2, planes + 2 * radius, keep, across), F32),
            pltpu.SemaphoreType.DMA((3,)),
        ],
        compiler_params=pltpu.CompilerParams(vmem_limit_bytes=LIMIT),
        name="pair_correction",
    )(weights, field, near, far)


def update_kernel(views, estimate, mine, other, result, held, sem):
    keep = mine.shape[1]
    half = half_of(lax.axis_index("view"))
    copy = pltpu.make_async_copy(
        estimate.at[:, pl.ds(pl.multiple_of(keep * half, 8), keep)], held, sem
    )
    copy.start()
    copy.wait()
    result[...] = held[...] * (mine[...] + other[...]) * (1.0 / views)


def update(views, estimate, mine, other):
    return pl.pallas_call(
        functools.partial(update_kernel, views),
        out_shape=jax.ShapeDtypeStruct(mine.shape, F32),
        in_specs=[ANY, VMEM, VMEM],
        out_specs=VMEM,
        scratch_shapes=[pltpu.VMEM(mine.shape, F32), pltpu.SemaphoreType.DMA],
        compiler_params=pltpu.CompilerParams(vmem_limit_bytes=LIMIT),
        name="update",
    )(estimate, mine, other)


def moments_kernel(
    views, depth_total, estimate, correction, labels, owner_row, owner_col, index_col,
    sent, held, marks, sums, sems,
):
    planes, keep, across = correction.shape
    height_total = estimate.shape[1]
    slots = owner_row.shape[1]
    half = half_of(lax.axis_index("view"))
    first = lax.axis_index("tile") * planes
    start = pl.multiple_of(keep * half, 8)
    copies = [
        pltpu.make_async_copy(estimate.at[:, pl.ds(start, keep)], held, sems.at[0]),
        pltpu.make_async_copy(labels.at[:, pl.ds(start, keep)], marks, sems.at[1]),
    ]
    for copy in copies:
        copy.start()
    for copy in copies:
        copy.wait()
    held[...] = held[...] * correction[...] * (1.0 / views)
    group = 16
    columns = lax.broadcasted_iota(jnp.int32, (across, LANES), 1)
    spot = (lax.broadcasted_iota(jnp.int32, (across, LANES), 0).astype(F32) + 0.5) / across
    one, line, square = jnp.ones_like(spot), spot, spot * spot

    def placed(*pairs):
        result = jnp.zeros((across, LANES), F32)
        for lane, value in pairs:
            result = jnp.where(columns == lane, value, result)
        return result

    factors = jnp.concatenate(
        [
            placed((0, one), (3, line), (6, square)),
            placed((2, one), (9, line)),
            placed((5, one)),
            placed((1, one), (8, line)),
            placed((7, one)),
            placed((4, one)),
        ],
        axis=0,
    )
    base = lax.broadcasted_iota(jnp.int32, (8, across), 0)

    def one_group(number, carry):
        def one_slot(inner, carry):
            slot = number * group + inner
            parts = [jnp.zeros((8, across), F32) for _ in range(6)]
            for row in range(0, keep, 8):
                high = ((base + (row + start)).astype(F32) + 0.5) / height_total
                flat = [jnp.zeros((8, across), F32) for _ in range(3)]
                for plane in range(planes):
                    deep = ((first + plane).astype(F32) + 0.5) / depth_total
                    hit = marks[plane, row : row + 8] == slot
                    value = jnp.where(hit, held[plane, row : row + 8], 0.0)
                    flat[0] = flat[0] + value
                    value = value * deep
                    flat[1] = flat[1] + value
                    flat[2] = flat[2] + value * deep
                scaled = flat[0] * high
                parts[0] = parts[0] + flat[0]
                parts[1] = parts[1] + scaled
                parts[2] = parts[2] + scaled * high
                parts[3] = parts[3] + flat[1]
                parts[4] = parts[4] + flat[1] * high
                parts[5] = parts[5] + flat[2]
            at = pl.multiple_of(inner * 8, 8)
            sums[pl.ds(at, 8), :] = jnp.concatenate(parts, axis=1)
            return carry

        lax.fori_loop(0, group, one_slot, 0)
        table = jnp.dot(
            sums[...], factors, precision=lax.Precision.HIGHEST, preferred_element_type=F32
        )
        table = jnp.sum(table.reshape(group, 8, LANES), axis=1)
        at = pl.multiple_of(number * group, group)
        ids = index_col[pl.ds(at, group), :].astype(F32)
        lanes = lax.broadcasted_iota(jnp.int32, (group, LANES), 1)
        table = jnp.where(lanes == MOM, ids, table)
        owner = owner_col[pl.ds(at, group), :]
        earlier = lax.broadcasted_iota(jnp.int32, (group, slots), 1) < (
            lax.broadcasted_iota(jnp.int32, (group, slots), 0) + number * group
        )
        same = (owner == owner_row[...]) & earlier
        rank = jnp.sum(same.astype(F32), axis=1, keepdims=True).astype(jnp.int32)
        place = owner * ROWS + rank
        spots = lax.broadcasted_iota(jnp.int32, (group, sent.shape[0]), 1)
        picked = (place == spots).astype(F32)
        sent[...] += lax.dot_general(
            picked, table, (((0,), (0,)), ((), ())),
            precision=lax.Precision.HIGHEST, preferred_element_type=F32,
        )
        return carry

    sent[...] = jnp.zeros_like(sent)
    lax.fori_loop(0, slots // group, one_group, 0)


def moment_rows(views, tiles, estimate, correction, labels, label_owner, label_index):
    slots = label_index.shape[1]
    planes, keep, across = correction.shape
    return pl.pallas_call(
        functools.partial(moments_kernel, views, tiles * planes),
        out_shape=jax.ShapeDtypeStruct((tiles * ROWS, LANES), F32),
        in_specs=[ANY, VMEM, ANY, VMEM, VMEM, VMEM],
        out_specs=VMEM,
        scratch_shapes=[
            pltpu.VMEM(correction.shape, F32),
            pltpu.VMEM(correction.shape, jnp.int32),
            pltpu.VMEM((16 * 8, 6 * across), F32),
            pltpu.SemaphoreType.DMA((2,)),
        ],
        compiler_params=pltpu.CompilerParams(vmem_limit_bytes=LIMIT),
        name="moment_rows",
    )(
        estimate, correction, labels,
        label_owner.reshape(1, slots), label_owner.reshape(slots, 1), label_index.reshape(slots, 1),
    )


def segments_kernel(rows, table):
    values = rows[...]
    ids = values[:, MOM : MOM + 1].astype(jnp.int32)
    spots = lax.broadcasted_iota(jnp.int32, (values.shape[0], NUC_DEV), 1)
    picked = (ids == spots).astype(F32)
    full = lax.dot_general(
        values, picked, (((0,), (0,)), ((), ())),
        precision=lax.Precision.HIGHEST, preferred_element_type=F32,
    )
    table[...] = full[: table.shape[0]]


def segment_table(rows):
    return pl.pallas_call(
        segments_kernel,
        out_shape=jax.ShapeDtypeStruct((16, NUC_DEV), F32),
        in_specs=[VMEM],
        out_specs=VMEM,
        compiler_params=pltpu.CompilerParams(vmem_limit_bytes=LIMIT),
        name="segment_table",
    )(rows)


def finish_kernel(scale, mine, other, first, second, third, fourth, whole, moments, sems):
    keep = mine.shape[1]
    half = half_of(lax.axis_index("view"))
    copies = [
        pltpu.make_async_copy(
            mine, whole.at[:, pl.ds(pl.multiple_of(keep * half, 8), keep)], sems.at[0]
        ),
        pltpu.make_async_copy(
            other, whole.at[:, pl.ds(pl.multiple_of(keep * (1 - half), 8), keep)], sems.at[1]
        ),
    ]
    for copy in copies:
        copy.start()
    table = (first[...] + second[...]) + (third[...] + fourth[...])
    mass = table[0:1]
    lines = lax.broadcasted_iota(jnp.int32, table.shape, 0)
    result = jnp.where(lines == 0, table * scale, table / jnp.maximum(mass, 1.0))
    moments[...] = result[:MOM]
    for copy in copies:
        copy.wait()


def finish(scale, mine, other, tables):
    planes, keep, across = mine.shape
    return pl.pallas_call(
        functools.partial(finish_kernel, scale),
        out_shape=(
            jax.ShapeDtypeStruct((planes, 2 * keep, across), F32),
            jax.ShapeDtypeStruct((MOM, NUC_DEV), F32),
        ),
        in_specs=[ANY, ANY, VMEM, VMEM, VMEM, VMEM],
        out_specs=(ANY, VMEM),
        scratch_shapes=[pltpu.SemaphoreType.DMA((2,))],
        compiler_params=pltpu.CompilerParams(vmem_limit_bytes=LIMIT),
        name="finish",
    )(mine, other, *tables)


def on_device(estimate, measured, kernels, labels, label_owner, label_index):
    tiles, views = lax.axis_size("tile"), lax.axis_size("view")
    planes, height, across = estimate.shape
    taps = kernels.shape[2]
    radius = (taps - 1) // 2
    keep = height // 2
    rows = min(height, -(-(keep + 2 * radius) // 16) * 16)
    parity = lax.axis_index("tile") % 2
    half = half_of(lax.axis_index("view"))
    near_pairs = [(i, i ^ 1) for i in range(tiles)]
    far_pairs = [(i, i + 1) for i in range(1, tiles - 1, 2)]
    far_pairs = far_pairs + [(b, a) for a, b in far_pairs]
    partner = [(i, i ^ 1) for i in range(views)]
    across_pairs = [(i, i ^ 3) for i in range(views)]

    shift = (height - rows) * half
    to_far = lax.dynamic_slice(estimate, (parity, shift, 0), (radius, rows, across))
    to_near = lax.dynamic_slice(estimate, (1 - parity, shift, 0), (radius, rows, across))
    to_partner = lax.dynamic_slice(measured[0], (0, (height - rows) * (1 - half), 0), (planes, rows, across))
    far = lax.ppermute(to_far, "tile", far_pairs)
    other_taps = lax.ppermute(kernels, "view", partner)
    near = lax.ppermute(to_near, "tile", near_pairs)
    swapped = lax.ppermute(to_partner, "view", partner)
    both = jnp.concatenate([kernels, other_taps], axis=0)
    weights = both / jnp.sum(both, axis=-1, keepdims=True)
    wide, tall, back = make_bands(0, kernels, other_taps, across, rows, keep)
    field, field_near, field_far = ratio_fields(
        weights, estimate, near, far, measured, swapped, wide, tall, back
    )
    rim_far = lax.ppermute(field_far, "tile", far_pairs)
    rim_near = lax.ppermute(field_near, "tile", near_pairs)
    mine = pair_correction(weights, field, rim_near, rim_far)
    other = lax.ppermute(mine, "view", across_pairs)
    sent = moment_rows(views, tiles, estimate, mine, labels, label_owner, label_index)
    got = lax.all_to_all(sent, "tile", split_axis=0, concat_axis=0, tiled=True)
    new_half = update(views, estimate, mine, other)
    new_other = lax.ppermute(new_half, "view", partner)
    table = segment_table(got)
    tables = [table] + [
        lax.ppermute(table, "view", [(i, i ^ step) for i in range(views)]) for step in (1, 2, 3)
    ]
    scale = label_index.shape[1] / (planes * height * across)
    new_estimate, moments = finish(scale, new_half, new_other, tables)
    return new_estimate, moments


def solution(mesh):
    placed = (
        P("tile", None, None),
        P("view", "tile", None, None),
        P("view", None, None),
        P("tile", None, None),
        P("tile", None, None),
        P("tile", None),
    )
    return jax.shard_map(
        on_device,
        mesh=mesh,
        in_specs=placed,
        out_specs=(P("tile", None, None), P(None, "tile")),
        check_vma=False,
    )
```

time: 151 us -> 73.7 us (0.49)
  waiting for transfers between devices: 43.5 us -> 14.8 us
  blocking collectives: 0 us -> 24.4 us
  other arithmetic: 20.8 us -> 0.08 us
  matrix products: 16.1 us -> 0 us
  local copies, waits for them, and re-layouts: 16.7 us -> 2.09 us
  starting transfers between devices: 32.9 us -> 18.8 us
  between operations: 14.3 us -> 0.81 us
  Pallas kernels: 0 us -> 12.5 us
  loops' own time: 6.1 us -> 0 us
    psum x1 -> x0, waiting for transfers between devices: 33.7 us -> none  [on_device(): total = lax.psum(correction, 'view')]
    all_to_all x0 -> x1, blocking collectives: none -> 24.4 us  [on_device(): got = lax.all_to_all(sent, 'tile', split_axis=0, concat_axis=0, tiled=True)]
    all_to_all x2 -> x0, starting transfers between devices: 16.5 us -> none  [the longest x1 12.8 us: owner_table(): lax.all_to_all(send_ids, 'tile', split_axis=1, concat_axis=1, tiled=True)]
    dot_general x12 -> x0, matrix products: 16.1 us -> none  [the longest x2 11.4 us: plane_blur(): jnp.einsum('zyx,xw->zyw', field, matrix_x, precision=lax.Precision.HIGHEST)]
    pallas_call x0 -> x7, Pallas kernels: none -> 12.5 us  [the longest x1 5.45 us: ratio_fields(): pl.pallas_call(forward_kernel, out_shape=(jax.ShapeDtypeStruct((2, planes...]
    add x19 -> x0, other arithmetic: 10.8 us -> none  [the longest x1 10.7 us: depth_blur(): result = result + taps[step] * padded[offset:offset + count]]
    ppermute x4 -> x11, waiting for transfers between devices: 5.04 us -> 14.8 us  [the longest x1 7.09 us: on_device(): other_taps = lax.ppermute(kernels, 'view', partner)]
    another operation x1 -> x0, loops' own time: 6.1 us -> none  [slot_table(): lax.scan(add_block, start_totals, (part.reshape(count, block), label_part...]
  transfers between devices with their start and end apart: 7 -> 11, of which waited for: 4 -> 6; matrix products, arithmetic and copies ran while one was open for 16% -> 0% of each run, Pallas kernels for 0% -> 5%
where the time goes in v1:
time: 73.7 us; the launch traced here: 73.5 us
  blocking collectives  24.4 us (33%)
  starting transfers between devices  18.8 us (26%)
  waiting for transfers between devices  14.8 us (20%)
  Pallas kernels  12.5 us (17%)
  local copies, waits for them, and re-layouts  2.09 us (3%)
  between operations  0.81 us (1%)
    all_to_all x1, blocking collectives, on_device(): got = lax.all_to_all(sent, 'tile', split_axis=0, concat_axis=0, tiled=True)  24.4 us
    ppermute x1, waiting for transfers between devices, on_device(): other_taps = lax.ppermute(kernels, 'view', partner)  7.09 us
    pallas_call x1, Pallas kernels, ratio_fields(): pl.pallas_call(forward_kernel, out_shape=(jax.ShapeDtypeStruct((2, planes...  5.45 us
    ppermute x1, waiting for transfers between devices, on_device(): other = lax.ppermute(mine, 'view', across_pairs)  4.46 us
    ppermute x3, starting transfers between devices, on_device(): lax.ppermute(table, 'view', [(i, i ^ step) for i in range(views)])  4.45 us
    ppermute x1, starting transfers between devices, on_device(): other = lax.ppermute(mine, 'view', across_pairs)  4.09 us
    ppermute x1, starting transfers between devices, on_device(): swapped = lax.ppermute(to_partner, 'view', partner)  2.82 us
    ppermute x1, starting transfers between devices, on_device(): new_other = lax.ppermute(new_half, 'view', partner)  2.78 us
  transfers between devices with their start and end apart: 11, of which 6 were waited for; matrix products, arithmetic and copies ran while one was open for 0% of the time, Pallas kernels for 5%

profile of v1, /device:TPU:0, one launch (start us, length us, event | category | flops | bytes accessed | tf_op | source)
XLA Modules:
  0.0 73.5 jit_solution(5492199244680511644)
XLA Ops:
  0.7 1.2 %constant_dynamic-slice_fusion = (f32[7,48,256]{2,1,0:T(8,128)S(1)}, f32[7,48,256]{2,1,0:T(8,128)S(1)}) fusion(f32[8,64,256]{2,1,0:T(8,128)} %estimate.5, s32[]{:T(128)S(6)} %select_n.23, s32[]{:T(128)S(6)} %select_n.22, s32[]{:T(128)S(6)} %select_n.21), kind=kLoop, calls=%fused_computation.5 | loop fusion | bytes 1376268 | tf_op jit(solution)/shard_map/dynamic_slice | solution.py:477
  1.9 0.0 copy-start
  1.9 0.5 collective-permute-start.1
  2.4 0.7 collective-permute-start.2
  3.1 0.0 copy-start.4
  3.1 2.8 %collective-permute-start.3 = (f32[8,48,256]{2,1,0:T(8,128)S(1)}, f32[8,48,256]{2,1,0:T(8,128)S(1)}, u32[]{:S(2)}, u32[]{:S(2)}) collective-permute-start(f32[8,48,256]{2,1,0:T(8,128)S(1)} %dynamic-slice_bitcast_fusion), channel_id=1, source_target_pairs={{0,1},{1,0},{2,3},{3,2},{4,5},{5,4},{6,7},{7,6},{8,9},{9,8},{10,11... | collective-permute-start | bytes 1179656 | tf_op jit(solution)/shard_map/ppermute | solution.py:483
  6.0 0.6 collective-permute-start
  6.5 7.1 %collective-permute-done.taps_other = f32[1,3,15]{2,1,0:T(4,128)S(1)} collective-permute-done((f32[1,3,15]{2,1,0:T(4,128)S(1)}, f32[1,3,15]{2,1,0:T(4,128)S(1)}, u32[]{:S(2)}, u32[]{:S(2)}) %collective-permute-start) | collective-permute-done | bytes 212 | tf_op jit(solution)/shard_map/ppermute | solution.py:481
  13.6 1.3 %bands.1 = (bf16[2,2,2,256,256]{4,3,2,1,0:T(8,128)(2,1)S(1)}, bf16[2,48,144]{2,1,0:T(8,128)(2,1)S(1)}, bf16[2,32,144]{2,1,0:T(8,128)(2,1)S(1)}) custom-call(f32[1,3,15]{2,1,0:T(4,128)S(1)} %get-tuple-element.16.taps_own, f32[1,3,15]{2,1,0:T(4,128)S(1)} %collective-permute-done.taps_other), custom_call_target="tpu_custom_call" | custom-call | tf_op jit(solution)/shard_map/bands/pallas_call | solution.py:66
  14.9 0.1 fusion.1.weights
  15.0 5.5 %ratio_fields.1 = (f32[2,8,32,256]{3,2,1,0:T(8,128)S(1)}, f32[2,7,32,256]{3,2,1,0:T(8,128)S(1)}, f32[2,7,32,256]{3,2,1,0:T(8,128)S(1)}) custom-call(f32[2,3,15]{2,1,0:T(4,128)S(1)} %fusion.1.weights, f32[8,64,256]{2,1,0:T(8,128)S(1)} %copy-done, f32[7,48,256]{2,1,0:T(8,128)S(1)} %collective-permute-done.1.near, ...), custom_call_target="tpu_custom_call" | custom-call | tf_op jit(solution)/shard_map/ratio_fields/pallas_call | solution.py:190
  20.5 2.2 %collective-permute-start.4 = (f32[2,7,32,256]{3,2,1,0:T(8,128)S(1)}, f32[2,7,32,256]{3,2,1,0:T(8,128)S(1)}, u32[]{:S(2)}, u32[]{:S(2)}) collective-permute-start(f32[2,7,32,256]{3,2,1,0:T(8,128)S(1)} %get-tuple-element.12), channel_id=1, source_target_pairs={{0,4},{4,0},{8,12},{12,8},{16,20},{20,16},{24,28},{28,24},{1,5},{5... | collective-permute-start | bytes 1376264 | tf_op jit(solution)/shard_map/ppermute | solution.py:491
  22.7 0.7 collective-permute-start.5
  23.4 0.8 %collective-permute-done.4.near = f32[2,7,32,256]{3,2,1,0:T(8,128)S(1)} collective-permute-done((f32[2,7,32,256]{3,2,1,0:T(8,128)S(1)}, f32[2,7,32,256]{3,2,1,0:T(8,128)S(1)}, u32[]{:S(2)}, u32[]{:S(2)}) %collective-permute-start.4) | collective-permute-done | bytes 458784 | tf_op jit(solution)/shard_map/ppermute | solution.py:491
  24.2 1.5 %pair_correction.1.mine.correction = f32[8,32,256]{2,1,0:T(8,128)S(1)} custom-call(f32[2,3,15]{2,1,0:T(4,128)S(1)} %fusion.1.weights, f32[2,8,32,256]{3,2,1,0:T(8,128)S(1)} %get-tuple-element.11.field, f32[2,7,32,256]{3,2,1,0:T(8,128)S(1)} %collective-permute-done.4.near, f32[2,7,32,256]{3,2,1,0:T(8,128)S(1)} %collective-permute-done.5.far), custom_call_target="tpu_custom_call" | custom-call | tf_op jit(solution)/shard_map/pair_correction/pallas_call | solution.py:244
  25.7 4.1 %collective-permute-start.6 = (f32[8,32,256]{2,1,0:T(8,128)S(1)}, f32[8,32,256]{2,1,0:T(8,128)S(1)}, u32[]{:S(2)}, u32[]{:S(2)}) collective-permute-start(f32[8,32,256]{2,1,0:T(8,128)S(1)} %pair_correction.1.mine.correction), channel_id=1, source_target_pairs={{0,3},{1,2},{2,1},{3,0},{4,7},{5,6},{6,5},{7,4},{8,11},{9,10},{10,... | collective-permute-start | bytes 786440 | tf_op jit(solution)/shard_map/ppermute | solution.py:493
  29.8 4.5 %collective-permute-done.6.other = f32[8,32,256]{2,1,0:T(8,128)S(1)} collective-permute-done((f32[8,32,256]{2,1,0:T(8,128)S(1)}, f32[8,32,256]{2,1,0:T(8,128)S(1)}, u32[]{:S(2)}, u32[]{:S(2)}) %collective-permute-start.6) | collective-permute-done | bytes 262176 | tf_op jit(solution)/shard_map/ppermute | solution.py:493
  34.3 0.1 update.1.mine
  34.3 0.0 copy-start.3
  34.3 2.8 %collective-permute-start.7 = (f32[8,32,256]{2,1,0:T(8,128)S(1)}, f32[8,32,256]{2,1,0:T(8,128)S(1)}, u32[]{:S(2)}, u32[]{:S(2)}) collective-permute-start(f32[8,32,256]{2,1,0:T(8,128)S(1)} %update.1.mine), channel_id=1, source_target_pairs={{0,1},{1,0},{2,3},{3,2},{4,5},{5,4},{6,7},{7,6},{8,9},{9,8},{10,11... | collective-permute-start | bytes 786440 | tf_op jit(solution)/shard_map/ppermute | solution.py:497
  37.1 0.1 copy.11.owner_col
  37.2 0.7 copy-done.5
  37.9 0.1 copy.12.index_col
  38.0 2.5 %moment_rows.1 = f32[64,128]{1,0:T(8,128)S(1)} custom-call(f32[8,64,256]{2,1,0:T(8,128)S(1)} %copy-done, f32[8,32,256]{2,1,0:T(8,128)S(1)} %pair_correction.1.mine.correction, s32[8,64,256]{2,1,0:T(8,128)S(1)} %copy-done.2, s32[1,16]{1,0:T(1,128)S(1)} %bitcast.11, s32[16,1]{1,0:T(8,128)S(1)} %copy.11.owner_col, s32[16,1]{1,0:T(8,128)S(1)} %copy.12.index_col), custom_call_target="tpu_custom_call" | custom-call | tf_op jit(solution)/shard_map/moment_rows/pallas_call | solution.py:381
  40.4 24.4 %all_to_all.11 = f32[8,8,128]{2,1,0:T(8,128)S(1)} all-to-all(f32[8,8,128]{2,1,0:T(8,128)S(1)} %bitcast.8), channel_id=1, replica_groups=mesh['tile'=8,'view'=4] {'tile'}, dimensions={0} | all-to-all | bytes 65536 | tf_op jit(solution)/shard_map/all_to_all | solution.py:495
  64.9 0.3 segment_table.1.first
  65.1 2.4 %collective-permute-start.10 = (f32[16,128]{1,0:T(8,128)S(1)}, f32[16,128]{1,0:T(8,128)S(1)}, u32[]{:S(2)}, u32[]{:S(2)}) collective-permute-start(f32[16,128]{1,0:T(8,128)S(1)} %segment_table.1.first), channel_id=1, source_target_pairs={{0,3},{1,2},{2,1},{3,0},{4,7},{5,6},{6,5},{7,4},{8,11},{9,10},{10,... | collective-permute-start | bytes 24584 | tf_op jit(solution)/shard_map/ppermute | solution.py:500
  67.5 2.0 %collective-permute-start.9 = (f32[16,128]{1,0:T(8,128)S(1)}, f32[16,128]{1,0:T(8,128)S(1)}, u32[]{:S(2)}, u32[]{:S(2)}) collective-permute-start(f32[16,128]{1,0:T(8,128)S(1)} %segment_table.1.first), channel_id=1, source_target_pairs={{0,2},{1,3},{2,0},{3,1},{4,6},{5,7},{6,4},{7,5},{8,10},{9,11},{10,... | collective-permute-start | bytes 24584 | tf_op jit(solution)/shard_map/ppermute | solution.py:500
  69.6 1.1 %collective-permute-done.10.fourth = f32[16,128]{1,0:T(8,128)S(1)} collective-permute-done((f32[16,128]{1,0:T(8,128)S(1)}, f32[16,128]{1,0:T(8,128)S(1)}, u32[]{:S(2)}, u32[]{:S(2)}) %collective-permute-start.10) | collective-permute-done | bytes 8224 | tf_op jit(solution)/shard_map/ppermute | solution.py:500
  70.7 0.5 collective-permute-done.8.second
  71.2 0.9 %collective-permute-done.9.third = f32[16,128]{1,0:T(8,128)S(1)} collective-permute-done((f32[16,128]{1,0:T(8,128)S(1)}, f32[16,128]{1,0:T(8,128)S(1)}, u32[]{:S(2)}, u32[]{:S(2)}) %collective-permute-start.9) | collective-permute-done | bytes 8224 | tf_op jit(solution)/shard_map/ppermute | solution.py:500
  72.1 1.4 %finish.1 = (f32[8,64,256]{2,1,0:T(8,128)}, f32[10,128]{1,0:T(8,128)}) custom-call(f32[8,32,256]{2,1,0:T(8,128)S(1)} %update.1.mine, f32[8,32,256]{2,1,0:T(8,128)S(1)} %collective-permute-done.7.other, f32[16,128]{1,0:T(8,128)S(1)} %segment_table.1.first, f32[16,128]{1,0:T(8,128)S(1)} %collective-permute-done.8.second, ...), custom_call_target="tpu_custom_call" | custom-call | tf_op jit(solution)/shard_map/finish/pallas_call | solution.py:447
  (17 shorter events, 0.1 us)
Async XLA Ops:
  0.7 2.4 %copy-start.1 = (f32[1,8,64,256]{3,2,1,0:T(8,128)S(1)}, f32[1,8,64,256]{3,2,1,0:T(8,128)}, u32[]{:S(2)}) copy-start(f32[1,8,64,256]{3,2,1,0:T(8,128)} %measured.1) | copy-start | bytes 1572868
  1.9 13.2 %copy-start = (f32[8,64,256]{2,1,0:T(8,128)S(1)}, f32[8,64,256]{2,1,0:T(8,128)}, u32[]{:S(2)}) copy-start(f32[8,64,256]{2,1,0:T(8,128)} %estimate.5) | copy-start | bytes 1572868
  1.9 13.1 %collective-permute-start.1 = (f32[7,48,256]{2,1,0:T(8,128)S(1)}, f32[7,48,256]{2,1,0:T(8,128)S(1)}, u32[]{:S(2)}, u32[]{:S(2)}) collective-permute-start(f32[7,48,256]{2,1,0:T(8,128)S(1)} %get-tuple-element.15), channel_id=1, source_target_pairs={{0,4},{4,0},{8,12},{12,8},{16,20},{20,16},{24,28},{28,24},{1,5},{5... | collective-permute-start | bytes 1032200 | tf_op jit(solution)/shard_map/ppermute | solution.py:482
  2.4 12.6 %collective-permute-start.2 = (f32[7,48,256]{2,1,0:T(8,128)S(1)}, f32[7,48,256]{2,1,0:T(8,128)S(1)}, u32[]{:S(2)}, u32[]{:S(2)}) collective-permute-start(f32[7,48,256]{2,1,0:T(8,128)S(1)} %get-tuple-element.14), channel_id=1, source_target_pairs={{4,8},{12,16},{20,24},{8,4},{16,12},{24,20},{5,9},{13,17},{21,25},... | collective-permute-start | bytes 1032200 | tf_op jit(solution)/shard_map/ppermute | solution.py:480
  3.1 2.9 %copy-start.4 = (f32[1,3,15]{2,0,1:T(1,128)S(1)}, f32[1,3,15]{2,0,1:T(1,128)}, u32[]{:S(2)}) copy-start(f32[1,3,15]{2,0,1:T(1,128)} %param.8) | copy-start | bytes 544
  3.1 11.9 %collective-permute-start.3 = (f32[8,48,256]{2,1,0:T(8,128)S(1)}, f32[8,48,256]{2,1,0:T(8,128)S(1)}, u32[]{:S(2)}, u32[]{:S(2)}) collective-permute-start(f32[8,48,256]{2,1,0:T(8,128)S(1)} %dynamic-slice_bitcast_fusion), channel_id=1, source_target_pairs={{0,1},{1,0},{2,3},{3,2},{4,5},{5,4},{6,7},{7,6},{8,9},{9,8},{10,11... | collective-permute-start | bytes 1179656 | tf_op jit(solution)/shard_map/ppermute | solution.py:483
  6.0 7.7 %collective-permute-start = (f32[1,3,15]{2,1,0:T(4,128)S(1)}, f32[1,3,15]{2,1,0:T(4,128)S(1)}, u32[]{:S(2)}, u32[]{:S(2)}) collective-permute-start(f32[1,3,15]{2,1,0:T(4,128)S(1)} %get-tuple-element.16.taps_own), channel_id=1, source_target_pairs={{0,1},{1,0},{2,3},{3,2},{4,5},{5,4},{6,7},{7,6},{8,9},{9,8},{10,11... | collective-permute-start | bytes 548 | tf_op jit(solution)/shard_map/ppermute | solution.py:481
  20.5 3.7 %collective-permute-start.4 = (f32[2,7,32,256]{3,2,1,0:T(8,128)S(1)}, f32[2,7,32,256]{3,2,1,0:T(8,128)S(1)}, u32[]{:S(2)}, u32[]{:S(2)}) collective-permute-start(f32[2,7,32,256]{3,2,1,0:T(8,128)S(1)} %get-tuple-element.12), channel_id=1, source_target_pairs={{0,4},{4,0},{8,12},{12,8},{16,20},{20,16},{24,28},{28,24},{1,5},{5... | collective-permute-start | bytes 1376264 | tf_op jit(solution)/shard_map/ppermute | solution.py:491
  22.7 1.4 %collective-permute-start.5 = (f32[2,7,32,256]{3,2,1,0:T(8,128)S(1)}, f32[2,7,32,256]{3,2,1,0:T(8,128)S(1)}, u32[]{:S(2)}, u32[]{:S(2)}) collective-permute-start(f32[2,7,32,256]{3,2,1,0:T(8,128)S(1)} %get-tuple-element.13), channel_id=1, source_target_pairs={{4,8},{12,16},{20,24},{8,4},{16,12},{24,20},{5,9},{13,17},{21,25},... | collective-permute-start | bytes 1376264 | tf_op jit(solution)/shard_map/ppermute | solution.py:490
  25.7 12.3 %copy-start.2 = (s32[8,64,256]{2,1,0:T(8,128)S(1)}, s32[8,64,256]{2,1,0:T(8,128)}, u32[]{:S(2)}) copy-start(s32[8,64,256]{2,1,0:T(8,128)} %labels.1) | copy-start | bytes 1572868
  25.7 8.5 %collective-permute-start.6 = (f32[8,32,256]{2,1,0:T(8,128)S(1)}, f32[8,32,256]{2,1,0:T(8,128)S(1)}, u32[]{:S(2)}, u32[]{:S(2)}) collective-permute-start(f32[8,32,256]{2,1,0:T(8,128)S(1)} %pair_correction.1.mine.correction), channel_id=1, source_target_pairs={{0,3},{1,2},{2,1},{3,0},{4,7},{5,6},{6,5},{7,4},{8,11},{9,10},{10,... | collective-permute-start | bytes 786440 | tf_op jit(solution)/shard_map/ppermute | solution.py:493
  34.3 2.8 %copy-start.3 = (s32[1,16,1]{1,2,0:T(1,128)S(1)}, s32[1,16,1]{1,2,0:T(1,128)}, u32[]{:S(2)}) copy-start(s32[1,16,1]{1,2,0:T(1,128)} %param.10) | copy-start | bytes 196
  34.3 37.7 %collective-permute-start.7 = (f32[8,32,256]{2,1,0:T(8,128)S(1)}, f32[8,32,256]{2,1,0:T(8,128)S(1)}, u32[]{:S(2)}, u32[]{:S(2)}) collective-permute-start(f32[8,32,256]{2,1,0:T(8,128)S(1)} %update.1.mine), channel_id=1, source_target_pairs={{0,1},{1,0},{2,3},{3,2},{4,5},{5,4},{6,7},{7,6},{8,9},{9,8},{10,11... | collective-permute-start | bytes 786440 | tf_op jit(solution)/shard_map/ppermute | solution.py:497
  37.2 0.7 copy-start.5
  65.1 5.5 %collective-permute-start.10 = (f32[16,128]{1,0:T(8,128)S(1)}, f32[16,128]{1,0:T(8,128)S(1)}, u32[]{:S(2)}, u32[]{:S(2)}) collective-permute-start(f32[16,128]{1,0:T(8,128)S(1)} %segment_table.1.first), channel_id=1, source_target_pairs={{0,3},{1,2},{2,1},{3,0},{4,7},{5,6},{6,5},{7,4},{8,11},{9,10},{10,... | collective-permute-start | bytes 24584 | tf_op jit(solution)/shard_map/ppermute | solution.py:500
  67.5 3.7 %collective-permute-start.8 = (f32[16,128]{1,0:T(8,128)S(1)}, f32[16,128]{1,0:T(8,128)S(1)}, u32[]{:S(2)}, u32[]{:S(2)}) collective-permute-start(f32[16,128]{1,0:T(8,128)S(1)} %segment_table.1.first), channel_id=1, source_target_pairs={{0,1},{1,0},{2,3},{3,2},{4,5},{5,4},{6,7},{7,6},{8,9},{9,8},{10,11... | collective-permute-start | bytes 24584 | tf_op jit(solution)/shard_map/ppermute | solution.py:500
  67.5 4.5 %collective-permute-start.9 = (f32[16,128]{1,0:T(8,128)S(1)}, f32[16,128]{1,0:T(8,128)S(1)}, u32[]{:S(2)}, u32[]{:S(2)}) collective-permute-start(f32[16,128]{1,0:T(8,128)S(1)} %segment_table.1.first), channel_id=1, source_target_pairs={{0,2},{1,3},{2,0},{3,1},{4,6},{5,7},{6,4},{7,5},{8,10},{9,11},{10,... | collective-permute-start | bytes 24584 | tf_op jit(solution)/shard_map/ppermute | solution.py:500

commit v2 on v1

v2 whole, which is shorter than its diff:
```python
import functools

import jax
import jax.numpy as jnp
from jax import lax
from jax.experimental import pallas as pl
from jax.experimental.pallas import tpu as pltpu
from jax.sharding import PartitionSpec as P

MOM = 10
ROWS = 8
NUC_DEV = 128
LANES = 128
F32 = jnp.float32
BF16 = jnp.bfloat16
ANY = pl.BlockSpec(memory_space=pl.ANY)
VMEM = pl.BlockSpec(memory_space=pltpu.VMEM)
LIMIT = 32 * 1024 * 1024


def half_of(view):
    return (view ^ (view >> 1)) & 1


def split(value):
    upper = value.astype(BF16)
    return upper, (value - upper.astype(F32)).astype(BF16)


def band(taps, shape, offset):
    rows = lax.broadcasted_iota(jnp.int32, shape, 0)
    cols = lax.broadcasted_iota(jnp.int32, shape, 1)
    place = cols - rows + offset
    result = jnp.zeros(shape, F32)
    for step, tap in enumerate(taps):
        result = jnp.where(place == step, tap, result)
    return result


def depth_terms(source, weights, first, last, planes, flipped):
    radius = (len(weights) - 1) // 2
    totals = {plane: None for plane in planes}
    for place in range(first, last):
        block = None
        for plane in planes:
            step = plane - place + radius if flipped else place - plane + radius
            if 0 <= step < len(weights):
                block = source(place) if block is None else block
                term = weights[step] * block
                totals[plane] = term if totals[plane] is None else totals[plane] + term
    return totals


def chunks(rows, across):
    return [(slice(row, row + 16), slice(lane, lane + LANES)) for row in range(0, rows, 16) for lane in range(0, across, LANES)]


def rims_out_kernel(estimate, to_far, to_near):
    planes, radius, rows = estimate.shape[0], to_far.shape[0], to_far.shape[1]
    odd = lax.axis_index("tile") % 2
    half = half_of(lax.axis_index("view"))
    start = pl.multiple_of((estimate.shape[1] - rows) * half, 8)
    to_far[...] = estimate[pl.ds(odd, radius), pl.ds(start, rows)]
    to_near[...] = estimate[pl.ds(1 - odd, radius), pl.ds(start, rows)]


def rims_out(estimate, radius, rows):
    shape = jax.ShapeDtypeStruct((radius, rows, estimate.shape[2]), F32)
    return pl.pallas_call(
        rims_out_kernel,
        out_shape=(shape, shape),
        in_specs=[VMEM],
        out_specs=(VMEM, VMEM),
        compiler_params=pltpu.CompilerParams(vmem_limit_bytes=LIMIT),
        name="rims_out",
    )(estimate)


def view_out_kernel(seen, measured, kernels, packed):
    planes, height = measured.shape[1], measured.shape[2]
    half = half_of(lax.axis_index("view"))
    start = pl.multiple_of((height - seen) * (1 - half), 8)
    for plane in range(planes):
        packed[plane * seen : (plane + 1) * seen] = measured[0, plane, pl.ds(start, seen)]
    packed[planes * seen :] = jnp.zeros((8, packed.shape[1]), F32)
    packed[planes * seen : planes * seen + kernels.shape[1], : kernels.shape[2]] = kernels[0]


def view_out(measured, kernels, seen):
    _, planes, _, across = measured.shape
    return pl.pallas_call(
        functools.partial(view_out_kernel, seen),
        out_shape=jax.ShapeDtypeStruct((planes * seen + 8, across), F32),
        in_specs=[VMEM, VMEM],
        out_specs=VMEM,
        compiler_params=pltpu.CompilerParams(vmem_limit_bytes=LIMIT),
        name="view_out",
    )(measured, kernels)


def prepare_kernel(packed, taps, source, estimate, wide, tall, back, part, spread):
    half = half_of(lax.axis_index("view"))
    across = wide.shape[-1]
    rows, keep, seen = part.shape[1], back.shape[0], tall.shape[0]
    planes = estimate.shape[0]
    radius = (taps - 1) // 2
    raw = source[source.shape[0] - 8 : source.shape[0] - 5, :taps] if packed else source[0]
    weights = raw / jnp.sum(raw, axis=-1, keepdims=True)
    deep, high, flat = [[weights[axis : axis + 1, t : t + 1] for t in range(taps)] for axis in range(3)]
    start = pl.multiple_of((2 * keep - rows) * half, 16)
    seen_start = (2 * keep - seen) * half
    upper, lower = split(band(flat[::-1], (across, across), radius))
    wide[0, 0] = upper
    wide[0, 1] = lower
    upper, lower = split(band(flat, (across, across), radius))
    wide[1, 0] = upper
    wide[1, 1] = lower
    upper, lower = split(band(high, (seen, rows), radius + start - seen_start))
    tall[...] = jnp.concatenate([upper, upper, lower], axis=1)
    upper, lower = split(band(high[::-1], (keep, rows), radius + seen_start - keep * half))
    back[...] = jnp.concatenate([upper, upper, lower], axis=1)
    factors = [jnp.broadcast_to(tap, (16, LANES)) for tap in deep]
    spread[...] = jnp.zeros_like(spread)
    for step in range(taps):
        spread[step : step + 1] = factors[step][:1]
    for row, lane in chunks(rows, across):
        where = pl.ds(pl.multiple_of(start + row.start, 16), 16)
        terms = depth_terms(
            lambda place: estimate[place, where, lane], factors, 0, planes, range(planes), False
        )
        for plane, block in terms.items():
            part[plane, row, lane] = block


def prepare(packed, taps, source, estimate, rows, seen, keep):
    planes, _, across = estimate.shape
    return pl.pallas_call(
        functools.partial(prepare_kernel, packed, taps),
        out_shape=(
            jax.ShapeDtypeStruct((2, 2, across, across), BF16),
            jax.ShapeDtypeStruct((seen, 3 * rows), BF16),
            jax.ShapeDtypeStruct((keep, 3 * rows), BF16),
            jax.ShapeDtypeStruct((planes, rows, across), F32),
            jax.ShapeDtypeStruct((-(-taps // 8) * 8, LANES), F32),
        ),
        in_specs=[VMEM, VMEM],
        out_specs=(VMEM,) * 5,
        compiler_params=pltpu.CompilerParams(vmem_limit_bytes=LIMIT),
        name="prepare",
    )(source, estimate)


def spread_factors(spread, taps):
    return [jnp.broadcast_to(spread[step : step + 1, :], (16, LANES)) for step in range(taps)]


def forward_kernel(
    wide_own, tall_own, back_own, part_own, spread_own,
    wide_other, tall_other, back_other, part_other, spread_other,
    near, far, measured, swapped,
    field, send_near, send_far,
    blur_hi, blur_lo, plane_hi, plane_lo,
):
    planes, radius = part_own.shape[0], near.shape[0]
    rows, across = near.shape[1], near.shape[2]
    keep, seen = back_own.shape[0], tall_own.shape[0]
    taps = 2 * radius + 1
    even = lax.axis_index("tile") % 2 == 0
    half = half_of(lax.axis_index("view"))
    seen_start = pl.multiple_of((2 * keep - seen) * half, 8)
    both = (
        (wide_own, tall_own, back_own, part_own, spread_own),
        (wide_other, tall_other, back_other, part_other, spread_other),
    )
    for which, (wide, tall, back, part, spread) in enumerate(both):
        factors = spread_factors(spread, taps)
        for row, lane in chunks(rows, across):

            def rim(place):
                if place < 0:
                    at = place + radius
                    return jnp.where(even, far[at, row, lane], near[at, row, lane])
                at = place - planes
                return jnp.where(even, near[at, row, lane], far[at, row, lane])

            below = depth_terms(rim, factors, -radius, 0, range(planes), False)
            above = depth_terms(rim, factors, planes, planes + radius, range(planes), False)
            for plane in range(planes):
                block = part[plane, row, lane]
                for term in (below[plane], above[plane]):
                    block = block if term is None else block + term
                upper, lower = split(block)
                at = slice(plane * rows + row.start, plane * rows + row.stop)
                blur_hi[which, at, lane] = upper
                blur_lo[which, at, lane] = lower
    for which, (wide, tall, back, part, spread) in enumerate(both):
        upper, lower = wide[0, 0], wide[0, 1]
        lines = jnp.dot(blur_hi[which], upper, preferred_element_type=F32)
        lines += jnp.dot(blur_lo[which], upper, preferred_element_type=F32)
        lines += jnp.dot(blur_hi[which], lower, preferred_element_type=F32)
        for plane in range(planes):
            hi, lo = split(lines[plane * rows : (plane + 1) * rows])
            forward = jnp.dot(
                tall[...], jnp.concatenate([hi, lo, hi], axis=0), preferred_element_type=F32
            )
            if which == 0:
                view = measured[0, plane, pl.ds(seen_start, seen), :]
            else:
                view = swapped[plane * seen : (plane + 1) * seen]
            ratio = view / forward
            if rows > seen:
                ratio = jnp.concatenate([ratio, jnp.zeros((rows - seen, across), F32)], axis=0)
            hi, lo = split(ratio)
            turned = jnp.dot(
                back[...], jnp.concatenate([hi, lo, hi], axis=0), preferred_element_type=F32
            )
            hi, lo = split(turned)
            plane_hi[which, plane * keep : (plane + 1) * keep] = hi
            plane_lo[which, plane * keep : (plane + 1) * keep] = lo
        upper, lower = wide[1, 0], wide[1, 1]
        lines = jnp.dot(plane_hi[which], upper, preferred_element_type=F32)
        lines += jnp.dot(plane_lo[which], upper, preferred_element_type=F32)
        lines += jnp.dot(plane_hi[which], lower, preferred_element_type=F32)
        field[which] = lines.reshape(planes, keep, across)
    for row, lane in chunks(keep, across):
        below, above = [], []
        for which in range(2):
            factors = spread_factors(both[which][4], taps)
            source = lambda place: field[which, place, row, lane]
            below.append(depth_terms(source, factors, 0, planes, range(-radius, 0), True))
            above.append(depth_terms(source, factors, 0, planes, range(planes, planes + radius), True))
        for at in range(radius):
            down = below[0][at - radius] + below[1][at - radius]
            up = above[0][at + planes] + above[1][at + planes]
            send_near[at, row, lane] = jnp.where(even, up, down)
            send_far[at, row, lane] = jnp.where(even, down, up)


def ratio_fields(own, others, near, far, measured, swapped):
    keep = own[2].shape[0]
    planes = own[3].shape[0]
    radius, rows, across = near.shape
    return pl.pallas_call(
        forward_kernel,
        out_shape=(
            jax.ShapeDtypeStruct((2, planes, keep, across), F32),
            jax.ShapeDtypeStruct((radius, keep, across), F32),
            jax.ShapeDtypeStruct((radius, keep, across), F32),
        ),
        in_specs=[VMEM] * 14,
        out_specs=(VMEM, VMEM, VMEM),
        scratch_shapes=[
            pltpu.VMEM((2, planes * rows, across), BF16),
            pltpu.VMEM((2, planes * rows, across), BF16),
            pltpu.VMEM((2, planes * keep, across), BF16),
            pltpu.VMEM((2, planes * keep, across), BF16),
        ],
        compiler_params=pltpu.CompilerParams(vmem_limit_bytes=LIMIT),
        name="ratio_fields",
    )(*own, *others, near, far, measured, swapped)


def own_kernel(taps, spread_own, spread_other, field, inner):
    planes, keep, across = inner.shape
    factors = [spread_factors(spread, taps) for spread in (spread_own, spread_other)]
    for row, lane in chunks(keep, across):
        parts = [
            depth_terms(
                lambda place: field[which, place, row, lane],
                factors[which], 0, planes, range(planes), True,
            )
            for which in range(2)
        ]
        for plane in range(planes):
            inner[plane, row, lane] = parts[0][plane] + parts[1][plane]


def own_planes(taps, spread_own, spread_other, field):
    return pl.pallas_call(
        functools.partial(own_kernel, taps),
        out_shape=jax.ShapeDtypeStruct(field.shape[1:], F32),
        in_specs=[VMEM] * 3,
        out_specs=VMEM,
        compiler_params=pltpu.CompilerParams(vmem_limit_bytes=LIMIT),
        name="own_planes",
    )(spread_own, spread_other, field)


def rims_kernel(inner, near, far, correction):
    planes, radius = inner.shape[0], near.shape[0]
    even = lax.axis_index("tile") % 2 == 0
    for plane in range(planes):
        total = inner[plane]
        if plane < radius:
            total += jnp.where(even, far[plane], near[plane])
        if plane >= planes - radius:
            at = plane - planes + radius
            total += jnp.where(even, near[at], far[at])
        correction[plane] = total


def add_rims(inner, near, far):
    return pl.pallas_call(
        rims_kernel,
        out_shape=jax.ShapeDtypeStruct(inner.shape, F32),
        in_specs=[VMEM] * 3,
        out_specs=VMEM,
        compiler_params=pltpu.CompilerParams(vmem_limit_bytes=LIMIT),
        name="add_rims",
    )(inner, near, far)


def update_kernel(views, estimate, mine, other, after, result):
    keep = mine.shape[1]
    half = half_of(lax.axis_index("view"))
    held = estimate[:, pl.ds(pl.multiple_of(keep * half, 8), keep)]
    result[...] = held * (mine[...] + other[...]) * (1.0 / views)


def update(views, estimate, mine, other, after):
    return pl.pallas_call(
        functools.partial(update_kernel, views),
        out_shape=jax.ShapeDtypeStruct(mine.shape, F32),
        in_specs=[VMEM, VMEM, VMEM, ANY],
        out_specs=VMEM,
        compiler_params=pltpu.CompilerParams(vmem_limit_bytes=LIMIT),
        name="update",
    )(estimate, mine, other, after)


def moments_kernel(
    views, depth_total, estimate, correction, labels, owner_row, owner_col, index_col,
    sent, held, sums,
):
    planes, keep, across = correction.shape
    height_total = estimate.shape[1]
    slots = owner_row.shape[1]
    half = half_of(lax.axis_index("view"))
    first = lax.axis_index("tile") * planes
    start = pl.multiple_of(keep * half, 8)
    held[...] = estimate[:, pl.ds(start, keep)] * correction[...] * (1.0 / views)
    group = 16
    columns = lax.broadcasted_iota(jnp.int32, (across, LANES), 1)
    spot = (lax.broadcasted_iota(jnp.int32, (across, LANES), 0).astype(F32) + 0.5) / across
    one, line, square = jnp.ones_like(spot), spot, spot * spot

    def placed(*pairs):
        result = jnp.zeros((across, LANES), F32)
        for lane, value in pairs:
            result = jnp.where(columns == lane, value, result)
        return result

    factors = jnp.concatenate(
        [
            placed((0, one), (3, line), (6, square)),
            placed((2, one), (9, line)),
            placed((5, one)),
            placed((1, one), (8, line)),
            placed((7, one)),
            placed((4, one)),
        ],
        axis=0,
    )
    base = lax.broadcasted_iota(jnp.int32, (8, across), 0)

    def one_group(number, carry):
        def one_slot(inner, carry):
            slot = number * group + inner
            parts = [jnp.zeros((8, across), F32) for _ in range(6)]
            for row in range(0, keep, 8):
                high = ((base + (row + start)).astype(F32) + 0.5) / height_total
                flat = [jnp.zeros((8, across), F32) for _ in range(3)]
                for plane in range(planes):
                    deep = ((first + plane).astype(F32) + 0.5) / depth_total
                    hit = labels[plane, pl.ds(pl.multiple_of(start + row, 8), 8)] == slot
                    value = jnp.where(hit, held[plane, row : row + 8], 0.0)
                    flat[0] = flat[0] + value
                    value = value * deep
                    flat[1] = flat[1] + value
                    flat[2] = flat[2] + value * deep
                scaled = flat[0] * high
                parts[0] = parts[0] + flat[0]
                parts[1] = parts[1] + scaled
                parts[2] = parts[2] + scaled * high
                parts[3] = parts[3] + flat[1]
                parts[4] = parts[4] + flat[1] * high
                parts[5] = parts[5] + flat[2]
            at = pl.multiple_of(inner * 8, 8)
            sums[pl.ds(at, 8), :] = jnp.concatenate(parts, axis=1)
            return carry

        lax.fori_loop(0, group, one_slot, 0)
        table = jnp.dot(
            sums[...], factors, precision=lax.Precision.HIGHEST, preferred_element_type=F32
        )
        table = jnp.sum(table.reshape(group, 8, LANES), axis=1)
        at = pl.multiple_of(number * group, group)
        ids = index_col[pl.ds(at, group), :].astype(F32)
        lanes = lax.broadcasted_iota(jnp.int32, (group, LANES), 1)
        table = jnp.where(lanes == MOM, ids, table)
        owner = owner_col[pl.ds(at, group), :]
        earlier = lax.broadcasted_iota(jnp.int32, (group, slots), 1) < (
            lax.broadcasted_iota(jnp.int32, (group, slots), 0) + number * group
        )
        same = (owner == owner_row[...]) & earlier
        rank = jnp.sum(same.astype(F32), axis=1, keepdims=True).astype(jnp.int32)
        place = owner * ROWS + rank
        spots = lax.broadcasted_iota(jnp.int32, (group, sent.shape[0]), 1)
        picked = (place == spots).astype(F32)
        sent[...] += lax.dot_general(
            picked, table, (((0,), (0,)), ((), ())),
            precision=lax.Precision.HIGHEST, preferred_element_type=F32,
        )
        return carry

    sent[...] = jnp.zeros_like(sent)
    lax.fori_loop(0, slots // group, one_group, 0)


def moment_rows(views, tiles, estimate, correction, labels, label_owner, label_index):
    slots = label_index.shape[1]
    planes, keep, across = correction.shape
    return pl.pallas_call(
        functools.partial(moments_kernel, views, tiles * planes),
        out_shape=jax.ShapeDtypeStruct((tiles * ROWS, LANES), F32),
        in_specs=[VMEM] * 6,
        out_specs=VMEM,
        scratch_shapes=[
            pltpu.VMEM(correction.shape, F32),
            pltpu.VMEM((16 * 8, 6 * across), F32),
        ],
        compiler_params=pltpu.CompilerParams(vmem_limit_bytes=LIMIT),
        name="moment_rows",
    )(
        estimate, correction, labels,
        label_owner.reshape(1, slots), label_owner.reshape(slots, 1), label_index.reshape(slots, 1),
    )


def segments_kernel(rows, table):
    values = rows[...]
    ids = values[:, MOM : MOM + 1].astype(jnp.int32)
    spots = lax.broadcasted_iota(jnp.int32, (values.shape[0], NUC_DEV), 1)
    picked = (ids == spots).astype(F32)
    full = lax.dot_general(
        values, picked, (((0,), (0,)), ((), ())),
        precision=lax.Precision.HIGHEST, preferred_element_type=F32,
    )
    table[...] = full[: table.shape[0]]


def segment_table(rows):
    return pl.pallas_call(
        segments_kernel,
        out_shape=jax.ShapeDtypeStruct((16, NUC_DEV), F32),
        in_specs=[VMEM],
        out_specs=VMEM,
        compiler_params=pltpu.CompilerParams(vmem_limit_bytes=LIMIT),
        name="segment_table",
    )(rows)


def finish_kernel(scale, mine, other, first, second, third, fourth, whole, moments, sems):
    keep = mine.shape[1]
    half = half_of(lax.axis_index("view"))
    copies = [
        pltpu.make_async_copy(
            mine, whole.at[:, pl.ds(pl.multiple_of(keep * half, 8), keep)], sems.at[0]
        ),
        pltpu.make_async_copy(
            other, whole.at[:, pl.ds(pl.multiple_of(keep * (1 - half), 8), keep)], sems.at[1]
        ),
    ]
    for copy in copies:
        copy.start()
    table = (first[...] + second[...]) + (third[...] + fourth[...])
    mass = table[0:1]
    lines = lax.broadcasted_iota(jnp.int32, table.shape, 0)
    result = jnp.where(lines == 0, table * scale, table / jnp.maximum(mass, 1.0))
    moments[...] = result[:MOM]
    for copy in copies:
        copy.wait()


def finish(scale, mine, other, tables):
    planes, keep, across = mine.shape
    return pl.pallas_call(
        functools.partial(finish_kernel, scale),
        out_shape=(
            jax.ShapeDtypeStruct((planes, 2 * keep, across), F32),
            jax.ShapeDtypeStruct((MOM, NUC_DEV), F32),
        ),
        in_specs=[ANY, ANY, VMEM, VMEM, VMEM, VMEM],
        out_specs=(ANY, VMEM),
        scratch_shapes=[pltpu.SemaphoreType.DMA((2,))],
        compiler_params=pltpu.CompilerParams(vmem_limit_bytes=LIMIT),
        name="finish",
    )(mine, other, *tables)


def on_device(estimate, measured, kernels, labels, label_owner, label_index):
    tiles, views = lax.axis_size("tile"), lax.axis_size("view")
    planes, height, across = estimate.shape
    taps = kernels.shape[2]
    radius = (taps - 1) // 2
    keep = height // 2
    seen = min(height, -(-(keep + radius) // 8) * 8)
    rows = min(height, -(-(keep + 2 * radius) // 16) * 16)
    near_pairs = [(i, i ^ 1) for i in range(tiles)]
    far_pairs = [(i, i + 1) for i in range(1, tiles - 1, 2)]
    far_pairs = far_pairs + [(b, a) for a, b in far_pairs]
    partner = [(i, i ^ 1) for i in range(views)]
    across_pairs = [(i, i ^ 3) for i in range(views)]

    to_far, to_near = rims_out(estimate, radius, rows)
    far = lax.ppermute(to_far, "tile", far_pairs)
    swapped = lax.ppermute(view_out(measured, kernels, seen), "view", partner)
    near = lax.ppermute(to_near, "tile", near_pairs)
    own = prepare(False, taps, kernels, estimate, rows, seen, keep)
    others = prepare(True, taps, swapped, estimate, rows, seen, keep)
    field, field_near, field_far = ratio_fields(own, others, near, far, measured, swapped)
    rim_far = lax.ppermute(field_far, "tile", far_pairs)
    rim_near = lax.ppermute(field_near, "tile", near_pairs)
    inner = own_planes(taps, own[4], others[4], field)
    mine = add_rims(inner, rim_near, rim_far)
    other = lax.ppermute(mine, "view", across_pairs)
    sent = moment_rows(views, tiles, estimate, mine, labels, label_owner, label_index)
    got = lax.all_to_all(sent, "tile", split_axis=0, concat_axis=0, tiled=True)
    new_half = update(views, estimate, mine, other, got)
    new_other = lax.ppermute(new_half, "view", partner)
    table = segment_table(got)
    tables = [table] + [
        lax.ppermute(table, "view", [(i, i ^ step) for i in range(views)]) for step in (1, 2, 3)
    ]
    scale = label_index.shape[1] / (planes * height * across)
    new_estimate, moments = finish(scale, new_half, new_other, tables)
    return new_estimate, moments


def solution(mesh):
    placed = (
        P("tile", None, None),
        P("view", "tile", None, None),
        P("view", None, None),
        P("tile", None, None),
        P("tile", None, None),
        P("tile", None),
    )
    return jax.shard_map(
        on_device,
        mesh=mesh,
        in_specs=placed,
        out_specs=(P("tile", None, None), P(None, "tile")),
        check_vma=False,
    )
```

time: 73.7 us -> 56 us (0.76)
  blocking collectives: 24.4 us -> 17.9 us
  waiting for transfers between devices: 14.8 us -> 9.21 us
  starting transfers between devices: 18.8 us -> 15.6 us
  Pallas kernels: 12.5 us -> 10.4 us
    all_to_all x1, blocking collectives: 24.4 us -> 17.9 us  [on_device(): got = lax.all_to_all(sent, 'tile', split_axis=0, concat_axis=0, tiled=True)]
    ppermute x1, waiting for transfers between devices: 4.46 us -> 0.01 us  [on_device(): other = lax.ppermute(mine, 'view', across_pairs)]
    ppermute x1, starting transfers between devices: 2.78 us -> 0.07 us  [on_device(): new_other = lax.ppermute(new_half, 'view', partner)]
    pallas_call x1, Pallas kernels: 5.45 us -> 3.52 us  [ratio_fields(): pl.pallas_call(forward_kernel, out_shape=(jax.ShapeDtypeStruct((2, planes...]
    ppermute x2 -> x1, waiting for transfers between devices: 7.09 us -> 5.37 us  [on_device(): swapped = lax.ppermute(view_out(measured, kernels, seen), 'view', partner)]
    dynamic_slice x2 -> x0, local copies, waits for them, and re-layouts: 1.23 us -> none  [the longest x1 1.2 us: on_device(): lax.dynamic_slice(estimate, (parity, shift, 0), (radius, rows, across))]
    ppermute x3, waiting for transfers between devices: 2.5 us -> 3.67 us  [on_device(): lax.ppermute(table, 'view', [(i, i ^ step) for i in range(views)])]
    unnamed x13 -> x15, local copies, waits for them, and re-layouts: 0.69 us -> 1.72 us
  transfers between devices with their start and end apart: 11 -> 10, of which waited for: 6 -> 3; matrix products, arithmetic and copies ran while one was open for 0% -> 0% of each run, Pallas kernels for 5% -> 10%
where the time goes in v2:
time: 56 us; the launch traced here: 55.8 us
  blocking collectives  17.9 us (32%)
  starting transfers between devices  15.6 us (28%)
  Pallas kernels  10.4 us (19%)
  waiting for transfers between devices  9.21 us (16%)
  local copies, waits for them, and re-layouts  1.89 us (3%)
  between operations  0.77 us (1%)
    all_to_all x1, blocking collectives, on_device(): got = lax.all_to_all(sent, 'tile', split_axis=0, concat_axis=0, tiled=True)  17.9 us
    ppermute x1, waiting for transfers between devices, on_device(): swapped = lax.ppermute(view_out(measured, kernels, seen), 'view', partner)  5.37 us
    ppermute x3, starting transfers between devices, on_device(): lax.ppermute(table, 'view', [(i, i ^ step) for i in range(views)])  4.52 us
    ppermute x1, starting transfers between devices, on_device(): other = lax.ppermute(mine, 'view', across_pairs)  4.11 us
    ppermute x3, waiting for transfers between devices, on_device(): lax.ppermute(table, 'view', [(i, i ^ step) for i in range(views)])  3.67 us
    pallas_call x1, Pallas kernels, ratio_fields(): pl.pallas_call(forward_kernel, out_shape=(jax.ShapeDtypeStruct((2, planes...  3.52 us
    ppermute x1, starting transfers between devices, on_device(): swapped = lax.ppermute(view_out(measured, kernels, seen), 'view', partner)  2.84 us
    pallas_call x1, Pallas kernels, moment_rows(): pl.pallas_call(functools.partial(moments_kernel, views, tiles * planes),...  2.66 us
  transfers between devices with their start and end apart: 10, of which 3 were waited for; matrix products, arithmetic and copies ran while one was open for 0% of the time, Pallas kernels for 10%

profile of v2, /device:TPU:0, one launch (start us, length us, event | category | flops | bytes accessed | tf_op | source)
XLA Modules:
  0.0 55.8 jit_solution(8268419856069059006)
XLA Ops:
  0.6 0.0 copy-start
  0.6 1.0 %copy-done = f32[8,64,256]{2,1,0:T(8,128)S(1)} copy-done((f32[8,64,256]{2,1,0:T(8,128)S(1)}, f32[8,64,256]{2,1,0:T(8,128)}, u32[]{:S(2)}) %copy-start) | copy-done | bytes 524312
  1.7 0.0 copy-start.1
  1.7 0.5 collective-permute-start.1
  2.3 0.7 %collective-permute-start.2 = (f32[7,48,256]{2,1,0:T(8,128)S(1)}, f32[7,48,256]{2,1,0:T(8,128)S(1)}, u32[]{:S(2)}, u32[]{:S(2)}) collective-permute-start(f32[7,48,256]{2,1,0:T(8,128)S(1)} %get-tuple-element.28), channel_id=1, source_target_pairs={{4,8},{12,16},{20,24},{8,4},{16,12},{24,20},{5,9},{13,17},{21,25},... | collective-permute-start | bytes 1032200 | tf_op jit(solution)/shard_map/ppermute | solution.py:516
  3.0 2.8 %collective-permute-start = (f32[328,256]{1,0:T(8,128)S(1)}, f32[328,256]{1,0:T(8,128)S(1)}, u32[]{:S(2)}, u32[]{:S(2)}) collective-permute-start(f32[328,256]{1,0:T(8,128)S(1)} %view_out.1), channel_id=1, source_target_pairs={{0,1},{1,0},{2,3},{3,2},{4,5},{5,4},{6,7},{7,6},{8,9},{9,8},{10,11... | collective-permute-start | bytes 1007624 | tf_op jit(solution)/shard_map/ppermute | solution.py:517
  5.9 1.0 %prepare.2 = (bf16[2,2,256,256]{3,2,1,0:T(8,128)(2,1)S(1)}, bf16[40,144]{1,0:T(8,128)(2,1)S(1)}, bf16[32,144]{1,0:T(8,128)(2,1)S(1)}, f32[8,48,256]{2,1,0:T(8,128)S(1)}, f32[16,128]{1,0:T(8,128)S(1)}) custom-call(f32[1,3,15]{2,1,0:T(4,128)S(1)} %copy.8.source.kernels, f32[8,64,256]{2,1,0:T(8,128)S(1)} %copy-done.1), custom_call_target="tpu_custom_call" | custom-call | tf_op jit(solution)/shard_map/prepare/pallas_call | solution.py:137
  6.9 5.4 %collective-permute-done.source.swapped = f32[328,256]{1,0:T(8,128)S(1)} collective-permute-done((f32[328,256]{1,0:T(8,128)S(1)}, f32[328,256]{1,0:T(8,128)S(1)}, u32[]{:S(2)}, u32[]{:S(2)}) %collective-permute-start) | collective-permute-done | bytes 335904 | tf_op jit(solution)/shard_map/ppermute | solution.py:517
  12.3 1.0 %prepare.3 = (bf16[2,2,256,256]{3,2,1,0:T(8,128)(2,1)S(1)}, bf16[40,144]{1,0:T(8,128)(2,1)S(1)}, bf16[32,144]{1,0:T(8,128)(2,1)S(1)}, f32[8,48,256]{2,1,0:T(8,128)S(1)}, f32[16,128]{1,0:T(8,128)S(1)}) custom-call(f32[328,256]{1,0:T(8,128)S(1)} %collective-permute-done.source.swapped, f32[8,64,256]{2,1,0:T(8,128)S(1)} %copy-done.1), custom_call_target="tpu_custom_call" | custom-call | tf_op jit(solution)/shard_map/prepare/pallas_call | solution.py:137
  13.3 0.0 collective-permute-done.1.near
  13.3 0.0 collective-permute-done.2.far
  13.3 3.5 %ratio_fields.1 = (f32[2,8,32,256]{3,2,1,0:T(8,128)S(1)}, f32[7,32,256]{2,1,0:T(8,128)S(1)}, f32[7,32,256]{2,1,0:T(8,128)S(1)}) custom-call(bf16[2,2,256,256]{3,2,1,0:T(8,128)(2,1)S(1)} %get-tuple-element.19.wide_own, bf16[40,144]{1,0:T(8,128)(2,1)S(1)} %get-tuple-element.20.tall_own, bf16[32,144]{1,0:T(8,128)(2,1)S(1)} %get-tuple-element.21.back_own, ...), custom_call_target="tpu_custom_call" | custom-call | tf_op jit(solution)/shard_map/ratio_fields/pallas_call | solution.py:243
  16.8 2.2 %collective-permute-start.3 = (f32[7,32,256]{2,1,0:T(8,128)S(1)}, f32[7,32,256]{2,1,0:T(8,128)S(1)}, u32[]{:S(2)}, u32[]{:S(2)}) collective-permute-start(f32[7,32,256]{2,1,0:T(8,128)S(1)} %get-tuple-element.30), channel_id=1, source_target_pairs={{0,4},{4,0},{8,12},{12,8},{16,20},{20,16},{24,28},{28,24},{1,5},{5... | collective-permute-start | bytes 688136 | tf_op jit(solution)/shard_map/ppermute | solution.py:523
  19.1 0.7 %collective-permute-start.4 = (f32[7,32,256]{2,1,0:T(8,128)S(1)}, f32[7,32,256]{2,1,0:T(8,128)S(1)}, u32[]{:S(2)}, u32[]{:S(2)}) collective-permute-start(f32[7,32,256]{2,1,0:T(8,128)S(1)} %get-tuple-element.31), channel_id=1, source_target_pairs={{4,8},{12,16},{20,24},{8,4},{16,12},{24,20},{5,9},{13,17},{21,25},... | collective-permute-start | bytes 688136 | tf_op jit(solution)/shard_map/ppermute | solution.py:522
  19.7 0.3 own_planes.1.inner
  20.0 0.0 copy-start.3
  20.0 0.1 collective-permute-done.3.near
  20.2 0.0 copy-start.4
  20.2 4.1 %collective-permute-start.5 = (f32[8,32,256]{2,1,0:T(8,128)S(1)}, f32[8,32,256]{2,1,0:T(8,128)S(1)}, u32[]{:S(2)}, u32[]{:S(2)}) collective-permute-start(f32[8,32,256]{2,1,0:T(8,128)S(1)} %add_rims.1.correction.mine), channel_id=1, source_target_pairs={{0,3},{1,2},{2,1},{3,0},{4,7},{5,6},{6,5},{7,4},{8,11},{9,10},{10,... | collective-permute-start | bytes 786440 | tf_op jit(solution)/shard_map/ppermute | solution.py:526
  24.4 0.1 copy.10.owner_col
  24.4 0.7 %copy-done.6 = s32[1,16]{1,0:T(1,128)S(1)} copy-done((s32[1,16]{1,0:T(1,128)S(1)}, s32[1,16]{1,0:T(1,128)}, u32[]{:S(2)}) %copy-start.6) | copy-done | bytes 88
  25.1 0.1 copy.11.index_col
  25.2 2.7 %moment_rows.1 = f32[64,128]{1,0:T(8,128)S(1)} custom-call(f32[8,64,256]{2,1,0:T(8,128)S(1)} %copy-done.1, f32[8,32,256]{2,1,0:T(8,128)S(1)} %add_rims.1.correction.mine, s32[8,64,256]{2,1,0:T(8,128)S(1)} %copy-done.3, s32[1,16]{1,0:T(1,128)S(1)} %bitcast.9, s32[16,1]{1,0:T(8,128)S(1)} %copy.10.owner_col, s32[16,1]{1,0:T(8,128)S(1)} %copy.11.index_col), custom_call_target="tpu_custom_call" | custom-call | tf_op jit(solution)/shard_map/moment_rows/pallas_call | solution.py:423
  27.8 17.9 %all_to_all.11 = f32[8,8,128]{2,1,0:T(8,128)S(1)} all-to-all(f32[8,8,128]{2,1,0:T(8,128)S(1)} %bitcast.7), channel_id=1, replica_groups=mesh['tile'=8,'view'=4] {'tile'}, dimensions={0} | all-to-all | bytes 65536 | tf_op jit(solution)/shard_map/all_to_all | solution.py:528
  45.8 0.0 collective-permute-done.5.other
  45.8 0.1 collective-permute-start.6
  45.9 0.3 segment_table.1.first
  46.2 2.1 %collective-permute-start.7 = (f32[16,128]{1,0:T(8,128)S(1)}, f32[16,128]{1,0:T(8,128)S(1)}, u32[]{:S(2)}, u32[]{:S(2)}) collective-permute-start(f32[16,128]{1,0:T(8,128)S(1)} %segment_table.1.first), channel_id=1, source_target_pairs={{0,1},{1,0},{2,3},{3,2},{4,5},{5,4},{6,7},{7,6},{8,9},{9,8},{10,11... | collective-permute-start | bytes 24584 | tf_op jit(solution)/shard_map/ppermute | solution.py:533
  48.2 0.0 collective-permute-start.8
  48.2 2.4 %collective-permute-start.9 = (f32[16,128]{1,0:T(8,128)S(1)}, f32[16,128]{1,0:T(8,128)S(1)}, u32[]{:S(2)}, u32[]{:S(2)}) collective-permute-start(f32[16,128]{1,0:T(8,128)S(1)} %segment_table.1.first), channel_id=1, source_target_pairs={{0,3},{1,2},{2,1},{3,0},{4,7},{5,6},{6,5},{7,4},{8,11},{9,10},{10,... | collective-permute-start | bytes 24584 | tf_op jit(solution)/shard_map/ppermute | solution.py:533
  50.7 3.7 %collective-permute-done.7.second = f32[16,128]{1,0:T(8,128)S(1)} collective-permute-done((f32[16,128]{1,0:T(8,128)S(1)}, f32[16,128]{1,0:T(8,128)S(1)}, u32[]{:S(2)}, u32[]{:S(2)}) %collective-permute-start.7) | collective-permute-done | bytes 8224 | tf_op jit(solution)/shard_map/ppermute | solution.py:533
  54.4 1.4 %finish.1 = (f32[8,64,256]{2,1,0:T(8,128)}, f32[10,128]{1,0:T(8,128)}) custom-call(f32[8,32,256]{2,1,0:T(8,128)S(1)} %update.1.mine, f32[8,32,256]{2,1,0:T(8,128)S(1)} %collective-permute-done.6.other, f32[16,128]{1,0:T(8,128)S(1)} %segment_table.1.first, f32[16,128]{1,0:T(8,128)S(1)} %collective-permute-done.7.second, ...), custom_call_target="tpu_custom_call" | custom-call | tf_op jit(solution)/shard_map/finish/pallas_call | solution.py:487
  (17 shorter events, 0.2 us)
Async XLA Ops:
  0.6 1.0 %copy-start = (f32[8,64,256]{2,1,0:T(8,128)S(1)}, f32[8,64,256]{2,1,0:T(8,128)}, u32[]{:S(2)}) copy-start(f32[8,64,256]{2,1,0:T(8,128)} %estimate.9) | copy-start | bytes 1572868
  1.7 1.3 %copy-start.5 = (f32[1,3,15]{2,0,1:T(1,128)S(1)}, f32[1,3,15]{2,0,1:T(1,128)}, u32[]{:S(2)}) copy-start(f32[1,3,15]{2,0,1:T(1,128)} %param.8) | copy-start | bytes 544
  1.7 1.3 %copy-start.2 = (f32[1,8,64,256]{3,2,1,0:T(8,128)S(1)}, f32[1,8,64,256]{3,2,1,0:T(8,128)}, u32[]{:S(2)}) copy-start(f32[1,8,64,256]{3,2,1,0:T(8,128)} %measured.3) | copy-start | bytes 1572868
  1.7 4.1 %copy-start.1 = (f32[8,64,256]{2,1,0:T(8,128)S(1)}, f32[8,64,256]{2,1,0:T(8,128)}, u32[]{:S(2)}) copy-start(f32[8,64,256]{2,1,0:T(8,128)} %estimate.9) | copy-start | bytes 1572868
  1.7 11.6 %collective-permute-start.1 = (f32[7,48,256]{2,1,0:T(8,128)S(1)}, f32[7,48,256]{2,1,0:T(8,128)S(1)}, u32[]{:S(2)}, u32[]{:S(2)}) collective-permute-start(f32[7,48,256]{2,1,0:T(8,128)S(1)} %get-tuple-element.27), channel_id=1, source_target_pairs={{0,4},{4,0},{8,12},{12,8},{16,20},{20,16},{24,28},{28,24},{1,5},{5... | collective-permute-start | bytes 1032200 | tf_op jit(solution)/shard_map/ppermute | solution.py:518
  2.3 11.0 %collective-permute-start.2 = (f32[7,48,256]{2,1,0:T(8,128)S(1)}, f32[7,48,256]{2,1,0:T(8,128)S(1)}, u32[]{:S(2)}, u32[]{:S(2)}) collective-permute-start(f32[7,48,256]{2,1,0:T(8,128)S(1)} %get-tuple-element.28), channel_id=1, source_target_pairs={{4,8},{12,16},{20,24},{8,4},{16,12},{24,20},{5,9},{13,17},{21,25},... | collective-permute-start | bytes 1032200 | tf_op jit(solution)/shard_map/ppermute | solution.py:516
  3.0 9.3 %collective-permute-start = (f32[328,256]{1,0:T(8,128)S(1)}, f32[328,256]{1,0:T(8,128)S(1)}, u32[]{:S(2)}, u32[]{:S(2)}) collective-permute-start(f32[328,256]{1,0:T(8,128)S(1)} %view_out.1), channel_id=1, source_target_pairs={{0,1},{1,0},{2,3},{3,2},{4,5},{5,4},{6,7},{7,6},{8,9},{9,8},{10,11... | collective-permute-start | bytes 1007624 | tf_op jit(solution)/shard_map/ppermute | solution.py:517
  16.8 3.3 %collective-permute-start.3 = (f32[7,32,256]{2,1,0:T(8,128)S(1)}, f32[7,32,256]{2,1,0:T(8,128)S(1)}, u32[]{:S(2)}, u32[]{:S(2)}) collective-permute-start(f32[7,32,256]{2,1,0:T(8,128)S(1)} %get-tuple-element.30), channel_id=1, source_target_pairs={{0,4},{4,0},{8,12},{12,8},{16,20},{20,16},{24,28},{28,24},{1,5},{5... | collective-permute-start | bytes 688136 | tf_op jit(solution)/shard_map/ppermute | solution.py:523
  19.1 1.1 %collective-permute-start.4 = (f32[7,32,256]{2,1,0:T(8,128)S(1)}, f32[7,32,256]{2,1,0:T(8,128)S(1)}, u32[]{:S(2)}, u32[]{:S(2)}) collective-permute-start(f32[7,32,256]{2,1,0:T(8,128)S(1)} %get-tuple-element.31), channel_id=1, source_target_pairs={{4,8},{12,16},{20,24},{8,4},{16,12},{24,20},{5,9},{13,17},{21,25},... | collective-permute-start | bytes 688136 | tf_op jit(solution)/shard_map/ppermute | solution.py:522
  20.0 5.2 %copy-start.3 = (s32[8,64,256]{2,1,0:T(8,128)S(1)}, s32[8,64,256]{2,1,0:T(8,128)}, u32[]{:S(2)}) copy-start(s32[8,64,256]{2,1,0:T(8,128)} %labels.1) | copy-start | bytes 1572868
  20.2 4.1 %copy-start.4 = (s32[1,16,1]{1,2,0:T(1,128)S(1)}, s32[1,16,1]{1,2,0:T(1,128)}, u32[]{:S(2)}) copy-start(s32[1,16,1]{1,2,0:T(1,128)} %param.10) | copy-start | bytes 196
  20.2 25.5 %collective-permute-start.5 = (f32[8,32,256]{2,1,0:T(8,128)S(1)}, f32[8,32,256]{2,1,0:T(8,128)S(1)}, u32[]{:S(2)}, u32[]{:S(2)}) collective-permute-start(f32[8,32,256]{2,1,0:T(8,128)S(1)} %add_rims.1.correction.mine), channel_id=1, source_target_pairs={{0,3},{1,2},{2,1},{3,0},{4,7},{5,6},{6,5},{7,4},{8,11},{9,10},{10,... | collective-permute-start | bytes 786440 | tf_op jit(solution)/shard_map/ppermute | solution.py:526
  24.4 0.7 %copy-start.6 = (s32[1,16]{1,0:T(1,128)S(1)}, s32[1,16]{1,0:T(1,128)}, u32[]{:S(2)}) copy-start(s32[1,16]{1,0:T(1,128)} %param.11) | copy-start | bytes 196
  45.8 8.5 %collective-permute-start.6 = (f32[8,32,256]{2,1,0:T(8,128)S(1)}, f32[8,32,256]{2,1,0:T(8,128)S(1)}, u32[]{:S(2)}, u32[]{:S(2)}) collective-permute-start(f32[8,32,256]{2,1,0:T(8,128)S(1)} %update.1.mine), channel_id=1, source_target_pairs={{0,1},{1,0},{2,3},{3,2},{4,5},{5,4},{6,7},{7,6},{8,9},{9,8},{10,11... | collective-permute-start | bytes 786440 | tf_op jit(solution)/shard_map/ppermute | solution.py:530
  46.2 8.2 %collective-permute-start.7 = (f32[16,128]{1,0:T(8,128)S(1)}, f32[16,128]{1,0:T(8,128)S(1)}, u32[]{:S(2)}, u32[]{:S(2)}) collective-permute-start(f32[16,128]{1,0:T(8,128)S(1)} %segment_table.1.first), channel_id=1, source_target_pairs={{0,1},{1,0},{2,3},{3,2},{4,5},{5,4},{6,7},{7,6},{8,9},{9,8},{10,11... | collective-permute-start | bytes 24584 | tf_op jit(solution)/shard_map/ppermute | solution.py:533
  48.2 6.1 %collective-permute-start.8 = (f32[16,128]{1,0:T(8,128)S(1)}, f32[16,128]{1,0:T(8,128)S(1)}, u32[]{:S(2)}, u32[]{:S(2)}) collective-permute-start(f32[16,128]{1,0:T(8,128)S(1)} %segment_table.1.first), channel_id=1, source_target_pairs={{0,2},{1,3},{2,0},{3,1},{4,6},{5,7},{6,4},{7,5},{8,10},{9,11},{10,... | collective-permute-start | bytes 24584 | tf_op jit(solution)/shard_map/ppermute | solution.py:533
  48.2 6.1 %collective-permute-start.9 = (f32[16,128]{1,0:T(8,128)S(1)}, f32[16,128]{1,0:T(8,128)S(1)}, u32[]{:S(2)}, u32[]{:S(2)}) collective-permute-start(f32[16,128]{1,0:T(8,128)S(1)} %segment_table.1.first), channel_id=1, source_target_pairs={{0,3},{1,2},{2,1},{3,0},{4,7},{5,6},{6,5},{7,4},{8,11},{9,10},{10,... | collective-permute-start | bytes 24584 | tf_op jit(solution)/shard_map/ppermute | solution.py:533

commit v3 on v2

v3 whole, which is shorter than its diff:
```python
import functools

import jax
import jax.numpy as jnp
from jax import lax
from jax.experimental import pallas as pl
from jax.experimental.pallas import tpu as pltpu
from jax.sharding import PartitionSpec as P

MOM = 10
ROWS = 8
NUC_DEV = 128
LANES = 128
F32 = jnp.float32
BF16 = jnp.bfloat16
ANY = pl.BlockSpec(memory_space=pl.ANY)
VMEM = pl.BlockSpec(memory_space=pltpu.VMEM)
LIMIT = 32 * 1024 * 1024


def half_of(view):
    return (view ^ (view >> 1)) & 1


def split(value):
    upper = value.astype(BF16)
    return upper, (value - upper.astype(F32)).astype(BF16)


def band(taps, shape, offset):
    rows = lax.broadcasted_iota(jnp.int32, shape, 0)
    cols = lax.broadcasted_iota(jnp.int32, shape, 1)
    place = cols - rows + offset
    result = jnp.zeros(shape, F32)
    for step, tap in enumerate(taps):
        result = jnp.where(place == step, tap, result)
    return result


def depth_terms(source, weights, first, last, planes, flipped):
    radius = (len(weights) - 1) // 2
    totals = {plane: None for plane in planes}
    for place in range(first, last):
        block = None
        for plane in planes:
            step = plane - place + radius if flipped else place - plane + radius
            if 0 <= step < len(weights):
                block = source(place) if block is None else block
                term = weights[step] * block
                totals[plane] = term if totals[plane] is None else totals[plane] + term
    return totals


def chunks(rows, across):
    return [(slice(row, row + 16), slice(lane, lane + LANES)) for row in range(0, rows, 16) for lane in range(0, across, LANES)]


def rims_out_kernel(estimate, to_far, to_near):
    planes, radius, rows = estimate.shape[0], to_far.shape[0], to_far.shape[1]
    odd = lax.axis_index("tile") % 2
    half = half_of(lax.axis_index("view"))
    start = pl.multiple_of((estimate.shape[1] - rows) * half, 8)
    to_far[...] = estimate[pl.ds(odd, radius), pl.ds(start, rows)]
    to_near[...] = estimate[pl.ds(1 - odd, radius), pl.ds(start, rows)]


def rims_out(estimate, radius, rows):
    shape = jax.ShapeDtypeStruct((radius, rows, estimate.shape[2]), F32)
    return pl.pallas_call(
        rims_out_kernel,
        out_shape=(shape, shape),
        in_specs=[VMEM],
        out_specs=(VMEM, VMEM),
        compiler_params=pltpu.CompilerParams(vmem_limit_bytes=LIMIT),
        name="rims_out",
    )(estimate)


def view_out_kernel(seen, measured, kernels, packed):
    planes, height = measured.shape[1], measured.shape[2]
    half = half_of(lax.axis_index("view"))
    start = pl.multiple_of((height - seen) * (1 - half), 8)
    for plane in range(planes):
        packed[plane * seen : (plane + 1) * seen] = measured[0, plane, pl.ds(start, seen)]
    packed[planes * seen :] = jnp.zeros((8, packed.shape[1]), F32)
    packed[planes * seen : planes * seen + kernels.shape[1], : kernels.shape[2]] = kernels[0]


def view_out(measured, kernels, seen):
    _, planes, _, across = measured.shape
    return pl.pallas_call(
        functools.partial(view_out_kernel, seen),
        out_shape=jax.ShapeDtypeStruct((planes * seen + 8, across), F32),
        in_specs=[VMEM, VMEM],
        out_specs=VMEM,
        compiler_params=pltpu.CompilerParams(vmem_limit_bytes=LIMIT),
        name="view_out",
    )(measured, kernels)


def prepare_kernel(packed, taps, source, estimate, after, wide, tall, back, part, spread):
    half = half_of(lax.axis_index("view"))
    across = wide.shape[-1]
    rows, keep, seen = part.shape[1], back.shape[0], tall.shape[0]
    planes = estimate.shape[0]
    radius = (taps - 1) // 2
    raw = source[source.shape[0] - 8 : source.shape[0] - 5, :taps] if packed else source[0]
    weights = raw / jnp.sum(raw, axis=-1, keepdims=True)
    deep, high, flat = [[weights[axis : axis + 1, t : t + 1] for t in range(taps)] for axis in range(3)]
    start = pl.multiple_of((2 * keep - rows) * half, 16)
    seen_start = (2 * keep - seen) * half
    upper, lower = split(band(flat[::-1], (across, across), radius))
    wide[0, 0] = upper
    wide[0, 1] = lower
    upper, lower = split(band(flat, (across, across), radius))
    wide[1, 0] = upper
    wide[1, 1] = lower
    upper, lower = split(band(high, (seen, rows), radius + start - seen_start))
    tall[...] = jnp.concatenate([upper, upper, lower], axis=1)
    upper, lower = split(band(high[::-1], (keep, rows), radius + seen_start - keep * half))
    back[...] = jnp.concatenate([upper, upper, lower], axis=1)
    factors = [jnp.broadcast_to(tap, (16, LANES)) for tap in deep]
    spread[...] = jnp.zeros_like(spread)
    for step in range(taps):
        spread[step : step + 1] = factors[step][:1]
    for row, lane in chunks(rows, across):
        where = pl.ds(pl.multiple_of(start + row.start, 16), 16)
        terms = depth_terms(
            lambda place: estimate[place, where, lane], factors, 0, planes, range(planes), False
        )
        for plane, block in terms.items():
            part[plane, row, lane] = block


def prepare(packed, taps, source, estimate, after, rows, seen, keep):
    planes, _, across = estimate.shape
    return pl.pallas_call(
        functools.partial(prepare_kernel, packed, taps),
        out_shape=(
            jax.ShapeDtypeStruct((2, 2, across, across), BF16),
            jax.ShapeDtypeStruct((seen, 3 * rows), BF16),
            jax.ShapeDtypeStruct((keep, 3 * rows), BF16),
            jax.ShapeDtypeStruct((planes, rows, across), F32),
            jax.ShapeDtypeStruct((-(-taps // 8) * 8, LANES), F32),
        ),
        in_specs=[VMEM, VMEM, ANY],
        out_specs=(VMEM,) * 5,
        compiler_params=pltpu.CompilerParams(vmem_limit_bytes=LIMIT),
        name="prepare",
    )(source, estimate, after)


def spread_factors(spread, taps):
    return [jnp.broadcast_to(spread[step : step + 1, :], (16, LANES)) for step in range(taps)]


def view_kernel(
    first, wide, tall, back, part, spread, far, near, view, begun_near, begun_far,
    field, send_near, send_far,
    blur_hi, blur_lo, plane_hi, plane_lo,
):
    planes, radius = part.shape[0], near.shape[0]
    rows, across = near.shape[1], near.shape[2]
    keep, seen = back.shape[0], tall.shape[0]
    taps = 2 * radius + 1
    even = lax.axis_index("tile") % 2 == 0
    half = half_of(lax.axis_index("view"))
    seen_start = pl.multiple_of((2 * keep - seen) * half, 8)
    factors = spread_factors(spread, taps)
    for row, lane in chunks(rows, across):

        def rim(place):
            if place < 0:
                at = place + radius
                return jnp.where(even, far[at, row, lane], near[at, row, lane])
            at = place - planes
            return jnp.where(even, near[at, row, lane], far[at, row, lane])

        below = depth_terms(rim, factors, -radius, 0, range(planes), False)
        above = depth_terms(rim, factors, planes, planes + radius, range(planes), False)
        for plane in range(planes):
            block = part[plane, row, lane]
            for term in (below[plane], above[plane]):
                block = block if term is None else block + term
            upper, lower = split(block)
            at = slice(plane * rows + row.start, plane * rows + row.stop)
            blur_hi[at, lane] = upper
            blur_lo[at, lane] = lower
    upper, lower = wide[0, 0], wide[0, 1]
    lines = jnp.dot(blur_hi[...], upper, preferred_element_type=F32)
    lines += jnp.dot(blur_lo[...], upper, preferred_element_type=F32)
    lines += jnp.dot(blur_hi[...], lower, preferred_element_type=F32)
    for plane in range(planes):
        hi, lo = split(lines[plane * rows : (plane + 1) * rows])
        forward = jnp.dot(
            tall[...], jnp.concatenate([hi, lo, hi], axis=0), preferred_element_type=F32
        )
        if first:
            recorded = view[0, plane, pl.ds(seen_start, seen), :]
        else:
            recorded = view[plane * seen : (plane + 1) * seen]
        ratio = recorded / forward
        if rows > seen:
            ratio = jnp.concatenate([ratio, jnp.zeros((rows - seen, across), F32)], axis=0)
        hi, lo = split(ratio)
        turned = jnp.dot(
            back[...], jnp.concatenate([hi, lo, hi], axis=0), preferred_element_type=F32
        )
        hi, lo = split(turned)
        plane_hi[plane * keep : (plane + 1) * keep] = hi
        plane_lo[plane * keep : (plane + 1) * keep] = lo
    upper, lower = wide[1, 0], wide[1, 1]
    lines = jnp.dot(plane_hi[...], upper, preferred_element_type=F32)
    lines += jnp.dot(plane_lo[...], upper, preferred_element_type=F32)
    lines += jnp.dot(plane_hi[...], lower, preferred_element_type=F32)
    field[...] = lines.reshape(planes, keep, across)
    for row, lane in chunks(keep, across):
        source = lambda place: field[place, row, lane]
        below = depth_terms(source, factors, 0, planes, range(-radius, 0), True)
        above = depth_terms(source, factors, 0, planes, range(planes, planes + radius), True)
        for at in range(radius):
            down, up = below[at - radius], above[at + planes]
            to_near, to_far = jnp.where(even, up, down), jnp.where(even, down, up)
            if not first:
                to_near += begun_near[at, row, lane]
                to_far += begun_far[at, row, lane]
            send_near[at, row, lane] = to_near
            send_far[at, row, lane] = to_far


def view_field(first, prepared, near, far, view, begun):
    keep = prepared[2].shape[0]
    planes = prepared[3].shape[0]
    radius, rows, across = near.shape

    def body(*refs):
        if first:
            refs = refs[:8] + (None, None) + refs[8:]
        view_kernel(first, *refs)

    return pl.pallas_call(
        body,
        out_shape=(
            jax.ShapeDtypeStruct((planes, keep, across), F32),
            jax.ShapeDtypeStruct((radius, keep, across), F32),
            jax.ShapeDtypeStruct((radius, keep, across), F32),
        ),
        in_specs=[VMEM] * (8 + len(begun)),
        out_specs=(VMEM, VMEM, VMEM),
        scratch_shapes=[
            pltpu.VMEM((planes * rows, across), BF16),
            pltpu.VMEM((planes * rows, across), BF16),
            pltpu.VMEM((planes * keep, across), BF16),
            pltpu.VMEM((planes * keep, across), BF16),
        ],
        compiler_params=pltpu.CompilerParams(vmem_limit_bytes=LIMIT),
        name="view_first" if first else "view_second",
    )(*prepared, far, near, view, *begun)


def own_kernel(taps, spread_own, spread_other, field_own, field_other, inner):
    planes, keep, across = inner.shape
    factors = [spread_factors(spread, taps) for spread in (spread_own, spread_other)]
    for row, lane in chunks(keep, across):
        parts = [
            depth_terms(
                lambda place: field[place, row, lane], factors[which], 0, planes, range(planes), True
            )
            for which, field in enumerate((field_own, field_other))
        ]
        for plane in range(planes):
            inner[plane, row, lane] = parts[0][plane] + parts[1][plane]


def own_planes(taps, spread_own, spread_other, field_own, field_other):
    return pl.pallas_call(
        functools.partial(own_kernel, taps),
        out_shape=jax.ShapeDtypeStruct(field_own.shape, F32),
        in_specs=[VMEM] * 4,
        out_specs=VMEM,
        compiler_params=pltpu.CompilerParams(vmem_limit_bytes=LIMIT),
        name="own_planes",
    )(spread_own, spread_other, field_own, field_other)


def rims_kernel(inner, far, near, correction):
    planes, radius = inner.shape[0], near.shape[0]
    even = lax.axis_index("tile") % 2 == 0
    for plane in range(planes):
        total = inner[plane]
        if plane < radius:
            total += jnp.where(even, far[plane], near[plane])
        if plane >= planes - radius:
            at = plane - planes + radius
            total += jnp.where(even, near[at], far[at])
        correction[plane] = total


def add_rims(inner, near, far):
    return pl.pallas_call(
        rims_kernel,
        out_shape=jax.ShapeDtypeStruct(inner.shape, F32),
        in_specs=[VMEM] * 3,
        out_specs=VMEM,
        compiler_params=pltpu.CompilerParams(vmem_limit_bytes=LIMIT),
        name="add_rims",
    )(inner, far, near)


def table_rows(table):
    return jnp.concatenate([table[:8], table[8:]], axis=1)


def update_kernel(views, estimate, mine, other, table, result):
    planes, keep, across = mine.shape
    half = half_of(lax.axis_index("view"))
    start = pl.multiple_of(keep * half, 8)
    for plane in range(planes):
        held = estimate[plane, pl.ds(start, keep)]
        at = slice(plane * keep, (plane + 1) * keep)
        result[at] = held * (mine[plane] + other[plane]) * (1.0 / views)
    result[planes * keep :] = jnp.zeros((8, across), F32)
    result[planes * keep :, : 2 * LANES] = table_rows(table[...])


def update(views, estimate, mine, other, table):
    planes, keep, across = mine.shape
    return pl.pallas_call(
        functools.partial(update_kernel, views),
        out_shape=jax.ShapeDtypeStruct((planes * keep + 8, across), F32),
        in_specs=[VMEM] * 4,
        out_specs=VMEM,
        compiler_params=pltpu.CompilerParams(vmem_limit_bytes=LIMIT),
        name="update",
    )(estimate, mine, other, table)


def slots_kernel(owner_row, index_row, picked, base):
    count = picked.shape[0]
    slots = owner_row.shape[1]
    tiles = count // ROWS
    owner = owner_row[...]
    member = (lax.broadcasted_iota(jnp.int32, (tiles, slots), 0) == owner).astype(F32)
    upto = (
        lax.broadcasted_iota(jnp.int32, (slots, slots), 0)
        <= lax.broadcasted_iota(jnp.int32, (slots, slots), 1)
    ).astype(F32)
    running = jnp.dot(member, upto, preferred_element_type=F32)
    rank = jnp.sum(member * running, axis=0, keepdims=True).astype(jnp.int32) - 1
    place = owner * ROWS + rank
    chosen = lax.broadcasted_iota(jnp.int32, (count, slots), 0) == place
    picked[...] = chosen.astype(F32)
    ids = jnp.sum(jnp.where(chosen, index_row[...].astype(F32), 0.0), axis=1, keepdims=True)
    lanes = lax.broadcasted_iota(jnp.int32, (count, LANES), 1)
    base[...] = jnp.where(lanes == MOM, ids, 0.0)


def slot_places(tiles, label_owner, label_index):
    slots = label_index.shape[1]
    return pl.pallas_call(
        slots_kernel,
        out_shape=(
            jax.ShapeDtypeStruct((tiles * ROWS, slots), F32),
            jax.ShapeDtypeStruct((tiles * ROWS, LANES), F32),
        ),
        in_specs=[VMEM, VMEM],
        out_specs=(VMEM, VMEM),
        compiler_params=pltpu.CompilerParams(vmem_limit_bytes=LIMIT),
        name="slot_places",
    )(label_owner.reshape(1, slots), label_index)


def moments_kernel(
    views, depth_total, estimate, correction, labels, picked, base, sent, held, sums, table
):
    planes, keep, across = correction.shape
    height_total = estimate.shape[1]
    slots = picked.shape[1]
    half = half_of(lax.axis_index("view"))
    first = (lax.axis_index("tile") * planes).astype(F32) + 0.5
    start = pl.multiple_of(keep * half, 8)
    held[...] = estimate[:, pl.ds(start, keep)] * correction[...] * (1.0 / views)
    group = 16
    columns = lax.broadcasted_iota(jnp.int32, (across, LANES), 1)
    spot = (lax.broadcasted_iota(jnp.int32, (across, LANES), 0).astype(F32) + 0.5) / across
    one, line, square = jnp.ones_like(spot), spot, spot * spot

    def placed(*pairs):
        result = jnp.zeros((across, LANES), F32)
        for lane, value in pairs:
            result = jnp.where(columns == lane, value, result)
        return result

    factors = jnp.concatenate(
        [
            placed((0, one), (3, line), (6, square)),
            placed((2, one), (9, line)),
            placed((5, one)),
            placed((1, one), (8, line)),
            placed((7, one)),
            placed((4, one)),
        ],
        axis=0,
    )
    base_row = lax.broadcasted_iota(jnp.int32, (8, across), 0)

    def one_group(number, carry):
        def one_slot(inner, carry):
            slot = number * group + inner
            parts = [jnp.zeros((8, across), F32) for _ in range(6)]
            for row in range(0, keep, 8):
                high = ((base_row + (row + start)).astype(F32) + 0.5) / height_total
                flat, once, twice = [jnp.zeros((8, across), F32) for _ in range(3)]
                for plane in reversed(range(planes)):
                    hit = labels[plane, pl.ds(pl.multiple_of(start + row, 8), 8)] == slot
                    flat = flat + jnp.where(hit, held[plane, row : row + 8], 0.0)
                    if plane > 0:
                        once = once + flat
                        twice = twice + once
                square_sum = 2.0 * twice - once
                deep = (first * flat + once) * (1.0 / depth_total)
                deeper = (first * (first * flat + 2.0 * once) + square_sum) * (1.0 / depth_total**2)
                scaled = flat * high
                parts[0] = parts[0] + flat
                parts[1] = parts[1] + scaled
                parts[2] = parts[2] + scaled * high
                parts[3] = parts[3] + deep
                parts[4] = parts[4] + deep * high
                parts[5] = parts[5] + deeper
            at = pl.multiple_of(inner * 8, 8)
            sums[pl.ds(at, 8), :] = jnp.concatenate(parts, axis=1)
            return carry

        lax.fori_loop(0, group, one_slot, 0)
        lines = jnp.dot(
            sums[...], factors, precision=lax.Precision.HIGHEST, preferred_element_type=F32
        )
        at = pl.multiple_of(number * group, group)
        table[pl.ds(at, group), :] = jnp.sum(lines.reshape(group, 8, LANES), axis=1)
        return carry

    lax.fori_loop(0, slots // group, one_group, 0)
    sent[...] = base[...] + jnp.dot(
        picked[...], table[...], precision=lax.Precision.HIGHEST, preferred_element_type=F32
    )


def moment_rows(views, tiles, estimate, correction, labels, places):
    planes, keep, across = correction.shape
    slots = places[0].shape[1]
    return pl.pallas_call(
        functools.partial(moments_kernel, views, tiles * planes),
        out_shape=jax.ShapeDtypeStruct((tiles * ROWS, LANES), F32),
        in_specs=[VMEM] * 5,
        out_specs=VMEM,
        scratch_shapes=[
            pltpu.VMEM(correction.shape, F32),
            pltpu.VMEM((16 * 8, 6 * across), F32),
            pltpu.VMEM((slots, LANES), F32),
        ],
        compiler_params=pltpu.CompilerParams(vmem_limit_bytes=LIMIT),
        name="moment_rows",
    )(estimate, correction, labels, *places)


def segments_kernel(rows, table):
    values = rows[...]
    ids = values[:, MOM : MOM + 1].astype(jnp.int32)
    spots = lax.broadcasted_iota(jnp.int32, (values.shape[0], NUC_DEV), 1)
    picked = (ids == spots).astype(F32)
    full = lax.dot_general(
        values, picked, (((0,), (0,)), ((), ())),
        precision=lax.Precision.HIGHEST, preferred_element_type=F32,
    )
    table[...] = full[: table.shape[0]]


def segment_table(rows):
    return pl.pallas_call(
        segments_kernel,
        out_shape=jax.ShapeDtypeStruct((16, NUC_DEV), F32),
        in_specs=[VMEM],
        out_specs=VMEM,
        compiler_params=pltpu.CompilerParams(vmem_limit_bytes=LIMIT),
        name="segment_table",
    )(rows)


def own_half_kernel(keep, mine, whole, sems):
    planes = whole.shape[0]
    start = pl.multiple_of(keep * half_of(lax.axis_index("view")), 8)
    copies = [
        pltpu.make_async_copy(
            mine.at[pl.ds(plane * keep, keep)], whole.at[plane, pl.ds(start, keep)], sems.at[plane]
        )
        for plane in range(planes)
    ]
    for copy in copies:
        copy.start()
    for copy in copies:
        copy.wait()


def own_half(mine, planes, keep):
    return pl.pallas_call(
        functools.partial(own_half_kernel, keep),
        out_shape=jax.ShapeDtypeStruct((planes, 2 * keep, mine.shape[1]), F32),
        in_specs=[ANY],
        out_specs=ANY,
        scratch_shapes=[pltpu.SemaphoreType.DMA((planes,))],
        compiler_params=pltpu.CompilerParams(vmem_limit_bytes=LIMIT),
        name="own_half",
    )(mine)


def finish_kernel(scale, keep, begun, other, first, third, fourth, whole, moments, sems):
    planes = whole.shape[0]
    start = pl.multiple_of(keep * (1 - half_of(lax.axis_index("view"))), 8)
    copies = [
        pltpu.make_async_copy(
            other.at[pl.ds(plane * keep, keep)], whole.at[plane, pl.ds(start, keep)], sems.at[plane]
        )
        for plane in range(planes)
    ]
    for copy in copies:
        copy.start()
    rows = other[planes * keep :]
    second = jnp.concatenate([rows[:, :LANES], rows[:, LANES : 2 * LANES]], axis=0)
    table = (first[...] + second) + (third[...] + fourth[...])
    mass = table[0:1]
    lines = lax.broadcasted_iota(jnp.int32, table.shape, 0)
    result = jnp.where(lines == 0, table * scale, table / jnp.maximum(mass, 1.0))
    moments[...] = result[:MOM]
    for copy in copies:
        copy.wait()


def finish(scale, keep, begun, other, tables):
    planes = begun.shape[0]
    return pl.pallas_call(
        functools.partial(finish_kernel, scale, keep),
        out_shape=(
            jax.ShapeDtypeStruct(begun.shape, F32),
            jax.ShapeDtypeStruct((MOM, NUC_DEV), F32),
        ),
        in_specs=[ANY] + [VMEM] * 4,
        out_specs=(ANY, VMEM),
        input_output_aliases={0: 0},
        scratch_shapes=[pltpu.SemaphoreType.DMA((planes,))],
        compiler_params=pltpu.CompilerParams(vmem_limit_bytes=LIMIT),
        name="finish",
    )(begun, other, *tables)


def on_device(estimate, measured, kernels, labels, label_owner, label_index):
    tiles, views = lax.axis_size("tile"), lax.axis_size("view")
    planes, height, across = estimate.shape
    taps = kernels.shape[2]
    radius = (taps - 1) // 2
    keep = height // 2
    seen = min(height, -(-(keep + radius) // 8) * 8)
    rows = min(height, -(-(keep + 2 * radius) // 16) * 16)
    near_pairs = [(i, i ^ 1) for i in range(tiles)]
    far_pairs = [(i, i + 1) for i in range(1, tiles - 1, 2)]
    far_pairs = far_pairs + [(b, a) for a, b in far_pairs]
    partner = [(i, i ^ 1) for i in range(views)]
    across_pairs = [(i, i ^ 3) for i in range(views)]

    packed = view_out(measured, kernels, seen)
    swapped = lax.ppermute(packed, "view", partner)
    to_far, to_near = rims_out(estimate, radius, rows)
    far = lax.ppermute(to_far, "tile", far_pairs)
    near = lax.ppermute(to_near, "tile", near_pairs)
    own = prepare(False, taps, kernels, estimate, kernels, rows, seen, keep)
    field_own, *begun = view_field(True, own, near, far, measured, ())
    others = prepare(True, taps, swapped, estimate, begun[0], rows, seen, keep)
    field_other, sum_near, sum_far = view_field(False, others, near, far, swapped, begun)
    rim_far = lax.ppermute(sum_far, "tile", far_pairs)
    rim_near = lax.ppermute(sum_near, "tile", near_pairs)
    inner = own_planes(taps, own[4], others[4], field_own, field_other)
    mine = add_rims(inner, rim_near, rim_far)
    other = lax.ppermute(mine, "view", across_pairs)
    places = slot_places(tiles, label_owner, label_index)
    sent = moment_rows(views, tiles, estimate, mine, labels, places)
    got = lax.all_to_all(sent, "tile", split_axis=0, concat_axis=0, tiled=True)
    table = segment_table(got)
    tables = [table] + [
        lax.ppermute(table, "view", [(i, i ^ step) for i in range(views)]) for step in (2, 3)
    ]
    new_half = update(views, estimate, mine, other, table)
    new_other = lax.ppermute(new_half, "view", partner)
    scale = label_index.shape[1] / (planes * height * across)
    return finish(scale, keep, own_half(new_half, planes, keep), new_other, tables)


def solution(mesh):
    placed = (
        P("tile", None, None),
        P("view", "tile", None, None),
        P("view", None, None),
        P("tile", None, None),
        P("tile", None, None),
        P("tile", None),
    )
    return jax.shard_map(
        on_device,
        mesh=mesh,
        in_specs=placed,
        out_specs=(P("tile", None, None), P(None, "tile")),
        check_vma=False,
    )
```

time: 56 us -> 55.2 us (0.986)
  blocking collectives: 17.9 us -> 13.5 us
  starting transfers between devices: 15.6 us -> 18.5 us
  Pallas kernels: 10.4 us -> 12 us
  local copies, waits for them, and re-layouts: 1.89 us -> 1.07 us
    all_to_all x1, blocking collectives: 17.9 us -> 13.5 us  [on_device(): got = lax.all_to_all(sent, 'tile', split_axis=0, concat_axis=0, tiled=True)]
    ppermute x1, starting transfers between devices: 0.52 us -> 4.34 us  [on_device(): near = lax.ppermute(to_near, 'tile', near_pairs)]
    pallas_call x2 -> x5, Pallas kernels: 4.94 us -> 6.77 us  [the longest x2 4.44 us: view_field(): pl.pallas_call(body, out_shape=(jax.ShapeDtypeStruct((planes, keep, acros...]
    ppermute x3 -> x2, waiting for transfers between devices: 3.67 us -> 2.68 us  [on_device(): lax.ppermute(table, 'view', [(i, i ^ step) for i in range(views)])]
    unnamed x15, local copies, waits for them, and re-layouts: 1.72 us -> 1.07 us
    ppermute x1, waiting for transfers between devices: 0.01 us -> 0.63 us  [on_device(): new_other = lax.ppermute(new_half, 'view', partner)]
    ppermute x3 -> x2, starting transfers between devices: 4.52 us -> 4.37 us  [on_device(): lax.ppermute(table, 'view', [(i, i ^ step) for i in range(views)])]
  transfers between devices with their start and end apart: 10 -> 9, of which waited for: 3 -> 5; matrix products, arithmetic and copies ran while one was open for 0% -> 0% of each run, Pallas kernels for 10% -> 13%
where the time goes in v3:
time: 55.2 us; the launch traced here: 55 us
  starting transfers between devices  18.5 us (34%)
  blocking collectives  13.5 us (24%)
  Pallas kernels  12 us (22%)
  waiting for transfers between devices  9.14 us (17%)
  local copies, waits for them, and re-layouts  1.07 us (2%)
  between operations  0.77 us (1%)
    all_to_all x1, blocking collectives, on_device(): got = lax.all_to_all(sent, 'tile', split_axis=0, concat_axis=0, tiled=True)  13.5 us
    ppermute x1, waiting for transfers between devices, on_device(): swapped = lax.ppermute(packed, 'view', partner)  5 us
    pallas_call x2, Pallas kernels, view_field(): pl.pallas_call(body, out_shape=(jax.ShapeDtypeStruct((planes, keep, acros...  4.44 us
    ppermute x2, starting transfers between devices, on_device(): lax.ppermute(table, 'view', [(i, i ^ step) for i in range(views)])  4.37 us
    ppermute x1, starting transfers between devices, on_device(): near = lax.ppermute(to_near, 'tile', near_pairs)  4.34 us
    ppermute x1, starting transfers between devices, on_device(): other = lax.ppermute(mine, 'view', across_pairs)  3.67 us
    ppermute x1, starting transfers between devices, on_device(): rim_near = lax.ppermute(sum_near, 'tile', near_pairs)  2.9 us
    ppermute x2, waiting for transfers between devices, on_device(): lax.ppermute(table, 'view', [(i, i ^ step) for i in range(views)])  2.68 us
  transfers between devices with their start and end apart: 9, of which 5 were waited for; matrix products, arithmetic and copies ran while one was open for 0% of the time, Pallas kernels for 13%

profile of v3, /device:TPU:0, one launch (start us, length us, event | category | flops | bytes accessed | tf_op | source)
XLA Modules:
  0.0 55.0 jit_solution(7452575364548123742)
XLA Ops:
  0.6 0.0 copy-start
  0.6 1.0 %copy-done = f32[8,64,256]{2,1,0:T(8,128)S(1)} copy-done((f32[8,64,256]{2,1,0:T(8,128)S(1)}, f32[8,64,256]{2,1,0:T(8,128)}, u32[]{:S(2)}) %copy-start) | copy-done | bytes 524312
  1.7 0.0 copy-start.1
  1.7 0.8 %collective-permute-start.1 = (f32[7,48,256]{2,1,0:T(8,128)S(1)}, f32[7,48,256]{2,1,0:T(8,128)S(1)}, u32[]{:S(2)}, u32[]{:S(2)}) collective-permute-start(f32[7,48,256]{2,1,0:T(8,128)S(1)} %get-tuple-element.27), channel_id=1, source_target_pairs={{4,8},{12,16},{20,24},{8,4},{16,12},{24,20},{5,9},{13,17},{21,25},... | collective-permute-start | bytes 1032200 | tf_op jit(solution)/shard_map/ppermute | solution.py:572
  2.6 4.3 %collective-permute-start.2 = (f32[7,48,256]{2,1,0:T(8,128)S(1)}, f32[7,48,256]{2,1,0:T(8,128)S(1)}, u32[]{:S(2)}, u32[]{:S(2)}) collective-permute-start(f32[7,48,256]{2,1,0:T(8,128)S(1)} %get-tuple-element.28), channel_id=1, source_target_pairs={{0,4},{4,0},{8,12},{12,8},{16,20},{20,16},{24,28},{28,24},{1,5},{5... | collective-permute-start | bytes 1032200 | tf_op jit(solution)/shard_map/ppermute | solution.py:573
  7.0 1.6 %collective-permute-start = (f32[328,256]{1,0:T(8,128)S(1)}, f32[328,256]{1,0:T(8,128)S(1)}, u32[]{:S(2)}, u32[]{:S(2)}) collective-permute-start(f32[328,256]{1,0:T(8,128)S(1)} %view_out.1), channel_id=1, source_target_pairs={{0,1},{1,0},{2,3},{3,2},{4,5},{5,4},{6,7},{7,6},{8,9},{9,8},{10,11... | collective-permute-start | bytes 1007624 | tf_op jit(solution)/shard_map/ppermute | solution.py:570
  8.6 1.0 %prepare.2 = (bf16[2,2,256,256]{3,2,1,0:T(8,128)(2,1)S(1)}, bf16[40,144]{1,0:T(8,128)(2,1)S(1)}, bf16[32,144]{1,0:T(8,128)(2,1)S(1)}, f32[8,48,256]{2,1,0:T(8,128)S(1)}, f32[16,128]{1,0:T(8,128)S(1)}) custom-call(f32[1,3,15]{2,1,0:T(4,128)S(1)} %copy.9.source.after.kernels, f32[8,64,256]{2,1,0:T(8,128)S(1)} %copy-done.1, ...), custom_call_target="tpu_custom_call" | custom-call | tf_op jit(solution)/shard_map/prepare/pallas_call | solution.py:137
  9.6 2.2 %view_first.1 = (f32[8,32,256]{2,1,0:T(8,128)S(1)}, f32[7,32,256]{2,1,0:T(8,128)S(1)}, f32[7,32,256]{2,1,0:T(8,128)S(1)}) custom-call(bf16[2,2,256,256]{3,2,1,0:T(8,128)(2,1)S(1)} %get-tuple-element.23.refs_0_, bf16[40,144]{1,0:T(8,128)(2,1)S(1)} %get-tuple-element.24.refs_1_, bf16[32,144]{1,0:T(8,128)(2,1)S(1)} %get-tuple-element.25.refs_2_, ...), custom_call_target="tpu_custom_call" | custom-call | tf_op jit(solution)/shard_map/view_first/pallas_call | solution.py:241
  11.8 5.0 %collective-permute-done.source.refs_7_ = f32[328,256]{1,0:T(8,128)S(1)} collective-permute-done((f32[328,256]{1,0:T(8,128)S(1)}, f32[328,256]{1,0:T(8,128)S(1)}, u32[]{:S(2)}, u32[]{:S(2)}) %collective-permute-start) | collective-permute-done | bytes 335904 | tf_op jit(solution)/shard_map/ppermute | solution.py:570
  16.9 1.0 %prepare.3 = (bf16[2,2,256,256]{3,2,1,0:T(8,128)(2,1)S(1)}, bf16[40,144]{1,0:T(8,128)(2,1)S(1)}, bf16[32,144]{1,0:T(8,128)(2,1)S(1)}, f32[8,48,256]{2,1,0:T(8,128)S(1)}, f32[16,128]{1,0:T(8,128)S(1)}) custom-call(f32[328,256]{1,0:T(8,128)S(1)} %collective-permute-done.source.refs_7_, f32[8,64,256]{2,1,0:T(8,128)S(1)} %copy-done.1, ...), custom_call_target="tpu_custom_call" | custom-call | tf_op jit(solution)/shard_map/prepare/pallas_call | solution.py:137
  17.9 2.2 %view_second.1 = (f32[8,32,256]{2,1,0:T(8,128)S(1)}, f32[7,32,256]{2,1,0:T(8,128)S(1)}, f32[7,32,256]{2,1,0:T(8,128)S(1)}) custom-call(bf16[2,2,256,256]{3,2,1,0:T(8,128)(2,1)S(1)} %get-tuple-element.32.refs_0_, bf16[40,144]{1,0:T(8,128)(2,1)S(1)} %get-tuple-element.33.refs_1_, bf16[32,144]{1,0:T(8,128)(2,1)S(1)} %get-tuple-element.34.refs_2_, ...), custom_call_target="tpu_custom_call" | custom-call | tf_op jit(solution)/shard_map/view_second/pallas_call | solution.py:241
  20.1 0.7 %collective-permute-start.3 = (f32[7,32,256]{2,1,0:T(8,128)S(1)}, f32[7,32,256]{2,1,0:T(8,128)S(1)}, u32[]{:S(2)}, u32[]{:S(2)}) collective-permute-start(f32[7,32,256]{2,1,0:T(8,128)S(1)} %get-tuple-element.38), channel_id=1, source_target_pairs={{4,8},{12,16},{20,24},{8,4},{16,12},{24,20},{5,9},{13,17},{21,25},... | collective-permute-start | bytes 688136 | tf_op jit(solution)/shard_map/ppermute | solution.py:578
  20.8 2.9 %collective-permute-start.4 = (f32[7,32,256]{2,1,0:T(8,128)S(1)}, f32[7,32,256]{2,1,0:T(8,128)S(1)}, u32[]{:S(2)}, u32[]{:S(2)}) collective-permute-start(f32[7,32,256]{2,1,0:T(8,128)S(1)} %get-tuple-element.39), channel_id=1, source_target_pairs={{0,4},{4,0},{8,12},{12,8},{16,20},{20,16},{24,28},{28,24},{1,5},{5... | collective-permute-start | bytes 688136 | tf_op jit(solution)/shard_map/ppermute | solution.py:579
  23.7 0.3 own_planes.1.inner
  24.0 0.0 copy-start.3
  24.0 0.8 %collective-permute-done.4.near = f32[7,32,256]{2,1,0:T(8,128)S(1)} collective-permute-done((f32[7,32,256]{2,1,0:T(8,128)S(1)}, f32[7,32,256]{2,1,0:T(8,128)S(1)}, u32[]{:S(2)}, u32[]{:S(2)}) %collective-permute-start.4) | collective-permute-done | bytes 229408 | tf_op jit(solution)/shard_map/ppermute | solution.py:579
  24.9 0.0 copy-start.4
  24.9 0.0 copy-start.5
  24.9 3.7 %collective-permute-start.5 = (f32[8,32,256]{2,1,0:T(8,128)S(1)}, f32[8,32,256]{2,1,0:T(8,128)S(1)}, u32[]{:S(2)}, u32[]{:S(2)}) collective-permute-start(f32[8,32,256]{2,1,0:T(8,128)S(1)} %add_rims.1.correction.mine), channel_id=1, source_target_pairs={{0,3},{1,2},{2,1},{3,0},{4,7},{5,6},{6,5},{7,4},{8,11},{9,10},{10,... | collective-permute-start | bytes 786440 | tf_op jit(solution)/shard_map/ppermute | solution.py:582
  28.6 0.2 slot_places.1
  28.8 2.4 %moment_rows.1 = f32[64,128]{1,0:T(8,128)S(1)} custom-call(f32[8,64,256]{2,1,0:T(8,128)S(1)} %copy-done.1, f32[8,32,256]{2,1,0:T(8,128)S(1)} %add_rims.1.correction.mine, s32[8,64,256]{2,1,0:T(8,128)S(1)} %copy-done.3, f32[64,16]{1,0:T(8,128)S(1)} %get-tuple-element.40.picked, f32[64,128]{1,0:T(8,128)S(1)} %get-tuple-element.41.base), custom_call_target="tpu_custom_call" | custom-call | tf_op jit(solution)/shard_map/moment_rows/pallas_call | solution.py:451
  31.2 13.5 %all_to_all.11 = f32[8,8,128]{2,1,0:T(8,128)S(1)} all-to-all(f32[8,8,128]{2,1,0:T(8,128)S(1)} %bitcast.3), channel_id=1, replica_groups=mesh['tile'=8,'view'=4] {'tile'}, dimensions={0} | all-to-all | bytes 65536 | tf_op jit(solution)/shard_map/all_to_all | solution.py:585
  44.7 0.3 segment_table.1.table.first
  45.0 0.1 update.1.mine
  45.1 0.1 collective-permute-start.6
  45.2 1.4 %collective-permute-start.7 = (f32[16,128]{1,0:T(8,128)S(1)}, f32[16,128]{1,0:T(8,128)S(1)}, u32[]{:S(2)}, u32[]{:S(2)}) collective-permute-start(f32[16,128]{1,0:T(8,128)S(1)} %segment_table.1.table.first), channel_id=1, source_target_pairs={{0,2},{1,3},{2,0},{3,1},{4,6},{5,7},{6,4},{7,5},{8,10},{9,11},{10,... | collective-permute-start | bytes 24584 | tf_op jit(solution)/shard_map/ppermute | solution.py:588
  46.5 3.0 %collective-permute-start.8 = (f32[16,128]{1,0:T(8,128)S(1)}, f32[16,128]{1,0:T(8,128)S(1)}, u32[]{:S(2)}, u32[]{:S(2)}) collective-permute-start(f32[16,128]{1,0:T(8,128)S(1)} %segment_table.1.table.first), channel_id=1, source_target_pairs={{0,3},{1,2},{2,1},{3,0},{4,7},{5,6},{6,5},{7,4},{8,11},{9,10},{10,... | collective-permute-start | bytes 24584 | tf_op jit(solution)/shard_map/ppermute | solution.py:588
  49.5 0.8 %own_half.1.begun = f32[8,64,256]{2,1,0:T(8,128)} custom-call(f32[264,256]{1,0:T(8,128)S(1)} %update.1.mine), custom_call_target="tpu_custom_call" | custom-call | tf_op jit(solution)/shard_map/own_half/pallas_call | solution.py:505
  50.3 1.0 %collective-permute-done.7.third = f32[16,128]{1,0:T(8,128)S(1)} collective-permute-done((f32[16,128]{1,0:T(8,128)S(1)}, f32[16,128]{1,0:T(8,128)S(1)}, u32[]{:S(2)}, u32[]{:S(2)}) %collective-permute-start.7) | collective-permute-done | bytes 8224 | tf_op jit(solution)/shard_map/ppermute | solution.py:588
  51.3 1.7 %collective-permute-done.8.fourth = f32[16,128]{1,0:T(8,128)S(1)} collective-permute-done((f32[16,128]{1,0:T(8,128)S(1)}, f32[16,128]{1,0:T(8,128)S(1)}, u32[]{:S(2)}, u32[]{:S(2)}) %collective-permute-start.8) | collective-permute-done | bytes 8224 | tf_op jit(solution)/shard_map/ppermute | solution.py:588
  53.0 0.6 %collective-permute-done.6.other = f32[264,256]{1,0:T(8,128)S(1)} collective-permute-done((f32[264,256]{1,0:T(8,128)S(1)}, f32[264,256]{1,0:T(8,128)S(1)}, u32[]{:S(2)}, u32[]{:S(2)}) %collective-permute-start.6) | collective-permute-done | bytes 270368 | tf_op jit(solution)/shard_map/ppermute | solution.py:591
  53.6 1.4 %finish.1 = (f32[8,64,256]{2,1,0:T(8,128)}, f32[10,128]{1,0:T(8,128)}) custom-call(f32[8,64,256]{2,1,0:T(8,128)} %own_half.1.begun, f32[264,256]{1,0:T(8,128)S(1)} %collective-permute-done.6.other, f32[16,128]{1,0:T(8,128)S(1)} %segment_table.1.table.first, f32[16,128]{1,0:T(8,128)S(1)} %collective-permute-done.7.third, ...), custom_call_target="tpu_custom_call", output_to_operand_aliasing={{0}: (0, {})} | custom-call | tf_op jit(solution)/shard_map/finish/pallas_call | solution.py:540
  (16 shorter events, 0.1 us)
Async XLA Ops:
  0.6 1.0 %copy-start = (f32[8,64,256]{2,1,0:T(8,128)S(1)}, f32[8,64,256]{2,1,0:T(8,128)}, u32[]{:S(2)}) copy-start(f32[8,64,256]{2,1,0:T(8,128)} %estimate.9) | copy-start | bytes 1572868
  1.7 5.2 %copy-start.6 = (f32[1,3,15]{2,0,1:T(1,128)S(1)}, f32[1,3,15]{2,0,1:T(1,128)}, u32[]{:S(2)}) copy-start(f32[1,3,15]{2,0,1:T(1,128)} %param.8) | copy-start | bytes 544
  1.7 5.2 %copy-start.2 = (f32[1,8,64,256]{3,2,1,0:T(8,128)S(1)}, f32[1,8,64,256]{3,2,1,0:T(8,128)}, u32[]{:S(2)}) copy-start(f32[1,8,64,256]{3,2,1,0:T(8,128)} %refs_7_.1) | copy-start | bytes 1572868
  1.7 6.9 %copy-start.1 = (f32[8,64,256]{2,1,0:T(8,128)S(1)}, f32[8,64,256]{2,1,0:T(8,128)}, u32[]{:S(2)}) copy-start(f32[8,64,256]{2,1,0:T(8,128)} %estimate.9) | copy-start | bytes 1572868
  1.7 7.9 %collective-permute-start.1 = (f32[7,48,256]{2,1,0:T(8,128)S(1)}, f32[7,48,256]{2,1,0:T(8,128)S(1)}, u32[]{:S(2)}, u32[]{:S(2)}) collective-permute-start(f32[7,48,256]{2,1,0:T(8,128)S(1)} %get-tuple-element.27), channel_id=1, source_target_pairs={{4,8},{12,16},{20,24},{8,4},{16,12},{24,20},{5,9},{13,17},{21,25},... | collective-permute-start | bytes 1032200 | tf_op jit(solution)/shard_map/ppermute | solution.py:572
  2.6 7.1 %collective-permute-start.2 = (f32[7,48,256]{2,1,0:T(8,128)S(1)}, f32[7,48,256]{2,1,0:T(8,128)S(1)}, u32[]{:S(2)}, u32[]{:S(2)}) collective-permute-start(f32[7,48,256]{2,1,0:T(8,128)S(1)} %get-tuple-element.28), channel_id=1, source_target_pairs={{0,4},{4,0},{8,12},{12,8},{16,20},{20,16},{24,28},{28,24},{1,5},{5... | collective-permute-start | bytes 1032200 | tf_op jit(solution)/shard_map/ppermute | solution.py:573
  7.0 9.9 %collective-permute-start = (f32[328,256]{1,0:T(8,128)S(1)}, f32[328,256]{1,0:T(8,128)S(1)}, u32[]{:S(2)}, u32[]{:S(2)}) collective-permute-start(f32[328,256]{1,0:T(8,128)S(1)} %view_out.1), channel_id=1, source_target_pairs={{0,1},{1,0},{2,3},{3,2},{4,5},{5,4},{6,7},{7,6},{8,9},{9,8},{10,11... | collective-permute-start | bytes 1007624 | tf_op jit(solution)/shard_map/ppermute | solution.py:570
  20.1 3.9 %collective-permute-start.3 = (f32[7,32,256]{2,1,0:T(8,128)S(1)}, f32[7,32,256]{2,1,0:T(8,128)S(1)}, u32[]{:S(2)}, u32[]{:S(2)}) collective-permute-start(f32[7,32,256]{2,1,0:T(8,128)S(1)} %get-tuple-element.38), channel_id=1, source_target_pairs={{4,8},{12,16},{20,24},{8,4},{16,12},{24,20},{5,9},{13,17},{21,25},... | collective-permute-start | bytes 688136 | tf_op jit(solution)/shard_map/ppermute | solution.py:578
  20.8 4.0 %collective-permute-start.4 = (f32[7,32,256]{2,1,0:T(8,128)S(1)}, f32[7,32,256]{2,1,0:T(8,128)S(1)}, u32[]{:S(2)}, u32[]{:S(2)}) collective-permute-start(f32[7,32,256]{2,1,0:T(8,128)S(1)} %get-tuple-element.39), channel_id=1, source_target_pairs={{0,4},{4,0},{8,12},{12,8},{16,20},{20,16},{24,28},{28,24},{1,5},{5... | collective-permute-start | bytes 688136 | tf_op jit(solution)/shard_map/ppermute | solution.py:579
  24.0 4.8 %copy-start.3 = (s32[8,64,256]{2,1,0:T(8,128)S(1)}, s32[8,64,256]{2,1,0:T(8,128)}, u32[]{:S(2)}) copy-start(s32[8,64,256]{2,1,0:T(8,128)} %labels.1) | copy-start | bytes 1572868
  24.9 3.7 %copy-start.4 = (s32[1,16,1]{1,2,0:T(1,128)S(1)}, s32[1,16,1]{1,2,0:T(1,128)}, u32[]{:S(2)}) copy-start(s32[1,16,1]{1,2,0:T(1,128)} %param.10) | copy-start | bytes 196
  24.9 3.7 %copy-start.5 = (s32[1,16]{1,0:T(1,128)S(1)}, s32[1,16]{1,0:T(1,128)}, u32[]{:S(2)}) copy-start(s32[1,16]{1,0:T(1,128)} %index_row.1) | copy-start | bytes 196
  24.9 20.1 %collective-permute-start.5 = (f32[8,32,256]{2,1,0:T(8,128)S(1)}, f32[8,32,256]{2,1,0:T(8,128)S(1)}, u32[]{:S(2)}, u32[]{:S(2)}) collective-permute-start(f32[8,32,256]{2,1,0:T(8,128)S(1)} %add_rims.1.correction.mine), channel_id=1, source_target_pairs={{0,3},{1,2},{2,1},{3,0},{4,7},{5,6},{6,5},{7,4},{8,11},{9,10},{10,... | collective-permute-start | bytes 786440 | tf_op jit(solution)/shard_map/ppermute | solution.py:582
  45.1 8.5 %collective-permute-start.6 = (f32[264,256]{1,0:T(8,128)S(1)}, f32[264,256]{1,0:T(8,128)S(1)}, u32[]{:S(2)}, u32[]{:S(2)}) collective-permute-start(f32[264,256]{1,0:T(8,128)S(1)} %update.1.mine), channel_id=1, source_target_pairs={{0,1},{1,0},{2,3},{3,2},{4,5},{5,4},{6,7},{7,6},{8,9},{9,8},{10,11... | collective-permute-start | bytes 811016 | tf_op jit(solution)/shard_map/ppermute | solution.py:591
  45.2 6.2 %collective-permute-start.7 = (f32[16,128]{1,0:T(8,128)S(1)}, f32[16,128]{1,0:T(8,128)S(1)}, u32[]{:S(2)}, u32[]{:S(2)}) collective-permute-start(f32[16,128]{1,0:T(8,128)S(1)} %segment_table.1.table.first), channel_id=1, source_target_pairs={{0,2},{1,3},{2,0},{3,1},{4,6},{5,7},{6,4},{7,5},{8,10},{9,11},{10,... | collective-permute-start | bytes 24584 | tf_op jit(solution)/shard_map/ppermute | solution.py:588
  46.5 6.4 %collective-permute-start.8 = (f32[16,128]{1,0:T(8,128)S(1)}, f32[16,128]{1,0:T(8,128)S(1)}, u32[]{:S(2)}, u32[]{:S(2)}) collective-permute-start(f32[16,128]{1,0:T(8,128)S(1)} %segment_table.1.table.first), channel_id=1, source_target_pairs={{0,3},{1,2},{2,1},{3,0},{4,7},{5,6},{6,5},{7,4},{8,11},{9,10},{10,... | collective-permute-start | bytes 24584 | tf_op jit(solution)/shard_map/ppermute | solution.py:588

commit v4 on v3

--- a/solution.py
+++ b/solution.py
@@ -11,6 +11,8 @@
 ROWS = 8
 NUC_DEV = 128
 LANES = 128
+PARTS = 2
+IDS = 24
 F32 = jnp.float32
 BF16 = jnp.bfloat16
 ANY = pl.BlockSpec(memory_space=pl.ANY)
@@ -109,12 +111,20 @@
     deep, high, flat = [[weights[axis : axis + 1, t : t + 1] for t in range(taps)] for axis in range(3)]
     start = pl.multiple_of((2 * keep - rows) * half, 16)
     seen_start = (2 * keep - seen) * half
-    upper, lower = split(band(flat[::-1], (across, across), radius))
-    wide[0, 0] = upper
-    wide[0, 1] = lower
-    upper, lower = split(band(flat, (across, across), radius))
-    wide[1, 0] = upper
-    wide[1, 1] = lower
+    near_diagonal = jnp.abs(
+        lax.broadcasted_iota(jnp.int32, (across, across), 1)
+        - lax.broadcasted_iota(jnp.int32, (across, across), 0)
+    ) <= radius
+    for turn, line in enumerate((flat[::-1], flat)):
+        first_row = jnp.concatenate(
+            line[radius:] + [jnp.zeros((1, across - taps), F32)] + line[:radius], axis=1
+        )
+        square = pltpu.roll(
+            jnp.broadcast_to(first_row, (across, across)), 0, 1, stride=1, stride_axis=0
+        )
+        upper, lower = split(jnp.where(near_diagonal, square, 0.0))
+        wide[turn, 0] = upper
+        wide[turn, 1] = lower
     upper, lower = split(band(high, (seen, rows), radius + start - seen_start))
     tall[...] = jnp.concatenate([upper, upper, lower], axis=1)
     upper, lower = split(band(high[::-1], (keep, rows), radius + seen_start - keep * half))
@@ -154,11 +164,11 @@
     return [jnp.broadcast_to(spread[step : step + 1, :], (16, LANES)) for step in range(taps)]
 
 
-def view_kernel(
-    first, wide, tall, back, part, spread, far, near, view, begun_near, begun_far,
-    field, send_near, send_far,
-    blur_hi, blur_lo, plane_hi, plane_lo,
-):
+def view_kernel(first, *refs):
+    wide, tall, back, part, spread, far, near, view = refs[:8]
+    begun, refs = ((), refs[8:]) if first else (refs[8 : 8 + 2 * PARTS], refs[8 + 2 * PARTS :])
+    field, *sends = refs[: 1 + 2 * PARTS]
+    blur_hi, blur_lo, plane_hi, plane_lo = refs[1 + 2 * PARTS :]
     planes, radius = part.shape[0], near.shape[0]
     rows, across = near.shape[1], near.shape[2]
     keep, seen = back.shape[0], tall.shape[0]
@@ -190,23 +200,28 @@
     lines = jnp.dot(blur_hi[...], upper, preferred_element_type=F32)
     lines += jnp.dot(blur_lo[...], upper, preferred_element_type=F32)
     lines += jnp.dot(blur_hi[...], lower, preferred_element_type=F32)
+    forwards = []
     for plane in range(planes):
         hi, lo = split(lines[plane * rows : (plane + 1) * rows])
-        forward = jnp.dot(
-            tall[...], jnp.concatenate([hi, lo, hi], axis=0), preferred_element_type=F32
+        forwards.append(
+            jnp.dot(tall[...], jnp.concatenate([hi, lo, hi], axis=0), preferred_element_type=F32)
         )
+    ratios = []
+    for plane in range(planes):
         if first:
             recorded = view[0, plane, pl.ds(seen_start, seen), :]
         else:
             recorded = view[plane * seen : (plane + 1) * seen]
-        ratio = recorded / forward
+        ratio = recorded / forwards[plane]
         if rows > seen:
             ratio = jnp.concatenate([ratio, jnp.zeros((rows - seen, across), F32)], axis=0)
-        hi, lo = split(ratio)
-        turned = jnp.dot(
-            back[...], jnp.concatenate([hi, lo, hi], axis=0), preferred_element_type=F32
-        )
-        hi, lo = split(turned)
+        ratios.append(split(ratio))
+    turned = [
+        jnp.dot(back[...], jnp.concatenate([hi, lo, hi], axis=0), preferred_element_type=F32)
+        for hi, lo in ratios
+    ]
+    for plane in range(planes):
+        hi, lo = split(turned[plane])
         plane_hi[plane * keep : (plane + 1) * keep] = hi
         plane_lo[plane * keep : (plane + 1) * keep] = lo
     upper, lower = wide[1, 0], wide[1, 1]
@@ -218,14 +233,16 @@
         source = lambda place: field[place, row, lane]
         below = depth_terms(source, factors, 0, planes, range(-radius, 0), True)
         above = depth_terms(source, factors, 0, planes, range(planes, planes + radius), True)
+        part_at, inside = divmod(row.start, keep // PARTS)
+        inside = slice(inside, inside + 16)
         for at in range(radius):
             down, up = below[at - radius], above[at + planes]
-            to_near, to_far = jnp.where(even, up, down), jnp.where(even, down, up)
+            to_far, to_near = jnp.where(even, down, up), jnp.where(even, up, down)
             if not first:
-                to_near += begun_near[at, row, lane]
-                to_far += begun_far[at, row, lane]
-            send_near[at, row, lane] = to_near
-            send_far[at, row, lane] = to_far
+                to_far += begun[2 * part_at][at, inside, lane]
+                to_near += begun[2 * part_at + 1][at, inside, lane]
+            sends[2 * part_at][at, inside, lane] = to_far
+            sends[2 * part_at + 1][at, inside, lane] = to_near
 
 
 def view_field(first, prepared, near, far, view, begun):
@@ -233,20 +250,12 @@
     planes = prepared[3].shape[0]
     radius, rows, across = near.shape
 
-    def body(*refs):
-        if first:
-            refs = refs[:8] + (None, None) + refs[8:]
-        view_kernel(first, *refs)
-
-    return pl.pallas_call(
-        body,
-        out_shape=(
-            jax.ShapeDtypeStruct((planes, keep, across), F32),
-            jax.ShapeDtypeStruct((radius, keep, across), F32),
-            jax.ShapeDtypeStruct((radius, keep, across), F32),
-        ),
+    send = jax.ShapeDtypeStruct((radius, keep // PARTS, across), F32)
+    return pl.pallas_call(
+        functools.partial(view_kernel, first),
+        out_shape=(jax.ShapeDtypeStruct((planes, keep, across), F32),) + (send,) * (2 * PARTS),
         in_specs=[VMEM] * (8 + len(begun)),
-        out_specs=(VMEM, VMEM, VMEM),
+        out_specs=(VMEM,) * (1 + 2 * PARTS),
         scratch_shapes=[
             pltpu.VMEM((planes * rows, across), BF16),
             pltpu.VMEM((planes * rows, across), BF16),
@@ -258,8 +267,8 @@
     )(*prepared, far, near, view, *begun)
 
 
-def own_kernel(taps, spread_own, spread_other, field_own, field_other, inner):
-    planes, keep, across = inner.shape
+def own_kernel(taps, spread_own, spread_other, field_own, field_other, *inner):
+    planes, keep, across = field_own.shape
     factors = [spread_factors(spread, taps) for spread in (spread_own, spread_other)]
     for row, lane in chunks(keep, across):
         parts = [
@@ -268,22 +277,25 @@
             )
             for which, field in enumerate((field_own, field_other))
         ]
+        part_at, inside = divmod(row.start, keep // PARTS)
         for plane in range(planes):
-            inner[plane, row, lane] = parts[0][plane] + parts[1][plane]
+            inner[part_at][plane, inside : inside + 16, lane] = parts[0][plane] + parts[1][plane]
 
 
 def own_planes(taps, spread_own, spread_other, field_own, field_other):
+    planes, keep, across = field_own.shape
     return pl.pallas_call(
         functools.partial(own_kernel, taps),
-        out_shape=jax.ShapeDtypeStruct(field_own.shape, F32),
+        out_shape=(jax.ShapeDtypeStruct((planes, keep // PARTS, across), F32),) * PARTS,
         in_specs=[VMEM] * 4,
-        out_specs=VMEM,
+        out_specs=(VMEM,) * PARTS,
         compiler_params=pltpu.CompilerParams(vmem_limit_bytes=LIMIT),
         name="own_planes",
     )(spread_own, spread_other, field_own, field_other)
 
 
-def rims_kernel(inner, far, near, correction):
+def rims_kernel(inner, far, near, *rest):
+    correction = rest[-1]
     planes, radius = inner.shape[0], near.shape[0]
     even = lax.axis_index("tile") % 2 == 0
     for plane in range(planes):
@@ -296,43 +308,46 @@
         correction[plane] = total
 
 
-def add_rims(inner, near, far):
+def add_rims(inner, far, near, *after):
     return pl.pallas_call(
         rims_kernel,
         out_shape=jax.ShapeDtypeStruct(inner.shape, F32),
-        in_specs=[VMEM] * 3,
+        in_specs=[VMEM] * 3 + [ANY] * len(after),
         out_specs=VMEM,
         compiler_params=pltpu.CompilerParams(vmem_limit_bytes=LIMIT),
         name="add_rims",
-    )(inner, far, near)
+    )(inner, far, near, *after)
 
 
 def table_rows(table):
     return jnp.concatenate([table[:8], table[8:]], axis=1)
 
 
-def update_kernel(views, estimate, mine, other, table, result):
-    planes, keep, across = mine.shape
-    half = half_of(lax.axis_index("view"))
-    start = pl.multiple_of(keep * half, 8)
+def update_kernel(views, part, tabled, estimate, mine, other, *rest):
+    planes, size, across = mine.shape
+    half = half_of(lax.axis_index("view"))
+    start = pl.multiple_of(size * (PARTS * half + part), 8)
+    result = rest[-1]
     for plane in range(planes):
-        held = estimate[plane, pl.ds(start, keep)]
-        at = slice(plane * keep, (plane + 1) * keep)
+        held = estimate[plane, pl.ds(start, size)]
+        at = slice(plane * size, (plane + 1) * size)
         result[at] = held * (mine[plane] + other[plane]) * (1.0 / views)
-    result[planes * keep :] = jnp.zeros((8, across), F32)
-    result[planes * keep :, : 2 * LANES] = table_rows(table[...])
-
-
-def update(views, estimate, mine, other, table):
-    planes, keep, across = mine.shape
-    return pl.pallas_call(
-        functools.partial(update_kernel, views),
-        out_shape=jax.ShapeDtypeStruct((planes * keep + 8, across), F32),
-        in_specs=[VMEM] * 4,
+    if tabled:
+        table = rest[0][...]
+        result[planes * size :] = jnp.zeros((8, across), F32)
+        result[planes * size :, : 2 * LANES] = jnp.concatenate([table[:8], table[8:]], axis=1)
+
+
+def update(views, part, estimate, mine, other, table, after):
+    planes, size, across = mine.shape
+    return pl.pallas_call(
+        functools.partial(update_kernel, views, part, len(table) > 0),
+        out_shape=jax.ShapeDtypeStruct((planes * size + 8 * len(table), across), F32),
+        in_specs=[VMEM] * (3 + len(table)) + [ANY] * len(after),
         out_specs=VMEM,
         compiler_params=pltpu.CompilerParams(vmem_limit_bytes=LIMIT),
         name="update",
-    )(estimate, mine, other, table)
+    )(estimate, mine, other, *table, *after)
 
 
 def slots_kernel(owner_row, index_row, picked, base):
@@ -352,7 +367,7 @@
     picked[...] = chosen.astype(F32)
     ids = jnp.sum(jnp.where(chosen, index_row[...].astype(F32), 0.0), axis=1, keepdims=True)
     lanes = lax.broadcasted_iota(jnp.int32, (count, LANES), 1)
-    base[...] = jnp.where(lanes == MOM, ids, 0.0)
+    base[...] = jnp.where(lanes == IDS, ids, 0.0)
 
 
 def slot_places(tiles, label_owner, label_index):
@@ -370,73 +385,69 @@
     )(label_owner.reshape(1, slots), label_index)
 
 
-def moments_kernel(
-    views, depth_total, estimate, correction, labels, picked, base, sent, held, sums, table
-):
-    planes, keep, across = correction.shape
+def moments_kernel(views, depth_total, estimate, labels, picked, base, *refs):
+    corrections, (sent, held, sums, table) = refs[:PARTS], refs[PARTS:]
+    planes, keep, across = held.shape
+    size = keep // PARTS
     height_total = estimate.shape[1]
     slots = picked.shape[1]
     half = half_of(lax.axis_index("view"))
     first = (lax.axis_index("tile") * planes).astype(F32) + 0.5
     start = pl.multiple_of(keep * half, 8)
-    held[...] = estimate[:, pl.ds(start, keep)] * correction[...] * (1.0 / views)
+    for part, correction in enumerate(corrections):
+        rows = pl.ds(pl.multiple_of(start + part * size, 8), size)
+        held[:, part * size : (part + 1) * size] = (
+            estimate[:, rows] * correction[...] * (1.0 / views)
+        )
     group = 16
-    columns = lax.broadcasted_iota(jnp.int32, (across, LANES), 1)
-    spot = (lax.broadcasted_iota(jnp.int32, (across, LANES), 0).astype(F32) + 0.5) / across
-    one, line, square = jnp.ones_like(spot), spot, spot * spot
-
-    def placed(*pairs):
-        result = jnp.zeros((across, LANES), F32)
-        for lane, value in pairs:
-            result = jnp.where(columns == lane, value, result)
-        return result
-
-    factors = jnp.concatenate(
-        [
-            placed((0, one), (3, line), (6, square)),
-            placed((2, one), (9, line)),
-            placed((5, one)),
-            placed((1, one), (8, line)),
-            placed((7, one)),
-            placed((4, one)),
-        ],
-        axis=0,
-    )
+    spot = lax.broadcasted_iota(jnp.int32, (across, LANES), 0)
+    lanes = lax.broadcasted_iota(jnp.int32, (across, LANES), 1)
+    low = (spot * spot) & 255
+    factors = jnp.where(lanes == 0, 1, jnp.where(lanes == 1, spot, 0))
+    factors = jnp.where(lanes == 2, spot * spot - low, jnp.where(lanes == 3, low, factors))
+    factors = factors.astype(F32).astype(BF16)
     base_row = lax.broadcasted_iota(jnp.int32, (8, across), 0)
 
     def one_group(number, carry):
-        def one_slot(inner, carry):
-            slot = number * group + inner
-            parts = [jnp.zeros((8, across), F32) for _ in range(6)]
+        for pair in range(0, group, 2):
+            slot = [number * group + pair, number * group + pair + 1]
+            parts = [[None] * 6 for _ in slot]
             for row in range(0, keep, 8):
-                high = ((base_row + (row + start)).astype(F32) + 0.5) / height_total
-                flat, once, twice = [jnp.zeros((8, across), F32) for _ in range(3)]
+                high = ((base_row + (row + start)).astype(F32) + 0.5) * (1.0 / height_total)
+                flat, once, twice = [[jnp.zeros((8, across), F32) for _ in slot] for _ in range(3)]
                 for plane in reversed(range(planes)):
-                    hit = labels[plane, pl.ds(pl.multiple_of(start + row, 8), 8)] == slot
-                    flat = flat + jnp.where(hit, held[plane, row : row + 8], 0.0)
-                    if plane > 0:
-                        once = once + flat
-                        twice = twice + once
-                square_sum = 2.0 * twice - once
-                deep = (first * flat + once) * (1.0 / depth_total)
-                deeper = (first * (first * flat + 2.0 * once) + square_sum) * (1.0 / depth_total**2)
-                scaled = flat * high
-                parts[0] = parts[0] + flat
-                parts[1] = parts[1] + scaled
-                parts[2] = parts[2] + scaled * high
-                parts[3] = parts[3] + deep
-                parts[4] = parts[4] + deep * high
-                parts[5] = parts[5] + deeper
-            at = pl.multiple_of(inner * 8, 8)
-            sums[pl.ds(at, 8), :] = jnp.concatenate(parts, axis=1)
-            return carry
-
-        lax.fori_loop(0, group, one_slot, 0)
+                    mark = labels[plane, pl.ds(pl.multiple_of(start + row, 8), 8)]
+                    value = held[plane, row : row + 8]
+                    for at in range(2):
+                        flat[at] = flat[at] + jnp.where(mark == slot[at], value, 0.0)
+                        if plane > 0:
+                            once[at] = once[at] + flat[at]
+                            twice[at] = twice[at] + once[at]
+                for at in range(2):
+                    square_sum = 2.0 * twice[at] - once[at]
+                    line = first * flat[at]
+                    deep = (line + once[at]) * (1.0 / depth_total)
+                    deeper = (first * (line + 2.0 * once[at]) + square_sum) * (1.0 / depth_total**2)
+                    scaled = flat[at] * high
+                    terms = (flat[at], scaled, scaled * high, deep, deep * high, deeper)
+                    parts[at] = [new if old is None else old + new for old, new in zip(parts[at], terms)]
+            for at in range(2):
+                for kind in range(6):
+                    row = kind * group + pair + at
+                    sums[row : row + 1, :] = jnp.sum(parts[at][kind], axis=0, keepdims=True)
+        whole = sums[...]
+        upper, rest = split(whole)
+        rest = whole - upper.astype(F32)
+        middle, lower = split(rest)
         lines = jnp.dot(
-            sums[...], factors, precision=lax.Precision.HIGHEST, preferred_element_type=F32
+            jnp.concatenate([upper, middle, lower], axis=0), factors, preferred_element_type=F32
         )
-        at = pl.multiple_of(number * group, group)
-        table[pl.ds(at, group), :] = jnp.sum(lines.reshape(group, 8, LANES), axis=1)
+        count = 6 * group
+        lines = lines[:count] + lines[count : 2 * count] + lines[2 * count :]
+        total = lines[:group]
+        for kind in range(1, 6):
+            total += pltpu.roll(lines[kind * group : (kind + 1) * group], 4 * kind, 1)
+        table[pl.ds(pl.multiple_of(number * group, group), group), :] = total
         return carry
 
     lax.fori_loop(0, slots // group, one_group, 0)
@@ -445,39 +456,51 @@
     )
 
 
-def moment_rows(views, tiles, estimate, correction, labels, places):
-    planes, keep, across = correction.shape
+def moment_rows(views, tiles, estimate, corrections, labels, places):
+    planes, size, across = corrections[0].shape
     slots = places[0].shape[1]
     return pl.pallas_call(
         functools.partial(moments_kernel, views, tiles * planes),
         out_shape=jax.ShapeDtypeStruct((tiles * ROWS, LANES), F32),
-        in_specs=[VMEM] * 5,
+        in_specs=[VMEM] * (4 + PARTS),
         out_specs=VMEM,
         scratch_shapes=[
-            pltpu.VMEM(correction.shape, F32),
-            pltpu.VMEM((16 * 8, 6 * across), F32),
+            pltpu.VMEM((planes, size * PARTS, across), F32),
+            pltpu.VMEM((6 * 16, across), F32),
             pltpu.VMEM((slots, LANES), F32),
         ],
         compiler_params=pltpu.CompilerParams(vmem_limit_bytes=LIMIT),
         name="moment_rows",
-    )(estimate, correction, labels, *places)
-
-
-def segments_kernel(rows, table):
+    )(estimate, labels, *places, *corrections)
+
+
+def segments_kernel(across, rows, table):
     values = rows[...]
-    ids = values[:, MOM : MOM + 1].astype(jnp.int32)
+    ids = values[:, IDS : IDS + 1].astype(jnp.int32)
     spots = lax.broadcasted_iota(jnp.int32, (values.shape[0], NUC_DEV), 1)
     picked = (ids == spots).astype(F32)
     full = lax.dot_general(
         values, picked, (((0,), (0,)), ((), ())),
         precision=lax.Precision.HIGHEST, preferred_element_type=F32,
     )
-    table[...] = full[: table.shape[0]]
-
-
-def segment_table(rows):
-    return pl.pallas_call(
-        segments_kernel,
+    mass, high, higher, deep, deep_high, deeper = [full[4 * kind : 4 * kind + 4] for kind in range(6)]
+    flat = lambda sums: sums[0:1]
+    line = lambda sums: (sums[1:2] + 0.5 * sums[0:1]) * (1.0 / across)
+    square = lambda sums: (sums[2:3] + sums[3:4] + sums[1:2] + 0.25 * sums[0:1]) * (1.0 / across**2)
+    table[...] = jnp.concatenate(
+        [
+            flat(mass), flat(deep), flat(high), line(mass),
+            flat(deeper), flat(higher), square(mass),
+            flat(deep_high), line(deep), line(high),
+            jnp.zeros((table.shape[0] - MOM, NUC_DEV), F32),
+        ],
+        axis=0,
+    )
+
+
+def segment_table(across, rows):
+    return pl.pallas_call(
+        functools.partial(segments_kernel, across),
         out_shape=jax.ShapeDtypeStruct((16, NUC_DEV), F32),
         in_specs=[VMEM],
         out_specs=VMEM,
@@ -486,70 +509,78 @@
     )(rows)
 
 
-def own_half_kernel(keep, mine, whole, sems):
-    planes = whole.shape[0]
-    start = pl.multiple_of(keep * half_of(lax.axis_index("view")), 8)
+def stores(source, whole, half, part, size, sems):
+    start = pl.multiple_of(size * (PARTS * half + part), 8)
     copies = [
         pltpu.make_async_copy(
-            mine.at[pl.ds(plane * keep, keep)], whole.at[plane, pl.ds(start, keep)], sems.at[plane]
+            source.at[pl.ds(plane * size, size)], whole.at[plane, pl.ds(start, size)], sems.at[plane]
         )
-        for plane in range(planes)
+        for plane in range(whole.shape[0])
     ]
     for copy in copies:
         copy.start()
+    return copies
+
+
+def store_kernel(own, part, size, other, *refs):
+    whole, token, sems = refs[-3:]
+    half = half_of(lax.axis_index("view"))
+    copies = stores(other, whole, half if own else 1 - half, part, size, sems)
+    token[...] = jnp.zeros_like(token)
     for copy in copies:
         copy.wait()
 
 
-def own_half(mine, planes, keep):
-    return pl.pallas_call(
-        functools.partial(own_half_kernel, keep),
-        out_shape=jax.ShapeDtypeStruct((planes, 2 * keep, mine.shape[1]), F32),
-        in_specs=[ANY],
-        out_specs=ANY,
-        scratch_shapes=[pltpu.SemaphoreType.DMA((planes,))],
-        compiler_params=pltpu.CompilerParams(vmem_limit_bytes=LIMIT),
-        name="own_half",
-    )(mine)
-
-
-def finish_kernel(scale, keep, begun, other, first, third, fourth, whole, moments, sems):
+def store_part(own, part, size, shape, other, begun):
+    return pl.pallas_call(
+        functools.partial(store_kernel, own, part, size),
+        out_shape=(jax.ShapeDtypeStruct(shape, F32), jax.ShapeDtypeStruct((8, LANES), F32)),
+        in_specs=[ANY] * (1 + len(begun)),
+        out_specs=(ANY, VMEM),
+        input_output_aliases={1: 0} if begun else {},
+        scratch_shapes=[pltpu.SemaphoreType.DMA((shape[0],))],
+        compiler_params=pltpu.CompilerParams(vmem_limit_bytes=LIMIT),
+        name="store_part",
+    )(other, *begun)
+
+
+def finish_kernel(
+    scale, size, begun, other, tabled, first, third, fourth, whole, moments, held, sems, sem
+):
     planes = whole.shape[0]
-    start = pl.multiple_of(keep * (1 - half_of(lax.axis_index("view"))), 8)
-    copies = [
-        pltpu.make_async_copy(
-            other.at[pl.ds(plane * keep, keep)], whole.at[plane, pl.ds(start, keep)], sems.at[plane]
-        )
-        for plane in range(planes)
-    ]
-    for copy in copies:
-        copy.start()
-    rows = other[planes * keep :]
+    half = half_of(lax.axis_index("view"))
+    copies = stores(other, whole, 1 - half, PARTS - 1, size, sems)
+    rows = tabled[planes * size :]
     second = jnp.concatenate([rows[:, :LANES], rows[:, LANES : 2 * LANES]], axis=0)
     table = (first[...] + second) + (third[...] + fourth[...])
-    mass = table[0:1]
     lines = lax.broadcasted_iota(jnp.int32, table.shape, 0)
-    result = jnp.where(lines == 0, table * scale, table / jnp.maximum(mass, 1.0))
-    moments[...] = result[:MOM]
+    result = jnp.where(lines == 0, table * scale, table / jnp.maximum(table[0:1], 1.0))
+    held[...] = result[:MOM]
+    last = pltpu.make_async_copy(held, moments, sem)
+    last.start()
     for copy in copies:
         copy.wait()
-
-
-def finish(scale, keep, begun, other, tables):
-    planes = begun.shape[0]
-    return pl.pallas_call(
-        functools.partial(finish_kernel, scale, keep),
+    last.wait()
+
+
+def finish(scale, size, begun, other, tabled, tables):
+    return pl.pallas_call(
+        functools.partial(finish_kernel, scale, size),
         out_shape=(
             jax.ShapeDtypeStruct(begun.shape, F32),
             jax.ShapeDtypeStruct((MOM, NUC_DEV), F32),
         ),
-        in_specs=[ANY] + [VMEM] * 4,
-        out_specs=(ANY, VMEM),
+        in_specs=[ANY] + [VMEM] * 5,
+        out_specs=(ANY, ANY),
         input_output_aliases={0: 0},
-        scratch_shapes=[pltpu.SemaphoreType.DMA((planes,))],
+        scratch_shapes=[
+            pltpu.VMEM((MOM, NUC_DEV), F32),
+            pltpu.SemaphoreType.DMA((begun.shape[0],)),
+            pltpu.SemaphoreType.DMA,
+        ],
         compiler_params=pltpu.CompilerParams(vmem_limit_bytes=LIMIT),
         name="finish",
-    )(begun, other, *tables)
+    )(begun, other, tabled, *tables)
 
 
 def on_device(estimate, measured, kernels, labels, label_owner, label_index):
@@ -571,26 +602,37 @@
     to_far, to_near = rims_out(estimate, radius, rows)
     far = lax.ppermute(to_far, "tile", far_pairs)
     near = lax.ppermute(to_near, "tile", near_pairs)
-    own = prepare(False, taps, kernels, estimate, kernels, rows, seen, keep)
+    places = slot_places(tiles, label_owner, label_index)
+    own = prepare(False, taps, kernels, estimate, places[1], rows, seen, keep)
     field_own, *begun = view_field(True, own, near, far, measured, ())
     others = prepare(True, taps, swapped, estimate, begun[0], rows, seen, keep)
-    field_other, sum_near, sum_far = view_field(False, others, near, far, swapped, begun)
-    rim_far = lax.ppermute(sum_far, "tile", far_pairs)
-    rim_near = lax.ppermute(sum_near, "tile", near_pairs)
+    field_other, *sends = view_field(False, others, near, far, swapped, begun)
+    rims = [
+        lax.ppermute(send, "tile", pairs) for send, pairs in zip(sends, (far_pairs, near_pairs) * PARTS)
+    ]
     inner = own_planes(taps, own[4], others[4], field_own, field_other)
-    mine = add_rims(inner, rim_near, rim_far)
-    other = lax.ppermute(mine, "view", across_pairs)
-    places = slot_places(tiles, label_owner, label_index)
+    mine = []
+    for part in range(PARTS):
+        mine.append(add_rims(inner[part], *rims[2 * part : 2 * part + 2], *mine[-1:]))
+    other = [lax.ppermute(part, "view", across_pairs) for part in mine]
     sent = moment_rows(views, tiles, estimate, mine, labels, places)
     got = lax.all_to_all(sent, "tile", split_axis=0, concat_axis=0, tiled=True)
-    table = segment_table(got)
+    table = segment_table(across, got)
     tables = [table] + [
         lax.ppermute(table, "view", [(i, i ^ step) for i in range(views)]) for step in (2, 3)
     ]
-    new_half = update(views, estimate, mine, other, table)
-    new_other = lax.ppermute(new_half, "view", partner)
+    size = keep // PARTS
+    new_other, begun, token = [], [], []
+    for part in range(PARTS):
+        last = [table] if part == 0 else []
+        new_mine = update(views, part, estimate, mine[part], other[part], last, token)
+        new_other.append(lax.ppermute(new_mine, "view", partner))
+        *begun, after = store_part(True, part, size, estimate.shape, new_mine, begun)
+        token = [after]
+    for part in range(PARTS - 1):
+        *begun, _ = store_part(False, part, size, estimate.shape, new_other[part], begun)
     scale = label_index.shape[1] / (planes * height * across)
-    return finish(scale, keep, own_half(new_half, planes, keep), new_other, tables)
+    return finish(scale, size, begun[0], new_other[-1], new_other[0], tables)
 
 
 def solution(mesh):

time: 55.2 us -> 52.5 us (0.951)
  starting transfers between devices: 18.5 us -> 21.9 us
  blocking collectives: 13.5 us -> 10.4 us
  Pallas kernels: 12 us -> 10.4 us
  waiting for transfers between devices: 9.14 us -> 7.68 us
    ppermute x4 -> x8, starting transfers between devices: 7.32 us -> 13.5 us  [the longest x4 7.15 us: on_device(): lax.ppermute(send, 'tile', pairs)]
    all_to_all x1, blocking collectives: 13.5 us -> 10.4 us  [on_device(): got = lax.all_to_all(sent, 'tile', split_axis=0, concat_axis=0, tiled=True)]
    ppermute x2, starting transfers between devices: 4.37 us -> 1.54 us  [on_device(): lax.ppermute(table, 'view', [(i, i ^ step) for i in range(views)])]
    ppermute x2, waiting for transfers between devices: 2.68 us -> 0.25 us  [on_device(): lax.ppermute(table, 'view', [(i, i ^ step) for i in range(views)])]
    ppermute x1, waiting for transfers between devices: 5 us -> 6.21 us  [on_device(): swapped = lax.ppermute(packed, 'view', partner)]
    pallas_call x2, Pallas kernels: 2.07 us -> 1.18 us  [prepare(): pl.pallas_call(functools.partial(prepare_kernel, packed, taps), out_shape...]
    pallas_call x1, Pallas kernels: 2.39 us -> 1.77 us  [moment_rows(): pl.pallas_call(functools.partial(moments_kernel, views, tiles * planes),...]
    ppermute x4 -> x8, waiting for transfers between devices: 1.45 us -> 1.21 us  [the longest x2 1.2 us: on_device(): new_other.append(lax.ppermute(new_mine, 'view', partner))]
  transfers between devices with their start and end apart: 9 -> 13, of which waited for: 5 -> 4; matrix products, arithmetic and copies ran while one was open for 0% -> 0% of each run, Pallas kernels for 13% -> 15%
where the time goes in v4:
time: 52.5 us; the launch traced here: 52.3 us
  starting transfers between devices  21.9 us (42%)
  Pallas kernels  10.4 us (20%)
  blocking collectives  10.4 us (20%)
  waiting for transfers between devices  7.68 us (15%)
  local copies, waits for them, and re-layouts  1.07 us (2%)
  between operations  0.85 us (2%)
    all_to_all x1, blocking collectives, on_device(): got = lax.all_to_all(sent, 'tile', split_axis=0, concat_axis=0, tiled=True)  10.4 us
    ppermute x4, starting transfers between devices, on_device(): lax.ppermute(send, 'tile', pairs)  7.15 us
    ppermute x1, waiting for transfers between devices, on_device(): swapped = lax.ppermute(packed, 'view', partner)  6.21 us
    ppermute x1, starting transfers between devices, on_device(): near = lax.ppermute(to_near, 'tile', near_pairs)  4.34 us
    ppermute x2, starting transfers between devices, on_device(): other = [lax.ppermute(part, 'view', across_pairs) for part in mine]  4.26 us
    pallas_call x3, Pallas kernels, store_part(): pl.pallas_call(functools.partial(store_kernel, own, part, size), out_shap...  3.33 us
    pallas_call x2, Pallas kernels, view_field(): pl.pallas_call(functools.partial(view_kernel, first), out_shape=(jax.Shap...  2.44 us
    ppermute x2, starting transfers between devices, on_device(): new_other.append(lax.ppermute(new_mine, 'view', partner))  2.14 us
  transfers between devices with their start and end apart: 13, of which 4 were waited for; matrix products, arithmetic and copies ran while one was open for 0% of the time, Pallas kernels for 15%

profile of v4, /device:TPU:0, one launch (start us, length us, event | category | flops | bytes accessed | tf_op | source)
XLA Modules:
  0.0 52.3 jit_solution(11381705013736938030)
XLA Ops:
  0.6 1.0 %copy-done = f32[8,64,256]{2,1,0:T(8,128)S(1)} copy-done((f32[8,64,256]{2,1,0:T(8,128)S(1)}, f32[8,64,256]{2,1,0:T(8,128)}, u32[]{:S(2)}) %copy-start) | copy-done | bytes 524312
  1.7 0.0 copy-start.1
  1.7 0.8 %collective-permute-start.1 = (f32[7,48,256]{2,1,0:T(8,128)S(1)}, f32[7,48,256]{2,1,0:T(8,128)S(1)}, u32[]{:S(2)}, u32[]{:S(2)}) collective-permute-start(f32[7,48,256]{2,1,0:T(8,128)S(1)} %get-tuple-element.38), channel_id=1, source_target_pairs={{4,8},{12,16},{20,24},{8,4},{16,12},{24,20},{5,9},{13,17},{21,25},... | collective-permute-start | bytes 1032200 | tf_op jit(solution)/shard_map/ppermute | solution.py:603
  2.6 4.3 %collective-permute-start.2 = (f32[7,48,256]{2,1,0:T(8,128)S(1)}, f32[7,48,256]{2,1,0:T(8,128)S(1)}, u32[]{:S(2)}, u32[]{:S(2)}) collective-permute-start(f32[7,48,256]{2,1,0:T(8,128)S(1)} %get-tuple-element.39), channel_id=1, source_target_pairs={{0,4},{4,0},{8,12},{12,8},{16,20},{20,16},{24,28},{28,24},{1,5},{5... | collective-permute-start | bytes 1032200 | tf_op jit(solution)/shard_map/ppermute | solution.py:604
  7.0 1.6 %collective-permute-start = (f32[328,256]{1,0:T(8,128)S(1)}, f32[328,256]{1,0:T(8,128)S(1)}, u32[]{:S(2)}, u32[]{:S(2)}) collective-permute-start(f32[328,256]{1,0:T(8,128)S(1)} %view_out.1), channel_id=1, source_target_pairs={{0,1},{1,0},{2,3},{3,2},{4,5},{5,4},{6,7},{7,6},{8,9},{9,8},{10,11... | collective-permute-start | bytes 1007624 | tf_op jit(solution)/shard_map/ppermute | solution.py:601
  8.6 0.2 slot_places.1
  8.8 0.6 %prepare.2 = (bf16[2,2,256,256]{3,2,1,0:T(8,128)(2,1)S(1)}, bf16[40,144]{1,0:T(8,128)(2,1)S(1)}, bf16[32,144]{1,0:T(8,128)(2,1)S(1)}, f32[8,48,256]{2,1,0:T(8,128)S(1)}, f32[16,128]{1,0:T(8,128)S(1)}) custom-call(f32[1,3,15]{2,1,0:T(4,128)S(1)} %copy.11.source.kernels, f32[8,64,256]{2,1,0:T(8,128)S(1)} %copy-done.1, f32[64,128]{1,0:T(8,128)S(1)} %get-tuple-element.32.after.base), custom_call_target="tpu_custom_call" | custom-call | tf_op jit(solution)/shard_map/prepare/pallas_call | solution.py:147
  9.5 1.2 %view_first.1 = (f32[8,32,256]{2,1,0:T(8,128)S(1)}, f32[7,16,256]{2,1,0:T(8,128)S(1)}, f32[7,16,256]{2,1,0:T(8,128)S(1)}, f32[7,16,256]{2,1,0:T(8,128)S(1)}, f32[7,16,256]{2,1,0:T(8,128)S(1)}) custom-call(bf16[2,2,256,256]{3,2,1,0:T(8,128)(2,1)S(1)} %get-tuple-element.34.refs_0_, bf16[40,144]{1,0:T(8,128)(2,1)S(1)} %get-tuple-element.35.refs_1_, ...), custom_call_target="tpu_custom_call" | custom-call | tf_op jit(solution)/shard_map/view_first/pallas_call | solution.py:254
  10.7 6.2 %collective-permute-done.source.refs_7_ = f32[328,256]{1,0:T(8,128)S(1)} collective-permute-done((f32[328,256]{1,0:T(8,128)S(1)}, f32[328,256]{1,0:T(8,128)S(1)}, u32[]{:S(2)}, u32[]{:S(2)}) %collective-permute-start) | collective-permute-done | bytes 335904 | tf_op jit(solution)/shard_map/ppermute | solution.py:601
  16.9 0.6 %prepare.3 = (bf16[2,2,256,256]{3,2,1,0:T(8,128)(2,1)S(1)}, bf16[40,144]{1,0:T(8,128)(2,1)S(1)}, bf16[32,144]{1,0:T(8,128)(2,1)S(1)}, f32[8,48,256]{2,1,0:T(8,128)S(1)}, f32[16,128]{1,0:T(8,128)S(1)}) custom-call(f32[328,256]{1,0:T(8,128)S(1)} %collective-permute-done.source.refs_7_, f32[8,64,256]{2,1,0:T(8,128)S(1)} %copy-done.1, ...), custom_call_target="tpu_custom_call" | custom-call | tf_op jit(solution)/shard_map/prepare/pallas_call | solution.py:147
  17.5 1.2 %view_second.1 = (f32[8,32,256]{2,1,0:T(8,128)S(1)}, f32[7,16,256]{2,1,0:T(8,128)S(1)}, f32[7,16,256]{2,1,0:T(8,128)S(1)}, f32[7,16,256]{2,1,0:T(8,128)S(1)}, f32[7,16,256]{2,1,0:T(8,128)S(1)}) custom-call(bf16[2,2,256,256]{3,2,1,0:T(8,128)(2,1)S(1)} %get-tuple-element.43.refs_0_, bf16[40,144]{1,0:T(8,128)(2,1)S(1)} %get-tuple-element.44.refs_1_, ...), custom_call_target="tpu_custom_call" | custom-call | tf_op jit(solution)/shard_map/view_second/pallas_call | solution.py:254
  18.7 0.7 %collective-permute-start.3 = (f32[7,16,256]{2,1,0:T(8,128)S(1)}, f32[7,16,256]{2,1,0:T(8,128)S(1)}, u32[]{:S(2)}, u32[]{:S(2)}) collective-permute-start(f32[7,16,256]{2,1,0:T(8,128)S(1)} %get-tuple-element.52), channel_id=1, source_target_pairs={{4,8},{12,16},{20,24},{8,4},{16,12},{24,20},{5,9},{13,17},{21,25},... | collective-permute-start | bytes 344072 | tf_op jit(solution)/shard_map/ppermute | solution.py:611
  19.4 2.9 %collective-permute-start.4 = (f32[7,16,256]{2,1,0:T(8,128)S(1)}, f32[7,16,256]{2,1,0:T(8,128)S(1)}, u32[]{:S(2)}, u32[]{:S(2)}) collective-permute-start(f32[7,16,256]{2,1,0:T(8,128)S(1)} %get-tuple-element.53), channel_id=1, source_target_pairs={{0,4},{4,0},{8,12},{12,8},{16,20},{20,16},{24,28},{28,24},{1,5},{5... | collective-permute-start | bytes 344072 | tf_op jit(solution)/shard_map/ppermute | solution.py:611
  22.3 0.7 %collective-permute-start.6 = (f32[7,16,256]{2,1,0:T(8,128)S(1)}, f32[7,16,256]{2,1,0:T(8,128)S(1)}, u32[]{:S(2)}, u32[]{:S(2)}) collective-permute-start(f32[7,16,256]{2,1,0:T(8,128)S(1)} %get-tuple-element.56), channel_id=1, source_target_pairs={{4,8},{12,16},{20,24},{8,4},{16,12},{24,20},{5,9},{13,17},{21,25},... | collective-permute-start | bytes 344072 | tf_op jit(solution)/shard_map/ppermute | solution.py:611
  23.0 2.9 %collective-permute-start.7 = (f32[7,16,256]{2,1,0:T(8,128)S(1)}, f32[7,16,256]{2,1,0:T(8,128)S(1)}, u32[]{:S(2)}, u32[]{:S(2)}) collective-permute-start(f32[7,16,256]{2,1,0:T(8,128)S(1)} %get-tuple-element.57), channel_id=1, source_target_pairs={{0,4},{4,0},{8,12},{12,8},{16,20},{20,16},{24,28},{28,24},{1,5},{5... | collective-permute-start | bytes 344072 | tf_op jit(solution)/shard_map/ppermute | solution.py:611
  25.9 0.3 own_planes.1
  26.2 3.7 %collective-permute-start.5 = (f32[8,16,256]{2,1,0:T(8,128)S(1)}, f32[8,16,256]{2,1,0:T(8,128)S(1)}, u32[]{:S(2)}, u32[]{:S(2)}) collective-permute-start(f32[8,16,256]{2,1,0:T(8,128)S(1)} %add_rims.2.rest_0_.refs_0_.mine), channel_id=1, source_target_pairs={{0,3},{1,2},{2,1},{3,0},{4,7},{5,6},{6,5},{7,4},{8,11},{9,10},{10,... | collective-permute-start | bytes 393224 | tf_op jit(solution)/shard_map/ppermute | solution.py:617
  29.9 0.6 %collective-permute-start.9 = (f32[8,16,256]{2,1,0:T(8,128)S(1)}, f32[8,16,256]{2,1,0:T(8,128)S(1)}, u32[]{:S(2)}, u32[]{:S(2)}) collective-permute-start(f32[8,16,256]{2,1,0:T(8,128)S(1)} %add_rims.3.refs_1_.mine), channel_id=1, source_target_pairs={{0,3},{1,2},{2,1},{3,0},{4,7},{5,6},{6,5},{7,4},{8,11},{9,10},{10,... | collective-permute-start | bytes 393224 | tf_op jit(solution)/shard_map/ppermute | solution.py:617
  30.5 1.8 %moment_rows.1 = f32[64,128]{1,0:T(8,128)S(1)} custom-call(f32[8,64,256]{2,1,0:T(8,128)S(1)} %copy-done.1, s32[8,64,256]{2,1,0:T(8,128)S(1)} %copy-done.3, f32[64,16]{1,0:T(8,128)S(1)} %get-tuple-element.54.picked, f32[64,128]{1,0:T(8,128)S(1)} %get-tuple-element.32.after.base, f32[8,16,256]{2,1,0:T(8,128)S(1)} %add_rims.2.rest_0_.refs_0_.mine, ...), custom_call_target="tpu_custom_call" | custom-call | tf_op jit(solution)/shard_map/moment_rows/pallas_call | solution.py:462
  32.3 10.4 %all_to_all.11 = f32[8,8,128]{2,1,0:T(8,128)S(1)} all-to-all(f32[8,8,128]{2,1,0:T(8,128)S(1)} %bitcast.3), channel_id=1, replica_groups=mesh['tile'=8,'view'=4] {'tile'}, dimensions={0} | all-to-all | bytes 65536 | tf_op jit(solution)/shard_map/all_to_all | solution.py:619
  42.7 0.3 segment_table.1.rest_0_.first
  43.0 0.1 collective-permute-start.8
  43.1 0.7 %store_part.3 = (f32[8,64,256]{2,1,0:T(8,128)}, f32[8,128]{1,0:T(8,128)S(1)}) custom-call(f32[136,256]{1,0:T(8,128)S(1)} %update.2.other), custom_call_target="tpu_custom_call" | custom-call | tf_op jit(solution)/shard_map/store_part/pallas_call | solution.py:535
  43.9 2.1 %collective-permute-start.10 = (f32[128,256]{1,0:T(8,128)S(1)}, f32[128,256]{1,0:T(8,128)S(1)}, u32[]{:S(2)}, u32[]{:S(2)}) collective-permute-start(f32[128,256]{1,0:T(8,128)S(1)} %update.3.other), channel_id=1, source_target_pairs={{0,1},{1,0},{2,3},{3,2},{4,5},{5,4},{6,7},{7,6},{8,9},{9,8},{10,11... | collective-permute-start | bytes 393224 | tf_op jit(solution)/shard_map/ppermute | solution.py:629
  45.9 0.4 collective-permute-start.12
  46.3 1.1 %collective-permute-start.11 = (f32[16,128]{1,0:T(8,128)S(1)}, f32[16,128]{1,0:T(8,128)S(1)}, u32[]{:S(2)}, u32[]{:S(2)}) collective-permute-start(f32[16,128]{1,0:T(8,128)S(1)} %segment_table.1.rest_0_.first), channel_id=1, source_target_pairs={{0,2},{1,3},{2,0},{3,1},{4,6},{5,7},{6,4},{7,5},{8,10},{9,11},{10,... | collective-permute-start | bytes 24584 | tf_op jit(solution)/shard_map/ppermute | solution.py:622
  47.5 1.3 %store_part.4 = (f32[8,64,256]{2,1,0:T(8,128)}, f32[8,128]{1,0:T(8,128)}) custom-call(f32[128,256]{1,0:T(8,128)S(1)} %update.3.other, f32[8,64,256]{2,1,0:T(8,128)} %get-tuple-element.59.refs_0_), custom_call_target="tpu_custom_call", output_to_operand_aliasing={{0}: (1, {})} | custom-call | tf_op jit(solution)/shard_map/store_part/pallas_call | solution.py:535
  48.8 1.0 %collective-permute-done.8.other.tabled = f32[136,256]{1,0:T(8,128)S(1)} collective-permute-done((f32[136,256]{1,0:T(8,128)S(1)}, f32[136,256]{1,0:T(8,128)S(1)}, u32[]{:S(2)}, u32[]{:S(2)}) %collective-permute-start.8) | collective-permute-done | bytes 139296 | tf_op jit(solution)/shard_map/ppermute | solution.py:629
  49.8 1.3 %store_part.5 = (f32[8,64,256]{2,1,0:T(8,128)}, f32[8,128]{1,0:T(8,128)}) custom-call(f32[136,256]{1,0:T(8,128)S(1)} %collective-permute-done.8.other.tabled, f32[8,64,256]{2,1,0:T(8,128)} %get-tuple-element.60.refs_0_), custom_call_target="tpu_custom_call", output_to_operand_aliasing={{0}: (1, {})} | custom-call | tf_op jit(solution)/shard_map/store_part/pallas_call | solution.py:535
  51.1 0.2 collective-permute-done.12.fourth
  51.4 0.1 collective-permute-done.10.other
  51.5 0.7 %finish.1 = (f32[8,64,256]{2,1,0:T(8,128)}, f32[10,128]{1,0:T(8,128)}) custom-call(f32[8,64,256]{2,1,0:T(8,128)} %get-tuple-element.61.begun, f32[128,256]{1,0:T(8,128)S(1)} %collective-permute-done.10.other, f32[136,256]{1,0:T(8,128)S(1)} %collective-permute-done.8.other.tabled, ...), custom_call_target="tpu_custom_call", output_to_operand_aliasing={{0}: (0, {})} | custom-call | tf_op jit(solution)/shard_map/finish/pallas_call | solution.py:567
  (28 shorter events, 0.3 us)
Async XLA Ops:
  0.6 1.0 %copy-start = (f32[8,64,256]{2,1,0:T(8,128)S(1)}, f32[8,64,256]{2,1,0:T(8,128)}, u32[]{:S(2)}) copy-start(f32[8,64,256]{2,1,0:T(8,128)} %estimate.11) | copy-start | bytes 1572868
  1.7 5.2 %copy-start.6 = (f32[1,3,15]{2,0,1:T(1,128)S(1)}, f32[1,3,15]{2,0,1:T(1,128)}, u32[]{:S(2)}) copy-start(f32[1,3,15]{2,0,1:T(1,128)} %param.8) | copy-start | bytes 544
  1.7 5.2 %copy-start.2 = (f32[1,8,64,256]{3,2,1,0:T(8,128)S(1)}, f32[1,8,64,256]{3,2,1,0:T(8,128)}, u32[]{:S(2)}) copy-start(f32[1,8,64,256]{3,2,1,0:T(8,128)} %refs_7_.1) | copy-start | bytes 1572868
  1.7 7.1 %copy-start.1 = (f32[8,64,256]{2,1,0:T(8,128)S(1)}, f32[8,64,256]{2,1,0:T(8,128)}, u32[]{:S(2)}) copy-start(f32[8,64,256]{2,1,0:T(8,128)} %estimate.11) | copy-start | bytes 1572868
  1.7 7.7 %collective-permute-start.1 = (f32[7,48,256]{2,1,0:T(8,128)S(1)}, f32[7,48,256]{2,1,0:T(8,128)S(1)}, u32[]{:S(2)}, u32[]{:S(2)}) collective-permute-start(f32[7,48,256]{2,1,0:T(8,128)S(1)} %get-tuple-element.38), channel_id=1, source_target_pairs={{4,8},{12,16},{20,24},{8,4},{16,12},{24,20},{5,9},{13,17},{21,25},... | collective-permute-start | bytes 1032200 | tf_op jit(solution)/shard_map/ppermute | solution.py:603
  2.6 6.9 %collective-permute-start.2 = (f32[7,48,256]{2,1,0:T(8,128)S(1)}, f32[7,48,256]{2,1,0:T(8,128)S(1)}, u32[]{:S(2)}, u32[]{:S(2)}) collective-permute-start(f32[7,48,256]{2,1,0:T(8,128)S(1)} %get-tuple-element.39), channel_id=1, source_target_pairs={{0,4},{4,0},{8,12},{12,8},{16,20},{20,16},{24,28},{28,24},{1,5},{5... | collective-permute-start | bytes 1032200 | tf_op jit(solution)/shard_map/ppermute | solution.py:604
  7.0 1.7 %copy-start.4 = (s32[1,16,1]{1,2,0:T(1,128)S(1)}, s32[1,16,1]{1,2,0:T(1,128)}, u32[]{:S(2)}) copy-start(s32[1,16,1]{1,2,0:T(1,128)} %param.10) | copy-start | bytes 196
  7.0 1.7 %copy-start.5 = (s32[1,16]{1,0:T(1,128)S(1)}, s32[1,16]{1,0:T(1,128)}, u32[]{:S(2)}) copy-start(s32[1,16]{1,0:T(1,128)} %index_row.1) | copy-start | bytes 196
  7.0 9.9 %collective-permute-start = (f32[328,256]{1,0:T(8,128)S(1)}, f32[328,256]{1,0:T(8,128)S(1)}, u32[]{:S(2)}, u32[]{:S(2)}) collective-permute-start(f32[328,256]{1,0:T(8,128)S(1)} %view_out.1), channel_id=1, source_target_pairs={{0,1},{1,0},{2,3},{3,2},{4,5},{5,4},{6,7},{7,6},{8,9},{9,8},{10,11... | collective-permute-start | bytes 1007624 | tf_op jit(solution)/shard_map/ppermute | solution.py:601
  18.7 7.5 %collective-permute-start.3 = (f32[7,16,256]{2,1,0:T(8,128)S(1)}, f32[7,16,256]{2,1,0:T(8,128)S(1)}, u32[]{:S(2)}, u32[]{:S(2)}) collective-permute-start(f32[7,16,256]{2,1,0:T(8,128)S(1)} %get-tuple-element.52), channel_id=1, source_target_pairs={{4,8},{12,16},{20,24},{8,4},{16,12},{24,20},{5,9},{13,17},{21,25},... | collective-permute-start | bytes 344072 | tf_op jit(solution)/shard_map/ppermute | solution.py:611
  19.4 6.8 %collective-permute-start.4 = (f32[7,16,256]{2,1,0:T(8,128)S(1)}, f32[7,16,256]{2,1,0:T(8,128)S(1)}, u32[]{:S(2)}, u32[]{:S(2)}) collective-permute-start(f32[7,16,256]{2,1,0:T(8,128)S(1)} %get-tuple-element.53), channel_id=1, source_target_pairs={{0,4},{4,0},{8,12},{12,8},{16,20},{20,16},{24,28},{28,24},{1,5},{5... | collective-permute-start | bytes 344072 | tf_op jit(solution)/shard_map/ppermute | solution.py:611
  22.3 7.6 %collective-permute-start.6 = (f32[7,16,256]{2,1,0:T(8,128)S(1)}, f32[7,16,256]{2,1,0:T(8,128)S(1)}, u32[]{:S(2)}, u32[]{:S(2)}) collective-permute-start(f32[7,16,256]{2,1,0:T(8,128)S(1)} %get-tuple-element.56), channel_id=1, source_target_pairs={{4,8},{12,16},{20,24},{8,4},{16,12},{24,20},{5,9},{13,17},{21,25},... | collective-permute-start | bytes 344072 | tf_op jit(solution)/shard_map/ppermute | solution.py:611
  23.0 6.9 %collective-permute-start.7 = (f32[7,16,256]{2,1,0:T(8,128)S(1)}, f32[7,16,256]{2,1,0:T(8,128)S(1)}, u32[]{:S(2)}, u32[]{:S(2)}) collective-permute-start(f32[7,16,256]{2,1,0:T(8,128)S(1)} %get-tuple-element.57), channel_id=1, source_target_pairs={{0,4},{4,0},{8,12},{12,8},{16,20},{20,16},{24,28},{28,24},{1,5},{5... | collective-permute-start | bytes 344072 | tf_op jit(solution)/shard_map/ppermute | solution.py:611
  26.2 4.4 %copy-start.3 = (s32[8,64,256]{2,1,0:T(8,128)S(1)}, s32[8,64,256]{2,1,0:T(8,128)}, u32[]{:S(2)}) copy-start(s32[8,64,256]{2,1,0:T(8,128)} %labels.1) | copy-start | bytes 1572868
  26.2 16.7 %collective-permute-start.5 = (f32[8,16,256]{2,1,0:T(8,128)S(1)}, f32[8,16,256]{2,1,0:T(8,128)S(1)}, u32[]{:S(2)}, u32[]{:S(2)}) collective-permute-start(f32[8,16,256]{2,1,0:T(8,128)S(1)} %add_rims.2.rest_0_.refs_0_.mine), channel_id=1, source_target_pairs={{0,3},{1,2},{2,1},{3,0},{4,7},{5,6},{6,5},{7,4},{8,11},{9,10},{10,... | collective-permute-start | bytes 393224 | tf_op jit(solution)/shard_map/ppermute | solution.py:617
  29.9 13.9 %collective-permute-start.9 = (f32[8,16,256]{2,1,0:T(8,128)S(1)}, f32[8,16,256]{2,1,0:T(8,128)S(1)}, u32[]{:S(2)}, u32[]{:S(2)}) collective-permute-start(f32[8,16,256]{2,1,0:T(8,128)S(1)} %add_rims.3.refs_1_.mine), channel_id=1, source_target_pairs={{0,3},{1,2},{2,1},{3,0},{4,7},{5,6},{6,5},{7,4},{8,11},{9,10},{10,... | collective-permute-start | bytes 393224 | tf_op jit(solution)/shard_map/ppermute | solution.py:617
  43.0 6.8 %collective-permute-start.8 = (f32[136,256]{1,0:T(8,128)S(1)}, f32[136,256]{1,0:T(8,128)S(1)}, u32[]{:S(2)}, u32[]{:S(2)}) collective-permute-start(f32[136,256]{1,0:T(8,128)S(1)} %update.2.other), channel_id=1, source_target_pairs={{0,1},{1,0},{2,3},{3,2},{4,5},{5,4},{6,7},{7,6},{8,9},{9,8},{10,11... | collective-permute-start | bytes 417800 | tf_op jit(solution)/shard_map/ppermute | solution.py:629
  43.9 7.7 %collective-permute-start.10 = (f32[128,256]{1,0:T(8,128)S(1)}, f32[128,256]{1,0:T(8,128)S(1)}, u32[]{:S(2)}, u32[]{:S(2)}) collective-permute-start(f32[128,256]{1,0:T(8,128)S(1)} %update.3.other), channel_id=1, source_target_pairs={{0,1},{1,0},{2,3},{3,2},{4,5},{5,4},{6,7},{7,6},{8,9},{9,8},{10,11... | collective-permute-start | bytes 393224 | tf_op jit(solution)/shard_map/ppermute | solution.py:629
  45.9 5.5 %collective-permute-start.12 = (f32[16,128]{1,0:T(8,128)S(1)}, f32[16,128]{1,0:T(8,128)S(1)}, u32[]{:S(2)}, u32[]{:S(2)}) collective-permute-start(f32[16,128]{1,0:T(8,128)S(1)} %segment_table.1.rest_0_.first), channel_id=1, source_target_pairs={{0,3},{1,2},{2,1},{3,0},{4,7},{5,6},{6,5},{7,4},{8,11},{9,10},{10,... | collective-permute-start | bytes 24584 | tf_op jit(solution)/shard_map/ppermute | solution.py:622
  46.3 5.1 %collective-permute-start.11 = (f32[16,128]{1,0:T(8,128)S(1)}, f32[16,128]{1,0:T(8,128)S(1)}, u32[]{:S(2)}, u32[]{:S(2)}) collective-permute-start(f32[16,128]{1,0:T(8,128)S(1)} %segment_table.1.rest_0_.first), channel_id=1, source_target_pairs={{0,2},{1,3},{2,0},{3,1},{4,6},{5,7},{6,4},{7,5},{8,10},{9,11},{10,... | collective-permute-start | bytes 24584 | tf_op jit(solution)/shard_map/ppermute | solution.py:622

commit v5 on v4

--- a/solution.py
+++ b/solution.py
@@ -385,20 +385,15 @@
     )(label_owner.reshape(1, slots), label_index)
 
 
-def moments_kernel(views, depth_total, estimate, labels, picked, base, *refs):
-    corrections, (sent, held, sums, table) = refs[:PARTS], refs[PARTS:]
-    planes, keep, across = held.shape
-    size = keep // PARTS
+def moments_kernel(views, depth_total, part, estimate, labels, picked, base, correction, *refs):
+    begun, (sent, held, sums, table) = refs[:-4], refs[-4:]
+    planes, size, across = correction.shape
     height_total = estimate.shape[1]
     slots = picked.shape[1]
     half = half_of(lax.axis_index("view"))
     first = (lax.axis_index("tile") * planes).astype(F32) + 0.5
-    start = pl.multiple_of(keep * half, 8)
-    for part, correction in enumerate(corrections):
-        rows = pl.ds(pl.multiple_of(start + part * size, 8), size)
-        held[:, part * size : (part + 1) * size] = (
-            estimate[:, rows] * correction[...] * (1.0 / views)
-        )
+    start = pl.multiple_of(size * (PARTS * half + part), 8)
+    held[...] = estimate[:, pl.ds(start, size)] * correction[...] * (1.0 / views)
     group = 16
     spot = lax.broadcasted_iota(jnp.int32, (across, LANES), 0)
     lanes = lax.broadcasted_iota(jnp.int32, (across, LANES), 1)
@@ -412,7 +407,7 @@
         for pair in range(0, group, 2):
             slot = [number * group + pair, number * group + pair + 1]
             parts = [[None] * 6 for _ in slot]
-            for row in range(0, keep, 8):
+            for row in range(0, size, 8):
                 high = ((base_row + (row + start)).astype(F32) + 0.5) * (1.0 / height_total)
                 flat, once, twice = [[jnp.zeros((8, across), F32) for _ in slot] for _ in range(3)]
                 for plane in reversed(range(planes)):
@@ -447,31 +442,36 @@
         total = lines[:group]
         for kind in range(1, 6):
             total += pltpu.roll(lines[kind * group : (kind + 1) * group], 4 * kind, 1)
-        table[pl.ds(pl.multiple_of(number * group, group), group), :] = total
+        rows = pl.ds(pl.multiple_of(number * group, group), group)
+        target = table if part == PARTS - 1 else sent
+        target[rows, :] = total + begun[0][rows, :] if begun else total
         return carry
 
     lax.fori_loop(0, slots // group, one_group, 0)
+    if part < PARTS - 1:
+        return
     sent[...] = base[...] + jnp.dot(
         picked[...], table[...], precision=lax.Precision.HIGHEST, preferred_element_type=F32
     )
 
 
-def moment_rows(views, tiles, estimate, corrections, labels, places):
-    planes, size, across = corrections[0].shape
+def moment_rows(views, tiles, part, estimate, correction, labels, places, begun):
+    planes, size, across = correction.shape
     slots = places[0].shape[1]
-    return pl.pallas_call(
-        functools.partial(moments_kernel, views, tiles * planes),
-        out_shape=jax.ShapeDtypeStruct((tiles * ROWS, LANES), F32),
-        in_specs=[VMEM] * (4 + PARTS),
+    count = tiles * ROWS if part == PARTS - 1 else slots
+    return pl.pallas_call(
+        functools.partial(moments_kernel, views, tiles * planes, part),
+        out_shape=jax.ShapeDtypeStruct((count, LANES), F32),
+        in_specs=[VMEM] * (5 + len(begun)),
         out_specs=VMEM,
         scratch_shapes=[
-            pltpu.VMEM((planes, size * PARTS, across), F32),
+            pltpu.VMEM((planes, size, across), F32),
             pltpu.VMEM((6 * 16, across), F32),
             pltpu.VMEM((slots, LANES), F32),
         ],
         compiler_params=pltpu.CompilerParams(vmem_limit_bytes=LIMIT),
         name="moment_rows",
-    )(estimate, labels, *places, *corrections)
+    )(estimate, labels, *places, correction, *begun)
 
 
 def segments_kernel(across, rows, table):
@@ -522,35 +522,51 @@
     return copies
 
 
-def store_kernel(own, part, size, other, *refs):
-    whole, token, sems = refs[-3:]
-    half = half_of(lax.axis_index("view"))
-    copies = stores(other, whole, half if own else 1 - half, part, size, sems)
-    token[...] = jnp.zeros_like(token)
+def token_kernel(source, token):
+    token[...] = source[:8, :LANES]
+
+
+def token_of(source):
+    return pl.pallas_call(
+        token_kernel,
+        out_shape=jax.ShapeDtypeStruct((8, LANES), F32),
+        in_specs=[VMEM],
+        out_specs=VMEM,
+        compiler_params=pltpu.CompilerParams(vmem_limit_bytes=LIMIT),
+        name="token_of",
+    )(source)
+
+
+def begin_kernel(size, *refs):
+    whole, sems = refs[-2:]
+    half = half_of(lax.axis_index("view"))
+    copies = []
+    for part in range(PARTS):
+        copies += stores(refs[part], whole, half, part, size, sems.at[part])
     for copy in copies:
         copy.wait()
 
 
-def store_part(own, part, size, shape, other, begun):
-    return pl.pallas_call(
-        functools.partial(store_kernel, own, part, size),
-        out_shape=(jax.ShapeDtypeStruct(shape, F32), jax.ShapeDtypeStruct((8, LANES), F32)),
-        in_specs=[ANY] * (1 + len(begun)),
-        out_specs=(ANY, VMEM),
-        input_output_aliases={1: 0} if begun else {},
-        scratch_shapes=[pltpu.SemaphoreType.DMA((shape[0],))],
-        compiler_params=pltpu.CompilerParams(vmem_limit_bytes=LIMIT),
-        name="store_part",
-    )(other, *begun)
-
-
-def finish_kernel(
-    scale, size, begun, other, tabled, first, third, fourth, whole, moments, held, sems, sem
-):
+def begin_result(size, shape, mine):
+    return pl.pallas_call(
+        functools.partial(begin_kernel, size),
+        out_shape=jax.ShapeDtypeStruct(shape, F32),
+        in_specs=[VMEM] * PARTS,
+        out_specs=ANY,
+        scratch_shapes=[pltpu.SemaphoreType.DMA((PARTS, shape[0]))],
+        compiler_params=pltpu.CompilerParams(vmem_limit_bytes=LIMIT),
+        name="begin_result",
+    )(*mine)
+
+
+def finish_kernel(scale, size, begun, *refs):
+    others, (first, third, fourth, whole, moments, held, sems, sem) = refs[:PARTS], refs[PARTS:]
     planes = whole.shape[0]
     half = half_of(lax.axis_index("view"))
-    copies = stores(other, whole, 1 - half, PARTS - 1, size, sems)
-    rows = tabled[planes * size :]
+    copies = []
+    for part in range(PARTS):
+        copies += stores(others[part], whole, 1 - half, part, size, sems.at[part])
+    rows = others[0][planes * size :]
     second = jnp.concatenate([rows[:, :LANES], rows[:, LANES : 2 * LANES]], axis=0)
     table = (first[...] + second) + (third[...] + fourth[...])
     lines = lax.broadcasted_iota(jnp.int32, table.shape, 0)
@@ -563,24 +579,24 @@
     last.wait()
 
 
-def finish(scale, size, begun, other, tabled, tables):
+def finish(scale, size, begun, others, tables):
     return pl.pallas_call(
         functools.partial(finish_kernel, scale, size),
         out_shape=(
             jax.ShapeDtypeStruct(begun.shape, F32),
             jax.ShapeDtypeStruct((MOM, NUC_DEV), F32),
         ),
-        in_specs=[ANY] + [VMEM] * 5,
+        in_specs=[ANY] + [VMEM] * (PARTS + 3),
         out_specs=(ANY, ANY),
         input_output_aliases={0: 0},
         scratch_shapes=[
             pltpu.VMEM((MOM, NUC_DEV), F32),
-            pltpu.SemaphoreType.DMA((begun.shape[0],)),
+            pltpu.SemaphoreType.DMA((PARTS, begun.shape[0])),
             pltpu.SemaphoreType.DMA,
         ],
         compiler_params=pltpu.CompilerParams(vmem_limit_bytes=LIMIT),
         name="finish",
-    )(begun, other, tabled, *tables)
+    )(begun, *others, *tables)
 
 
 def on_device(estimate, measured, kernels, labels, label_owner, label_index):
@@ -611,28 +627,27 @@
         lax.ppermute(send, "tile", pairs) for send, pairs in zip(sends, (far_pairs, near_pairs) * PARTS)
     ]
     inner = own_planes(taps, own[4], others[4], field_own, field_other)
-    mine = []
+    mine, other, sums = [], [], []
     for part in range(PARTS):
-        mine.append(add_rims(inner[part], *rims[2 * part : 2 * part + 2], *mine[-1:]))
-    other = [lax.ppermute(part, "view", across_pairs) for part in mine]
-    sent = moment_rows(views, tiles, estimate, mine, labels, places)
+        mine.append(add_rims(inner[part], *rims[2 * part : 2 * part + 2], *sums))
+        other.append(lax.ppermute(mine[part], "view", across_pairs))
+        sums = [moment_rows(views, tiles, part, estimate, mine[part], labels, places, sums)]
+    sent = sums[0]
     got = lax.all_to_all(sent, "tile", split_axis=0, concat_axis=0, tiled=True)
     table = segment_table(across, got)
     tables = [table] + [
         lax.ppermute(table, "view", [(i, i ^ step) for i in range(views)]) for step in (2, 3)
     ]
     size = keep // PARTS
-    new_other, begun, token = [], [], []
+    new_mine, new_other, token = [], [], []
     for part in range(PARTS):
         last = [table] if part == 0 else []
-        new_mine = update(views, part, estimate, mine[part], other[part], last, token)
-        new_other.append(lax.ppermute(new_mine, "view", partner))
-        *begun, after = store_part(True, part, size, estimate.shape, new_mine, begun)
-        token = [after]
-    for part in range(PARTS - 1):
-        *begun, _ = store_part(False, part, size, estimate.shape, new_other[part], begun)
+        new_mine.append(update(views, part, estimate, mine[part], other[part], last, token))
+        new_other.append(lax.ppermute(new_mine[part], "view", partner))
+        token = [token_of(new_mine[part])]
     scale = label_index.shape[1] / (planes * height * across)
-    return finish(scale, size, begun[0], new_other[-1], new_other[0], tables)
+    begun = begin_result(size, estimate.shape, new_mine)
+    return finish(scale, size, begun, new_other, tables)
 
 
 def solution(mesh):

time: 52.5 us -> 52.2 us (level)
  waiting for transfers between devices: 7.68 us -> 10.2 us
  Pallas kernels: 10.4 us -> 8.47 us
  blocking collectives: 10.4 us -> 9.64 us
    ppermute x2, waiting for transfers between devices: 0.25 us -> 3.78 us  [on_device(): lax.ppermute(table, 'view', [(i, i ^ step) for i in range(views)])]
    pallas_call x4, Pallas kernels: 5.1 us -> 3.04 us  [the longest x2 2.21 us: moment_rows(): pl.pallas_call(functools.partial(moments_kernel, views, tiles * planes, p...]
    ppermute x4, waiting for transfers between devices: 1.2 us -> 0.19 us  [the longest x2 0.19 us: on_device(): new_other.append(lax.ppermute(new_mine[part], 'view', partner))]
    all_to_all x1, blocking collectives: 10.4 us -> 9.64 us  [on_device(): got = lax.all_to_all(sent, 'tile', split_axis=0, concat_axis=0, tiled=True)]
  transfers between devices with their start and end apart: 13 -> 13, of which waited for: 4 -> 4; matrix products, arithmetic and copies ran while one was open for 0% -> 0% of each run, Pallas kernels for 15% -> 11%
where the time goes in v5:
time: 52.2 us; the launch traced here: 52 us
  starting transfers between devices  21.7 us (42%)
  waiting for transfers between devices  10.2 us (20%)
  blocking collectives  9.64 us (18%)
  Pallas kernels  8.47 us (16%)
  local copies, waits for them, and re-layouts  1.07 us (2%)
  between operations  0.87 us (2%)
    all_to_all x1, blocking collectives, on_device(): got = lax.all_to_all(sent, 'tile', split_axis=0, concat_axis=0, tiled=True)  9.64 us
    ppermute x4, starting transfers between devices, on_device(): lax.ppermute(send, 'tile', pairs)  7.28 us
    ppermute x1, waiting for transfers between devices, on_device(): swapped = lax.ppermute(packed, 'view', partner)  6.21 us
    ppermute x1, starting transfers between devices, on_device(): near = lax.ppermute(to_near, 'tile', near_pairs)  4.34 us
    ppermute x2, starting transfers between devices, on_device(): other.append(lax.ppermute(mine[part], 'view', across_pairs))  3.95 us
    ppermute x2, waiting for transfers between devices, on_device(): lax.ppermute(table, 'view', [(i, i ^ step) for i in range(views)])  3.78 us
    pallas_call x2, Pallas kernels, view_field(): pl.pallas_call(functools.partial(view_kernel, first), out_shape=(jax.Shap...  2.44 us
    pallas_call x2, Pallas kernels, moment_rows(): pl.pallas_call(functools.partial(moments_kernel, views, tiles * planes, p...  2.21 us
  transfers between devices with their start and end apart: 13, of which 4 were waited for; matrix products, arithmetic and copies ran while one was open for 0% of the time, Pallas kernels for 11%

profile of v5, /device:TPU:0, one launch (start us, length us, event | category | flops | bytes accessed | tf_op | source)
XLA Modules:
  0.0 52.0 jit_solution(7279668066622964503)
XLA Ops:
  0.6 0.0 copy-start
  0.6 1.0 %copy-done = f32[8,64,256]{2,1,0:T(8,128)S(1)} copy-done((f32[8,64,256]{2,1,0:T(8,128)S(1)}, f32[8,64,256]{2,1,0:T(8,128)}, u32[]{:S(2)}) %copy-start) | copy-done | bytes 524312
  1.7 0.0 copy-start.1
  1.7 0.8 %collective-permute-start.1 = (f32[7,48,256]{2,1,0:T(8,128)S(1)}, f32[7,48,256]{2,1,0:T(8,128)S(1)}, u32[]{:S(2)}, u32[]{:S(2)}) collective-permute-start(f32[7,48,256]{2,1,0:T(8,128)S(1)} %get-tuple-element.34), channel_id=1, source_target_pairs={{4,8},{12,16},{20,24},{8,4},{16,12},{24,20},{5,9},{13,17},{21,25},... | collective-permute-start | bytes 1032200 | tf_op jit(solution)/shard_map/ppermute | solution.py:619
  2.6 4.3 %collective-permute-start.2 = (f32[7,48,256]{2,1,0:T(8,128)S(1)}, f32[7,48,256]{2,1,0:T(8,128)S(1)}, u32[]{:S(2)}, u32[]{:S(2)}) collective-permute-start(f32[7,48,256]{2,1,0:T(8,128)S(1)} %get-tuple-element.35), channel_id=1, source_target_pairs={{0,4},{4,0},{8,12},{12,8},{16,20},{20,16},{24,28},{28,24},{1,5},{5... | collective-permute-start | bytes 1032200 | tf_op jit(solution)/shard_map/ppermute | solution.py:620
  7.0 1.6 %collective-permute-start = (f32[328,256]{1,0:T(8,128)S(1)}, f32[328,256]{1,0:T(8,128)S(1)}, u32[]{:S(2)}, u32[]{:S(2)}) collective-permute-start(f32[328,256]{1,0:T(8,128)S(1)} %view_out.1), channel_id=1, source_target_pairs={{0,1},{1,0},{2,3},{3,2},{4,5},{5,4},{6,7},{7,6},{8,9},{9,8},{10,11... | collective-permute-start | bytes 1007624 | tf_op jit(solution)/shard_map/ppermute | solution.py:617
  8.6 0.2 slot_places.1
  8.8 0.6 %prepare.2 = (bf16[2,2,256,256]{3,2,1,0:T(8,128)(2,1)S(1)}, bf16[40,144]{1,0:T(8,128)(2,1)S(1)}, bf16[32,144]{1,0:T(8,128)(2,1)S(1)}, f32[8,48,256]{2,1,0:T(8,128)S(1)}, f32[16,128]{1,0:T(8,128)S(1)}) custom-call(f32[1,3,15]{2,1,0:T(4,128)S(1)} %copy.9.source.kernels, f32[8,64,256]{2,1,0:T(8,128)S(1)} %copy-done.1, f32[64,128]{1,0:T(8,128)S(1)} %get-tuple-element.28.after.base), custom_call_target="tpu_custom_call" | custom-call | tf_op jit(solution)/shard_map/prepare/pallas_call | solution.py:147
  9.5 1.2 %view_first.1 = (f32[8,32,256]{2,1,0:T(8,128)S(1)}, f32[7,16,256]{2,1,0:T(8,128)S(1)}, f32[7,16,256]{2,1,0:T(8,128)S(1)}, f32[7,16,256]{2,1,0:T(8,128)S(1)}, f32[7,16,256]{2,1,0:T(8,128)S(1)}) custom-call(bf16[2,2,256,256]{3,2,1,0:T(8,128)(2,1)S(1)} %get-tuple-element.30.refs_0_, bf16[40,144]{1,0:T(8,128)(2,1)S(1)} %get-tuple-element.31.refs_1_, ...), custom_call_target="tpu_custom_call" | custom-call | tf_op jit(solution)/shard_map/view_first/pallas_call | solution.py:254
  10.7 6.2 %collective-permute-done.source.refs_7_ = f32[328,256]{1,0:T(8,128)S(1)} collective-permute-done((f32[328,256]{1,0:T(8,128)S(1)}, f32[328,256]{1,0:T(8,128)S(1)}, u32[]{:S(2)}, u32[]{:S(2)}) %collective-permute-start) | collective-permute-done | bytes 335904 | tf_op jit(solution)/shard_map/ppermute | solution.py:617
  16.9 0.6 %prepare.3 = (bf16[2,2,256,256]{3,2,1,0:T(8,128)(2,1)S(1)}, bf16[40,144]{1,0:T(8,128)(2,1)S(1)}, bf16[32,144]{1,0:T(8,128)(2,1)S(1)}, f32[8,48,256]{2,1,0:T(8,128)S(1)}, f32[16,128]{1,0:T(8,128)S(1)}) custom-call(f32[328,256]{1,0:T(8,128)S(1)} %collective-permute-done.source.refs_7_, f32[8,64,256]{2,1,0:T(8,128)S(1)} %copy-done.1, ...), custom_call_target="tpu_custom_call" | custom-call | tf_op jit(solution)/shard_map/prepare/pallas_call | solution.py:147
  17.5 1.2 %view_second.1 = (f32[8,32,256]{2,1,0:T(8,128)S(1)}, f32[7,16,256]{2,1,0:T(8,128)S(1)}, f32[7,16,256]{2,1,0:T(8,128)S(1)}, f32[7,16,256]{2,1,0:T(8,128)S(1)}, f32[7,16,256]{2,1,0:T(8,128)S(1)}) custom-call(bf16[2,2,256,256]{3,2,1,0:T(8,128)(2,1)S(1)} %get-tuple-element.39.refs_0_, bf16[40,144]{1,0:T(8,128)(2,1)S(1)} %get-tuple-element.40.refs_1_, ...), custom_call_target="tpu_custom_call" | custom-call | tf_op jit(solution)/shard_map/view_second/pallas_call | solution.py:254
  18.7 0.8 %collective-permute-start.3 = (f32[7,16,256]{2,1,0:T(8,128)S(1)}, f32[7,16,256]{2,1,0:T(8,128)S(1)}, u32[]{:S(2)}, u32[]{:S(2)}) collective-permute-start(f32[7,16,256]{2,1,0:T(8,128)S(1)} %get-tuple-element.48), channel_id=1, source_target_pairs={{4,8},{12,16},{20,24},{8,4},{16,12},{24,20},{5,9},{13,17},{21,25},... | collective-permute-start | bytes 344072 | tf_op jit(solution)/shard_map/ppermute | solution.py:627
  19.5 2.9 %collective-permute-start.4 = (f32[7,16,256]{2,1,0:T(8,128)S(1)}, f32[7,16,256]{2,1,0:T(8,128)S(1)}, u32[]{:S(2)}, u32[]{:S(2)}) collective-permute-start(f32[7,16,256]{2,1,0:T(8,128)S(1)} %get-tuple-element.49), channel_id=1, source_target_pairs={{0,4},{4,0},{8,12},{12,8},{16,20},{20,16},{24,28},{28,24},{1,5},{5... | collective-permute-start | bytes 344072 | tf_op jit(solution)/shard_map/ppermute | solution.py:627
  22.4 0.7 %collective-permute-start.6 = (f32[7,16,256]{2,1,0:T(8,128)S(1)}, f32[7,16,256]{2,1,0:T(8,128)S(1)}, u32[]{:S(2)}, u32[]{:S(2)}) collective-permute-start(f32[7,16,256]{2,1,0:T(8,128)S(1)} %get-tuple-element.52), channel_id=1, source_target_pairs={{4,8},{12,16},{20,24},{8,4},{16,12},{24,20},{5,9},{13,17},{21,25},... | collective-permute-start | bytes 344072 | tf_op jit(solution)/shard_map/ppermute | solution.py:627
  23.1 2.9 %collective-permute-start.7 = (f32[7,16,256]{2,1,0:T(8,128)S(1)}, f32[7,16,256]{2,1,0:T(8,128)S(1)}, u32[]{:S(2)}, u32[]{:S(2)}) collective-permute-start(f32[7,16,256]{2,1,0:T(8,128)S(1)} %get-tuple-element.53), channel_id=1, source_target_pairs={{0,4},{4,0},{8,12},{12,8},{16,20},{20,16},{24,28},{28,24},{1,5},{5... | collective-permute-start | bytes 344072 | tf_op jit(solution)/shard_map/ppermute | solution.py:627
  26.0 0.3 own_planes.1
  26.4 3.7 %collective-permute-start.5 = (f32[8,16,256]{2,1,0:T(8,128)S(1)}, f32[8,16,256]{2,1,0:T(8,128)S(1)}, u32[]{:S(2)}, u32[]{:S(2)}) collective-permute-start(f32[8,16,256]{2,1,0:T(8,128)S(1)} %add_rims.2.correction.mine), channel_id=1, source_target_pairs={{0,3},{1,2},{2,1},{3,0},{4,7},{5,6},{6,5},{7,4},{8,11},{9,10},{10,... | collective-permute-start | bytes 393224 | tf_op jit(solution)/shard_map/ppermute | solution.py:633
  30.0 1.0 %moment_rows.2.rest_0_.refs_0_ = f32[16,128]{1,0:T(8,128)S(1)} custom-call(f32[8,64,256]{2,1,0:T(8,128)S(1)} %copy-done.1, s32[8,64,256]{2,1,0:T(8,128)S(1)} %copy-done.2, f32[64,16]{1,0:T(8,128)S(1)} %get-tuple-element.50.picked, f32[64,128]{1,0:T(8,128)S(1)} %get-tuple-element.28.after.base, f32[8,16,256]{2,1,0:T(8,128)S(1)} %add_rims.2.correction.mine), custom_call_target="tpu_custom_call" | custom-call | tf_op jit(solution)/shard_map/moment_rows/pallas_call | solution.py:462
  31.1 0.3 collective-permute-start.8
  31.4 1.2 %moment_rows.3 = f32[64,128]{1,0:T(8,128)S(1)} custom-call(f32[8,64,256]{2,1,0:T(8,128)S(1)} %copy-done.1, s32[8,64,256]{2,1,0:T(8,128)S(1)} %copy-done.2, f32[64,16]{1,0:T(8,128)S(1)} %get-tuple-element.50.picked, f32[64,128]{1,0:T(8,128)S(1)} %get-tuple-element.28.after.base, f32[8,16,256]{2,1,0:T(8,128)S(1)} %add_rims.3.correction.mine, ...), custom_call_target="tpu_custom_call" | custom-call | tf_op jit(solution)/shard_map/moment_rows/pallas_call | solution.py:462
  32.6 9.6 %all_to_all.11 = f32[8,8,128]{2,1,0:T(8,128)S(1)} all-to-all(f32[8,8,128]{2,1,0:T(8,128)S(1)} %bitcast.3), channel_id=1, replica_groups=mesh['tile'=8,'view'=4] {'tile'}, dimensions={0} | all-to-all | bytes 65536 | tf_op jit(solution)/shard_map/all_to_all | solution.py:636
  42.2 0.3 segment_table.1.rest_0_.refs_2_
  42.6 0.1 collective-permute-start.9
  42.7 2.1 %collective-permute-start.10 = (f32[128,256]{1,0:T(8,128)S(1)}, f32[128,256]{1,0:T(8,128)S(1)}, u32[]{:S(2)}, u32[]{:S(2)}) collective-permute-start(f32[128,256]{1,0:T(8,128)S(1)} %update.3.refs_1_), channel_id=1, source_target_pairs={{0,1},{1,0},{2,3},{3,2},{4,5},{5,4},{6,7},{7,6},{8,9},{9,8},{10,11... | collective-permute-start | bytes 393224 | tf_op jit(solution)/shard_map/ppermute | solution.py:646
  44.8 1.4 %collective-permute-start.12 = (f32[16,128]{1,0:T(8,128)S(1)}, f32[16,128]{1,0:T(8,128)S(1)}, u32[]{:S(2)}, u32[]{:S(2)}) collective-permute-start(f32[16,128]{1,0:T(8,128)S(1)} %segment_table.1.rest_0_.refs_2_), channel_id=1, source_target_pairs={{0,3},{1,2},{2,1},{3,0},{4,7},{5,6},{6,5},{7,4},{8,11},{9,10},{10,... | collective-permute-start | bytes 24584 | tf_op jit(solution)/shard_map/ppermute | solution.py:639
  46.2 0.1 collective-permute-start.11
  46.3 0.8 %begin_result.1.begun = f32[8,64,256]{2,1,0:T(8,128)} custom-call(f32[136,256]{1,0:T(8,128)S(1)} %update.2.source.refs_0_, f32[128,256]{1,0:T(8,128)S(1)} %update.3.refs_1_), custom_call_target="tpu_custom_call" | custom-call | tf_op jit(solution)/shard_map/begin_result/pallas_call | solution.py:551
  47.1 3.7 %collective-permute-done.12.refs_4_ = f32[16,128]{1,0:T(8,128)S(1)} collective-permute-done((f32[16,128]{1,0:T(8,128)S(1)}, f32[16,128]{1,0:T(8,128)S(1)}, u32[]{:S(2)}, u32[]{:S(2)}) %collective-permute-start.12) | collective-permute-done | bytes 8224 | tf_op jit(solution)/shard_map/ppermute | solution.py:639
  50.8 0.1 collective-permute-done.11.refs_3_
  50.9 0.2 collective-permute-done.10.refs_1_
  51.1 0.8 %finish.1 = (f32[8,64,256]{2,1,0:T(8,128)}, f32[10,128]{1,0:T(8,128)}) custom-call(f32[8,64,256]{2,1,0:T(8,128)} %begin_result.1.begun, f32[136,256]{1,0:T(8,128)S(1)} %collective-permute-done.9.refs_0_, f32[128,256]{1,0:T(8,128)S(1)} %collective-permute-done.10.refs_1_, ...), custom_call_target="tpu_custom_call", output_to_operand_aliasing={{0}: (0, {})} | custom-call | tf_op jit(solution)/shard_map/finish/pallas_call | solution.py:583
  (28 shorter events, 0.3 us)
Async XLA Ops:
  0.6 1.0 %copy-start = (f32[8,64,256]{2,1,0:T(8,128)S(1)}, f32[8,64,256]{2,1,0:T(8,128)}, u32[]{:S(2)}) copy-start(f32[8,64,256]{2,1,0:T(8,128)} %estimate.13) | copy-start | bytes 1572868
  1.7 5.2 %copy-start.6 = (f32[1,3,15]{2,0,1:T(1,128)S(1)}, f32[1,3,15]{2,0,1:T(1,128)}, u32[]{:S(2)}) copy-start(f32[1,3,15]{2,0,1:T(1,128)} %param.8) | copy-start | bytes 544
  1.7 5.2 %copy-start.3 = (f32[1,8,64,256]{3,2,1,0:T(8,128)S(1)}, f32[1,8,64,256]{3,2,1,0:T(8,128)}, u32[]{:S(2)}) copy-start(f32[1,8,64,256]{3,2,1,0:T(8,128)} %refs_7_.1) | copy-start | bytes 1572868
  1.7 7.1 %copy-start.1 = (f32[8,64,256]{2,1,0:T(8,128)S(1)}, f32[8,64,256]{2,1,0:T(8,128)}, u32[]{:S(2)}) copy-start(f32[8,64,256]{2,1,0:T(8,128)} %estimate.13) | copy-start | bytes 1572868
  1.7 7.7 %collective-permute-start.1 = (f32[7,48,256]{2,1,0:T(8,128)S(1)}, f32[7,48,256]{2,1,0:T(8,128)S(1)}, u32[]{:S(2)}, u32[]{:S(2)}) collective-permute-start(f32[7,48,256]{2,1,0:T(8,128)S(1)} %get-tuple-element.34), channel_id=1, source_target_pairs={{4,8},{12,16},{20,24},{8,4},{16,12},{24,20},{5,9},{13,17},{21,25},... | collective-permute-start | bytes 1032200 | tf_op jit(solution)/shard_map/ppermute | solution.py:619
  2.6 6.9 %collective-permute-start.2 = (f32[7,48,256]{2,1,0:T(8,128)S(1)}, f32[7,48,256]{2,1,0:T(8,128)S(1)}, u32[]{:S(2)}, u32[]{:S(2)}) collective-permute-start(f32[7,48,256]{2,1,0:T(8,128)S(1)} %get-tuple-element.35), channel_id=1, source_target_pairs={{0,4},{4,0},{8,12},{12,8},{16,20},{20,16},{24,28},{28,24},{1,5},{5... | collective-permute-start | bytes 1032200 | tf_op jit(solution)/shard_map/ppermute | solution.py:620
  7.0 1.7 %copy-start.4 = (s32[1,16,1]{1,2,0:T(1,128)S(1)}, s32[1,16,1]{1,2,0:T(1,128)}, u32[]{:S(2)}) copy-start(s32[1,16,1]{1,2,0:T(1,128)} %param.10) | copy-start | bytes 196
  7.0 1.7 %copy-start.5 = (s32[1,16]{1,0:T(1,128)S(1)}, s32[1,16]{1,0:T(1,128)}, u32[]{:S(2)}) copy-start(s32[1,16]{1,0:T(1,128)} %index_row.1) | copy-start | bytes 196
  7.0 9.9 %collective-permute-start = (f32[328,256]{1,0:T(8,128)S(1)}, f32[328,256]{1,0:T(8,128)S(1)}, u32[]{:S(2)}, u32[]{:S(2)}) collective-permute-start(f32[328,256]{1,0:T(8,128)S(1)} %view_out.1), channel_id=1, source_target_pairs={{0,1},{1,0},{2,3},{3,2},{4,5},{5,4},{6,7},{7,6},{8,9},{9,8},{10,11... | collective-permute-start | bytes 1007624 | tf_op jit(solution)/shard_map/ppermute | solution.py:617
  18.7 11.3 %copy-start.2 = (s32[8,64,256]{2,1,0:T(8,128)S(1)}, s32[8,64,256]{2,1,0:T(8,128)}, u32[]{:S(2)}) copy-start(s32[8,64,256]{2,1,0:T(8,128)} %labels.3) | copy-start | bytes 1572868
  18.7 7.6 %collective-permute-start.3 = (f32[7,16,256]{2,1,0:T(8,128)S(1)}, f32[7,16,256]{2,1,0:T(8,128)S(1)}, u32[]{:S(2)}, u32[]{:S(2)}) collective-permute-start(f32[7,16,256]{2,1,0:T(8,128)S(1)} %get-tuple-element.48), channel_id=1, source_target_pairs={{4,8},{12,16},{20,24},{8,4},{16,12},{24,20},{5,9},{13,17},{21,25},... | collective-permute-start | bytes 344072 | tf_op jit(solution)/shard_map/ppermute | solution.py:627
  19.5 6.8 %collective-permute-start.4 = (f32[7,16,256]{2,1,0:T(8,128)S(1)}, f32[7,16,256]{2,1,0:T(8,128)S(1)}, u32[]{:S(2)}, u32[]{:S(2)}) collective-permute-start(f32[7,16,256]{2,1,0:T(8,128)S(1)} %get-tuple-element.49), channel_id=1, source_target_pairs={{0,4},{4,0},{8,12},{12,8},{16,20},{20,16},{24,28},{28,24},{1,5},{5... | collective-permute-start | bytes 344072 | tf_op jit(solution)/shard_map/ppermute | solution.py:627
  22.4 8.6 %collective-permute-start.6 = (f32[7,16,256]{2,1,0:T(8,128)S(1)}, f32[7,16,256]{2,1,0:T(8,128)S(1)}, u32[]{:S(2)}, u32[]{:S(2)}) collective-permute-start(f32[7,16,256]{2,1,0:T(8,128)S(1)} %get-tuple-element.52), channel_id=1, source_target_pairs={{4,8},{12,16},{20,24},{8,4},{16,12},{24,20},{5,9},{13,17},{21,25},... | collective-permute-start | bytes 344072 | tf_op jit(solution)/shard_map/ppermute | solution.py:627
  23.1 8.0 %collective-permute-start.7 = (f32[7,16,256]{2,1,0:T(8,128)S(1)}, f32[7,16,256]{2,1,0:T(8,128)S(1)}, u32[]{:S(2)}, u32[]{:S(2)}) collective-permute-start(f32[7,16,256]{2,1,0:T(8,128)S(1)} %get-tuple-element.53), channel_id=1, source_target_pairs={{0,4},{4,0},{8,12},{12,8},{16,20},{20,16},{24,28},{28,24},{1,5},{5... | collective-permute-start | bytes 344072 | tf_op jit(solution)/shard_map/ppermute | solution.py:627
  26.4 16.2 %collective-permute-start.5 = (f32[8,16,256]{2,1,0:T(8,128)S(1)}, f32[8,16,256]{2,1,0:T(8,128)S(1)}, u32[]{:S(2)}, u32[]{:S(2)}) collective-permute-start(f32[8,16,256]{2,1,0:T(8,128)S(1)} %add_rims.2.correction.mine), channel_id=1, source_target_pairs={{0,3},{1,2},{2,1},{3,0},{4,7},{5,6},{6,5},{7,4},{8,11},{9,10},{10,... | collective-permute-start | bytes 393224 | tf_op jit(solution)/shard_map/ppermute | solution.py:633
  31.1 11.5 %collective-permute-start.8 = (f32[8,16,256]{2,1,0:T(8,128)S(1)}, f32[8,16,256]{2,1,0:T(8,128)S(1)}, u32[]{:S(2)}, u32[]{:S(2)}) collective-permute-start(f32[8,16,256]{2,1,0:T(8,128)S(1)} %add_rims.3.correction.mine), channel_id=1, source_target_pairs={{0,3},{1,2},{2,1},{3,0},{4,7},{5,6},{6,5},{7,4},{8,11},{9,10},{10,... | collective-permute-start | bytes 393224 | tf_op jit(solution)/shard_map/ppermute | solution.py:633
  42.6 8.5 %collective-permute-start.9 = (f32[136,256]{1,0:T(8,128)S(1)}, f32[136,256]{1,0:T(8,128)S(1)}, u32[]{:S(2)}, u32[]{:S(2)}) collective-permute-start(f32[136,256]{1,0:T(8,128)S(1)} %update.2.source.refs_0_), channel_id=1, source_target_pairs={{0,1},{1,0},{2,3},{3,2},{4,5},{5,4},{6,7},{7,6},{8,9},{9,8},{10,11... | collective-permute-start | bytes 417800 | tf_op jit(solution)/shard_map/ppermute | solution.py:646
  42.7 8.4 %collective-permute-start.10 = (f32[128,256]{1,0:T(8,128)S(1)}, f32[128,256]{1,0:T(8,128)S(1)}, u32[]{:S(2)}, u32[]{:S(2)}) collective-permute-start(f32[128,256]{1,0:T(8,128)S(1)} %update.3.refs_1_), channel_id=1, source_target_pairs={{0,1},{1,0},{2,3},{3,2},{4,5},{5,4},{6,7},{7,6},{8,9},{9,8},{10,11... | collective-permute-start | bytes 393224 | tf_op jit(solution)/shard_map/ppermute | solution.py:646
  44.8 6.1 %collective-permute-start.12 = (f32[16,128]{1,0:T(8,128)S(1)}, f32[16,128]{1,0:T(8,128)S(1)}, u32[]{:S(2)}, u32[]{:S(2)}) collective-permute-start(f32[16,128]{1,0:T(8,128)S(1)} %segment_table.1.rest_0_.refs_2_), channel_id=1, source_target_pairs={{0,3},{1,2},{2,1},{3,0},{4,7},{5,6},{6,5},{7,4},{8,11},{9,10},{10,... | collective-permute-start | bytes 24584 | tf_op jit(solution)/shard_map/ppermute | solution.py:639
  46.2 4.7 %collective-permute-start.11 = (f32[16,128]{1,0:T(8,128)S(1)}, f32[16,128]{1,0:T(8,128)S(1)}, u32[]{:S(2)}, u32[]{:S(2)}) collective-permute-start(f32[16,128]{1,0:T(8,128)S(1)} %segment_table.1.rest_0_.refs_2_), channel_id=1, source_target_pairs={{0,2},{1,3},{2,0},{3,1},{4,6},{5,7},{6,4},{7,5},{8,10},{9,11},{10,... | collective-permute-start | bytes 24584 | tf_op jit(solution)/shard_map/ppermute | solution.py:639

commit v6 on v5

--- a/solution.py
+++ b/solution.py
@@ -12,6 +12,7 @@
 NUC_DEV = 128
 LANES = 128
 PARTS = 2
+TAIL = 24
 IDS = 24
 F32 = jnp.float32
 BF16 = jnp.bfloat16
@@ -84,7 +85,7 @@
     start = pl.multiple_of((height - seen) * (1 - half), 8)
     for plane in range(planes):
         packed[plane * seen : (plane + 1) * seen] = measured[0, plane, pl.ds(start, seen)]
-    packed[planes * seen :] = jnp.zeros((8, packed.shape[1]), F32)
+    packed[planes * seen :] = jnp.zeros((TAIL, packed.shape[1]), F32)
     packed[planes * seen : planes * seen + kernels.shape[1], : kernels.shape[2]] = kernels[0]
 
 
@@ -92,7 +93,7 @@
     _, planes, _, across = measured.shape
     return pl.pallas_call(
         functools.partial(view_out_kernel, seen),
-        out_shape=jax.ShapeDtypeStruct((planes * seen + 8, across), F32),
+        out_shape=jax.ShapeDtypeStruct((planes * seen + TAIL, across), F32),
         in_specs=[VMEM, VMEM],
         out_specs=VMEM,
         compiler_params=pltpu.CompilerParams(vmem_limit_bytes=LIMIT),
@@ -106,7 +107,8 @@
     rows, keep, seen = part.shape[1], back.shape[0], tall.shape[0]
     planes = estimate.shape[0]
     radius = (taps - 1) // 2
-    raw = source[source.shape[0] - 8 : source.shape[0] - 5, :taps] if packed else source[0]
+    at = source.shape[0] - TAIL
+    raw = source[at : at + 3, :taps] if packed else source[0]
     weights = raw / jnp.sum(raw, axis=-1, keepdims=True)
     deep, high, flat = [[weights[axis : axis + 1, t : t + 1] for t in range(taps)] for axis in range(3)]
     start = pl.multiple_of((2 * keep - rows) * half, 16)
@@ -164,107 +166,115 @@
     return [jnp.broadcast_to(spread[step : step + 1, :], (16, LANES)) for step in range(taps)]
 
 
-def view_kernel(first, *refs):
-    wide, tall, back, part, spread, far, near, view = refs[:8]
-    begun, refs = ((), refs[8:]) if first else (refs[8 : 8 + 2 * PARTS], refs[8 + 2 * PARTS :])
-    field, *sends = refs[: 1 + 2 * PARTS]
-    blur_hi, blur_lo, plane_hi, plane_lo = refs[1 + 2 * PARTS :]
-    planes, radius = part.shape[0], near.shape[0]
-    rows, across = near.shape[1], near.shape[2]
-    keep, seen = back.shape[0], tall.shape[0]
+def fields_kernel(*refs):
+    sets, (far, near, measured, swapped), refs = (refs[:5], refs[5:10]), refs[10:14], refs[14:]
+    fields, sends, (blur_hi, blur_lo, plane_hi, plane_lo) = refs[:2], refs[2:-4], refs[-4:]
+    planes = sets[0][3].shape[0]
+    radius, rows, across = near.shape
+    keep, seen = sets[0][2].shape[0], sets[0][1].shape[0]
     taps = 2 * radius + 1
     even = lax.axis_index("tile") % 2 == 0
     half = half_of(lax.axis_index("view"))
     seen_start = pl.multiple_of((2 * keep - seen) * half, 8)
-    factors = spread_factors(spread, taps)
-    for row, lane in chunks(rows, across):
-
-        def rim(place):
-            if place < 0:
-                at = place + radius
-                return jnp.where(even, far[at, row, lane], near[at, row, lane])
-            at = place - planes
-            return jnp.where(even, near[at, row, lane], far[at, row, lane])
-
-        below = depth_terms(rim, factors, -radius, 0, range(planes), False)
-        above = depth_terms(rim, factors, planes, planes + radius, range(planes), False)
-        for plane in range(planes):
-            block = part[plane, row, lane]
-            for term in (below[plane], above[plane]):
-                block = block if term is None else block + term
-            upper, lower = split(block)
-            at = slice(plane * rows + row.start, plane * rows + row.stop)
-            blur_hi[at, lane] = upper
-            blur_lo[at, lane] = lower
-    upper, lower = wide[0, 0], wide[0, 1]
-    lines = jnp.dot(blur_hi[...], upper, preferred_element_type=F32)
-    lines += jnp.dot(blur_lo[...], upper, preferred_element_type=F32)
-    lines += jnp.dot(blur_hi[...], lower, preferred_element_type=F32)
-    forwards = []
-    for plane in range(planes):
-        hi, lo = split(lines[plane * rows : (plane + 1) * rows])
-        forwards.append(
-            jnp.dot(tall[...], jnp.concatenate([hi, lo, hi], axis=0), preferred_element_type=F32)
-        )
-    ratios = []
-    for plane in range(planes):
-        if first:
-            recorded = view[0, plane, pl.ds(seen_start, seen), :]
+    factors = [spread_factors(spread, taps) for _, _, _, _, spread in sets]
+    for which, (_, _, _, part, _) in enumerate(sets):
+        for row, lane in chunks(rows, across):
+
+            def rim(place):
+                if place < 0:
+                    at = place + radius
+                    return jnp.where(even, far[at, row, lane], near[at, row, lane])
+                at = place - planes
+                return jnp.where(even, near[at, row, lane], far[at, row, lane])
+
+            below = depth_terms(rim, factors[which], -radius, 0, range(planes), False)
+            above = depth_terms(rim, factors[which], planes, planes + radius, range(planes), False)
+            for plane in range(planes):
+                block = part[plane, row, lane]
+                for term in (below[plane], above[plane]):
+                    block = block if term is None else block + term
+                upper, lower = split(block)
+                at = slice(plane * rows + row.start, plane * rows + row.stop)
+                blur_hi[which, at, lane] = upper
+                blur_lo[which, at, lane] = lower
+    lines = []
+    for which, (wide, _, _, _, _) in enumerate(sets):
+        upper, lower = wide[0, 0], wide[0, 1]
+        lines.append(
+            jnp.dot(blur_hi[which], upper, preferred_element_type=F32)
+            + jnp.dot(blur_lo[which], upper, preferred_element_type=F32)
+            + jnp.dot(blur_hi[which], lower, preferred_element_type=F32)
+        )
+    both = [(which, plane) for which in range(2) for plane in range(planes)]
+    forwards = {}
+    for which, plane in both:
+        hi, lo = split(lines[which][plane * rows : (plane + 1) * rows])
+        forwards[which, plane] = jnp.dot(
+            sets[which][1][...], jnp.concatenate([hi, lo, hi], axis=0), preferred_element_type=F32
+        )
+    ratios = {}
+    for which, plane in both:
+        if which == 0:
+            recorded = measured[0, plane, pl.ds(seen_start, seen), :]
         else:
-            recorded = view[plane * seen : (plane + 1) * seen]
-        ratio = recorded / forwards[plane]
+            recorded = swapped[plane * seen : (plane + 1) * seen]
+        ratio = recorded / forwards[which, plane]
         if rows > seen:
             ratio = jnp.concatenate([ratio, jnp.zeros((rows - seen, across), F32)], axis=0)
-        ratios.append(split(ratio))
-    turned = [
-        jnp.dot(back[...], jnp.concatenate([hi, lo, hi], axis=0), preferred_element_type=F32)
-        for hi, lo in ratios
-    ]
-    for plane in range(planes):
-        hi, lo = split(turned[plane])
-        plane_hi[plane * keep : (plane + 1) * keep] = hi
-        plane_lo[plane * keep : (plane + 1) * keep] = lo
-    upper, lower = wide[1, 0], wide[1, 1]
-    lines = jnp.dot(plane_hi[...], upper, preferred_element_type=F32)
-    lines += jnp.dot(plane_lo[...], upper, preferred_element_type=F32)
-    lines += jnp.dot(plane_hi[...], lower, preferred_element_type=F32)
-    field[...] = lines.reshape(planes, keep, across)
+        ratios[which, plane] = split(ratio)
+    turned = {}
+    for which, plane in both:
+        hi, lo = ratios[which, plane]
+        turned[which, plane] = jnp.dot(
+            sets[which][2][...], jnp.concatenate([hi, lo, hi], axis=0), preferred_element_type=F32
+        )
+    for which, plane in both:
+        hi, lo = split(turned[which, plane])
+        plane_hi[which, plane * keep : (plane + 1) * keep] = hi
+        plane_lo[which, plane * keep : (plane + 1) * keep] = lo
+    for which, (wide, _, _, _, _) in enumerate(sets):
+        upper, lower = wide[1, 0], wide[1, 1]
+        result = (
+            jnp.dot(plane_hi[which], upper, preferred_element_type=F32)
+            + jnp.dot(plane_lo[which], upper, preferred_element_type=F32)
+            + jnp.dot(plane_hi[which], lower, preferred_element_type=F32)
+        )
+        fields[which][...] = result.reshape(planes, keep, across)
     for row, lane in chunks(keep, across):
-        source = lambda place: field[place, row, lane]
-        below = depth_terms(source, factors, 0, planes, range(-radius, 0), True)
-        above = depth_terms(source, factors, 0, planes, range(planes, planes + radius), True)
+        below, above = [], []
+        for which in range(2):
+            source = lambda place: fields[which][place, row, lane]
+            outer = range(planes, planes + radius)
+            below.append(depth_terms(source, factors[which], 0, planes, range(-radius, 0), True))
+            above.append(depth_terms(source, factors[which], 0, planes, outer, True))
         part_at, inside = divmod(row.start, keep // PARTS)
         inside = slice(inside, inside + 16)
         for at in range(radius):
-            down, up = below[at - radius], above[at + planes]
-            to_far, to_near = jnp.where(even, down, up), jnp.where(even, up, down)
-            if not first:
-                to_far += begun[2 * part_at][at, inside, lane]
-                to_near += begun[2 * part_at + 1][at, inside, lane]
-            sends[2 * part_at][at, inside, lane] = to_far
-            sends[2 * part_at + 1][at, inside, lane] = to_near
-
-
-def view_field(first, prepared, near, far, view, begun):
-    keep = prepared[2].shape[0]
-    planes = prepared[3].shape[0]
+            down = below[0][at - radius] + below[1][at - radius]
+            up = above[0][at + planes] + above[1][at + planes]
+            sends[2 * part_at][at, inside, lane] = jnp.where(even, down, up)
+            sends[2 * part_at + 1][at, inside, lane] = jnp.where(even, up, down)
+
+
+def ratio_fields(own, others, far, near, measured, swapped):
+    keep, planes = own[2].shape[0], own[3].shape[0]
     radius, rows, across = near.shape
-
+    field = jax.ShapeDtypeStruct((planes, keep, across), F32)
     send = jax.ShapeDtypeStruct((radius, keep // PARTS, across), F32)
     return pl.pallas_call(
-        functools.partial(view_kernel, first),
-        out_shape=(jax.ShapeDtypeStruct((planes, keep, across), F32),) + (send,) * (2 * PARTS),
-        in_specs=[VMEM] * (8 + len(begun)),
-        out_specs=(VMEM,) * (1 + 2 * PARTS),
+        fields_kernel,
+        out_shape=(field,) * 2 + (send,) * (2 * PARTS),
+        in_specs=[VMEM] * 14,
+        out_specs=(VMEM,) * (2 + 2 * PARTS),
         scratch_shapes=[
-            pltpu.VMEM((planes * rows, across), BF16),
-            pltpu.VMEM((planes * rows, across), BF16),
-            pltpu.VMEM((planes * keep, across), BF16),
-            pltpu.VMEM((planes * keep, across), BF16),
+            pltpu.VMEM((2, planes * rows, across), BF16),
+            pltpu.VMEM((2, planes * rows, across), BF16),
+            pltpu.VMEM((2, planes * keep, across), BF16),
+            pltpu.VMEM((2, planes * keep, across), BF16),
         ],
         compiler_params=pltpu.CompilerParams(vmem_limit_bytes=LIMIT),
-        name="view_first" if first else "view_second",
-    )(*prepared, far, near, view, *begun)
+        name="ratio_fields",
+    )(*own, *others, far, near, measured, swapped)
 
 
 def own_kernel(taps, spread_own, spread_other, field_own, field_other, *inner):
@@ -620,9 +630,8 @@
     near = lax.ppermute(to_near, "tile", near_pairs)
     places = slot_places(tiles, label_owner, label_index)
     own = prepare(False, taps, kernels, estimate, places[1], rows, seen, keep)
-    field_own, *begun = view_field(True, own, near, far, measured, ())
-    others = prepare(True, taps, swapped, estimate, begun[0], rows, seen, keep)
-    field_other, *sends = view_field(False, others, near, far, swapped, begun)
+    others = prepare(True, taps, swapped, estimate, kernels, rows, seen, keep)
+    field_own, field_other, *sends = ratio_fields(own, others, far, near, measured, swapped)
     rims = [
         lax.ppermute(send, "tile", pairs) for send, pairs in zip(sends, (far_pairs, near_pairs) * PARTS)
     ]

time: 52.2 us -> 51.9 us (level)
  starting transfers between devices: 21.7 us -> 25.6 us
  waiting for transfers between devices: 10.2 us -> 7.14 us
  blocking collectives: 9.64 us -> 8.36 us
  local copies, waits for them, and re-layouts: 1.07 us -> 1.81 us
  Pallas kernels: 8.47 us -> 7.85 us
    ppermute x4, starting transfers between devices: 7.28 us -> 10.7 us  [on_device(): lax.ppermute(send, 'tile', pairs)]
    ppermute x1, waiting for transfers between devices: 6.21 us -> 3.75 us  [on_device(): swapped = lax.ppermute(packed, 'view', partner)]
    ppermute x1, starting transfers between devices: 4.34 us -> 2.9 us  [on_device(): near = lax.ppermute(to_near, 'tile', near_pairs)]
    ppermute x1, starting transfers between devices: 1.64 us -> 3.09 us  [on_device(): swapped = lax.ppermute(packed, 'view', partner)]
    all_to_all x1, blocking collectives: 9.64 us -> 8.36 us  [on_device(): got = lax.all_to_all(sent, 'tile', split_axis=0, concat_axis=0, tiled=True)]
    unnamed x15 -> x13, local copies, waits for them, and re-layouts: 1.07 us -> 1.81 us
    pallas_call x2 -> x1, Pallas kernels: 2.44 us -> 1.82 us  [ratio_fields(): pl.pallas_call(fields_kernel, out_shape=(field,) * 2 + (send,) * (2 * PAR...]
    ppermute x2, starting transfers between devices: 1.54 us -> 2.14 us  [on_device(): lax.ppermute(table, 'view', [(i, i ^ step) for i in range(views)])]
  transfers between devices with their start and end apart: 13 -> 13, of which waited for: 4 -> 4; matrix products, arithmetic and copies ran while one was open for 0% -> 0% of each run, Pallas kernels for 11% -> 10%
where the time goes in v6:
time: 51.9 us; the launch traced here: 51.6 us
  starting transfers between devices  25.6 us (49%)
  blocking collectives  8.36 us (16%)
  Pallas kernels  7.85 us (15%)
  waiting for transfers between devices  7.14 us (14%)
  local copies, waits for them, and re-layouts  1.81 us (3%)
  between operations  0.83 us (2%)
    ppermute x4, starting transfers between devices, on_device(): lax.ppermute(send, 'tile', pairs)  10.7 us
    all_to_all x1, blocking collectives, on_device(): got = lax.all_to_all(sent, 'tile', split_axis=0, concat_axis=0, tiled=True)  8.36 us
    ppermute x2, starting transfers between devices, on_device(): other.append(lax.ppermute(mine[part], 'view', across_pairs))  3.95 us
    ppermute x1, waiting for transfers between devices, on_device(): swapped = lax.ppermute(packed, 'view', partner)  3.75 us
    ppermute x2, waiting for transfers between devices, on_device(): lax.ppermute(table, 'view', [(i, i ^ step) for i in range(views)])  3.25 us
    ppermute x1, starting transfers between devices, on_device(): swapped = lax.ppermute(packed, 'view', partner)  3.09 us
    ppermute x1, starting transfers between devices, on_device(): near = lax.ppermute(to_near, 'tile', near_pairs)  2.9 us
    pallas_call x2, Pallas kernels, moment_rows(): pl.pallas_call(functools.partial(moments_kernel, views, tiles * planes, p...  2.21 us
  transfers between devices with their start and end apart: 13, of which 4 were waited for; matrix products, arithmetic and copies ran while one was open for 0% of the time, Pallas kernels for 10%

profile of v6, /device:TPU:0, one launch (start us, length us, event | category | flops | bytes accessed | tf_op | source)
XLA Modules:
  0.0 51.6 jit_solution(10327311029680307925)
XLA Ops:
  0.6 0.7 %copy.9.source.kernels.after = f32[1,3,15]{2,1,0:T(4,128)S(1)} copy(f32[1,3,15]{2,0,1:T(1,128)} %param.8) | data formatting | bytes 360 | tf_op args[2]
  1.4 1.0 %copy-done.2 = f32[1,8,64,256]{3,2,1,0:T(8,128)S(1)} copy-done((f32[1,8,64,256]{3,2,1,0:T(8,128)S(1)}, f32[1,8,64,256]{3,2,1,0:T(8,128)}, u32[]{:S(2)}) %copy-start.2) | copy-done | bytes 524312
  2.4 3.1 %collective-permute-start = (f32[344,256]{1,0:T(8,128)S(1)}, f32[344,256]{1,0:T(8,128)S(1)}, u32[]{:S(2)}, u32[]{:S(2)}) collective-permute-start(f32[344,256]{1,0:T(8,128)S(1)} %view_out.1), channel_id=1, source_target_pairs={{0,1},{1,0},{2,3},{3,2},{4,5},{5,4},{6,7},{7,6},{8,9},{9,8},{10,11... | collective-permute-start | bytes 1056776 | tf_op jit(solution)/shard_map/ppermute | solution.py:627
  5.6 0.7 %collective-permute-start.1 = (f32[7,48,256]{2,1,0:T(8,128)S(1)}, f32[7,48,256]{2,1,0:T(8,128)S(1)}, u32[]{:S(2)}, u32[]{:S(2)}) collective-permute-start(f32[7,48,256]{2,1,0:T(8,128)S(1)} %get-tuple-element.35), channel_id=1, source_target_pairs={{4,8},{12,16},{20,24},{8,4},{16,12},{24,20},{5,9},{13,17},{21,25},... | collective-permute-start | bytes 1032200 | tf_op jit(solution)/shard_map/ppermute | solution.py:629
  6.3 0.0 copy-start.4
  6.3 0.0 copy-start.5
  6.3 2.9 %collective-permute-start.2 = (f32[7,48,256]{2,1,0:T(8,128)S(1)}, f32[7,48,256]{2,1,0:T(8,128)S(1)}, u32[]{:S(2)}, u32[]{:S(2)}) collective-permute-start(f32[7,48,256]{2,1,0:T(8,128)S(1)} %get-tuple-element.36), channel_id=1, source_target_pairs={{0,4},{4,0},{8,12},{12,8},{16,20},{20,16},{24,28},{28,24},{1,5},{5... | collective-permute-start | bytes 1032200 | tf_op jit(solution)/shard_map/ppermute | solution.py:630
  9.2 0.2 slot_places.1
  9.4 0.6 %prepare.2 = (bf16[2,2,256,256]{3,2,1,0:T(8,128)(2,1)S(1)}, bf16[40,144]{1,0:T(8,128)(2,1)S(1)}, bf16[32,144]{1,0:T(8,128)(2,1)S(1)}, f32[8,48,256]{2,1,0:T(8,128)S(1)}, f32[16,128]{1,0:T(8,128)S(1)}) custom-call(f32[1,3,15]{2,1,0:T(4,128)S(1)} %copy.9.source.kernels.after, f32[8,64,256]{2,1,0:T(8,128)S(1)} %copy-done, ...), custom_call_target="tpu_custom_call" | custom-call | tf_op jit(solution)/shard_map/prepare/pallas_call | solution.py:149
  10.0 3.8 %collective-permute-done.source.refs_13_ = f32[344,256]{1,0:T(8,128)S(1)} collective-permute-done((f32[344,256]{1,0:T(8,128)S(1)}, f32[344,256]{1,0:T(8,128)S(1)}, u32[]{:S(2)}, u32[]{:S(2)}) %collective-permute-start) | collective-permute-done | bytes 352288 | tf_op jit(solution)/shard_map/ppermute | solution.py:627
  13.8 0.6 %prepare.3 = (bf16[2,2,256,256]{3,2,1,0:T(8,128)(2,1)S(1)}, bf16[40,144]{1,0:T(8,128)(2,1)S(1)}, bf16[32,144]{1,0:T(8,128)(2,1)S(1)}, f32[8,48,256]{2,1,0:T(8,128)S(1)}, f32[16,128]{1,0:T(8,128)S(1)}) custom-call(f32[344,256]{1,0:T(8,128)S(1)} %collective-permute-done.source.refs_13_, f32[8,64,256]{2,1,0:T(8,128)S(1)} %copy-done, ...), custom_call_target="tpu_custom_call" | custom-call | tf_op jit(solution)/shard_map/prepare/pallas_call | solution.py:149
  14.4 1.8 %ratio_fields.1 = (f32[8,32,256]{2,1,0:T(8,128)S(1)}, f32[8,32,256]{2,1,0:T(8,128)S(1)}, f32[7,16,256]{2,1,0:T(8,128)S(1)}, f32[7,16,256]{2,1,0:T(8,128)S(1)}, f...) custom-call(bf16[2,2,256,256]{3,2,1,0:T(8,128)(2,1)S(1)} %get-tuple-element.27.refs_0_, ...), custom_call_target="tpu_custom_call" | custom-call | tf_op jit(solution)/shard_map/ratio_fields/pallas_call | solution.py:264
  16.2 0.8 %collective-permute-start.3 = (f32[7,16,256]{2,1,0:T(8,128)S(1)}, f32[7,16,256]{2,1,0:T(8,128)S(1)}, u32[]{:S(2)}, u32[]{:S(2)}) collective-permute-start(f32[7,16,256]{2,1,0:T(8,128)S(1)} %get-tuple-element.40), channel_id=1, source_target_pairs={{4,8},{12,16},{20,24},{8,4},{16,12},{24,20},{5,9},{13,17},{21,25},... | collective-permute-start | bytes 344072 | tf_op jit(solution)/shard_map/ppermute | solution.py:636
  17.0 3.8 %collective-permute-start.4 = (f32[7,16,256]{2,1,0:T(8,128)S(1)}, f32[7,16,256]{2,1,0:T(8,128)S(1)}, u32[]{:S(2)}, u32[]{:S(2)}) collective-permute-start(f32[7,16,256]{2,1,0:T(8,128)S(1)} %get-tuple-element.41), channel_id=1, source_target_pairs={{0,4},{4,0},{8,12},{12,8},{16,20},{20,16},{24,28},{28,24},{1,5},{5... | collective-permute-start | bytes 344072 | tf_op jit(solution)/shard_map/ppermute | solution.py:636
  20.8 0.7 %collective-permute-start.6 = (f32[7,16,256]{2,1,0:T(8,128)S(1)}, f32[7,16,256]{2,1,0:T(8,128)S(1)}, u32[]{:S(2)}, u32[]{:S(2)}) collective-permute-start(f32[7,16,256]{2,1,0:T(8,128)S(1)} %get-tuple-element.44), channel_id=1, source_target_pairs={{4,8},{12,16},{20,24},{8,4},{16,12},{24,20},{5,9},{13,17},{21,25},... | collective-permute-start | bytes 344072 | tf_op jit(solution)/shard_map/ppermute | solution.py:636
  21.5 5.5 %collective-permute-start.7 = (f32[7,16,256]{2,1,0:T(8,128)S(1)}, f32[7,16,256]{2,1,0:T(8,128)S(1)}, u32[]{:S(2)}, u32[]{:S(2)}) collective-permute-start(f32[7,16,256]{2,1,0:T(8,128)S(1)} %get-tuple-element.45), channel_id=1, source_target_pairs={{0,4},{4,0},{8,12},{12,8},{16,20},{20,16},{24,28},{28,24},{1,5},{5... | collective-permute-start | bytes 344072 | tf_op jit(solution)/shard_map/ppermute | solution.py:636
  27.0 0.3 own_planes.1
  27.3 2.5 %collective-permute-start.5 = (f32[8,16,256]{2,1,0:T(8,128)S(1)}, f32[8,16,256]{2,1,0:T(8,128)S(1)}, u32[]{:S(2)}, u32[]{:S(2)}) collective-permute-start(f32[8,16,256]{2,1,0:T(8,128)S(1)} %add_rims.2.correction.mine), channel_id=1, source_target_pairs={{0,3},{1,2},{2,1},{3,0},{4,7},{5,6},{6,5},{7,4},{8,11},{9,10},{10,... | collective-permute-start | bytes 393224 | tf_op jit(solution)/shard_map/ppermute | solution.py:642
  29.9 1.0 %moment_rows.2.rest_0_.refs_0_ = f32[16,128]{1,0:T(8,128)S(1)} custom-call(f32[8,64,256]{2,1,0:T(8,128)S(1)} %copy-done, s32[8,64,256]{2,1,0:T(8,128)S(1)} %copy-done.1, f32[64,16]{1,0:T(8,128)S(1)} %get-tuple-element.42.picked, f32[64,128]{1,0:T(8,128)S(1)} %get-tuple-element.24.after.base, f32[8,16,256]{2,1,0:T(8,128)S(1)} %add_rims.2.correction.mine), custom_call_target="tpu_custom_call" | custom-call | tf_op jit(solution)/shard_map/moment_rows/pallas_call | solution.py:472
  31.0 1.4 %collective-permute-start.8 = (f32[8,16,256]{2,1,0:T(8,128)S(1)}, f32[8,16,256]{2,1,0:T(8,128)S(1)}, u32[]{:S(2)}, u32[]{:S(2)}) collective-permute-start(f32[8,16,256]{2,1,0:T(8,128)S(1)} %add_rims.3.correction.mine), channel_id=1, source_target_pairs={{0,3},{1,2},{2,1},{3,0},{4,7},{5,6},{6,5},{7,4},{8,11},{9,10},{10,... | collective-permute-start | bytes 393224 | tf_op jit(solution)/shard_map/ppermute | solution.py:642
  32.4 1.2 %moment_rows.3 = f32[64,128]{1,0:T(8,128)S(1)} custom-call(f32[8,64,256]{2,1,0:T(8,128)S(1)} %copy-done, s32[8,64,256]{2,1,0:T(8,128)S(1)} %copy-done.1, f32[64,16]{1,0:T(8,128)S(1)} %get-tuple-element.42.picked, f32[64,128]{1,0:T(8,128)S(1)} %get-tuple-element.24.after.base, f32[8,16,256]{2,1,0:T(8,128)S(1)} %add_rims.3.correction.mine, ...), custom_call_target="tpu_custom_call" | custom-call | tf_op jit(solution)/shard_map/moment_rows/pallas_call | solution.py:472
  33.6 8.4 %all_to_all.11 = f32[8,8,128]{2,1,0:T(8,128)S(1)} all-to-all(f32[8,8,128]{2,1,0:T(8,128)S(1)} %bitcast.3), channel_id=1, replica_groups=mesh['tile'=8,'view'=4] {'tile'}, dimensions={0} | all-to-all | bytes 65536 | tf_op jit(solution)/shard_map/all_to_all | solution.py:645
  41.9 0.3 segment_table.1.rest_0_.refs_2_
  42.3 0.7 %collective-permute-start.9 = (f32[136,256]{1,0:T(8,128)S(1)}, f32[136,256]{1,0:T(8,128)S(1)}, u32[]{:S(2)}, u32[]{:S(2)}) collective-permute-start(f32[136,256]{1,0:T(8,128)S(1)} %update.2.source.refs_0_), channel_id=1, source_target_pairs={{0,1},{1,0},{2,3},{3,2},{4,5},{5,4},{6,7},{7,6},{8,9},{9,8},{10,11... | collective-permute-start | bytes 417800 | tf_op jit(solution)/shard_map/ppermute | solution.py:655
  43.0 1.4 %collective-permute-start.10 = (f32[128,256]{1,0:T(8,128)S(1)}, f32[128,256]{1,0:T(8,128)S(1)}, u32[]{:S(2)}, u32[]{:S(2)}) collective-permute-start(f32[128,256]{1,0:T(8,128)S(1)} %update.3.refs_1_), channel_id=1, source_target_pairs={{0,1},{1,0},{2,3},{3,2},{4,5},{5,4},{6,7},{7,6},{8,9},{9,8},{10,11... | collective-permute-start | bytes 393224 | tf_op jit(solution)/shard_map/ppermute | solution.py:655
  44.4 1.5 %collective-permute-start.12 = (f32[16,128]{1,0:T(8,128)S(1)}, f32[16,128]{1,0:T(8,128)S(1)}, u32[]{:S(2)}, u32[]{:S(2)}) collective-permute-start(f32[16,128]{1,0:T(8,128)S(1)} %segment_table.1.rest_0_.refs_2_), channel_id=1, source_target_pairs={{0,3},{1,2},{2,1},{3,0},{4,7},{5,6},{6,5},{7,4},{8,11},{9,10},{10,... | collective-permute-start | bytes 24584 | tf_op jit(solution)/shard_map/ppermute | solution.py:648
  46.0 0.6 %collective-permute-start.11 = (f32[16,128]{1,0:T(8,128)S(1)}, f32[16,128]{1,0:T(8,128)S(1)}, u32[]{:S(2)}, u32[]{:S(2)}) collective-permute-start(f32[16,128]{1,0:T(8,128)S(1)} %segment_table.1.rest_0_.refs_2_), channel_id=1, source_target_pairs={{0,2},{1,3},{2,0},{3,1},{4,6},{5,7},{6,4},{7,5},{8,10},{9,11},{10,... | collective-permute-start | bytes 24584 | tf_op jit(solution)/shard_map/ppermute | solution.py:648
  46.6 0.8 %begin_result.1.begun = f32[8,64,256]{2,1,0:T(8,128)} custom-call(f32[136,256]{1,0:T(8,128)S(1)} %update.2.source.refs_0_, f32[128,256]{1,0:T(8,128)S(1)} %update.3.refs_1_), custom_call_target="tpu_custom_call" | custom-call | tf_op jit(solution)/shard_map/begin_result/pallas_call | solution.py:561
  47.4 3.2 %collective-permute-done.12.refs_4_ = f32[16,128]{1,0:T(8,128)S(1)} collective-permute-done((f32[16,128]{1,0:T(8,128)S(1)}, f32[16,128]{1,0:T(8,128)S(1)}, u32[]{:S(2)}, u32[]{:S(2)}) %collective-permute-start.12) | collective-permute-done | bytes 8224 | tf_op jit(solution)/shard_map/ppermute | solution.py:648
  50.6 0.1 collective-permute-done.11.refs_3_
  50.7 0.1 collective-permute-done.10.refs_1_
  50.8 0.8 %finish.1 = (f32[8,64,256]{2,1,0:T(8,128)}, f32[10,128]{1,0:T(8,128)}) custom-call(f32[8,64,256]{2,1,0:T(8,128)} %begin_result.1.begun, f32[136,256]{1,0:T(8,128)S(1)} %collective-permute-done.9.refs_0_, f32[128,256]{1,0:T(8,128)S(1)} %collective-permute-done.10.refs_1_, ...), custom_call_target="tpu_custom_call", output_to_operand_aliasing={{0}: (0, {})} | custom-call | tf_op jit(solution)/shard_map/finish/pallas_call | solution.py:593
  (25 shorter events, 0.2 us)
Async XLA Ops:
  0.6 4.9 %copy-start = (f32[8,64,256]{2,1,0:T(8,128)S(1)}, f32[8,64,256]{2,1,0:T(8,128)}, u32[]{:S(2)}) copy-start(f32[8,64,256]{2,1,0:T(8,128)} %estimate.13) | copy-start | bytes 1572868
  1.4 1.0 %copy-start.2 = (f32[1,8,64,256]{3,2,1,0:T(8,128)S(1)}, f32[1,8,64,256]{3,2,1,0:T(8,128)}, u32[]{:S(2)}) copy-start(f32[1,8,64,256]{3,2,1,0:T(8,128)} %refs_12_.1) | copy-start | bytes 1572868
  2.4 11.3 %collective-permute-start = (f32[344,256]{1,0:T(8,128)S(1)}, f32[344,256]{1,0:T(8,128)S(1)}, u32[]{:S(2)}, u32[]{:S(2)}) collective-permute-start(f32[344,256]{1,0:T(8,128)S(1)} %view_out.1), channel_id=1, source_target_pairs={{0,1},{1,0},{2,3},{3,2},{4,5},{5,4},{6,7},{7,6},{8,9},{9,8},{10,11... | collective-permute-start | bytes 1056776 | tf_op jit(solution)/shard_map/ppermute | solution.py:627
  5.6 8.8 %collective-permute-start.1 = (f32[7,48,256]{2,1,0:T(8,128)S(1)}, f32[7,48,256]{2,1,0:T(8,128)S(1)}, u32[]{:S(2)}, u32[]{:S(2)}) collective-permute-start(f32[7,48,256]{2,1,0:T(8,128)S(1)} %get-tuple-element.35), channel_id=1, source_target_pairs={{4,8},{12,16},{20,24},{8,4},{16,12},{24,20},{5,9},{13,17},{21,25},... | collective-permute-start | bytes 1032200 | tf_op jit(solution)/shard_map/ppermute | solution.py:629
  6.3 2.9 %copy-start.4 = (s32[1,16,1]{1,2,0:T(1,128)S(1)}, s32[1,16,1]{1,2,0:T(1,128)}, u32[]{:S(2)}) copy-start(s32[1,16,1]{1,2,0:T(1,128)} %param.10) | copy-start | bytes 196
  6.3 2.9 %copy-start.5 = (s32[1,16]{1,0:T(1,128)S(1)}, s32[1,16]{1,0:T(1,128)}, u32[]{:S(2)}) copy-start(s32[1,16]{1,0:T(1,128)} %index_row.1) | copy-start | bytes 196
  6.3 8.1 %collective-permute-start.2 = (f32[7,48,256]{2,1,0:T(8,128)S(1)}, f32[7,48,256]{2,1,0:T(8,128)S(1)}, u32[]{:S(2)}, u32[]{:S(2)}) collective-permute-start(f32[7,48,256]{2,1,0:T(8,128)S(1)} %get-tuple-element.36), channel_id=1, source_target_pairs={{0,4},{4,0},{8,12},{12,8},{16,20},{20,16},{24,28},{28,24},{1,5},{5... | collective-permute-start | bytes 1032200 | tf_op jit(solution)/shard_map/ppermute | solution.py:630
  10.0 4.4 %copy-start.3 = (f32[1,8,64,256]{3,2,1,0:T(8,128)S(1)}, f32[1,8,64,256]{3,2,1,0:T(8,128)}, u32[]{:S(2)}) copy-start(f32[1,8,64,256]{3,2,1,0:T(8,128)} %refs_12_.1) | copy-start | bytes 1572868
  16.2 13.6 %copy-start.1 = (s32[8,64,256]{2,1,0:T(8,128)S(1)}, s32[8,64,256]{2,1,0:T(8,128)}, u32[]{:S(2)}) copy-start(s32[8,64,256]{2,1,0:T(8,128)} %labels.3) | copy-start | bytes 1572868
  16.2 11.0 %collective-permute-start.3 = (f32[7,16,256]{2,1,0:T(8,128)S(1)}, f32[7,16,256]{2,1,0:T(8,128)S(1)}, u32[]{:S(2)}, u32[]{:S(2)}) collective-permute-start(f32[7,16,256]{2,1,0:T(8,128)S(1)} %get-tuple-element.40), channel_id=1, source_target_pairs={{4,8},{12,16},{20,24},{8,4},{16,12},{24,20},{5,9},{13,17},{21,25},... | collective-permute-start | bytes 344072 | tf_op jit(solution)/shard_map/ppermute | solution.py:636
  17.0 10.2 %collective-permute-start.4 = (f32[7,16,256]{2,1,0:T(8,128)S(1)}, f32[7,16,256]{2,1,0:T(8,128)S(1)}, u32[]{:S(2)}, u32[]{:S(2)}) collective-permute-start(f32[7,16,256]{2,1,0:T(8,128)S(1)} %get-tuple-element.41), channel_id=1, source_target_pairs={{0,4},{4,0},{8,12},{12,8},{16,20},{20,16},{24,28},{28,24},{1,5},{5... | collective-permute-start | bytes 344072 | tf_op jit(solution)/shard_map/ppermute | solution.py:636
  20.8 10.1 %collective-permute-start.6 = (f32[7,16,256]{2,1,0:T(8,128)S(1)}, f32[7,16,256]{2,1,0:T(8,128)S(1)}, u32[]{:S(2)}, u32[]{:S(2)}) collective-permute-start(f32[7,16,256]{2,1,0:T(8,128)S(1)} %get-tuple-element.44), channel_id=1, source_target_pairs={{4,8},{12,16},{20,24},{8,4},{16,12},{24,20},{5,9},{13,17},{21,25},... | collective-permute-start | bytes 344072 | tf_op jit(solution)/shard_map/ppermute | solution.py:636
  21.5 9.5 %collective-permute-start.7 = (f32[7,16,256]{2,1,0:T(8,128)S(1)}, f32[7,16,256]{2,1,0:T(8,128)S(1)}, u32[]{:S(2)}, u32[]{:S(2)}) collective-permute-start(f32[7,16,256]{2,1,0:T(8,128)S(1)} %get-tuple-element.45), channel_id=1, source_target_pairs={{0,4},{4,0},{8,12},{12,8},{16,20},{20,16},{24,28},{28,24},{1,5},{5... | collective-permute-start | bytes 344072 | tf_op jit(solution)/shard_map/ppermute | solution.py:636
  27.3 14.9 %collective-permute-start.5 = (f32[8,16,256]{2,1,0:T(8,128)S(1)}, f32[8,16,256]{2,1,0:T(8,128)S(1)}, u32[]{:S(2)}, u32[]{:S(2)}) collective-permute-start(f32[8,16,256]{2,1,0:T(8,128)S(1)} %add_rims.2.correction.mine), channel_id=1, source_target_pairs={{0,3},{1,2},{2,1},{3,0},{4,7},{5,6},{6,5},{7,4},{8,11},{9,10},{10,... | collective-permute-start | bytes 393224 | tf_op jit(solution)/shard_map/ppermute | solution.py:642
  31.0 12.0 %collective-permute-start.8 = (f32[8,16,256]{2,1,0:T(8,128)S(1)}, f32[8,16,256]{2,1,0:T(8,128)S(1)}, u32[]{:S(2)}, u32[]{:S(2)}) collective-permute-start(f32[8,16,256]{2,1,0:T(8,128)S(1)} %add_rims.3.correction.mine), channel_id=1, source_target_pairs={{0,3},{1,2},{2,1},{3,0},{4,7},{5,6},{6,5},{7,4},{8,11},{9,10},{10,... | collective-permute-start | bytes 393224 | tf_op jit(solution)/shard_map/ppermute | solution.py:642
  42.3 8.5 %collective-permute-start.9 = (f32[136,256]{1,0:T(8,128)S(1)}, f32[136,256]{1,0:T(8,128)S(1)}, u32[]{:S(2)}, u32[]{:S(2)}) collective-permute-start(f32[136,256]{1,0:T(8,128)S(1)} %update.2.source.refs_0_), channel_id=1, source_target_pairs={{0,1},{1,0},{2,3},{3,2},{4,5},{5,4},{6,7},{7,6},{8,9},{9,8},{10,11... | collective-permute-start | bytes 417800 | tf_op jit(solution)/shard_map/ppermute | solution.py:655
  43.0 7.8 %collective-permute-start.10 = (f32[128,256]{1,0:T(8,128)S(1)}, f32[128,256]{1,0:T(8,128)S(1)}, u32[]{:S(2)}, u32[]{:S(2)}) collective-permute-start(f32[128,256]{1,0:T(8,128)S(1)} %update.3.refs_1_), channel_id=1, source_target_pairs={{0,1},{1,0},{2,3},{3,2},{4,5},{5,4},{6,7},{7,6},{8,9},{9,8},{10,11... | collective-permute-start | bytes 393224 | tf_op jit(solution)/shard_map/ppermute | solution.py:655
  44.4 6.1 %collective-permute-start.12 = (f32[16,128]{1,0:T(8,128)S(1)}, f32[16,128]{1,0:T(8,128)S(1)}, u32[]{:S(2)}, u32[]{:S(2)}) collective-permute-start(f32[16,128]{1,0:T(8,128)S(1)} %segment_table.1.rest_0_.refs_2_), channel_id=1, source_target_pairs={{0,3},{1,2},{2,1},{3,0},{4,7},{5,6},{6,5},{7,4},{8,11},{9,10},{10,... | collective-permute-start | bytes 24584 | tf_op jit(solution)/shard_map/ppermute | solution.py:648
  46.0 4.7 %collective-permute-start.11 = (f32[16,128]{1,0:T(8,128)S(1)}, f32[16,128]{1,0:T(8,128)S(1)}, u32[]{:S(2)}, u32[]{:S(2)}) collective-permute-start(f32[16,128]{1,0:T(8,128)S(1)} %segment_table.1.rest_0_.refs_2_), channel_id=1, source_target_pairs={{0,2},{1,3},{2,0},{3,1},{4,6},{5,7},{6,4},{7,5},{8,10},{9,11},{10,... | collective-permute-start | bytes 24584 | tf_op jit(solution)/shard_map/ppermute | solution.py:648

commit v7 on v6

--- a/solution.py
+++ b/solution.py
@@ -79,14 +79,16 @@
     )(estimate)
 
 
-def view_out_kernel(seen, measured, kernels, packed):
+def view_out_kernel(seen, measured, taps, packed):
     planes, height = measured.shape[1], measured.shape[2]
     half = half_of(lax.axis_index("view"))
     start = pl.multiple_of((height - seen) * (1 - half), 8)
     for plane in range(planes):
         packed[plane * seen : (plane + 1) * seen] = measured[0, plane, pl.ds(start, seen)]
     packed[planes * seen :] = jnp.zeros((TAIL, packed.shape[1]), F32)
-    packed[planes * seen : planes * seen + kernels.shape[1], : kernels.shape[2]] = kernels[0]
+    for axis in range(taps.shape[0]):
+        at = planes * seen + axis
+        packed[at : at + 1, : taps.shape[2]] = taps[axis]
 
 
 def view_out(measured, kernels, seen):
@@ -108,7 +110,10 @@
     planes = estimate.shape[0]
     radius = (taps - 1) // 2
     at = source.shape[0] - TAIL
-    raw = source[at : at + 3, :taps] if packed else source[0]
+    if packed:
+        raw = source[at : at + 3, :taps]
+    else:
+        raw = jnp.concatenate([source[axis] for axis in range(source.shape[0])], axis=0)
     weights = raw / jnp.sum(raw, axis=-1, keepdims=True)
     deep, high, flat = [[weights[axis : axis + 1, t : t + 1] for t in range(taps)] for axis in range(3)]
     start = pl.multiple_of((2 * keep - rows) * half, 16)
@@ -342,9 +347,10 @@
         held = estimate[plane, pl.ds(start, size)]
         at = slice(plane * size, (plane + 1) * size)
         result[at] = held * (mine[plane] + other[plane]) * (1.0 / views)
+    rows = result.shape[0] - planes * size
+    result[planes * size :] = jnp.zeros((rows, across), F32)
     if tabled:
         table = rest[0][...]
-        result[planes * size :] = jnp.zeros((8, across), F32)
         result[planes * size :, : 2 * LANES] = jnp.concatenate([table[:8], table[8:]], axis=1)
 
 
@@ -352,7 +358,7 @@
     planes, size, across = mine.shape
     return pl.pallas_call(
         functools.partial(update_kernel, views, part, len(table) > 0),
-        out_shape=jax.ShapeDtypeStruct((planes * size + 8 * len(table), across), F32),
+        out_shape=jax.ShapeDtypeStruct((planes * size + 8 * (PARTS - part), across), F32),
         in_specs=[VMEM] * (3 + len(table)) + [ANY] * len(after),
         out_specs=VMEM,
         compiler_params=pltpu.CompilerParams(vmem_limit_bytes=LIMIT),
@@ -576,7 +582,7 @@
     copies = []
     for part in range(PARTS):
         copies += stores(others[part], whole, 1 - half, part, size, sems.at[part])
-    rows = others[0][planes * size :]
+    rows = others[-1][planes * size :]
     second = jnp.concatenate([rows[:, :LANES], rows[:, LANES : 2 * LANES]], axis=0)
     table = (first[...] + second) + (third[...] + fourth[...])
     lines = lax.broadcasted_iota(jnp.int32, table.shape, 0)
@@ -623,14 +629,15 @@
     partner = [(i, i ^ 1) for i in range(views)]
     across_pairs = [(i, i ^ 3) for i in range(views)]
 
-    packed = view_out(measured, kernels, seen)
+    lines = jnp.transpose(kernels, (1, 0, 2))
+    packed = view_out(measured, lines, seen)
     swapped = lax.ppermute(packed, "view", partner)
     to_far, to_near = rims_out(estimate, radius, rows)
     far = lax.ppermute(to_far, "tile", far_pairs)
     near = lax.ppermute(to_near, "tile", near_pairs)
     places = slot_places(tiles, label_owner, label_index)
-    own = prepare(False, taps, kernels, estimate, places[1], rows, seen, keep)
-    others = prepare(True, taps, swapped, estimate, kernels, rows, seen, keep)
+    own = prepare(False, taps, lines, estimate, places[1], rows, seen, keep)
+    others = prepare(True, taps, swapped, estimate, lines, rows, seen, keep)
     field_own, field_other, *sends = ratio_fields(own, others, far, near, measured, swapped)
     rims = [
         lax.ppermute(send, "tile", pairs) for send, pairs in zip(sends, (far_pairs, near_pairs) * PARTS)
@@ -650,7 +657,7 @@
     size = keep // PARTS
     new_mine, new_other, token = [], [], []
     for part in range(PARTS):
-        last = [table] if part == 0 else []
+        last = [table] if part == PARTS - 1 else []
         new_mine.append(update(views, part, estimate, mine[part], other[part], last, token))
         new_other.append(lax.ppermute(new_mine[part], "view", partner))
         token = [token_of(new_mine[part])]

time: 51.9 us -> 51.1 us (0.985)
  blocking collectives: 8.36 us -> 0 us
  starting transfers between devices: 25.6 us -> 31.2 us
  waiting for transfers between devices: 7.14 us -> 7.96 us
  Pallas kernels: 7.85 us -> 8.47 us
    all_to_all x1 -> x0, blocking collectives: 8.36 us -> none  [on_device(): got = lax.all_to_all(sent, 'tile', split_axis=0, concat_axis=0, tiled=True)]
    all_to_all x0 -> x1, starting transfers between devices: none -> 3.72 us  [on_device(): got = lax.all_to_all(sent, 'tile', split_axis=0, concat_axis=0, tiled=True)]
    all_to_all x0 -> x1, waiting for transfers between devices: none -> 2.2 us  [on_device(): got = lax.all_to_all(sent, 'tile', split_axis=0, concat_axis=0, tiled=True)]
    ppermute x2, starting transfers between devices: 2.16 us -> 3.35 us  [on_device(): new_other.append(lax.ppermute(new_mine[part], 'view', partner))]
    ppermute x2, waiting for transfers between devices: 3.25 us -> 2.45 us  [on_device(): lax.ppermute(table, 'view', [(i, i ^ step) for i in range(views)])]
    ppermute x2, starting transfers between devices: 2.14 us -> 2.81 us  [on_device(): lax.ppermute(table, 'view', [(i, i ^ step) for i in range(views)])]
    pallas_call x2, Pallas kernels: 2.21 us -> 2.83 us  [moment_rows(): pl.pallas_call(functools.partial(moments_kernel, views, tiles * planes, p...]
    unnamed x13 -> x16, local copies, waits for them, and re-layouts: 1.81 us -> 2.27 us
  transfers between devices with their start and end apart: 13 -> 14, of which waited for: 4 -> 4; matrix products, arithmetic and copies ran while one was open for 0% -> 0% of each run, Pallas kernels for 10% -> 11%
where the time goes in v7:
time: 51.1 us; the launch traced here: 50.8 us
  starting transfers between devices  31.2 us (61%)
  Pallas kernels  8.47 us (17%)
  waiting for transfers between devices  7.96 us (16%)
  local copies, waits for them, and re-layouts  2.27 us (4%)
  between operations  0.86 us (2%)
    ppermute x4, starting transfers between devices, on_device(): lax.ppermute(send, 'tile', pairs)  10.7 us
    ppermute x2, starting transfers between devices, on_device(): other.append(lax.ppermute(mine[part], 'view', across_pairs))  3.95 us
    all_to_all x1, starting transfers between devices, on_device(): got = lax.all_to_all(sent, 'tile', split_axis=0, concat_axis=0, tiled=True)  3.72 us
    ppermute x2, starting transfers between devices, on_device(): new_other.append(lax.ppermute(new_mine[part], 'view', partner))  3.35 us
    ppermute x1, waiting for transfers between devices, on_device(): swapped = lax.ppermute(packed, 'view', partner)  3.29 us
    ppermute x1, starting transfers between devices, on_device(): swapped = lax.ppermute(packed, 'view', partner)  3.09 us
    ppermute x1, starting transfers between devices, on_device(): near = lax.ppermute(to_near, 'tile', near_pairs)  2.9 us
    pallas_call x2, Pallas kernels, moment_rows(): pl.pallas_call(functools.partial(moments_kernel, views, tiles * planes, p...  2.83 us
  transfers between devices with their start and end apart: 14, of which 4 were waited for; matrix products, arithmetic and copies ran while one was open for 0% of the time, Pallas kernels for 11%

profile of v7, /device:TPU:0, one launch (start us, length us, event | category | flops | bytes accessed | tf_op | source)
XLA Modules:
  0.0 50.8 jit_solution(6537404536061869220)
XLA Ops:
  0.6 0.0 copy-start.1
  0.7 1.1 %copy-done.1 = f32[1,8,64,256]{3,2,1,0:T(8,128)S(1)} copy-done((f32[1,8,64,256]{3,2,1,0:T(8,128)S(1)}, f32[1,8,64,256]{3,2,1,0:T(8,128)}, u32[]{:S(2)}) %copy-start.1) | copy-done | bytes 524312
  1.7 0.7 %copy-done.4 = f32[1,3,15]{2,0,1:T(1,128)S(1)} copy-done((f32[1,3,15]{2,0,1:T(1,128)S(1)}, f32[1,3,15]{2,0,1:T(1,128)}, u32[]{:S(2)}) %copy-start.4) | copy-done | bytes 204
  2.5 3.1 %collective-permute-start = (f32[344,256]{1,0:T(8,128)S(1)}, f32[344,256]{1,0:T(8,128)S(1)}, u32[]{:S(2)}, u32[]{:S(2)}) collective-permute-start(f32[344,256]{1,0:T(8,128)S(1)} %view_out.1), channel_id=1, source_target_pairs={{0,1},{1,0},{2,3},{3,2},{4,5},{5,4},{6,7},{7,6},{8,9},{9,8},{10,11... | collective-permute-start | bytes 1056776 | tf_op jit(solution)/shard_map/ppermute | solution.py:634
  5.6 0.7 %collective-permute-start.1 = (f32[7,48,256]{2,1,0:T(8,128)S(1)}, f32[7,48,256]{2,1,0:T(8,128)S(1)}, u32[]{:S(2)}, u32[]{:S(2)}) collective-permute-start(f32[7,48,256]{2,1,0:T(8,128)S(1)} %get-tuple-element.35), channel_id=1, source_target_pairs={{4,8},{12,16},{20,24},{8,4},{16,12},{24,20},{5,9},{13,17},{21,25},... | collective-permute-start | bytes 1032200 | tf_op jit(solution)/shard_map/ppermute | solution.py:636
  6.3 2.9 %collective-permute-start.2 = (f32[7,48,256]{2,1,0:T(8,128)S(1)}, f32[7,48,256]{2,1,0:T(8,128)S(1)}, u32[]{:S(2)}, u32[]{:S(2)}) collective-permute-start(f32[7,48,256]{2,1,0:T(8,128)S(1)} %get-tuple-element.36), channel_id=1, source_target_pairs={{0,4},{4,0},{8,12},{12,8},{16,20},{20,16},{24,28},{28,24},{1,5},{5... | collective-permute-start | bytes 1032200 | tf_op jit(solution)/shard_map/ppermute | solution.py:637
  9.2 0.2 slot_places.1
  9.4 0.5 copy-done.5
  9.9 0.6 %prepare.2 = (bf16[2,2,256,256]{3,2,1,0:T(8,128)(2,1)S(1)}, bf16[40,144]{1,0:T(8,128)(2,1)S(1)}, bf16[32,144]{1,0:T(8,128)(2,1)S(1)}, f32[8,48,256]{2,1,0:T(8,128)S(1)}, f32[16,128]{1,0:T(8,128)S(1)}) custom-call(f32[3,1,15]{2,1,0:T(1,128)S(1)} %bitcast.6, f32[8,64,256]{2,1,0:T(8,128)S(1)} %copy-done, f32[64,128]{1,0:T(8,128)S(1)} %get-tuple-element.24.after.base), custom_call_target="tpu_custom_call" | custom-call | tf_op jit(solution)/shard_map/prepare/pallas_call | solution.py:154
  10.5 3.3 %collective-permute-done.source.refs_13_ = f32[344,256]{1,0:T(8,128)S(1)} collective-permute-done((f32[344,256]{1,0:T(8,128)S(1)}, f32[344,256]{1,0:T(8,128)S(1)}, u32[]{:S(2)}, u32[]{:S(2)}) %collective-permute-start) | collective-permute-done | bytes 352288 | tf_op jit(solution)/shard_map/ppermute | solution.py:634
  13.8 0.6 %prepare.3 = (bf16[2,2,256,256]{3,2,1,0:T(8,128)(2,1)S(1)}, bf16[40,144]{1,0:T(8,128)(2,1)S(1)}, bf16[32,144]{1,0:T(8,128)(2,1)S(1)}, f32[8,48,256]{2,1,0:T(8,128)S(1)}, f32[16,128]{1,0:T(8,128)S(1)}) custom-call(f32[344,256]{1,0:T(8,128)S(1)} %collective-permute-done.source.refs_13_, f32[8,64,256]{2,1,0:T(8,128)S(1)} %copy-done, f32[3,1,15]{2,1,0:T(1,128)S(1)} %bitcast.7), custom_call_target="tpu_custom_call" | custom-call | tf_op jit(solution)/shard_map/prepare/pallas_call | solution.py:154
  14.4 1.8 %ratio_fields.1 = (f32[8,32,256]{2,1,0:T(8,128)S(1)}, f32[8,32,256]{2,1,0:T(8,128)S(1)}, f32[7,16,256]{2,1,0:T(8,128)S(1)}, f32[7,16,256]{2,1,0:T(8,128)S(1)}, f...) custom-call(bf16[2,2,256,256]{3,2,1,0:T(8,128)(2,1)S(1)} %get-tuple-element.27.refs_0_, ...), custom_call_target="tpu_custom_call" | custom-call | tf_op jit(solution)/shard_map/ratio_fields/pallas_call | solution.py:269
  16.2 0.8 %collective-permute-start.3 = (f32[7,16,256]{2,1,0:T(8,128)S(1)}, f32[7,16,256]{2,1,0:T(8,128)S(1)}, u32[]{:S(2)}, u32[]{:S(2)}) collective-permute-start(f32[7,16,256]{2,1,0:T(8,128)S(1)} %get-tuple-element.40), channel_id=1, source_target_pairs={{4,8},{12,16},{20,24},{8,4},{16,12},{24,20},{5,9},{13,17},{21,25},... | collective-permute-start | bytes 344072 | tf_op jit(solution)/shard_map/ppermute | solution.py:643
  17.0 3.8 %collective-permute-start.4 = (f32[7,16,256]{2,1,0:T(8,128)S(1)}, f32[7,16,256]{2,1,0:T(8,128)S(1)}, u32[]{:S(2)}, u32[]{:S(2)}) collective-permute-start(f32[7,16,256]{2,1,0:T(8,128)S(1)} %get-tuple-element.41), channel_id=1, source_target_pairs={{0,4},{4,0},{8,12},{12,8},{16,20},{20,16},{24,28},{28,24},{1,5},{5... | collective-permute-start | bytes 344072 | tf_op jit(solution)/shard_map/ppermute | solution.py:643
  20.8 0.7 %collective-permute-start.6 = (f32[7,16,256]{2,1,0:T(8,128)S(1)}, f32[7,16,256]{2,1,0:T(8,128)S(1)}, u32[]{:S(2)}, u32[]{:S(2)}) collective-permute-start(f32[7,16,256]{2,1,0:T(8,128)S(1)} %get-tuple-element.43), channel_id=1, source_target_pairs={{4,8},{12,16},{20,24},{8,4},{16,12},{24,20},{5,9},{13,17},{21,25},... | collective-permute-start | bytes 344072 | tf_op jit(solution)/shard_map/ppermute | solution.py:643
  21.5 5.5 %collective-permute-start.7 = (f32[7,16,256]{2,1,0:T(8,128)S(1)}, f32[7,16,256]{2,1,0:T(8,128)S(1)}, u32[]{:S(2)}, u32[]{:S(2)}) collective-permute-start(f32[7,16,256]{2,1,0:T(8,128)S(1)} %get-tuple-element.44), channel_id=1, source_target_pairs={{0,4},{4,0},{8,12},{12,8},{16,20},{20,16},{24,28},{28,24},{1,5},{5... | collective-permute-start | bytes 344072 | tf_op jit(solution)/shard_map/ppermute | solution.py:643
  27.0 0.3 own_planes.1
  27.3 2.5 %collective-permute-start.5 = (f32[8,16,256]{2,1,0:T(8,128)S(1)}, f32[8,16,256]{2,1,0:T(8,128)S(1)}, u32[]{:S(2)}, u32[]{:S(2)}) collective-permute-start(f32[8,16,256]{2,1,0:T(8,128)S(1)} %add_rims.2.mine.correction), channel_id=1, source_target_pairs={{0,3},{1,2},{2,1},{3,0},{4,7},{5,6},{6,5},{7,4},{8,11},{9,10},{10,... | collective-permute-start | bytes 393224 | tf_op jit(solution)/shard_map/ppermute | solution.py:649
  29.9 1.0 %moment_rows.2.rest_0_.refs_0_ = f32[16,128]{1,0:T(8,128)S(1)} custom-call(f32[8,64,256]{2,1,0:T(8,128)S(1)} %copy-done, s32[8,64,256]{2,1,0:T(8,128)S(1)} %copy-done.3, f32[64,16]{1,0:T(8,128)S(1)} %get-tuple-element.45.picked, f32[64,128]{1,0:T(8,128)S(1)} %get-tuple-element.24.after.base, f32[8,16,256]{2,1,0:T(8,128)S(1)} %add_rims.2.mine.correction), custom_call_target="tpu_custom_call" | custom-call | tf_op jit(solution)/shard_map/moment_rows/pallas_call | solution.py:478
  31.0 1.4 %collective-permute-start.8 = (f32[8,16,256]{2,1,0:T(8,128)S(1)}, f32[8,16,256]{2,1,0:T(8,128)S(1)}, u32[]{:S(2)}, u32[]{:S(2)}) collective-permute-start(f32[8,16,256]{2,1,0:T(8,128)S(1)} %add_rims.3.correction.mine), channel_id=1, source_target_pairs={{0,3},{1,2},{2,1},{3,0},{4,7},{5,6},{6,5},{7,4},{8,11},{9,10},{10,... | collective-permute-start | bytes 393224 | tf_op jit(solution)/shard_map/ppermute | solution.py:649
  32.4 1.8 %moment_rows.3 = f32[64,128]{1,0:T(8,128)} custom-call(f32[8,64,256]{2,1,0:T(8,128)S(1)} %copy-done, s32[8,64,256]{2,1,0:T(8,128)S(1)} %copy-done.3, f32[64,16]{1,0:T(8,128)S(1)} %get-tuple-element.45.picked, f32[64,128]{1,0:T(8,128)S(1)} %get-tuple-element.24.after.base, f32[8,16,256]{2,1,0:T(8,128)S(1)} %add_rims.3.correction.mine, ...), custom_call_target="tpu_custom_call" | custom-call | tf_op jit(solution)/shard_map/moment_rows/pallas_call | solution.py:478
  34.2 3.7 %all-to-all-start = ((f32[8,8,128]{2,1,0:T(8,128)}), f32[8,8,128]{2,1,0:T(8,128)S(1)}, u32[]{:S(2)}, u32[]{:S(2)}) async-start(f32[8,8,128]{2,1,0:T(8,128)} %bitcast.2), calls=%async_computation | async-start | bytes 65536 | tf_op jit(solution)/shard_map/all_to_all | solution.py:652
  37.9 2.6 %collective-permute-start.9 = (f32[144,256]{1,0:T(8,128)S(1)}, f32[144,256]{1,0:T(8,128)S(1)}, u32[]{:S(2)}, u32[]{:S(2)}) collective-permute-start(f32[144,256]{1,0:T(8,128)S(1)} %update.2.source.refs_0_), channel_id=1, source_target_pairs={{0,1},{1,0},{2,3},{3,2},{4,5},{5,4},{6,7},{7,6},{8,9},{9,8},{10,11... | collective-permute-start | bytes 442376 | tf_op jit(solution)/shard_map/ppermute | solution.py:662
  40.6 2.2 %all-to-all-done = f32[8,8,128]{2,1,0:T(8,128)S(1)} async-done(((f32[8,8,128]{2,1,0:T(8,128)}), f32[8,8,128]{2,1,0:T(8,128)S(1)}, u32[]{:S(2)}, u32[]{:S(2)}) %all-to-all-start) | async-done | bytes 32800 | tf_op jit(solution)/shard_map/all_to_all | solution.py:652
  42.8 0.3 segment_table.1.rest_0_.refs_2_
  43.1 0.7 %collective-permute-start.10 = (f32[136,256]{1,0:T(8,128)S(1)}, f32[136,256]{1,0:T(8,128)S(1)}, u32[]{:S(2)}, u32[]{:S(2)}) collective-permute-start(f32[136,256]{1,0:T(8,128)S(1)} %update.3.refs_1_), channel_id=1, source_target_pairs={{0,1},{1,0},{2,3},{3,2},{4,5},{5,4},{6,7},{7,6},{8,9},{9,8},{10,11... | collective-permute-start | bytes 417800 | tf_op jit(solution)/shard_map/ppermute | solution.py:662
  43.8 1.5 %collective-permute-start.12 = (f32[16,128]{1,0:T(8,128)S(1)}, f32[16,128]{1,0:T(8,128)S(1)}, u32[]{:S(2)}, u32[]{:S(2)}) collective-permute-start(f32[16,128]{1,0:T(8,128)S(1)} %segment_table.1.rest_0_.refs_2_), channel_id=1, source_target_pairs={{0,3},{1,2},{2,1},{3,0},{4,7},{5,6},{6,5},{7,4},{8,11},{9,10},{10,... | collective-permute-start | bytes 24584 | tf_op jit(solution)/shard_map/ppermute | solution.py:655
  45.4 1.3 %collective-permute-start.11 = (f32[16,128]{1,0:T(8,128)S(1)}, f32[16,128]{1,0:T(8,128)S(1)}, u32[]{:S(2)}, u32[]{:S(2)}) collective-permute-start(f32[16,128]{1,0:T(8,128)S(1)} %segment_table.1.rest_0_.refs_2_), channel_id=1, source_target_pairs={{0,2},{1,3},{2,0},{3,1},{4,6},{5,7},{6,4},{7,5},{8,10},{9,11},{10,... | collective-permute-start | bytes 24584 | tf_op jit(solution)/shard_map/ppermute | solution.py:655
  46.6 0.8 %begin_result.1.begun = f32[8,64,256]{2,1,0:T(8,128)} custom-call(f32[144,256]{1,0:T(8,128)S(1)} %update.2.source.refs_0_, f32[136,256]{1,0:T(8,128)S(1)} %update.3.refs_1_), custom_call_target="tpu_custom_call" | custom-call | tf_op jit(solution)/shard_map/begin_result/pallas_call | solution.py:567
  47.5 2.3 %collective-permute-done.12.refs_4_ = f32[16,128]{1,0:T(8,128)S(1)} collective-permute-done((f32[16,128]{1,0:T(8,128)S(1)}, f32[16,128]{1,0:T(8,128)S(1)}, u32[]{:S(2)}, u32[]{:S(2)}) %collective-permute-start.12) | collective-permute-done | bytes 8224 | tf_op jit(solution)/shard_map/ppermute | solution.py:655
  49.8 0.1 collective-permute-done.11.refs_3_
  49.9 0.8 %finish.1 = (f32[8,64,256]{2,1,0:T(8,128)}, f32[10,128]{1,0:T(8,128)}) custom-call(f32[8,64,256]{2,1,0:T(8,128)} %begin_result.1.begun, f32[144,256]{1,0:T(8,128)S(1)} %collective-permute-done.9.refs_0_, f32[136,256]{1,0:T(8,128)S(1)} %collective-permute-done.10.refs_1_, ...), custom_call_target="tpu_custom_call", output_to_operand_aliasing={{0}: (0, {})} | custom-call | tf_op jit(solution)/shard_map/finish/pallas_call | solution.py:599
  (29 shorter events, 0.3 us)
Async XLA Ops:
  0.6 4.9 %copy-start = (f32[8,64,256]{2,1,0:T(8,128)S(1)}, f32[8,64,256]{2,1,0:T(8,128)}, u32[]{:S(2)}) copy-start(f32[8,64,256]{2,1,0:T(8,128)} %estimate.13) | copy-start | bytes 1572868
  0.6 1.1 %copy-start.1 = (f32[1,8,64,256]{3,2,1,0:T(8,128)S(1)}, f32[1,8,64,256]{3,2,1,0:T(8,128)}, u32[]{:S(2)}) copy-start(f32[1,8,64,256]{3,2,1,0:T(8,128)} %refs_12_.1) | copy-start | bytes 1572868
  1.7 0.7 %copy-start.4 = (f32[1,3,15]{2,0,1:T(1,128)S(1)}, f32[1,3,15]{2,0,1:T(1,128)}, u32[]{:S(2)}) copy-start(f32[1,3,15]{2,0,1:T(1,128)} %param.8) | copy-start | bytes 544
  2.5 11.3 %collective-permute-start = (f32[344,256]{1,0:T(8,128)S(1)}, f32[344,256]{1,0:T(8,128)S(1)}, u32[]{:S(2)}, u32[]{:S(2)}) collective-permute-start(f32[344,256]{1,0:T(8,128)S(1)} %view_out.1), channel_id=1, source_target_pairs={{0,1},{1,0},{2,3},{3,2},{4,5},{5,4},{6,7},{7,6},{8,9},{9,8},{10,11... | collective-permute-start | bytes 1056776 | tf_op jit(solution)/shard_map/ppermute | solution.py:634
  5.6 8.8 %collective-permute-start.1 = (f32[7,48,256]{2,1,0:T(8,128)S(1)}, f32[7,48,256]{2,1,0:T(8,128)S(1)}, u32[]{:S(2)}, u32[]{:S(2)}) collective-permute-start(f32[7,48,256]{2,1,0:T(8,128)S(1)} %get-tuple-element.35), channel_id=1, source_target_pairs={{4,8},{12,16},{20,24},{8,4},{16,12},{24,20},{5,9},{13,17},{21,25},... | collective-permute-start | bytes 1032200 | tf_op jit(solution)/shard_map/ppermute | solution.py:636
  6.3 2.9 %copy-start.6 = (s32[1,16,1]{1,2,0:T(1,128)S(1)}, s32[1,16,1]{1,2,0:T(1,128)}, u32[]{:S(2)}) copy-start(s32[1,16,1]{1,2,0:T(1,128)} %param.10) | copy-start | bytes 196
  6.3 2.9 %copy-start.7 = (s32[1,16]{1,0:T(1,128)S(1)}, s32[1,16]{1,0:T(1,128)}, u32[]{:S(2)}) copy-start(s32[1,16]{1,0:T(1,128)} %index_row.1) | copy-start | bytes 196
  6.3 8.1 %collective-permute-start.2 = (f32[7,48,256]{2,1,0:T(8,128)S(1)}, f32[7,48,256]{2,1,0:T(8,128)S(1)}, u32[]{:S(2)}, u32[]{:S(2)}) collective-permute-start(f32[7,48,256]{2,1,0:T(8,128)S(1)} %get-tuple-element.36), channel_id=1, source_target_pairs={{0,4},{4,0},{8,12},{12,8},{16,20},{20,16},{24,28},{28,24},{1,5},{5... | collective-permute-start | bytes 1032200 | tf_op jit(solution)/shard_map/ppermute | solution.py:637
  9.2 0.7 %copy-start.5 = (f32[1,3,15]{2,0,1:T(1,128)S(1)}, f32[1,3,15]{2,0,1:T(1,128)}, u32[]{:S(2)}) copy-start(f32[1,3,15]{2,0,1:T(1,128)} %param.8) | copy-start | bytes 544
  10.5 3.9 %copy-start.2 = (f32[1,8,64,256]{3,2,1,0:T(8,128)S(1)}, f32[1,8,64,256]{3,2,1,0:T(8,128)}, u32[]{:S(2)}) copy-start(f32[1,8,64,256]{3,2,1,0:T(8,128)} %refs_12_.1) | copy-start | bytes 1572868
  16.2 13.6 %copy-start.3 = (s32[8,64,256]{2,1,0:T(8,128)S(1)}, s32[8,64,256]{2,1,0:T(8,128)}, u32[]{:S(2)}) copy-start(s32[8,64,256]{2,1,0:T(8,128)} %labels.3) | copy-start | bytes 1572868
  16.2 11.0 %collective-permute-start.3 = (f32[7,16,256]{2,1,0:T(8,128)S(1)}, f32[7,16,256]{2,1,0:T(8,128)S(1)}, u32[]{:S(2)}, u32[]{:S(2)}) collective-permute-start(f32[7,16,256]{2,1,0:T(8,128)S(1)} %get-tuple-element.40), channel_id=1, source_target_pairs={{4,8},{12,16},{20,24},{8,4},{16,12},{24,20},{5,9},{13,17},{21,25},... | collective-permute-start | bytes 344072 | tf_op jit(solution)/shard_map/ppermute | solution.py:643
  17.0 10.2 %collective-permute-start.4 = (f32[7,16,256]{2,1,0:T(8,128)S(1)}, f32[7,16,256]{2,1,0:T(8,128)S(1)}, u32[]{:S(2)}, u32[]{:S(2)}) collective-permute-start(f32[7,16,256]{2,1,0:T(8,128)S(1)} %get-tuple-element.41), channel_id=1, source_target_pairs={{0,4},{4,0},{8,12},{12,8},{16,20},{20,16},{24,28},{28,24},{1,5},{5... | collective-permute-start | bytes 344072 | tf_op jit(solution)/shard_map/ppermute | solution.py:643
  20.8 10.1 %collective-permute-start.6 = (f32[7,16,256]{2,1,0:T(8,128)S(1)}, f32[7,16,256]{2,1,0:T(8,128)S(1)}, u32[]{:S(2)}, u32[]{:S(2)}) collective-permute-start(f32[7,16,256]{2,1,0:T(8,128)S(1)} %get-tuple-element.43), channel_id=1, source_target_pairs={{4,8},{12,16},{20,24},{8,4},{16,12},{24,20},{5,9},{13,17},{21,25},... | collective-permute-start | bytes 344072 | tf_op jit(solution)/shard_map/ppermute | solution.py:643
  21.5 9.5 %collective-permute-start.7 = (f32[7,16,256]{2,1,0:T(8,128)S(1)}, f32[7,16,256]{2,1,0:T(8,128)S(1)}, u32[]{:S(2)}, u32[]{:S(2)}) collective-permute-start(f32[7,16,256]{2,1,0:T(8,128)S(1)} %get-tuple-element.44), channel_id=1, source_target_pairs={{0,4},{4,0},{8,12},{12,8},{16,20},{20,16},{24,28},{28,24},{1,5},{5... | collective-permute-start | bytes 344072 | tf_op jit(solution)/shard_map/ppermute | solution.py:643
  27.3 10.6 %collective-permute-start.5 = (f32[8,16,256]{2,1,0:T(8,128)S(1)}, f32[8,16,256]{2,1,0:T(8,128)S(1)}, u32[]{:S(2)}, u32[]{:S(2)}) collective-permute-start(f32[8,16,256]{2,1,0:T(8,128)S(1)} %add_rims.2.mine.correction), channel_id=1, source_target_pairs={{0,3},{1,2},{2,1},{3,0},{4,7},{5,6},{6,5},{7,4},{8,11},{9,10},{10,... | collective-permute-start | bytes 393224 | tf_op jit(solution)/shard_map/ppermute | solution.py:649
  31.0 12.1 %collective-permute-start.8 = (f32[8,16,256]{2,1,0:T(8,128)S(1)}, f32[8,16,256]{2,1,0:T(8,128)S(1)}, u32[]{:S(2)}, u32[]{:S(2)}) collective-permute-start(f32[8,16,256]{2,1,0:T(8,128)S(1)} %add_rims.3.correction.mine), channel_id=1, source_target_pairs={{0,3},{1,2},{2,1},{3,0},{4,7},{5,6},{6,5},{7,4},{8,11},{9,10},{10,... | collective-permute-start | bytes 393224 | tf_op jit(solution)/shard_map/ppermute | solution.py:649
  34.2 8.6 %all-to-all-start = ((f32[8,8,128]{2,1,0:T(8,128)}), f32[8,8,128]{2,1,0:T(8,128)S(1)}, u32[]{:S(2)}, u32[]{:S(2)}) async-start(f32[8,8,128]{2,1,0:T(8,128)} %bitcast.2), calls=%async_computation | async-start | bytes 65536 | tf_op jit(solution)/shard_map/all_to_all | solution.py:652
  37.9 12.0 %collective-permute-start.9 = (f32[144,256]{1,0:T(8,128)S(1)}, f32[144,256]{1,0:T(8,128)S(1)}, u32[]{:S(2)}, u32[]{:S(2)}) collective-permute-start(f32[144,256]{1,0:T(8,128)S(1)} %update.2.source.refs_0_), channel_id=1, source_target_pairs={{0,1},{1,0},{2,3},{3,2},{4,5},{5,4},{6,7},{7,6},{8,9},{9,8},{10,11... | collective-permute-start | bytes 442376 | tf_op jit(solution)/shard_map/ppermute | solution.py:662
  43.1 6.8 %collective-permute-start.10 = (f32[136,256]{1,0:T(8,128)S(1)}, f32[136,256]{1,0:T(8,128)S(1)}, u32[]{:S(2)}, u32[]{:S(2)}) collective-permute-start(f32[136,256]{1,0:T(8,128)S(1)} %update.3.refs_1_), channel_id=1, source_target_pairs={{0,1},{1,0},{2,3},{3,2},{4,5},{5,4},{6,7},{7,6},{8,9},{9,8},{10,11... | collective-permute-start | bytes 417800 | tf_op jit(solution)/shard_map/ppermute | solution.py:662
  43.8 6.0 %collective-permute-start.12 = (f32[16,128]{1,0:T(8,128)S(1)}, f32[16,128]{1,0:T(8,128)S(1)}, u32[]{:S(2)}, u32[]{:S(2)}) collective-permute-start(f32[16,128]{1,0:T(8,128)S(1)} %segment_table.1.rest_0_.refs_2_), channel_id=1, source_target_pairs={{0,3},{1,2},{2,1},{3,0},{4,7},{5,6},{6,5},{7,4},{8,11},{9,10},{10,... | collective-permute-start | bytes 24584 | tf_op jit(solution)/shard_map/ppermute | solution.py:655
  45.4 4.5 %collective-permute-start.11 = (f32[16,128]{1,0:T(8,128)S(1)}, f32[16,128]{1,0:T(8,128)S(1)}, u32[]{:S(2)}, u32[]{:S(2)}) collective-permute-start(f32[16,128]{1,0:T(8,128)S(1)} %segment_table.1.rest_0_.refs_2_), channel_id=1, source_target_pairs={{0,2},{1,3},{2,0},{3,1},{4,6},{5,7},{6,4},{7,5},{8,10},{9,11},{10,... | collective-permute-start | bytes 24584 | tf_op jit(solution)/shard_map/ppermute | solution.py:655

commit v8 on v7

--- a/solution.py
+++ b/solution.py
@@ -12,7 +12,7 @@
 NUC_DEV = 128
 LANES = 128
 PARTS = 2
-TAIL = 24
+TAIL = 8
 IDS = 24
 F32 = jnp.float32
 BF16 = jnp.bfloat16
@@ -338,27 +338,28 @@
     return jnp.concatenate([table[:8], table[8:]], axis=1)
 
 
-def update_kernel(views, part, tabled, estimate, mine, other, *rest):
-    planes, size, across = mine.shape
+def update_kernel(views, keep, part, low, tabled, estimate, mine, other, *rest):
+    planes, whole, across = mine.shape
+    result = rest[-1]
+    size = low[1] - low[0]
     half = half_of(lax.axis_index("view"))
-    start = pl.multiple_of(size * (PARTS * half + part), 8)
-    result = rest[-1]
+    start = pl.multiple_of(keep * half + whole * part + low[0], 8)
     for plane in range(planes):
         held = estimate[plane, pl.ds(start, size)]
         at = slice(plane * size, (plane + 1) * size)
-        result[at] = held * (mine[plane] + other[plane]) * (1.0 / views)
-    rows = result.shape[0] - planes * size
-    result[planes * size :] = jnp.zeros((rows, across), F32)
+        rows = slice(low[0], low[1])
+        result[at] = held * (mine[plane, rows] + other[plane, rows]) * (1.0 / views)
+    result[planes * size :] = jnp.zeros((result.shape[0] - planes * size, across), F32)
     if tabled:
         table = rest[0][...]
         result[planes * size :, : 2 * LANES] = jnp.concatenate([table[:8], table[8:]], axis=1)
 
 
-def update(views, part, estimate, mine, other, table, after):
-    planes, size, across = mine.shape
-    return pl.pallas_call(
-        functools.partial(update_kernel, views, part, len(table) > 0),
-        out_shape=jax.ShapeDtypeStruct((planes * size + 8 * (PARTS - part), across), F32),
+def update(views, keep, part, low, spare, estimate, mine, other, table, after):
+    planes, _, across = mine.shape
+    return pl.pallas_call(
+        functools.partial(update_kernel, views, keep, part, low, len(table) > 0),
+        out_shape=jax.ShapeDtypeStruct((planes * (low[1] - low[0]) + spare, across), F32),
         in_specs=[VMEM] * (3 + len(table)) + [ANY] * len(after),
         out_specs=VMEM,
         compiler_params=pltpu.CompilerParams(vmem_limit_bytes=LIMIT),
@@ -401,6 +402,25 @@
     )(label_owner.reshape(1, slots), label_index)
 
 
+def merge_rows(blocks):
+    rows = lax.broadcasted_iota(jnp.int32, blocks[0].shape, 0)
+    step = 4
+    while step:
+        low = (rows & step) == 0
+        half = len(blocks) // 2
+        merged = []
+        for one, two in zip(blocks[:half], blocks[half:]):
+            kept = jnp.where(low, one, two)
+            turned = jnp.where(low, two, one)
+            moved = pltpu.roll(turned, step, 0)
+            if step < 4:
+                moved = jnp.where(low, pltpu.roll(turned, 8 - step, 0), moved)
+            merged.append(kept + moved)
+        blocks = merged
+        step //= 2
+    return blocks[0]
+
+
 def moments_kernel(views, depth_total, part, estimate, labels, picked, base, correction, *refs):
     begun, (sent, held, sums, table) = refs[:-4], refs[-4:]
     planes, size, across = correction.shape
@@ -420,6 +440,7 @@
     base_row = lax.broadcasted_iota(jnp.int32, (8, across), 0)
 
     def one_group(number, carry):
+        held_parts = []
         for pair in range(0, group, 2):
             slot = [number * group + pair, number * group + pair + 1]
             parts = [[None] * 6 for _ in slot]
@@ -435,17 +456,15 @@
                             once[at] = once[at] + flat[at]
                             twice[at] = twice[at] + once[at]
                 for at in range(2):
-                    square_sum = 2.0 * twice[at] - once[at]
-                    line = first * flat[at]
-                    deep = (line + once[at]) * (1.0 / depth_total)
-                    deeper = (first * (line + 2.0 * once[at]) + square_sum) * (1.0 / depth_total**2)
                     scaled = flat[at] * high
-                    terms = (flat[at], scaled, scaled * high, deep, deep * high, deeper)
+                    terms = (flat[at], scaled, scaled * high, once[at], once[at] * high, twice[at])
                     parts[at] = [new if old is None else old + new for old, new in zip(parts[at], terms)]
-            for at in range(2):
+            held_parts += parts
+            if len(held_parts) == 8:
                 for kind in range(6):
-                    row = kind * group + pair + at
-                    sums[row : row + 1, :] = jnp.sum(parts[at][kind], axis=0, keepdims=True)
+                    row = kind * group + pair + 2 - 8
+                    sums[row : row + 8, :] = merge_rows([parts[kind] for parts in held_parts])
+                held_parts = []
         whole = sums[...]
         upper, rest = split(whole)
         rest = whole - upper.astype(F32)
@@ -455,9 +474,16 @@
         )
         count = 6 * group
         lines = lines[:count] + lines[count : 2 * count] + lines[2 * count :]
-        total = lines[:group]
-        for kind in range(1, 6):
-            total += pltpu.roll(lines[kind * group : (kind + 1) * group], 4 * kind, 1)
+        flat, high_flat, square_flat, once, high_once, twice = [
+            lines[kind * group : (kind + 1) * group] for kind in range(6)
+        ]
+        deep = (first * flat + once) * (1.0 / depth_total)
+        deep_high = (first * high_flat + high_once) * (1.0 / depth_total)
+        deeper = first * (first * flat + 2.0 * once) + (2.0 * twice - once)
+        deeper = deeper * (1.0 / depth_total**2)
+        total = flat
+        for kind, sums_of in enumerate((high_flat, square_flat, deep, deep_high, deeper), 1):
+            total += pltpu.roll(sums_of, 4 * kind, 1)
         rows = pl.ds(pl.multiple_of(number * group, group), group)
         target = table if part == PARTS - 1 else sent
         target[rows, :] = total + begun[0][rows, :] if begun else total
@@ -490,7 +516,7 @@
     )(estimate, labels, *places, correction, *begun)
 
 
-def segments_kernel(across, rows, table):
+def segments_kernel(across, rows, after, table):
     values = rows[...]
     ids = values[:, IDS : IDS + 1].astype(jnp.int32)
     spots = lax.broadcasted_iota(jnp.int32, (values.shape[0], NUC_DEV), 1)
@@ -514,25 +540,30 @@
     )
 
 
-def segment_table(across, rows):
+def segment_table(across, rows, after):
     return pl.pallas_call(
         functools.partial(segments_kernel, across),
         out_shape=jax.ShapeDtypeStruct((16, NUC_DEV), F32),
-        in_specs=[VMEM],
+        in_specs=[VMEM, ANY],
         out_specs=VMEM,
         compiler_params=pltpu.CompilerParams(vmem_limit_bytes=LIMIT),
         name="segment_table",
-    )(rows)
-
-
-def stores(source, whole, half, part, size, sems):
-    start = pl.multiple_of(size * (PARTS * half + part), 8)
-    copies = [
-        pltpu.make_async_copy(
-            source.at[pl.ds(plane * size, size)], whole.at[plane, pl.ds(start, size)], sems.at[plane]
-        )
-        for plane in range(whole.shape[0])
-    ]
+    )(rows, after)
+
+
+def stores(pieces, sources, whole, half, sems):
+    keep = whole.shape[1] // 2
+    copies = []
+    for number, ((first, size), source) in enumerate(zip(pieces, sources)):
+        start = pl.multiple_of(keep * half + first, 8)
+        for plane in range(whole.shape[0]):
+            copies.append(
+                pltpu.make_async_copy(
+                    source.at[pl.ds(plane * size, size)],
+                    whole.at[plane, pl.ds(start, size)],
+                    sems.at[number, plane],
+                )
+            )
     for copy in copies:
         copy.start()
     return copies
@@ -553,38 +584,32 @@
     )(source)
 
 
-def begin_kernel(size, *refs):
-    whole, sems = refs[-2:]
-    half = half_of(lax.axis_index("view"))
-    copies = []
-    for part in range(PARTS):
-        copies += stores(refs[part], whole, half, part, size, sems.at[part])
-    for copy in copies:
+def begin_kernel(pieces, *refs):
+    sources, (whole, sems) = refs[:-2], refs[-2:]
+    for copy in stores(pieces, sources, whole, half_of(lax.axis_index("view")), sems):
         copy.wait()
 
 
-def begin_result(size, shape, mine):
-    return pl.pallas_call(
-        functools.partial(begin_kernel, size),
+def begin_result(pieces, shape, mine):
+    return pl.pallas_call(
+        functools.partial(begin_kernel, pieces),
         out_shape=jax.ShapeDtypeStruct(shape, F32),
-        in_specs=[VMEM] * PARTS,
+        in_specs=[VMEM] * len(mine),
         out_specs=ANY,
-        scratch_shapes=[pltpu.SemaphoreType.DMA((PARTS, shape[0]))],
+        scratch_shapes=[pltpu.SemaphoreType.DMA((len(pieces), shape[0]))],
         compiler_params=pltpu.CompilerParams(vmem_limit_bytes=LIMIT),
         name="begin_result",
     )(*mine)
 
 
-def finish_kernel(scale, size, begun, *refs):
-    others, (first, third, fourth, whole, moments, held, sems, sem) = refs[:PARTS], refs[PARTS:]
-    planes = whole.shape[0]
-    half = half_of(lax.axis_index("view"))
-    copies = []
-    for part in range(PARTS):
-        copies += stores(others[part], whole, 1 - half, part, size, sems.at[part])
-    rows = others[-1][planes * size :]
-    second = jnp.concatenate([rows[:, :LANES], rows[:, LANES : 2 * LANES]], axis=0)
-    table = (first[...] + second) + (third[...] + fourth[...])
+def finish_kernel(scale, pieces, begun, *refs):
+    others, tables = refs[: len(pieces)], refs[len(pieces) : -5]
+    whole, moments, held, sems, sem = refs[-5:]
+    copies = stores(pieces, others, whole, 1 - half_of(lax.axis_index("view")), sems)
+    rows = others[-1][whole.shape[0] * pieces[-1][1] :]
+    table = jnp.concatenate([rows[:, :LANES], rows[:, LANES : 2 * LANES]], axis=0)
+    for other in tables:
+        table += other[...]
     lines = lax.broadcasted_iota(jnp.int32, table.shape, 0)
     result = jnp.where(lines == 0, table * scale, table / jnp.maximum(table[0:1], 1.0))
     held[...] = result[:MOM]
@@ -595,19 +620,19 @@
     last.wait()
 
 
-def finish(scale, size, begun, others, tables):
-    return pl.pallas_call(
-        functools.partial(finish_kernel, scale, size),
+def finish(scale, pieces, begun, others, tables):
+    return pl.pallas_call(
+        functools.partial(finish_kernel, scale, pieces),
         out_shape=(
             jax.ShapeDtypeStruct(begun.shape, F32),
             jax.ShapeDtypeStruct((MOM, NUC_DEV), F32),
         ),
-        in_specs=[ANY] + [VMEM] * (PARTS + 3),
+        in_specs=[ANY] + [VMEM] * (len(others) + len(tables)),
         out_specs=(ANY, ANY),
         input_output_aliases={0: 0},
         scratch_shapes=[
             pltpu.VMEM((MOM, NUC_DEV), F32),
-            pltpu.SemaphoreType.DMA((PARTS, begun.shape[0])),
+            pltpu.SemaphoreType.DMA((len(pieces), begun.shape[0])),
             pltpu.SemaphoreType.DMA,
         ],
         compiler_params=pltpu.CompilerParams(vmem_limit_bytes=LIMIT),
@@ -650,20 +675,24 @@
         sums = [moment_rows(views, tiles, part, estimate, mine[part], labels, places, sums)]
     sent = sums[0]
     got = lax.all_to_all(sent, "tile", split_axis=0, concat_axis=0, tiled=True)
-    table = segment_table(across, got)
-    tables = [table] + [
-        lax.ppermute(table, "view", [(i, i ^ step) for i in range(views)]) for step in (2, 3)
+    size = keep // PARTS
+    cuts = [(part, (0, size), 8 * (PARTS + 1 - part)) for part in range(PARTS - 1)]
+    cuts += [(PARTS - 1, (0, size // 2), 16), (PARTS - 1, (size // 2, size), 8)]
+    pieces = [(part * size + low, high - low) for part, (low, high), _ in cuts]
+    new_mine, new_other, token, table = [], [], [sent], []
+    for number, (part, low, spare) in enumerate(cuts):
+        if number == len(cuts) - 1:
+            table = [segment_table(across, got, token[0])]
+        piece = update(views, keep, part, low, spare, estimate, mine[part], other[part], table, token)
+        new_mine.append(piece)
+        new_other.append(lax.ppermute(piece, "view", partner))
+        token = [token_of(piece)]
+    tables = table + [
+        lax.ppermute(table[0], "view", [(i, i ^ step) for i in range(views)]) for step in (2, 3)
     ]
-    size = keep // PARTS
-    new_mine, new_other, token = [], [], []
-    for part in range(PARTS):
-        last = [table] if part == PARTS - 1 else []
-        new_mine.append(update(views, part, estimate, mine[part], other[part], last, token))
-        new_other.append(lax.ppermute(new_mine[part], "view", partner))
-        token = [token_of(new_mine[part])]
     scale = label_index.shape[1] / (planes * height * across)
-    begun = begin_result(size, estimate.shape, new_mine)
-    return finish(scale, size, begun, new_other, tables)
+    begun = begin_result(pieces, estimate.shape, new_mine)
+    return finish(scale, pieces, begun, new_other, tables)
 
 
 def solution(mesh):

time: 51.1 us -> 57.3 us (1.12)
  waiting for transfers between devices: 7.96 us -> 15.5 us
  local copies, waits for them, and re-layouts: 2.27 us -> 1.07 us
    ppermute x1, waiting for transfers between devices: 3.29 us -> 7.44 us  [on_device(): swapped = lax.ppermute(packed, 'view', partner)]
    ppermute x4 -> x5, starting transfers between devices: 6.16 us -> 9.89 us  [the longest x3 6.43 us: on_device(): new_other.append(lax.ppermute(piece, 'view', partner))]
    ppermute x4, starting transfers between devices: 10.7 us -> 7.28 us  [on_device(): lax.ppermute(send, 'tile', pairs)]
    all_to_all x1, waiting for transfers between devices: 2.2 us -> 4.6 us  [on_device(): got = lax.all_to_all(sent, 'tile', split_axis=0, concat_axis=0, tiled=True)]
    ppermute x1, starting transfers between devices: 2.9 us -> 4.34 us  [on_device(): near = lax.ppermute(to_near, 'tile', near_pairs)]
    ppermute x1, starting transfers between devices: 3.09 us -> 1.64 us  [on_device(): swapped = lax.ppermute(packed, 'view', partner)]
    unnamed x16 -> x14, local copies, waits for them, and re-layouts: 2.27 us -> 1.07 us
    ppermute x2, waiting for transfers between devices: 0.01 us -> 0.93 us  [on_device(): other.append(lax.ppermute(mine[part], 'view', across_pairs))]
  transfers between devices with their start and end apart: 14 -> 15, of which waited for: 4 -> 5; matrix products, arithmetic and copies ran while one was open for 0% -> 0% of each run, Pallas kernels for 11% -> 10%
where the time goes in v8:
time: 57.3 us; the launch traced here: 57 us
  starting transfers between devices  31.3 us (55%)
  waiting for transfers between devices  15.5 us (27%)
  Pallas kernels  8.35 us (15%)
  local copies, waits for them, and re-layouts  1.07 us (2%)
  between operations  0.85 us (1%)
    ppermute x1, waiting for transfers between devices, on_device(): swapped = lax.ppermute(packed, 'view', partner)  7.44 us
    ppermute x4, starting transfers between devices, on_device(): lax.ppermute(send, 'tile', pairs)  7.28 us
    ppermute x3, starting transfers between devices, on_device(): new_other.append(lax.ppermute(piece, 'view', partner))  6.43 us
    all_to_all x1, waiting for transfers between devices, on_device(): got = lax.all_to_all(sent, 'tile', split_axis=0, concat_axis=0, tiled=True)  4.6 us
    ppermute x1, starting transfers between devices, on_device(): near = lax.ppermute(to_near, 'tile', near_pairs)  4.34 us
    ppermute x2, starting transfers between devices, on_device(): other.append(lax.ppermute(mine[part], 'view', across_pairs))  3.95 us
    ppermute x2, starting transfers between devices, on_device(): lax.ppermute(table[0], 'view', [(i, i ^ step) for i in range(views)])  3.47 us
    all_to_all x1, starting transfers between devices, on_device(): got = lax.all_to_all(sent, 'tile', split_axis=0, concat_axis=0, tiled=True)  3.34 us
  transfers between devices with their start and end apart: 15, of which 5 were waited for; matrix products, arithmetic and copies ran while one was open for 0% of the time, Pallas kernels for 10%

profile of v8, /device:TPU:0, one launch (start us, length us, event | category | flops | bytes accessed | tf_op | source)
XLA Modules:
  0.0 57.0 jit_solution(15377410985322194087)
XLA Ops:
  0.6 0.0 copy-start
  0.6 1.0 %copy-done = f32[8,64,256]{2,1,0:T(8,128)S(1)} copy-done((f32[8,64,256]{2,1,0:T(8,128)S(1)}, f32[8,64,256]{2,1,0:T(8,128)}, u32[]{:S(2)}) %copy-start) | copy-done | bytes 524312
  1.7 0.8 %collective-permute-start.1 = (f32[7,48,256]{2,1,0:T(8,128)S(1)}, f32[7,48,256]{2,1,0:T(8,128)S(1)}, u32[]{:S(2)}, u32[]{:S(2)}) collective-permute-start(f32[7,48,256]{2,1,0:T(8,128)S(1)} %get-tuple-element.35), channel_id=1, source_target_pairs={{4,8},{12,16},{20,24},{8,4},{16,12},{24,20},{5,9},{13,17},{21,25},... | collective-permute-start | bytes 1032200 | tf_op jit(solution)/shard_map/ppermute | solution.py:661
  2.6 4.3 %collective-permute-start.2 = (f32[7,48,256]{2,1,0:T(8,128)S(1)}, f32[7,48,256]{2,1,0:T(8,128)S(1)}, u32[]{:S(2)}, u32[]{:S(2)}) collective-permute-start(f32[7,48,256]{2,1,0:T(8,128)S(1)} %get-tuple-element.36), channel_id=1, source_target_pairs={{0,4},{4,0},{8,12},{12,8},{16,20},{20,16},{24,28},{28,24},{1,5},{5... | collective-permute-start | bytes 1032200 | tf_op jit(solution)/shard_map/ppermute | solution.py:662
  7.0 1.6 %collective-permute-start = (f32[328,256]{1,0:T(8,128)S(1)}, f32[328,256]{1,0:T(8,128)S(1)}, u32[]{:S(2)}, u32[]{:S(2)}) collective-permute-start(f32[328,256]{1,0:T(8,128)S(1)} %view_out.1), channel_id=1, source_target_pairs={{0,1},{1,0},{2,3},{3,2},{4,5},{5,4},{6,7},{7,6},{8,9},{9,8},{10,11... | collective-permute-start | bytes 1007624 | tf_op jit(solution)/shard_map/ppermute | solution.py:659
  8.6 0.2 slot_places.1
  8.8 0.6 %prepare.2 = (bf16[2,2,256,256]{3,2,1,0:T(8,128)(2,1)S(1)}, bf16[40,144]{1,0:T(8,128)(2,1)S(1)}, bf16[32,144]{1,0:T(8,128)(2,1)S(1)}, f32[8,48,256]{2,1,0:T(8,128)S(1)}, f32[16,128]{1,0:T(8,128)S(1)}) custom-call(f32[3,1,15]{2,1,0:T(1,128)S(1)} %bitcast.6, f32[8,64,256]{2,1,0:T(8,128)S(1)} %copy-done.1, f32[64,128]{1,0:T(8,128)S(1)} %get-tuple-element.24.after.base), custom_call_target="tpu_custom_call" | custom-call | tf_op jit(solution)/shard_map/prepare/pallas_call | solution.py:154
  9.4 7.4 %collective-permute-done.source.refs_13_ = f32[328,256]{1,0:T(8,128)S(1)} collective-permute-done((f32[328,256]{1,0:T(8,128)S(1)}, f32[328,256]{1,0:T(8,128)S(1)}, u32[]{:S(2)}, u32[]{:S(2)}) %collective-permute-start) | collective-permute-done | bytes 335904 | tf_op jit(solution)/shard_map/ppermute | solution.py:659
  16.9 0.6 %prepare.3 = (bf16[2,2,256,256]{3,2,1,0:T(8,128)(2,1)S(1)}, bf16[40,144]{1,0:T(8,128)(2,1)S(1)}, bf16[32,144]{1,0:T(8,128)(2,1)S(1)}, f32[8,48,256]{2,1,0:T(8,128)S(1)}, f32[16,128]{1,0:T(8,128)S(1)}) custom-call(f32[328,256]{1,0:T(8,128)S(1)} %collective-permute-done.source.refs_13_, f32[8,64,256]{2,1,0:T(8,128)S(1)} %copy-done.1, f32[3,1,15]{2,1,0:T(1,128)S(1)} %bitcast.7), custom_call_target="tpu_custom_call" | custom-call | tf_op jit(solution)/shard_map/prepare/pallas_call | solution.py:154
  17.5 1.8 %ratio_fields.1 = (f32[8,32,256]{2,1,0:T(8,128)S(1)}, f32[8,32,256]{2,1,0:T(8,128)S(1)}, f32[7,16,256]{2,1,0:T(8,128)S(1)}, f32[7,16,256]{2,1,0:T(8,128)S(1)}, f...) custom-call(bf16[2,2,256,256]{3,2,1,0:T(8,128)(2,1)S(1)} %get-tuple-element.27.refs_0_, ...), custom_call_target="tpu_custom_call" | custom-call | tf_op jit(solution)/shard_map/ratio_fields/pallas_call | solution.py:269
  19.3 0.8 %collective-permute-start.3 = (f32[7,16,256]{2,1,0:T(8,128)S(1)}, f32[7,16,256]{2,1,0:T(8,128)S(1)}, u32[]{:S(2)}, u32[]{:S(2)}) collective-permute-start(f32[7,16,256]{2,1,0:T(8,128)S(1)} %get-tuple-element.40), channel_id=1, source_target_pairs={{4,8},{12,16},{20,24},{8,4},{16,12},{24,20},{5,9},{13,17},{21,25},... | collective-permute-start | bytes 344072 | tf_op jit(solution)/shard_map/ppermute | solution.py:668
  20.1 2.9 %collective-permute-start.4 = (f32[7,16,256]{2,1,0:T(8,128)S(1)}, f32[7,16,256]{2,1,0:T(8,128)S(1)}, u32[]{:S(2)}, u32[]{:S(2)}) collective-permute-start(f32[7,16,256]{2,1,0:T(8,128)S(1)} %get-tuple-element.41), channel_id=1, source_target_pairs={{0,4},{4,0},{8,12},{12,8},{16,20},{20,16},{24,28},{28,24},{1,5},{5... | collective-permute-start | bytes 344072 | tf_op jit(solution)/shard_map/ppermute | solution.py:668
  23.0 0.7 %collective-permute-start.6 = (f32[7,16,256]{2,1,0:T(8,128)S(1)}, f32[7,16,256]{2,1,0:T(8,128)S(1)}, u32[]{:S(2)}, u32[]{:S(2)}) collective-permute-start(f32[7,16,256]{2,1,0:T(8,128)S(1)} %get-tuple-element.44), channel_id=1, source_target_pairs={{4,8},{12,16},{20,24},{8,4},{16,12},{24,20},{5,9},{13,17},{21,25},... | collective-permute-start | bytes 344072 | tf_op jit(solution)/shard_map/ppermute | solution.py:668
  23.7 2.9 %collective-permute-start.7 = (f32[7,16,256]{2,1,0:T(8,128)S(1)}, f32[7,16,256]{2,1,0:T(8,128)S(1)}, u32[]{:S(2)}, u32[]{:S(2)}) collective-permute-start(f32[7,16,256]{2,1,0:T(8,128)S(1)} %get-tuple-element.45), channel_id=1, source_target_pairs={{0,4},{4,0},{8,12},{12,8},{16,20},{20,16},{24,28},{28,24},{1,5},{5... | collective-permute-start | bytes 344072 | tf_op jit(solution)/shard_map/ppermute | solution.py:668
  26.6 0.3 own_planes.1
  27.0 3.7 %collective-permute-start.5 = (f32[8,16,256]{2,1,0:T(8,128)S(1)}, f32[8,16,256]{2,1,0:T(8,128)S(1)}, u32[]{:S(2)}, u32[]{:S(2)}) collective-permute-start(f32[8,16,256]{2,1,0:T(8,128)S(1)} %add_rims.2.correction.mine), channel_id=1, source_target_pairs={{0,3},{1,2},{2,1},{3,0},{4,7},{5,6},{6,5},{7,4},{8,11},{9,10},{10,... | collective-permute-start | bytes 393224 | tf_op jit(solution)/shard_map/ppermute | solution.py:674
  30.6 0.8 %moment_rows.2.rest_0_.refs_0_ = f32[16,128]{1,0:T(8,128)S(1)} custom-call(f32[8,64,256]{2,1,0:T(8,128)S(1)} %copy-done.1, s32[8,64,256]{2,1,0:T(8,128)S(1)} %copy-done.3, f32[64,16]{1,0:T(8,128)S(1)} %get-tuple-element.42.picked, f32[64,128]{1,0:T(8,128)S(1)} %get-tuple-element.24.after.base, f32[8,16,256]{2,1,0:T(8,128)S(1)} %add_rims.2.correction.mine), custom_call_target="tpu_custom_call" | custom-call | tf_op jit(solution)/shard_map/moment_rows/pallas_call | solution.py:504
  31.6 0.3 collective-permute-start.8
  31.8 1.7 %moment_rows.3.rest_0_ = f32[64,128]{1,0:T(8,128)} custom-call(f32[8,64,256]{2,1,0:T(8,128)S(1)} %copy-done.1, s32[8,64,256]{2,1,0:T(8,128)S(1)} %copy-done.3, f32[64,16]{1,0:T(8,128)S(1)} %get-tuple-element.42.picked, f32[64,128]{1,0:T(8,128)S(1)} %get-tuple-element.24.after.base, f32[8,16,256]{2,1,0:T(8,128)S(1)} %add_rims.3.correction.mine, ...), custom_call_target="tpu_custom_call" | custom-call | tf_op jit(solution)/shard_map/moment_rows/pallas_call | solution.py:504
  33.5 0.9 %collective-permute-done.5.other = f32[8,16,256]{2,1,0:T(8,128)S(1)} collective-permute-done((f32[8,16,256]{2,1,0:T(8,128)S(1)}, f32[8,16,256]{2,1,0:T(8,128)S(1)}, u32[]{:S(2)}, u32[]{:S(2)}) %collective-permute-start.5) | collective-permute-done | bytes 131104 | tf_op jit(solution)/shard_map/ppermute | solution.py:674
  34.5 6.2 %collective-permute-start.9 = (f32[152,256]{1,0:T(8,128)S(1)}, f32[152,256]{1,0:T(8,128)S(1)}, u32[]{:S(2)}, u32[]{:S(2)}) collective-permute-start(f32[152,256]{1,0:T(8,128)S(1)} %update.3.source.refs_0_), channel_id=1, source_target_pairs={{0,1},{1,0},{2,3},{3,2},{4,5},{5,4},{6,7},{7,6},{8,9},{9,8},{10,11... | collective-permute-start | bytes 466952 | tf_op jit(solution)/shard_map/ppermute | solution.py:688
  40.7 3.3 %all-to-all-start = ((f32[8,8,128]{2,1,0:T(8,128)}), f32[8,8,128]{2,1,0:T(8,128)S(1)}, u32[]{:S(2)}, u32[]{:S(2)}) async-start(f32[8,8,128]{2,1,0:T(8,128)} %bitcast.2), calls=%async_computation | async-start | bytes 65536 | tf_op jit(solution)/shard_map/all_to_all | solution.py:677
  44.1 0.1 collective-permute-start.10
  44.2 4.6 %all-to-all-done = f32[8,8,128]{2,1,0:T(8,128)S(1)} async-done(((f32[8,8,128]{2,1,0:T(8,128)}), f32[8,8,128]{2,1,0:T(8,128)S(1)}, u32[]{:S(2)}, u32[]{:S(2)}) %all-to-all-start) | async-done | bytes 32800 | tf_op jit(solution)/shard_map/all_to_all | solution.py:677
  48.8 0.3 segment_table.1.rest_0_.refs_3_
  49.1 0.1 collective-permute-start.11
  49.2 2.3 %collective-permute-start.13 = (f32[16,128]{1,0:T(8,128)S(1)}, f32[16,128]{1,0:T(8,128)S(1)}, u32[]{:S(2)}, u32[]{:S(2)}) collective-permute-start(f32[16,128]{1,0:T(8,128)S(1)} %segment_table.1.rest_0_.refs_3_), channel_id=1, source_target_pairs={{0,3},{1,2},{2,1},{3,0},{4,7},{5,6},{6,5},{7,4},{8,11},{9,10},{10,... | collective-permute-start | bytes 24584 | tf_op jit(solution)/shard_map/ppermute | solution.py:691
  51.5 1.1 %collective-permute-start.12 = (f32[16,128]{1,0:T(8,128)S(1)}, f32[16,128]{1,0:T(8,128)S(1)}, u32[]{:S(2)}, u32[]{:S(2)}) collective-permute-start(f32[16,128]{1,0:T(8,128)S(1)} %segment_table.1.rest_0_.refs_3_), channel_id=1, source_target_pairs={{0,2},{1,3},{2,0},{3,1},{4,6},{5,7},{6,4},{7,5},{8,10},{9,11},{10,... | collective-permute-start | bytes 24584 | tf_op jit(solution)/shard_map/ppermute | solution.py:691
  52.7 0.9 %begin_result.1.begun = f32[8,64,256]{2,1,0:T(8,128)} custom-call(f32[152,256]{1,0:T(8,128)S(1)} %update.3.source.refs_0_, f32[80,256]{1,0:T(8,128)S(1)} %update.4.source.refs_1_, f32[72,256]{1,0:T(8,128)S(1)} %update.5.refs_2_), custom_call_target="tpu_custom_call" | custom-call | tf_op jit(solution)/shard_map/begin_result/pallas_call | solution.py:594
  53.6 1.1 %collective-permute-done.13.refs_5_ = f32[16,128]{1,0:T(8,128)S(1)} collective-permute-done((f32[16,128]{1,0:T(8,128)S(1)}, f32[16,128]{1,0:T(8,128)S(1)}, u32[]{:S(2)}, u32[]{:S(2)}) %collective-permute-start.13) | collective-permute-done | bytes 8224 | tf_op jit(solution)/shard_map/ppermute | solution.py:691
  54.7 1.4 %collective-permute-done.12.refs_4_ = f32[16,128]{1,0:T(8,128)S(1)} collective-permute-done((f32[16,128]{1,0:T(8,128)S(1)}, f32[16,128]{1,0:T(8,128)S(1)}, u32[]{:S(2)}, u32[]{:S(2)}) %collective-permute-start.12) | collective-permute-done | bytes 8224 | tf_op jit(solution)/shard_map/ppermute | solution.py:691
  56.1 0.9 %finish.1 = (f32[8,64,256]{2,1,0:T(8,128)}, f32[10,128]{1,0:T(8,128)}) custom-call(f32[8,64,256]{2,1,0:T(8,128)} %begin_result.1.begun, f32[152,256]{1,0:T(8,128)S(1)} %collective-permute-done.9.refs_0_, f32[80,256]{1,0:T(8,128)S(1)} %collective-permute-done.10.refs_1_, ...), custom_call_target="tpu_custom_call", output_to_operand_aliasing={{0}: (0, {})} | custom-call | tf_op jit(solution)/shard_map/finish/pallas_call | solution.py:624
  (31 shorter events, 0.3 us)
Async XLA Ops:
  0.6 1.0 %copy-start = (f32[8,64,256]{2,1,0:T(8,128)S(1)}, f32[8,64,256]{2,1,0:T(8,128)}, u32[]{:S(2)}) copy-start(f32[8,64,256]{2,1,0:T(8,128)} %estimate.15) | copy-start | bytes 1572868
  1.7 5.2 %copy-start.2 = (f32[1,8,64,256]{3,2,1,0:T(8,128)S(1)}, f32[1,8,64,256]{3,2,1,0:T(8,128)}, u32[]{:S(2)}) copy-start(f32[1,8,64,256]{3,2,1,0:T(8,128)} %refs_12_.1) | copy-start | bytes 1572868
  1.7 5.2 %copy-start.4 = (f32[1,3,15]{2,0,1:T(1,128)S(1)}, f32[1,3,15]{2,0,1:T(1,128)}, u32[]{:S(2)}) copy-start(f32[1,3,15]{2,0,1:T(1,128)} %param.8) | copy-start | bytes 544
  1.7 7.1 %copy-start.1 = (f32[8,64,256]{2,1,0:T(8,128)S(1)}, f32[8,64,256]{2,1,0:T(8,128)}, u32[]{:S(2)}) copy-start(f32[8,64,256]{2,1,0:T(8,128)} %estimate.15) | copy-start | bytes 1572868
  1.7 15.7 %collective-permute-start.1 = (f32[7,48,256]{2,1,0:T(8,128)S(1)}, f32[7,48,256]{2,1,0:T(8,128)S(1)}, u32[]{:S(2)}, u32[]{:S(2)}) collective-permute-start(f32[7,48,256]{2,1,0:T(8,128)S(1)} %get-tuple-element.35), channel_id=1, source_target_pairs={{4,8},{12,16},{20,24},{8,4},{16,12},{24,20},{5,9},{13,17},{21,25},... | collective-permute-start | bytes 1032200 | tf_op jit(solution)/shard_map/ppermute | solution.py:661
  2.6 14.9 %collective-permute-start.2 = (f32[7,48,256]{2,1,0:T(8,128)S(1)}, f32[7,48,256]{2,1,0:T(8,128)S(1)}, u32[]{:S(2)}, u32[]{:S(2)}) collective-permute-start(f32[7,48,256]{2,1,0:T(8,128)S(1)} %get-tuple-element.36), channel_id=1, source_target_pairs={{0,4},{4,0},{8,12},{12,8},{16,20},{20,16},{24,28},{28,24},{1,5},{5... | collective-permute-start | bytes 1032200 | tf_op jit(solution)/shard_map/ppermute | solution.py:662
  6.9 1.7 %copy-start.5 = (s32[1,16,1]{1,2,0:T(1,128)S(1)}, s32[1,16,1]{1,2,0:T(1,128)}, u32[]{:S(2)}) copy-start(s32[1,16,1]{1,2,0:T(1,128)} %param.10) | copy-start | bytes 196
  7.0 1.7 %copy-start.6 = (s32[1,16]{1,0:T(1,128)S(1)}, s32[1,16]{1,0:T(1,128)}, u32[]{:S(2)}) copy-start(s32[1,16]{1,0:T(1,128)} %index_row.1) | copy-start | bytes 196
  7.0 9.9 %collective-permute-start = (f32[328,256]{1,0:T(8,128)S(1)}, f32[328,256]{1,0:T(8,128)S(1)}, u32[]{:S(2)}, u32[]{:S(2)}) collective-permute-start(f32[328,256]{1,0:T(8,128)S(1)} %view_out.1), channel_id=1, source_target_pairs={{0,1},{1,0},{2,3},{3,2},{4,5},{5,4},{6,7},{7,6},{8,9},{9,8},{10,11... | collective-permute-start | bytes 1007624 | tf_op jit(solution)/shard_map/ppermute | solution.py:659
  19.3 11.3 %copy-start.3 = (s32[8,64,256]{2,1,0:T(8,128)S(1)}, s32[8,64,256]{2,1,0:T(8,128)}, u32[]{:S(2)}) copy-start(s32[8,64,256]{2,1,0:T(8,128)} %labels.3) | copy-start | bytes 1572868
  19.3 7.6 %collective-permute-start.3 = (f32[7,16,256]{2,1,0:T(8,128)S(1)}, f32[7,16,256]{2,1,0:T(8,128)S(1)}, u32[]{:S(2)}, u32[]{:S(2)}) collective-permute-start(f32[7,16,256]{2,1,0:T(8,128)S(1)} %get-tuple-element.40), channel_id=1, source_target_pairs={{4,8},{12,16},{20,24},{8,4},{16,12},{24,20},{5,9},{13,17},{21,25},... | collective-permute-start | bytes 344072 | tf_op jit(solution)/shard_map/ppermute | solution.py:668
  20.1 6.8 %collective-permute-start.4 = (f32[7,16,256]{2,1,0:T(8,128)S(1)}, f32[7,16,256]{2,1,0:T(8,128)S(1)}, u32[]{:S(2)}, u32[]{:S(2)}) collective-permute-start(f32[7,16,256]{2,1,0:T(8,128)S(1)} %get-tuple-element.41), channel_id=1, source_target_pairs={{0,4},{4,0},{8,12},{12,8},{16,20},{20,16},{24,28},{28,24},{1,5},{5... | collective-permute-start | bytes 344072 | tf_op jit(solution)/shard_map/ppermute | solution.py:668
  23.0 8.5 %collective-permute-start.6 = (f32[7,16,256]{2,1,0:T(8,128)S(1)}, f32[7,16,256]{2,1,0:T(8,128)S(1)}, u32[]{:S(2)}, u32[]{:S(2)}) collective-permute-start(f32[7,16,256]{2,1,0:T(8,128)S(1)} %get-tuple-element.44), channel_id=1, source_target_pairs={{4,8},{12,16},{20,24},{8,4},{16,12},{24,20},{5,9},{13,17},{21,25},... | collective-permute-start | bytes 344072 | tf_op jit(solution)/shard_map/ppermute | solution.py:668
  23.7 7.8 %collective-permute-start.7 = (f32[7,16,256]{2,1,0:T(8,128)S(1)}, f32[7,16,256]{2,1,0:T(8,128)S(1)}, u32[]{:S(2)}, u32[]{:S(2)}) collective-permute-start(f32[7,16,256]{2,1,0:T(8,128)S(1)} %get-tuple-element.45), channel_id=1, source_target_pairs={{0,4},{4,0},{8,12},{12,8},{16,20},{20,16},{24,28},{28,24},{1,5},{5... | collective-permute-start | bytes 344072 | tf_op jit(solution)/shard_map/ppermute | solution.py:668
  27.0 7.5 %collective-permute-start.5 = (f32[8,16,256]{2,1,0:T(8,128)S(1)}, f32[8,16,256]{2,1,0:T(8,128)S(1)}, u32[]{:S(2)}, u32[]{:S(2)}) collective-permute-start(f32[8,16,256]{2,1,0:T(8,128)S(1)} %add_rims.2.correction.mine), channel_id=1, source_target_pairs={{0,3},{1,2},{2,1},{3,0},{4,7},{5,6},{6,5},{7,4},{8,11},{9,10},{10,... | collective-permute-start | bytes 393224 | tf_op jit(solution)/shard_map/ppermute | solution.py:674
  31.6 12.5 %collective-permute-start.8 = (f32[8,16,256]{2,1,0:T(8,128)S(1)}, f32[8,16,256]{2,1,0:T(8,128)S(1)}, u32[]{:S(2)}, u32[]{:S(2)}) collective-permute-start(f32[8,16,256]{2,1,0:T(8,128)S(1)} %add_rims.3.correction.mine), channel_id=1, source_target_pairs={{0,3},{1,2},{2,1},{3,0},{4,7},{5,6},{6,5},{7,4},{8,11},{9,10},{10,... | collective-permute-start | bytes 393224 | tf_op jit(solution)/shard_map/ppermute | solution.py:674
  34.5 21.6 %collective-permute-start.9 = (f32[152,256]{1,0:T(8,128)S(1)}, f32[152,256]{1,0:T(8,128)S(1)}, u32[]{:S(2)}, u32[]{:S(2)}) collective-permute-start(f32[152,256]{1,0:T(8,128)S(1)} %update.3.source.refs_0_), channel_id=1, source_target_pairs={{0,1},{1,0},{2,3},{3,2},{4,5},{5,4},{6,7},{7,6},{8,9},{9,8},{10,11... | collective-permute-start | bytes 466952 | tf_op jit(solution)/shard_map/ppermute | solution.py:688
  40.7 8.1 %all-to-all-start = ((f32[8,8,128]{2,1,0:T(8,128)}), f32[8,8,128]{2,1,0:T(8,128)S(1)}, u32[]{:S(2)}, u32[]{:S(2)}) async-start(f32[8,8,128]{2,1,0:T(8,128)} %bitcast.2), calls=%async_computation | async-start | bytes 65536 | tf_op jit(solution)/shard_map/all_to_all | solution.py:677
  44.1 12.0 %collective-permute-start.10 = (f32[80,256]{1,0:T(8,128)S(1)}, f32[80,256]{1,0:T(8,128)S(1)}, u32[]{:S(2)}, u32[]{:S(2)}) collective-permute-start(f32[80,256]{1,0:T(8,128)S(1)} %update.4.source.refs_1_), channel_id=1, source_target_pairs={{0,1},{1,0},{2,3},{3,2},{4,5},{5,4},{6,7},{7,6},{8,9},{9,8},{10,11... | collective-permute-start | bytes 245768 | tf_op jit(solution)/shard_map/ppermute | solution.py:688
  49.1 7.0 %collective-permute-start.11 = (f32[72,256]{1,0:T(8,128)S(1)}, f32[72,256]{1,0:T(8,128)S(1)}, u32[]{:S(2)}, u32[]{:S(2)}) collective-permute-start(f32[72,256]{1,0:T(8,128)S(1)} %update.5.refs_2_), channel_id=1, source_target_pairs={{0,1},{1,0},{2,3},{3,2},{4,5},{5,4},{6,7},{7,6},{8,9},{9,8},{10,11... | collective-permute-start | bytes 221192 | tf_op jit(solution)/shard_map/ppermute | solution.py:688
  49.2 5.5 %collective-permute-start.13 = (f32[16,128]{1,0:T(8,128)S(1)}, f32[16,128]{1,0:T(8,128)S(1)}, u32[]{:S(2)}, u32[]{:S(2)}) collective-permute-start(f32[16,128]{1,0:T(8,128)S(1)} %segment_table.1.rest_0_.refs_3_), channel_id=1, source_target_pairs={{0,3},{1,2},{2,1},{3,0},{4,7},{5,6},{6,5},{7,4},{8,11},{9,10},{10,... | collective-permute-start | bytes 24584 | tf_op jit(solution)/shard_map/ppermute | solution.py:691
  51.5 4.5 %collective-permute-start.12 = (f32[16,128]{1,0:T(8,128)S(1)}, f32[16,128]{1,0:T(8,128)S(1)}, u32[]{:S(2)}, u32[]{:S(2)}) collective-permute-start(f32[16,128]{1,0:T(8,128)S(1)} %segment_table.1.rest_0_.refs_3_), channel_id=1, source_target_pairs={{0,2},{1,3},{2,0},{3,1},{4,6},{5,7},{6,4},{7,5},{8,10},{9,11},{10,... | collective-permute-start | bytes 24584 | tf_op jit(solution)/shard_map/ppermute | solution.py:691

commit v9 on v8

--- a/solution.py
+++ b/solution.py
@@ -338,39 +338,37 @@
     return jnp.concatenate([table[:8], table[8:]], axis=1)
 
 
-def update_kernel(views, keep, part, low, tabled, estimate, mine, other, *rest):
-    planes, whole, across = mine.shape
+def update_kernel(views, part, estimate, mine, other, *rest):
+    planes, size, across = mine.shape
     result = rest[-1]
-    size = low[1] - low[0]
     half = half_of(lax.axis_index("view"))
-    start = pl.multiple_of(keep * half + whole * part + low[0], 8)
+    start = pl.multiple_of(size * (PARTS * half + part), 8)
     for plane in range(planes):
         held = estimate[plane, pl.ds(start, size)]
         at = slice(plane * size, (plane + 1) * size)
-        rows = slice(low[0], low[1])
-        result[at] = held * (mine[plane, rows] + other[plane, rows]) * (1.0 / views)
-    result[planes * size :] = jnp.zeros((result.shape[0] - planes * size, across), F32)
-    if tabled:
-        table = rest[0][...]
-        result[planes * size :, : 2 * LANES] = jnp.concatenate([table[:8], table[8:]], axis=1)
-
-
-def update(views, keep, part, low, spare, estimate, mine, other, table, after):
-    planes, _, across = mine.shape
-    return pl.pallas_call(
-        functools.partial(update_kernel, views, keep, part, low, len(table) > 0),
-        out_shape=jax.ShapeDtypeStruct((planes * (low[1] - low[0]) + spare, across), F32),
-        in_specs=[VMEM] * (3 + len(table)) + [ANY] * len(after),
+        result[at] = held * (mine[plane] + other[plane]) * (1.0 / views)
+    spare = result.shape[0] - planes * size
+    if spare:
+        result[planes * size :] = jnp.zeros((spare, across), F32)
+
+
+def update(views, part, estimate, mine, other, after):
+    planes, size, across = mine.shape
+    spare = 8 * (PARTS - 1 - part)
+    return pl.pallas_call(
+        functools.partial(update_kernel, views, part),
+        out_shape=jax.ShapeDtypeStruct((planes * size + spare, across), F32),
+        in_specs=[VMEM] * 3 + [ANY] * len(after),
         out_specs=VMEM,
         compiler_params=pltpu.CompilerParams(vmem_limit_bytes=LIMIT),
         name="update",
-    )(estimate, mine, other, *table, *after)
-
-
-def slots_kernel(owner_row, index_row, picked, base):
+    )(estimate, mine, other, *after)
+
+
+def slots_kernel(views, owner_row, index_row, picked, base):
     count = picked.shape[0]
     slots = owner_row.shape[1]
-    tiles = count // ROWS
+    tiles = count // (views * ROWS)
     owner = owner_row[...]
     member = (lax.broadcasted_iota(jnp.int32, (tiles, slots), 0) == owner).astype(F32)
     upto = (
@@ -379,21 +377,23 @@
     ).astype(F32)
     running = jnp.dot(member, upto, preferred_element_type=F32)
     rank = jnp.sum(member * running, axis=0, keepdims=True).astype(jnp.int32) - 1
-    place = owner * ROWS + rank
-    chosen = lax.broadcasted_iota(jnp.int32, (count, slots), 0) == place
+    line = lax.broadcasted_iota(jnp.int32, (count, slots), 0)
+    spot = (line // (views * ROWS)) * ROWS + line % ROWS
+    chosen = spot == owner * ROWS + rank
     picked[...] = chosen.astype(F32)
     ids = jnp.sum(jnp.where(chosen, index_row[...].astype(F32), 0.0), axis=1, keepdims=True)
     lanes = lax.broadcasted_iota(jnp.int32, (count, LANES), 1)
     base[...] = jnp.where(lanes == IDS, ids, 0.0)
 
 
-def slot_places(tiles, label_owner, label_index):
+def slot_places(tiles, views, label_owner, label_index):
     slots = label_index.shape[1]
-    return pl.pallas_call(
-        slots_kernel,
+    count = tiles * views * ROWS
+    return pl.pallas_call(
+        functools.partial(slots_kernel, views),
         out_shape=(
-            jax.ShapeDtypeStruct((tiles * ROWS, slots), F32),
-            jax.ShapeDtypeStruct((tiles * ROWS, LANES), F32),
+            jax.ShapeDtypeStruct((count, slots), F32),
+            jax.ShapeDtypeStruct((count, LANES), F32),
         ),
         in_specs=[VMEM, VMEM],
         out_specs=(VMEM, VMEM),
@@ -500,7 +500,7 @@
 def moment_rows(views, tiles, part, estimate, correction, labels, places, begun):
     planes, size, across = correction.shape
     slots = places[0].shape[1]
-    count = tiles * ROWS if part == PARTS - 1 else slots
+    count = places[0].shape[0] if part == PARTS - 1 else slots
     return pl.pallas_call(
         functools.partial(moments_kernel, views, tiles * planes, part),
         out_shape=jax.ShapeDtypeStruct((count, LANES), F32),
@@ -516,7 +516,7 @@
     )(estimate, labels, *places, correction, *begun)
 
 
-def segments_kernel(across, rows, after, table):
+def segments_kernel(across, scale, rows, moments):
     values = rows[...]
     ids = values[:, IDS : IDS + 1].astype(jnp.int32)
     spots = lax.broadcasted_iota(jnp.int32, (values.shape[0], NUC_DEV), 1)
@@ -529,26 +529,27 @@
     flat = lambda sums: sums[0:1]
     line = lambda sums: (sums[1:2] + 0.5 * sums[0:1]) * (1.0 / across)
     square = lambda sums: (sums[2:3] + sums[3:4] + sums[1:2] + 0.25 * sums[0:1]) * (1.0 / across**2)
-    table[...] = jnp.concatenate(
+    whole = flat(mass)
+    sums = jnp.concatenate(
         [
-            flat(mass), flat(deep), flat(high), line(mass),
+            flat(deep), flat(high), line(mass),
             flat(deeper), flat(higher), square(mass),
             flat(deep_high), line(deep), line(high),
-            jnp.zeros((table.shape[0] - MOM, NUC_DEV), F32),
         ],
         axis=0,
     )
-
-
-def segment_table(across, rows, after):
-    return pl.pallas_call(
-        functools.partial(segments_kernel, across),
-        out_shape=jax.ShapeDtypeStruct((16, NUC_DEV), F32),
-        in_specs=[VMEM, ANY],
+    moments[...] = jnp.concatenate([whole * scale, sums / jnp.maximum(whole, 1.0)], axis=0)
+
+
+def nucleus_table(across, scale, rows):
+    return pl.pallas_call(
+        functools.partial(segments_kernel, across, scale),
+        out_shape=jax.ShapeDtypeStruct((MOM, NUC_DEV), F32),
+        in_specs=[VMEM],
         out_specs=VMEM,
         compiler_params=pltpu.CompilerParams(vmem_limit_bytes=LIMIT),
-        name="segment_table",
-    )(rows, after)
+        name="nucleus_table",
+    )(rows)
 
 
 def stores(pieces, sources, whole, half, sems):
@@ -602,42 +603,23 @@
     )(*mine)
 
 
-def finish_kernel(scale, pieces, begun, *refs):
-    others, tables = refs[: len(pieces)], refs[len(pieces) : -5]
-    whole, moments, held, sems, sem = refs[-5:]
-    copies = stores(pieces, others, whole, 1 - half_of(lax.axis_index("view")), sems)
-    rows = others[-1][whole.shape[0] * pieces[-1][1] :]
-    table = jnp.concatenate([rows[:, :LANES], rows[:, LANES : 2 * LANES]], axis=0)
-    for other in tables:
-        table += other[...]
-    lines = lax.broadcasted_iota(jnp.int32, table.shape, 0)
-    result = jnp.where(lines == 0, table * scale, table / jnp.maximum(table[0:1], 1.0))
-    held[...] = result[:MOM]
-    last = pltpu.make_async_copy(held, moments, sem)
-    last.start()
-    for copy in copies:
+def finish_kernel(pieces, begun, *refs):
+    others, (whole, sems) = refs[:-2], refs[-2:]
+    for copy in stores(pieces, others, whole, 1 - half_of(lax.axis_index("view")), sems):
         copy.wait()
-    last.wait()
-
-
-def finish(scale, pieces, begun, others, tables):
-    return pl.pallas_call(
-        functools.partial(finish_kernel, scale, pieces),
-        out_shape=(
-            jax.ShapeDtypeStruct(begun.shape, F32),
-            jax.ShapeDtypeStruct((MOM, NUC_DEV), F32),
-        ),
-        in_specs=[ANY] + [VMEM] * (len(others) + len(tables)),
-        out_specs=(ANY, ANY),
+
+
+def finish(pieces, begun, others):
+    return pl.pallas_call(
+        functools.partial(finish_kernel, pieces),
+        out_shape=jax.ShapeDtypeStruct(begun.shape, F32),
+        in_specs=[ANY] + [VMEM] * len(others),
+        out_specs=ANY,
         input_output_aliases={0: 0},
-        scratch_shapes=[
-            pltpu.VMEM((MOM, NUC_DEV), F32),
-            pltpu.SemaphoreType.DMA((len(pieces), begun.shape[0])),
-            pltpu.SemaphoreType.DMA,
-        ],
+        scratch_shapes=[pltpu.SemaphoreType.DMA((len(pieces), begun.shape[0]))],
         compiler_params=pltpu.CompilerParams(vmem_limit_bytes=LIMIT),
         name="finish",
-    )(begun, *others, *tables)
+    )(begun, *others)
 
 
 def on_device(estimate, measured, kernels, labels, label_owner, label_index):
@@ -660,7 +642,7 @@
     to_far, to_near = rims_out(estimate, radius, rows)
     far = lax.ppermute(to_far, "tile", far_pairs)
     near = lax.ppermute(to_near, "tile", near_pairs)
-    places = slot_places(tiles, label_owner, label_index)
+    places = slot_places(tiles, views, label_owner, label_index)
     own = prepare(False, taps, lines, estimate, places[1], rows, seen, keep)
     others = prepare(True, taps, swapped, estimate, lines, rows, seen, keep)
     field_own, field_other, *sends = ratio_fields(own, others, far, near, measured, swapped)
@@ -674,25 +656,18 @@
         other.append(lax.ppermute(mine[part], "view", across_pairs))
         sums = [moment_rows(views, tiles, part, estimate, mine[part], labels, places, sums)]
     sent = sums[0]
-    got = lax.all_to_all(sent, "tile", split_axis=0, concat_axis=0, tiled=True)
+    got = lax.all_to_all(sent, ("tile", "view"), split_axis=0, concat_axis=0, tiled=True)
     size = keep // PARTS
-    cuts = [(part, (0, size), 8 * (PARTS + 1 - part)) for part in range(PARTS - 1)]
-    cuts += [(PARTS - 1, (0, size // 2), 16), (PARTS - 1, (size // 2, size), 8)]
-    pieces = [(part * size + low, high - low) for part, (low, high), _ in cuts]
-    new_mine, new_other, token, table = [], [], [sent], []
-    for number, (part, low, spare) in enumerate(cuts):
-        if number == len(cuts) - 1:
-            table = [segment_table(across, got, token[0])]
-        piece = update(views, keep, part, low, spare, estimate, mine[part], other[part], table, token)
-        new_mine.append(piece)
-        new_other.append(lax.ppermute(piece, "view", partner))
-        token = [token_of(piece)]
-    tables = table + [
-        lax.ppermute(table[0], "view", [(i, i ^ step) for i in range(views)]) for step in (2, 3)
-    ]
+    pieces = [(part * size, size) for part in range(PARTS)]
+    new_mine, new_other, token = [], [], [sent]
+    for part in range(PARTS):
+        new_mine.append(update(views, part, estimate, mine[part], other[part], token))
+        new_other.append(lax.ppermute(new_mine[part], "view", partner))
+        token = [token_of(new_mine[part])]
     scale = label_index.shape[1] / (planes * height * across)
+    moments = nucleus_table(across, scale, got)
     begun = begin_result(pieces, estimate.shape, new_mine)
-    return finish(scale, pieces, begun, new_other, tables)
+    return finish(pieces, begun, new_other), moments
 
 
 def solution(mesh):

time: 57.3 us -> 50.3 us (0.88)
  waiting for transfers between devices: 15.5 us -> 11.2 us
  starting transfers between devices: 31.3 us -> 27.9 us
  Pallas kernels: 8.35 us -> 8.97 us
    ppermute x5 -> x2, starting transfers between devices: 9.89 us -> 5.11 us  [on_device(): new_other.append(lax.ppermute(new_mine[part], 'view', partner))]
    all_to_all x1, waiting for transfers between devices: 4.6 us -> 2.6 us  [on_device(): lax.all_to_all(sent, ('tile', 'view'), split_axis=0, concat_axis=0, tiled...]
    all_to_all x1, starting transfers between devices: 3.34 us -> 4.78 us  [on_device(): lax.all_to_all(sent, ('tile', 'view'), split_axis=0, concat_axis=0, tiled...]
    ppermute x5 -> x2, waiting for transfers between devices: 2.51 us -> 1.2 us  [on_device(): new_other.append(lax.ppermute(new_mine[part], 'view', partner))]
    ppermute x2, waiting for transfers between devices: 0.93 us -> 0.01 us  [on_device(): other.append(lax.ppermute(mine[part], 'view', across_pairs))]
    pallas_call x6 -> x5, Pallas kernels: 1.5 us -> 2.06 us  [the longest x1 0.95 us: nucleus_table(): pl.pallas_call(functools.partial(segments_kernel, across, scale), out_sha...]
  transfers between devices with their start and end apart: 15 -> 12, of which waited for: 5 -> 3; matrix products, arithmetic and copies ran while one was open for 0% -> 0% of each run, Pallas kernels for 10% -> 13%
where the time goes in v9:
time: 50.3 us; the launch traced here: 50 us
  starting transfers between devices  27.9 us (55%)
  waiting for transfers between devices  11.2 us (22%)
  Pallas kernels  8.97 us (18%)
  local copies, waits for them, and re-layouts  1.07 us (2%)
  between operations  0.84 us (2%)
    ppermute x1, waiting for transfers between devices, on_device(): swapped = lax.ppermute(packed, 'view', partner)  7.41 us
    ppermute x4, starting transfers between devices, on_device(): lax.ppermute(send, 'tile', pairs)  7.28 us
    ppermute x2, starting transfers between devices, on_device(): new_other.append(lax.ppermute(new_mine[part], 'view', partner))  5.11 us
    all_to_all x1, starting transfers between devices, on_device(): lax.all_to_all(sent, ('tile', 'view'), split_axis=0, concat_axis=0, tiled...  4.78 us
    ppermute x1, starting transfers between devices, on_device(): near = lax.ppermute(to_near, 'tile', near_pairs)  4.34 us
    ppermute x2, starting transfers between devices, on_device(): other.append(lax.ppermute(mine[part], 'view', across_pairs))  3.95 us
    pallas_call x2, Pallas kernels, moment_rows(): pl.pallas_call(functools.partial(moments_kernel, views, tiles * planes, p...  2.66 us
    all_to_all x1, waiting for transfers between devices, on_device(): lax.all_to_all(sent, ('tile', 'view'), split_axis=0, concat_axis=0, tiled...  2.6 us
  transfers between devices with their start and end apart: 12, of which 3 were waited for; matrix products, arithmetic and copies ran while one was open for 0% of the time, Pallas kernels for 13%

profile of v9, /device:TPU:0, one launch (start us, length us, event | category | flops | bytes accessed | tf_op | source)
XLA Modules:
  0.0 50.0 jit_solution(7292802667971212866)
XLA Ops:
  0.6 0.0 copy-start
  0.6 1.0 %copy-done = f32[8,64,256]{2,1,0:T(8,128)S(1)} copy-done((f32[8,64,256]{2,1,0:T(8,128)S(1)}, f32[8,64,256]{2,1,0:T(8,128)}, u32[]{:S(2)}) %copy-start) | copy-done | bytes 524312
  1.7 0.0 copy-start.1
  1.7 0.8 %collective-permute-start.1 = (f32[7,48,256]{2,1,0:T(8,128)S(1)}, f32[7,48,256]{2,1,0:T(8,128)S(1)}, u32[]{:S(2)}, u32[]{:S(2)}) collective-permute-start(f32[7,48,256]{2,1,0:T(8,128)S(1)} %get-tuple-element.35), channel_id=1, source_target_pairs={{4,8},{12,16},{20,24},{8,4},{16,12},{24,20},{5,9},{13,17},{21,25},... | collective-permute-start | bytes 1032200 | tf_op jit(solution)/shard_map/ppermute | solution.py:643
  2.6 4.3 %collective-permute-start.2 = (f32[7,48,256]{2,1,0:T(8,128)S(1)}, f32[7,48,256]{2,1,0:T(8,128)S(1)}, u32[]{:S(2)}, u32[]{:S(2)}) collective-permute-start(f32[7,48,256]{2,1,0:T(8,128)S(1)} %get-tuple-element.36), channel_id=1, source_target_pairs={{0,4},{4,0},{8,12},{12,8},{16,20},{20,16},{24,28},{28,24},{1,5},{5... | collective-permute-start | bytes 1032200 | tf_op jit(solution)/shard_map/ppermute | solution.py:644
  6.9 0.0 copy-start.5
  7.0 0.0 copy-start.6
  7.0 1.6 %collective-permute-start = (f32[328,256]{1,0:T(8,128)S(1)}, f32[328,256]{1,0:T(8,128)S(1)}, u32[]{:S(2)}, u32[]{:S(2)}) collective-permute-start(f32[328,256]{1,0:T(8,128)S(1)} %view_out.1), channel_id=1, source_target_pairs={{0,1},{1,0},{2,3},{3,2},{4,5},{5,4},{6,7},{7,6},{8,9},{9,8},{10,11... | collective-permute-start | bytes 1007624 | tf_op jit(solution)/shard_map/ppermute | solution.py:641
  8.6 0.2 slot_places.1
  8.9 0.6 %prepare.2 = (bf16[2,2,256,256]{3,2,1,0:T(8,128)(2,1)S(1)}, bf16[40,144]{1,0:T(8,128)(2,1)S(1)}, bf16[32,144]{1,0:T(8,128)(2,1)S(1)}, f32[8,48,256]{2,1,0:T(8,128)S(1)}, f32[16,128]{1,0:T(8,128)S(1)}) custom-call(f32[3,1,15]{2,1,0:T(1,128)S(1)} %bitcast.6, f32[8,64,256]{2,1,0:T(8,128)S(1)} %copy-done.1, f32[256,128]{1,0:T(8,128)S(1)} %get-tuple-element.24.after.base), custom_call_target="tpu_custom_call" | custom-call | tf_op jit(solution)/shard_map/prepare/pallas_call | solution.py:154
  9.5 7.4 %collective-permute-done.source.refs_13_ = f32[328,256]{1,0:T(8,128)S(1)} collective-permute-done((f32[328,256]{1,0:T(8,128)S(1)}, f32[328,256]{1,0:T(8,128)S(1)}, u32[]{:S(2)}, u32[]{:S(2)}) %collective-permute-start) | collective-permute-done | bytes 335904 | tf_op jit(solution)/shard_map/ppermute | solution.py:641
  16.9 0.6 %prepare.3 = (bf16[2,2,256,256]{3,2,1,0:T(8,128)(2,1)S(1)}, bf16[40,144]{1,0:T(8,128)(2,1)S(1)}, bf16[32,144]{1,0:T(8,128)(2,1)S(1)}, f32[8,48,256]{2,1,0:T(8,128)S(1)}, f32[16,128]{1,0:T(8,128)S(1)}) custom-call(f32[328,256]{1,0:T(8,128)S(1)} %collective-permute-done.source.refs_13_, f32[8,64,256]{2,1,0:T(8,128)S(1)} %copy-done.1, f32[3,1,15]{2,1,0:T(1,128)S(1)} %bitcast.7), custom_call_target="tpu_custom_call" | custom-call | tf_op jit(solution)/shard_map/prepare/pallas_call | solution.py:154
  17.5 0.0 collective-permute-done.1.refs_10_
  17.5 1.8 %ratio_fields.1 = (f32[8,32,256]{2,1,0:T(8,128)S(1)}, f32[8,32,256]{2,1,0:T(8,128)S(1)}, f32[7,16,256]{2,1,0:T(8,128)S(1)}, f32[7,16,256]{2,1,0:T(8,128)S(1)}, f...) custom-call(bf16[2,2,256,256]{3,2,1,0:T(8,128)(2,1)S(1)} %get-tuple-element.27.refs_0_, ...), custom_call_target="tpu_custom_call" | custom-call | tf_op jit(solution)/shard_map/ratio_fields/pallas_call | solution.py:269
  19.3 0.0 copy-start.3
  19.3 0.8 %collective-permute-start.3 = (f32[7,16,256]{2,1,0:T(8,128)S(1)}, f32[7,16,256]{2,1,0:T(8,128)S(1)}, u32[]{:S(2)}, u32[]{:S(2)}) collective-permute-start(f32[7,16,256]{2,1,0:T(8,128)S(1)} %get-tuple-element.40), channel_id=1, source_target_pairs={{4,8},{12,16},{20,24},{8,4},{16,12},{24,20},{5,9},{13,17},{21,25},... | collective-permute-start | bytes 344072 | tf_op jit(solution)/shard_map/ppermute | solution.py:650
  20.1 2.9 %collective-permute-start.4 = (f32[7,16,256]{2,1,0:T(8,128)S(1)}, f32[7,16,256]{2,1,0:T(8,128)S(1)}, u32[]{:S(2)}, u32[]{:S(2)}) collective-permute-start(f32[7,16,256]{2,1,0:T(8,128)S(1)} %get-tuple-element.41), channel_id=1, source_target_pairs={{0,4},{4,0},{8,12},{12,8},{16,20},{20,16},{24,28},{28,24},{1,5},{5... | collective-permute-start | bytes 344072 | tf_op jit(solution)/shard_map/ppermute | solution.py:650
  23.0 0.7 %collective-permute-start.6 = (f32[7,16,256]{2,1,0:T(8,128)S(1)}, f32[7,16,256]{2,1,0:T(8,128)S(1)}, u32[]{:S(2)}, u32[]{:S(2)}) collective-permute-start(f32[7,16,256]{2,1,0:T(8,128)S(1)} %get-tuple-element.44), channel_id=1, source_target_pairs={{4,8},{12,16},{20,24},{8,4},{16,12},{24,20},{5,9},{13,17},{21,25},... | collective-permute-start | bytes 344072 | tf_op jit(solution)/shard_map/ppermute | solution.py:650
  23.7 2.9 %collective-permute-start.7 = (f32[7,16,256]{2,1,0:T(8,128)S(1)}, f32[7,16,256]{2,1,0:T(8,128)S(1)}, u32[]{:S(2)}, u32[]{:S(2)}) collective-permute-start(f32[7,16,256]{2,1,0:T(8,128)S(1)} %get-tuple-element.45), channel_id=1, source_target_pairs={{0,4},{4,0},{8,12},{12,8},{16,20},{20,16},{24,28},{28,24},{1,5},{5... | collective-permute-start | bytes 344072 | tf_op jit(solution)/shard_map/ppermute | solution.py:650
  26.6 0.3 own_planes.1
  26.9 3.7 %collective-permute-start.5 = (f32[8,16,256]{2,1,0:T(8,128)S(1)}, f32[8,16,256]{2,1,0:T(8,128)S(1)}, u32[]{:S(2)}, u32[]{:S(2)}) collective-permute-start(f32[8,16,256]{2,1,0:T(8,128)S(1)} %add_rims.2.correction.mine), channel_id=1, source_target_pairs={{0,3},{1,2},{2,1},{3,0},{4,7},{5,6},{6,5},{7,4},{8,11},{9,10},{10,... | collective-permute-start | bytes 393224 | tf_op jit(solution)/shard_map/ppermute | solution.py:656
  30.6 0.8 %moment_rows.2.rest_0_.refs_0_ = f32[16,128]{1,0:T(8,128)S(1)} custom-call(f32[8,64,256]{2,1,0:T(8,128)S(1)} %copy-done.1, s32[8,64,256]{2,1,0:T(8,128)S(1)} %copy-done.3, f32[256,16]{1,0:T(8,128)S(1)} %get-tuple-element.42.picked, f32[256,128]{1,0:T(8,128)S(1)} %get-tuple-element.24.after.base, f32[8,16,256]{2,1,0:T(8,128)S(1)} %add_rims.2.correction.mine), custom_call_target="tpu_custom_call" | custom-call | tf_op jit(solution)/shard_map/moment_rows/pallas_call | solution.py:504
  31.5 0.3 collective-permute-start.8
  31.8 1.8 %moment_rows.3.rest_0_ = f32[256,128]{1,0:T(8,128)} custom-call(f32[8,64,256]{2,1,0:T(8,128)S(1)} %copy-done.1, s32[8,64,256]{2,1,0:T(8,128)S(1)} %copy-done.3, f32[256,16]{1,0:T(8,128)S(1)} %get-tuple-element.42.picked, f32[256,128]{1,0:T(8,128)S(1)} %get-tuple-element.24.after.base, f32[8,16,256]{2,1,0:T(8,128)S(1)} %add_rims.3.correction.mine, ...), custom_call_target="tpu_custom_call" | custom-call | tf_op jit(solution)/shard_map/moment_rows/pallas_call | solution.py:504
  33.6 4.8 %all-to-all-start = ((f32[32,8,128]{2,1,0:T(8,128)}), f32[32,8,128]{2,1,0:T(8,128)S(1)}, u32[]{:S(2)}, u32[]{:S(2)}) async-start(f32[32,8,128]{2,1,0:T(8,128)} %bitcast.2), calls=%async_computation | async-start | bytes 262144 | tf_op jit(solution)/shard_map/all_to_all | solution.py:659
  38.5 2.2 %collective-permute-start.9 = (f32[136,256]{1,0:T(8,128)S(1)}, f32[136,256]{1,0:T(8,128)S(1)}, u32[]{:S(2)}, u32[]{:S(2)}) collective-permute-start(f32[136,256]{1,0:T(8,128)S(1)} %update.2.source.refs_0_), channel_id=1, source_target_pairs={{0,1},{1,0},{2,3},{3,2},{4,5},{5,4},{6,7},{7,6},{8,9},{9,8},{10,11... | collective-permute-start | bytes 417800 | tf_op jit(solution)/shard_map/ppermute | solution.py:665
  40.7 2.9 %collective-permute-start.10 = (f32[128,256]{1,0:T(8,128)S(1)}, f32[128,256]{1,0:T(8,128)S(1)}, u32[]{:S(2)}, u32[]{:S(2)}) collective-permute-start(f32[128,256]{1,0:T(8,128)S(1)} %update.3.refs_1_), channel_id=1, source_target_pairs={{0,1},{1,0},{2,3},{3,2},{4,5},{5,4},{6,7},{7,6},{8,9},{9,8},{10,11... | collective-permute-start | bytes 393224 | tf_op jit(solution)/shard_map/ppermute | solution.py:665
  43.6 0.8 %begin_result.1.begun = f32[8,64,256]{2,1,0:T(8,128)} custom-call(f32[136,256]{1,0:T(8,128)S(1)} %update.2.source.refs_0_, f32[128,256]{1,0:T(8,128)S(1)} %update.3.refs_1_), custom_call_target="tpu_custom_call" | custom-call | tf_op jit(solution)/shard_map/begin_result/pallas_call | solution.py:595
  44.4 2.6 %all-to-all-done = f32[32,8,128]{2,1,0:T(8,128)S(1)} async-done(((f32[32,8,128]{2,1,0:T(8,128)}), f32[32,8,128]{2,1,0:T(8,128)S(1)}, u32[]{:S(2)}, u32[]{:S(2)}) %all-to-all-start) | async-done | bytes 131104 | tf_op jit(solution)/shard_map/all_to_all | solution.py:659
  47.0 1.0 %nucleus_table.1 = f32[10,128]{1,0:T(8,128)} custom-call(f32[256,128]{1,0:T(8,128)S(1)} %bitcast.4), custom_call_target="tpu_custom_call" | custom-call | tf_op jit(solution)/shard_map/nucleus_table/pallas_call | solution.py:545
  48.0 1.2 %collective-permute-done.10.refs_1_ = f32[128,256]{1,0:T(8,128)S(1)} collective-permute-done((f32[128,256]{1,0:T(8,128)S(1)}, f32[128,256]{1,0:T(8,128)S(1)}, u32[]{:S(2)}, u32[]{:S(2)}) %collective-permute-start.10) | collective-permute-done | bytes 131104 | tf_op jit(solution)/shard_map/ppermute | solution.py:665
  49.2 0.8 %finish.1 = f32[8,64,256]{2,1,0:T(8,128)} custom-call(f32[8,64,256]{2,1,0:T(8,128)} %begin_result.1.begun, f32[136,256]{1,0:T(8,128)S(1)} %collective-permute-done.9.refs_0_, f32[128,256]{1,0:T(8,128)S(1)} %collective-permute-done.10.refs_1_), custom_call_target="tpu_custom_call", output_to_operand_aliasing={{}: (0, {})} | custom-call | tf_op jit(solution)/shard_map/finish/pallas_call | solution.py:613
  (23 shorter events, 0.2 us)
Async XLA Ops:
  0.6 1.0 %copy-start = (f32[8,64,256]{2,1,0:T(8,128)S(1)}, f32[8,64,256]{2,1,0:T(8,128)}, u32[]{:S(2)}) copy-start(f32[8,64,256]{2,1,0:T(8,128)} %estimate.13) | copy-start | bytes 1572868
  1.7 5.2 %copy-start.2 = (f32[1,8,64,256]{3,2,1,0:T(8,128)S(1)}, f32[1,8,64,256]{3,2,1,0:T(8,128)}, u32[]{:S(2)}) copy-start(f32[1,8,64,256]{3,2,1,0:T(8,128)} %refs_12_.1) | copy-start | bytes 1572868
  1.7 5.2 %copy-start.4 = (f32[1,3,15]{2,0,1:T(1,128)S(1)}, f32[1,3,15]{2,0,1:T(1,128)}, u32[]{:S(2)}) copy-start(f32[1,3,15]{2,0,1:T(1,128)} %param.8) | copy-start | bytes 544
  1.7 7.1 %copy-start.1 = (f32[8,64,256]{2,1,0:T(8,128)S(1)}, f32[8,64,256]{2,1,0:T(8,128)}, u32[]{:S(2)}) copy-start(f32[8,64,256]{2,1,0:T(8,128)} %estimate.13) | copy-start | bytes 1572868
  1.7 15.7 %collective-permute-start.1 = (f32[7,48,256]{2,1,0:T(8,128)S(1)}, f32[7,48,256]{2,1,0:T(8,128)S(1)}, u32[]{:S(2)}, u32[]{:S(2)}) collective-permute-start(f32[7,48,256]{2,1,0:T(8,128)S(1)} %get-tuple-element.35), channel_id=1, source_target_pairs={{4,8},{12,16},{20,24},{8,4},{16,12},{24,20},{5,9},{13,17},{21,25},... | collective-permute-start | bytes 1032200 | tf_op jit(solution)/shard_map/ppermute | solution.py:643
  2.6 14.9 %collective-permute-start.2 = (f32[7,48,256]{2,1,0:T(8,128)S(1)}, f32[7,48,256]{2,1,0:T(8,128)S(1)}, u32[]{:S(2)}, u32[]{:S(2)}) collective-permute-start(f32[7,48,256]{2,1,0:T(8,128)S(1)} %get-tuple-element.36), channel_id=1, source_target_pairs={{0,4},{4,0},{8,12},{12,8},{16,20},{20,16},{24,28},{28,24},{1,5},{5... | collective-permute-start | bytes 1032200 | tf_op jit(solution)/shard_map/ppermute | solution.py:644
  6.9 1.7 %copy-start.5 = (s32[1,16,1]{1,2,0:T(1,128)S(1)}, s32[1,16,1]{1,2,0:T(1,128)}, u32[]{:S(2)}) copy-start(s32[1,16,1]{1,2,0:T(1,128)} %param.10) | copy-start | bytes 196
  7.0 1.7 %copy-start.6 = (s32[1,16]{1,0:T(1,128)S(1)}, s32[1,16]{1,0:T(1,128)}, u32[]{:S(2)}) copy-start(s32[1,16]{1,0:T(1,128)} %index_row.1) | copy-start | bytes 196
  7.0 9.9 %collective-permute-start = (f32[328,256]{1,0:T(8,128)S(1)}, f32[328,256]{1,0:T(8,128)S(1)}, u32[]{:S(2)}, u32[]{:S(2)}) collective-permute-start(f32[328,256]{1,0:T(8,128)S(1)} %view_out.1), channel_id=1, source_target_pairs={{0,1},{1,0},{2,3},{3,2},{4,5},{5,4},{6,7},{7,6},{8,9},{9,8},{10,11... | collective-permute-start | bytes 1007624 | tf_op jit(solution)/shard_map/ppermute | solution.py:641
  19.3 11.3 %copy-start.3 = (s32[8,64,256]{2,1,0:T(8,128)S(1)}, s32[8,64,256]{2,1,0:T(8,128)}, u32[]{:S(2)}) copy-start(s32[8,64,256]{2,1,0:T(8,128)} %labels.3) | copy-start | bytes 1572868
  19.3 7.6 %collective-permute-start.3 = (f32[7,16,256]{2,1,0:T(8,128)S(1)}, f32[7,16,256]{2,1,0:T(8,128)S(1)}, u32[]{:S(2)}, u32[]{:S(2)}) collective-permute-start(f32[7,16,256]{2,1,0:T(8,128)S(1)} %get-tuple-element.40), channel_id=1, source_target_pairs={{4,8},{12,16},{20,24},{8,4},{16,12},{24,20},{5,9},{13,17},{21,25},... | collective-permute-start | bytes 344072 | tf_op jit(solution)/shard_map/ppermute | solution.py:650
  20.1 6.8 %collective-permute-start.4 = (f32[7,16,256]{2,1,0:T(8,128)S(1)}, f32[7,16,256]{2,1,0:T(8,128)S(1)}, u32[]{:S(2)}, u32[]{:S(2)}) collective-permute-start(f32[7,16,256]{2,1,0:T(8,128)S(1)} %get-tuple-element.41), channel_id=1, source_target_pairs={{0,4},{4,0},{8,12},{12,8},{16,20},{20,16},{24,28},{28,24},{1,5},{5... | collective-permute-start | bytes 344072 | tf_op jit(solution)/shard_map/ppermute | solution.py:650
  23.0 8.5 %collective-permute-start.6 = (f32[7,16,256]{2,1,0:T(8,128)S(1)}, f32[7,16,256]{2,1,0:T(8,128)S(1)}, u32[]{:S(2)}, u32[]{:S(2)}) collective-permute-start(f32[7,16,256]{2,1,0:T(8,128)S(1)} %get-tuple-element.44), channel_id=1, source_target_pairs={{4,8},{12,16},{20,24},{8,4},{16,12},{24,20},{5,9},{13,17},{21,25},... | collective-permute-start | bytes 344072 | tf_op jit(solution)/shard_map/ppermute | solution.py:650
  23.7 7.8 %collective-permute-start.7 = (f32[7,16,256]{2,1,0:T(8,128)S(1)}, f32[7,16,256]{2,1,0:T(8,128)S(1)}, u32[]{:S(2)}, u32[]{:S(2)}) collective-permute-start(f32[7,16,256]{2,1,0:T(8,128)S(1)} %get-tuple-element.45), channel_id=1, source_target_pairs={{0,4},{4,0},{8,12},{12,8},{16,20},{20,16},{24,28},{28,24},{1,5},{5... | collective-permute-start | bytes 344072 | tf_op jit(solution)/shard_map/ppermute | solution.py:650
  26.9 11.5 %collective-permute-start.5 = (f32[8,16,256]{2,1,0:T(8,128)S(1)}, f32[8,16,256]{2,1,0:T(8,128)S(1)}, u32[]{:S(2)}, u32[]{:S(2)}) collective-permute-start(f32[8,16,256]{2,1,0:T(8,128)S(1)} %add_rims.2.correction.mine), channel_id=1, source_target_pairs={{0,3},{1,2},{2,1},{3,0},{4,7},{5,6},{6,5},{7,4},{8,11},{9,10},{10,... | collective-permute-start | bytes 393224 | tf_op jit(solution)/shard_map/ppermute | solution.py:656
  31.5 9.1 %collective-permute-start.8 = (f32[8,16,256]{2,1,0:T(8,128)S(1)}, f32[8,16,256]{2,1,0:T(8,128)S(1)}, u32[]{:S(2)}, u32[]{:S(2)}) collective-permute-start(f32[8,16,256]{2,1,0:T(8,128)S(1)} %add_rims.3.correction.mine), channel_id=1, source_target_pairs={{0,3},{1,2},{2,1},{3,0},{4,7},{5,6},{6,5},{7,4},{8,11},{9,10},{10,... | collective-permute-start | bytes 393224 | tf_op jit(solution)/shard_map/ppermute | solution.py:656
  33.6 13.4 %all-to-all-start = ((f32[32,8,128]{2,1,0:T(8,128)}), f32[32,8,128]{2,1,0:T(8,128)S(1)}, u32[]{:S(2)}, u32[]{:S(2)}) async-start(f32[32,8,128]{2,1,0:T(8,128)} %bitcast.2), calls=%async_computation | async-start | bytes 262144 | tf_op jit(solution)/shard_map/all_to_all | solution.py:659
  38.5 10.7 %collective-permute-start.9 = (f32[136,256]{1,0:T(8,128)S(1)}, f32[136,256]{1,0:T(8,128)S(1)}, u32[]{:S(2)}, u32[]{:S(2)}) collective-permute-start(f32[136,256]{1,0:T(8,128)S(1)} %update.2.source.refs_0_), channel_id=1, source_target_pairs={{0,1},{1,0},{2,3},{3,2},{4,5},{5,4},{6,7},{7,6},{8,9},{9,8},{10,11... | collective-permute-start | bytes 417800 | tf_op jit(solution)/shard_map/ppermute | solution.py:665
  40.7 8.5 %collective-permute-start.10 = (f32[128,256]{1,0:T(8,128)S(1)}, f32[128,256]{1,0:T(8,128)S(1)}, u32[]{:S(2)}, u32[]{:S(2)}) collective-permute-start(f32[128,256]{1,0:T(8,128)S(1)} %update.3.refs_1_), channel_id=1, source_target_pairs={{0,1},{1,0},{2,3},{3,2},{4,5},{5,4},{6,7},{7,6},{8,9},{9,8},{10,11... | collective-permute-start | bytes 393224 | tf_op jit(solution)/shard_map/ppermute | solution.py:665

commit v10 on v9

--- a/solution.py
+++ b/solution.py
@@ -8,7 +8,8 @@
 from jax.sharding import PartitionSpec as P
 
 MOM = 10
-ROWS = 8
+CAP = 5
+WIDTH = 25
 NUC_DEV = 128
 LANES = 128
 PARTS = 2
@@ -366,33 +367,35 @@
 
 
 def slots_kernel(views, owner_row, index_row, picked, base):
-    count = picked.shape[0]
+    count = base.shape[0]
     slots = owner_row.shape[1]
-    tiles = count // (views * ROWS)
     owner = owner_row[...]
-    member = (lax.broadcasted_iota(jnp.int32, (tiles, slots), 0) == owner).astype(F32)
+    member = (lax.broadcasted_iota(jnp.int32, (count // views, slots), 0) == owner).astype(F32)
     upto = (
         lax.broadcasted_iota(jnp.int32, (slots, slots), 0)
         <= lax.broadcasted_iota(jnp.int32, (slots, slots), 1)
     ).astype(F32)
     running = jnp.dot(member, upto, preferred_element_type=F32)
     rank = jnp.sum(member * running, axis=0, keepdims=True).astype(jnp.int32) - 1
-    line = lax.broadcasted_iota(jnp.int32, (count, slots), 0)
-    spot = (line // (views * ROWS)) * ROWS + line % ROWS
-    chosen = spot == owner * ROWS + rank
-    picked[...] = chosen.astype(F32)
-    ids = jnp.sum(jnp.where(chosen, index_row[...].astype(F32), 0.0), axis=1, keepdims=True)
+    named = lax.broadcasted_iota(jnp.int32, (count, slots), 0) // views == owner
+    index = index_row[...].astype(F32)
     lanes = lax.broadcasted_iota(jnp.int32, (count, LANES), 1)
-    base[...] = jnp.where(lanes == IDS, ids, 0.0)
+    result = jnp.zeros((count, LANES), F32)
+    for place in range(CAP):
+        chosen = named & (rank == place)
+        picked[place * count : (place + 1) * count] = chosen.astype(F32)
+        ids = jnp.sum(jnp.where(chosen, index, 0.0), axis=1, keepdims=True)
+        result = jnp.where(lanes == place * WIDTH + IDS, ids, result)
+    base[...] = result
 
 
 def slot_places(tiles, views, label_owner, label_index):
     slots = label_index.shape[1]
-    count = tiles * views * ROWS
+    count = tiles * views
     return pl.pallas_call(
         functools.partial(slots_kernel, views),
         out_shape=(
-            jax.ShapeDtypeStruct((count, slots), F32),
+            jax.ShapeDtypeStruct((CAP * count, slots), F32),
             jax.ShapeDtypeStruct((count, LANES), F32),
         ),
         in_specs=[VMEM, VMEM],
@@ -492,15 +495,20 @@
     lax.fori_loop(0, slots // group, one_group, 0)
     if part < PARTS - 1:
         return
-    sent[...] = base[...] + jnp.dot(
+    rows = jnp.dot(
         picked[...], table[...], precision=lax.Precision.HIGHEST, preferred_element_type=F32
     )
+    total = base[...]
+    count = total.shape[0]
+    for place in range(CAP):
+        total += pltpu.roll(rows[place * count : (place + 1) * count], place * WIDTH, 1)
+    sent[...] = total
 
 
 def moment_rows(views, tiles, part, estimate, correction, labels, places, begun):
     planes, size, across = correction.shape
     slots = places[0].shape[1]
-    count = places[0].shape[0] if part == PARTS - 1 else slots
+    count = places[1].shape[0] if part == PARTS - 1 else slots
     return pl.pallas_call(
         functools.partial(moments_kernel, views, tiles * planes, part),
         out_shape=jax.ShapeDtypeStruct((count, LANES), F32),
@@ -517,7 +525,9 @@
 
 
 def segments_kernel(across, scale, rows, moments):
-    values = rows[...]
+    whole = rows[...]
+    parts = [whole] + [pltpu.roll(whole, LANES - place * WIDTH, 1) for place in range(1, CAP)]
+    values = jnp.concatenate(parts, axis=0)
     ids = values[:, IDS : IDS + 1].astype(jnp.int32)
     spots = lax.broadcasted_iota(jnp.int32, (values.shape[0], NUC_DEV), 1)
     picked = (ids == spots).astype(F32)
@@ -529,7 +539,7 @@
     flat = lambda sums: sums[0:1]
     line = lambda sums: (sums[1:2] + 0.5 * sums[0:1]) * (1.0 / across)
     square = lambda sums: (sums[2:3] + sums[3:4] + sums[1:2] + 0.25 * sums[0:1]) * (1.0 / across**2)
-    whole = flat(mass)
+    total = flat(mass)
     sums = jnp.concatenate(
         [
             flat(deep), flat(high), line(mass),
@@ -538,7 +548,7 @@
         ],
         axis=0,
     )
-    moments[...] = jnp.concatenate([whole * scale, sums / jnp.maximum(whole, 1.0)], axis=0)
+    moments[...] = jnp.concatenate([total * scale, sums / jnp.maximum(total, 1.0)], axis=0)
 
 
 def nucleus_table(across, scale, rows):
@@ -548,6 +558,7 @@
         in_specs=[VMEM],
         out_specs=VMEM,
         compiler_params=pltpu.CompilerParams(vmem_limit_bytes=LIMIT),
+        cost_estimate=pl.CostEstimate(flops=10_000_000_000, bytes_accessed=20_000_000, transcendentals=0),
         name="nucleus_table",
     )(rows)
 

time: 50.3 us -> 48.6 us (0.966)
  starting transfers between devices: 27.9 us -> 26.8 us
  waiting for transfers between devices: 11.2 us -> 10.5 us
    ppermute x2, waiting for transfers between devices: 1.2 us -> 0.01 us  [on_device(): new_other.append(lax.ppermute(new_mine[part], 'view', partner))]
    ppermute x2, starting transfers between devices: 5.11 us -> 4.04 us  [on_device(): new_other.append(lax.ppermute(new_mine[part], 'view', partner))]
  transfers between devices with their start and end apart: 12 -> 12, of which waited for: 3 -> 2; matrix products, arithmetic and copies ran while one was open for 0% -> 0% of each run, Pallas kernels for 13% -> 13%
where the time goes in v10:
time: 48.6 us; the launch traced here: 48.3 us
  starting transfers between devices  26.8 us (55%)
  waiting for transfers between devices  10.5 us (22%)
  Pallas kernels  9.02 us (19%)
  local copies, waits for them, and re-layouts  1.07 us (2%)
  between operations  0.86 us (2%)
    ppermute x1, waiting for transfers between devices, on_device(): swapped = lax.ppermute(packed, 'view', partner)  7.42 us
    ppermute x4, starting transfers between devices, on_device(): lax.ppermute(send, 'tile', pairs)  7.28 us
    all_to_all x1, starting transfers between devices, on_device(): lax.all_to_all(sent, ('tile', 'view'), split_axis=0, concat_axis=0, tiled...  4.78 us
    ppermute x1, starting transfers between devices, on_device(): near = lax.ppermute(to_near, 'tile', near_pairs)  4.34 us
    ppermute x2, starting transfers between devices, on_device(): new_other.append(lax.ppermute(new_mine[part], 'view', partner))  4.04 us
    ppermute x2, starting transfers between devices, on_device(): other.append(lax.ppermute(mine[part], 'view', across_pairs))  3.95 us
    all_to_all x1, waiting for transfers between devices, on_device(): lax.all_to_all(sent, ('tile', 'view'), split_axis=0, concat_axis=0, tiled...  3.08 us
    pallas_call x2, Pallas kernels, moment_rows(): pl.pallas_call(functools.partial(moments_kernel, views, tiles * planes, p...  2.64 us
  transfers between devices with their start and end apart: 12, of which 2 were waited for; matrix products, arithmetic and copies ran while one was open for 0% of the time, Pallas kernels for 13%

profile of v10, /device:TPU:0, one launch (start us, length us, event | category | flops | bytes accessed | tf_op | source)
XLA Modules:
  0.0 48.3 jit_solution(11770912607540233810)
XLA Ops:
  0.6 0.0 copy-start
  0.6 1.0 %copy-done = f32[8,64,256]{2,1,0:T(8,128)S(1)} copy-done((f32[8,64,256]{2,1,0:T(8,128)S(1)}, f32[8,64,256]{2,1,0:T(8,128)}, u32[]{:S(2)}) %copy-start) | copy-done | bytes 524312
  1.7 0.0 copy-start.1
  1.7 0.8 %collective-permute-start.1 = (f32[7,48,256]{2,1,0:T(8,128)S(1)}, f32[7,48,256]{2,1,0:T(8,128)S(1)}, u32[]{:S(2)}, u32[]{:S(2)}) collective-permute-start(f32[7,48,256]{2,1,0:T(8,128)S(1)} %get-tuple-element.35), channel_id=1, source_target_pairs={{4,8},{12,16},{20,24},{8,4},{16,12},{24,20},{5,9},{13,17},{21,25},... | collective-permute-start | bytes 1032200 | tf_op jit(solution)/shard_map/ppermute | solution.py:654
  2.6 4.3 %collective-permute-start.2 = (f32[7,48,256]{2,1,0:T(8,128)S(1)}, f32[7,48,256]{2,1,0:T(8,128)S(1)}, u32[]{:S(2)}, u32[]{:S(2)}) collective-permute-start(f32[7,48,256]{2,1,0:T(8,128)S(1)} %get-tuple-element.36), channel_id=1, source_target_pairs={{0,4},{4,0},{8,12},{12,8},{16,20},{20,16},{24,28},{28,24},{1,5},{5... | collective-permute-start | bytes 1032200 | tf_op jit(solution)/shard_map/ppermute | solution.py:655
  6.9 0.0 copy-start.5
  7.0 0.0 copy-start.6
  7.0 1.6 %collective-permute-start = (f32[328,256]{1,0:T(8,128)S(1)}, f32[328,256]{1,0:T(8,128)S(1)}, u32[]{:S(2)}, u32[]{:S(2)}) collective-permute-start(f32[328,256]{1,0:T(8,128)S(1)} %view_out.1), channel_id=1, source_target_pairs={{0,1},{1,0},{2,3},{3,2},{4,5},{5,4},{6,7},{7,6},{8,9},{9,8},{10,11... | collective-permute-start | bytes 1007624 | tf_op jit(solution)/shard_map/ppermute | solution.py:652
  8.6 0.2 slot_places.1
  8.9 0.6 %prepare.2 = (bf16[2,2,256,256]{3,2,1,0:T(8,128)(2,1)S(1)}, bf16[40,144]{1,0:T(8,128)(2,1)S(1)}, bf16[32,144]{1,0:T(8,128)(2,1)S(1)}, f32[8,48,256]{2,1,0:T(8,128)S(1)}, f32[16,128]{1,0:T(8,128)S(1)}) custom-call(f32[3,1,15]{2,1,0:T(1,128)S(1)} %bitcast.8, f32[8,64,256]{2,1,0:T(8,128)S(1)} %copy-done.1, f32[32,128]{1,0:T(8,128)S(1)} %get-tuple-element.24.after.base), custom_call_target="tpu_custom_call" | custom-call | tf_op jit(solution)/shard_map/prepare/pallas_call | solution.py:155
  9.4 7.4 %collective-permute-done.source.refs_13_ = f32[328,256]{1,0:T(8,128)S(1)} collective-permute-done((f32[328,256]{1,0:T(8,128)S(1)}, f32[328,256]{1,0:T(8,128)S(1)}, u32[]{:S(2)}, u32[]{:S(2)}) %collective-permute-start) | collective-permute-done | bytes 335904 | tf_op jit(solution)/shard_map/ppermute | solution.py:652
  16.9 0.6 %prepare.3 = (bf16[2,2,256,256]{3,2,1,0:T(8,128)(2,1)S(1)}, bf16[40,144]{1,0:T(8,128)(2,1)S(1)}, bf16[32,144]{1,0:T(8,128)(2,1)S(1)}, f32[8,48,256]{2,1,0:T(8,128)S(1)}, f32[16,128]{1,0:T(8,128)S(1)}) custom-call(f32[328,256]{1,0:T(8,128)S(1)} %collective-permute-done.source.refs_13_, f32[8,64,256]{2,1,0:T(8,128)S(1)} %copy-done.1, f32[3,1,15]{2,1,0:T(1,128)S(1)} %bitcast.9), custom_call_target="tpu_custom_call" | custom-call | tf_op jit(solution)/shard_map/prepare/pallas_call | solution.py:155
  17.5 0.0 collective-permute-done.2.refs_11_
  17.5 1.8 %ratio_fields.1 = (f32[8,32,256]{2,1,0:T(8,128)S(1)}, f32[8,32,256]{2,1,0:T(8,128)S(1)}, f32[7,16,256]{2,1,0:T(8,128)S(1)}, f32[7,16,256]{2,1,0:T(8,128)S(1)}, f...) custom-call(bf16[2,2,256,256]{3,2,1,0:T(8,128)(2,1)S(1)} %get-tuple-element.27.refs_0_, ...), custom_call_target="tpu_custom_call" | custom-call | tf_op jit(solution)/shard_map/ratio_fields/pallas_call | solution.py:270
  19.3 0.0 copy-start.3
  19.3 0.8 %collective-permute-start.3 = (f32[7,16,256]{2,1,0:T(8,128)S(1)}, f32[7,16,256]{2,1,0:T(8,128)S(1)}, u32[]{:S(2)}, u32[]{:S(2)}) collective-permute-start(f32[7,16,256]{2,1,0:T(8,128)S(1)} %get-tuple-element.40), channel_id=1, source_target_pairs={{4,8},{12,16},{20,24},{8,4},{16,12},{24,20},{5,9},{13,17},{21,25},... | collective-permute-start | bytes 344072 | tf_op jit(solution)/shard_map/ppermute | solution.py:661
  20.1 2.9 %collective-permute-start.4 = (f32[7,16,256]{2,1,0:T(8,128)S(1)}, f32[7,16,256]{2,1,0:T(8,128)S(1)}, u32[]{:S(2)}, u32[]{:S(2)}) collective-permute-start(f32[7,16,256]{2,1,0:T(8,128)S(1)} %get-tuple-element.41), channel_id=1, source_target_pairs={{0,4},{4,0},{8,12},{12,8},{16,20},{20,16},{24,28},{28,24},{1,5},{5... | collective-permute-start | bytes 344072 | tf_op jit(solution)/shard_map/ppermute | solution.py:661
  23.0 0.7 %collective-permute-start.6 = (f32[7,16,256]{2,1,0:T(8,128)S(1)}, f32[7,16,256]{2,1,0:T(8,128)S(1)}, u32[]{:S(2)}, u32[]{:S(2)}) collective-permute-start(f32[7,16,256]{2,1,0:T(8,128)S(1)} %get-tuple-element.44), channel_id=1, source_target_pairs={{4,8},{12,16},{20,24},{8,4},{16,12},{24,20},{5,9},{13,17},{21,25},... | collective-permute-start | bytes 344072 | tf_op jit(solution)/shard_map/ppermute | solution.py:661
  23.7 2.9 %collective-permute-start.7 = (f32[7,16,256]{2,1,0:T(8,128)S(1)}, f32[7,16,256]{2,1,0:T(8,128)S(1)}, u32[]{:S(2)}, u32[]{:S(2)}) collective-permute-start(f32[7,16,256]{2,1,0:T(8,128)S(1)} %get-tuple-element.45), channel_id=1, source_target_pairs={{0,4},{4,0},{8,12},{12,8},{16,20},{20,16},{24,28},{28,24},{1,5},{5... | collective-permute-start | bytes 344072 | tf_op jit(solution)/shard_map/ppermute | solution.py:661
  26.6 0.3 own_planes.1
  26.9 0.0 collective-permute-done.3.far
  27.0 3.7 %collective-permute-start.5 = (f32[8,16,256]{2,1,0:T(8,128)S(1)}, f32[8,16,256]{2,1,0:T(8,128)S(1)}, u32[]{:S(2)}, u32[]{:S(2)}) collective-permute-start(f32[8,16,256]{2,1,0:T(8,128)S(1)} %add_rims.2.correction.mine), channel_id=1, source_target_pairs={{0,3},{1,2},{2,1},{3,0},{4,7},{5,6},{6,5},{7,4},{8,11},{9,10},{10,... | collective-permute-start | bytes 393224 | tf_op jit(solution)/shard_map/ppermute | solution.py:667
  30.6 0.8 %moment_rows.2.rest_0_.refs_0_ = f32[16,128]{1,0:T(8,128)S(1)} custom-call(f32[8,64,256]{2,1,0:T(8,128)S(1)} %copy-done.1, s32[8,64,256]{2,1,0:T(8,128)S(1)} %copy-done.3, f32[160,16]{1,0:T(8,128)S(1)} %get-tuple-element.42.picked, f32[32,128]{1,0:T(8,128)S(1)} %get-tuple-element.24.after.base, f32[8,16,256]{2,1,0:T(8,128)S(1)} %add_rims.2.correction.mine), custom_call_target="tpu_custom_call" | custom-call | tf_op jit(solution)/shard_map/moment_rows/pallas_call | solution.py:512
  31.5 0.3 collective-permute-start.8
  31.8 1.8 %moment_rows.3.rest_0_ = f32[32,128]{1,0:T(8,128)} custom-call(f32[8,64,256]{2,1,0:T(8,128)S(1)} %copy-done.1, s32[8,64,256]{2,1,0:T(8,128)S(1)} %copy-done.3, f32[160,16]{1,0:T(8,128)S(1)} %get-tuple-element.42.picked, f32[32,128]{1,0:T(8,128)S(1)} %get-tuple-element.24.after.base, f32[8,16,256]{2,1,0:T(8,128)S(1)} %add_rims.3.correction.mine, ...), custom_call_target="tpu_custom_call" | custom-call | tf_op jit(solution)/shard_map/moment_rows/pallas_call | solution.py:512
  33.6 4.8 %all-to-all-start = ((f32[32,1,128]{2,1,0:T(1,128)}), f32[32,1,128]{2,1,0:T(1,128)S(1)}, u32[]{:S(2)}, u32[]{:S(2)}) async-start(f32[32,1,128]{2,1,0:T(1,128)} %bitcast.3), calls=%async_computation | async-start | bytes 32768 | tf_op jit(solution)/shard_map/all_to_all | solution.py:670
  38.5 2.2 %collective-permute-start.9 = (f32[136,256]{1,0:T(8,128)S(1)}, f32[136,256]{1,0:T(8,128)S(1)}, u32[]{:S(2)}, u32[]{:S(2)}) collective-permute-start(f32[136,256]{1,0:T(8,128)S(1)} %update.2.source.refs_0_), channel_id=1, source_target_pairs={{0,1},{1,0},{2,3},{3,2},{4,5},{5,4},{6,7},{7,6},{8,9},{9,8},{10,11... | collective-permute-start | bytes 417800 | tf_op jit(solution)/shard_map/ppermute | solution.py:676
  40.7 1.8 %collective-permute-start.10 = (f32[128,256]{1,0:T(8,128)S(1)}, f32[128,256]{1,0:T(8,128)S(1)}, u32[]{:S(2)}, u32[]{:S(2)}) collective-permute-start(f32[128,256]{1,0:T(8,128)S(1)} %update.3.refs_1_), channel_id=1, source_target_pairs={{0,1},{1,0},{2,3},{3,2},{4,5},{5,4},{6,7},{7,6},{8,9},{9,8},{10,11... | collective-permute-start | bytes 393224 | tf_op jit(solution)/shard_map/ppermute | solution.py:676
  42.5 3.1 %all-to-all-done = f32[32,1,128]{2,1,0:T(1,128)S(1)} async-done(((f32[32,1,128]{2,1,0:T(1,128)}), f32[32,1,128]{2,1,0:T(1,128)S(1)}, u32[]{:S(2)}, u32[]{:S(2)}) %all-to-all-start) | async-done | bytes 16416 | tf_op jit(solution)/shard_map/all_to_all | solution.py:670
  45.6 1.0 %nucleus_table.1 = f32[10,128]{1,0:T(8,128)} custom-call(f32[32,128]{1,0:T(8,128)S(1)} %bitcast.6), custom_call_target="tpu_custom_call" | custom-call | flops 10000000000 | bytes 20000000 | tf_op jit(solution)/shard_map/nucleus_table/pallas_call | solution.py:555
  46.6 0.8 %begin_result.1.begun = f32[8,64,256]{2,1,0:T(8,128)} custom-call(f32[136,256]{1,0:T(8,128)S(1)} %update.2.source.refs_0_, f32[128,256]{1,0:T(8,128)S(1)} %update.3.refs_1_), custom_call_target="tpu_custom_call" | custom-call | tf_op jit(solution)/shard_map/begin_result/pallas_call | solution.py:606
  47.5 0.8 %finish.1 = f32[8,64,256]{2,1,0:T(8,128)} custom-call(f32[8,64,256]{2,1,0:T(8,128)} %begin_result.1.begun, f32[136,256]{1,0:T(8,128)S(1)} %collective-permute-done.9.refs_0_, f32[128,256]{1,0:T(8,128)S(1)} %collective-permute-done.10.refs_1_), custom_call_target="tpu_custom_call", output_to_operand_aliasing={{}: (0, {})} | custom-call | tf_op jit(solution)/shard_map/finish/pallas_call | solution.py:624
  (23 shorter events, 0.2 us)
Async XLA Ops:
  0.6 1.0 %copy-start = (f32[8,64,256]{2,1,0:T(8,128)S(1)}, f32[8,64,256]{2,1,0:T(8,128)}, u32[]{:S(2)}) copy-start(f32[8,64,256]{2,1,0:T(8,128)} %estimate.13) | copy-start | bytes 1572868
  1.7 5.2 %copy-start.2 = (f32[1,8,64,256]{3,2,1,0:T(8,128)S(1)}, f32[1,8,64,256]{3,2,1,0:T(8,128)}, u32[]{:S(2)}) copy-start(f32[1,8,64,256]{3,2,1,0:T(8,128)} %refs_12_.1) | copy-start | bytes 1572868
  1.7 5.2 %copy-start.4 = (f32[1,3,15]{2,0,1:T(1,128)S(1)}, f32[1,3,15]{2,0,1:T(1,128)}, u32[]{:S(2)}) copy-start(f32[1,3,15]{2,0,1:T(1,128)} %param.8) | copy-start | bytes 544
  1.7 7.1 %copy-start.1 = (f32[8,64,256]{2,1,0:T(8,128)S(1)}, f32[8,64,256]{2,1,0:T(8,128)}, u32[]{:S(2)}) copy-start(f32[8,64,256]{2,1,0:T(8,128)} %estimate.13) | copy-start | bytes 1572868
  1.7 15.7 %collective-permute-start.1 = (f32[7,48,256]{2,1,0:T(8,128)S(1)}, f32[7,48,256]{2,1,0:T(8,128)S(1)}, u32[]{:S(2)}, u32[]{:S(2)}) collective-permute-start(f32[7,48,256]{2,1,0:T(8,128)S(1)} %get-tuple-element.35), channel_id=1, source_target_pairs={{4,8},{12,16},{20,24},{8,4},{16,12},{24,20},{5,9},{13,17},{21,25},... | collective-permute-start | bytes 1032200 | tf_op jit(solution)/shard_map/ppermute | solution.py:654
  2.6 14.9 %collective-permute-start.2 = (f32[7,48,256]{2,1,0:T(8,128)S(1)}, f32[7,48,256]{2,1,0:T(8,128)S(1)}, u32[]{:S(2)}, u32[]{:S(2)}) collective-permute-start(f32[7,48,256]{2,1,0:T(8,128)S(1)} %get-tuple-element.36), channel_id=1, source_target_pairs={{0,4},{4,0},{8,12},{12,8},{16,20},{20,16},{24,28},{28,24},{1,5},{5... | collective-permute-start | bytes 1032200 | tf_op jit(solution)/shard_map/ppermute | solution.py:655
  6.9 1.7 %copy-start.5 = (s32[1,16,1]{1,2,0:T(1,128)S(1)}, s32[1,16,1]{1,2,0:T(1,128)}, u32[]{:S(2)}) copy-start(s32[1,16,1]{1,2,0:T(1,128)} %param.10) | copy-start | bytes 196
  7.0 1.7 %copy-start.6 = (s32[1,16]{1,0:T(1,128)S(1)}, s32[1,16]{1,0:T(1,128)}, u32[]{:S(2)}) copy-start(s32[1,16]{1,0:T(1,128)} %index_row.1) | copy-start | bytes 196
  7.0 9.9 %collective-permute-start = (f32[328,256]{1,0:T(8,128)S(1)}, f32[328,256]{1,0:T(8,128)S(1)}, u32[]{:S(2)}, u32[]{:S(2)}) collective-permute-start(f32[328,256]{1,0:T(8,128)S(1)} %view_out.1), channel_id=1, source_target_pairs={{0,1},{1,0},{2,3},{3,2},{4,5},{5,4},{6,7},{7,6},{8,9},{9,8},{10,11... | collective-permute-start | bytes 1007624 | tf_op jit(solution)/shard_map/ppermute | solution.py:652
  19.3 11.3 %copy-start.3 = (s32[8,64,256]{2,1,0:T(8,128)S(1)}, s32[8,64,256]{2,1,0:T(8,128)}, u32[]{:S(2)}) copy-start(s32[8,64,256]{2,1,0:T(8,128)} %labels.3) | copy-start | bytes 1572868
  19.3 7.6 %collective-permute-start.3 = (f32[7,16,256]{2,1,0:T(8,128)S(1)}, f32[7,16,256]{2,1,0:T(8,128)S(1)}, u32[]{:S(2)}, u32[]{:S(2)}) collective-permute-start(f32[7,16,256]{2,1,0:T(8,128)S(1)} %get-tuple-element.40), channel_id=1, source_target_pairs={{4,8},{12,16},{20,24},{8,4},{16,12},{24,20},{5,9},{13,17},{21,25},... | collective-permute-start | bytes 344072 | tf_op jit(solution)/shard_map/ppermute | solution.py:661
  20.1 6.8 %collective-permute-start.4 = (f32[7,16,256]{2,1,0:T(8,128)S(1)}, f32[7,16,256]{2,1,0:T(8,128)S(1)}, u32[]{:S(2)}, u32[]{:S(2)}) collective-permute-start(f32[7,16,256]{2,1,0:T(8,128)S(1)} %get-tuple-element.41), channel_id=1, source_target_pairs={{0,4},{4,0},{8,12},{12,8},{16,20},{20,16},{24,28},{28,24},{1,5},{5... | collective-permute-start | bytes 344072 | tf_op jit(solution)/shard_map/ppermute | solution.py:661
  23.0 8.5 %collective-permute-start.6 = (f32[7,16,256]{2,1,0:T(8,128)S(1)}, f32[7,16,256]{2,1,0:T(8,128)S(1)}, u32[]{:S(2)}, u32[]{:S(2)}) collective-permute-start(f32[7,16,256]{2,1,0:T(8,128)S(1)} %get-tuple-element.44), channel_id=1, source_target_pairs={{4,8},{12,16},{20,24},{8,4},{16,12},{24,20},{5,9},{13,17},{21,25},... | collective-permute-start | bytes 344072 | tf_op jit(solution)/shard_map/ppermute | solution.py:661
  23.7 7.8 %collective-permute-start.7 = (f32[7,16,256]{2,1,0:T(8,128)S(1)}, f32[7,16,256]{2,1,0:T(8,128)S(1)}, u32[]{:S(2)}, u32[]{:S(2)}) collective-permute-start(f32[7,16,256]{2,1,0:T(8,128)S(1)} %get-tuple-element.45), channel_id=1, source_target_pairs={{0,4},{4,0},{8,12},{12,8},{16,20},{20,16},{24,28},{28,24},{1,5},{5... | collective-permute-start | bytes 344072 | tf_op jit(solution)/shard_map/ppermute | solution.py:661
  27.0 11.5 %collective-permute-start.5 = (f32[8,16,256]{2,1,0:T(8,128)S(1)}, f32[8,16,256]{2,1,0:T(8,128)S(1)}, u32[]{:S(2)}, u32[]{:S(2)}) collective-permute-start(f32[8,16,256]{2,1,0:T(8,128)S(1)} %add_rims.2.correction.mine), channel_id=1, source_target_pairs={{0,3},{1,2},{2,1},{3,0},{4,7},{5,6},{6,5},{7,4},{8,11},{9,10},{10,... | collective-permute-start | bytes 393224 | tf_op jit(solution)/shard_map/ppermute | solution.py:667
  31.5 9.1 %collective-permute-start.8 = (f32[8,16,256]{2,1,0:T(8,128)S(1)}, f32[8,16,256]{2,1,0:T(8,128)S(1)}, u32[]{:S(2)}, u32[]{:S(2)}) collective-permute-start(f32[8,16,256]{2,1,0:T(8,128)S(1)} %add_rims.3.correction.mine), channel_id=1, source_target_pairs={{0,3},{1,2},{2,1},{3,0},{4,7},{5,6},{6,5},{7,4},{8,11},{9,10},{10,... | collective-permute-start | bytes 393224 | tf_op jit(solution)/shard_map/ppermute | solution.py:667
  33.6 12.0 %all-to-all-start = ((f32[32,1,128]{2,1,0:T(1,128)}), f32[32,1,128]{2,1,0:T(1,128)S(1)}, u32[]{:S(2)}, u32[]{:S(2)}) async-start(f32[32,1,128]{2,1,0:T(1,128)} %bitcast.3), calls=%async_computation | async-start | bytes 32768 | tf_op jit(solution)/shard_map/all_to_all | solution.py:670
  38.5 9.0 %collective-permute-start.9 = (f32[136,256]{1,0:T(8,128)S(1)}, f32[136,256]{1,0:T(8,128)S(1)}, u32[]{:S(2)}, u32[]{:S(2)}) collective-permute-start(f32[136,256]{1,0:T(8,128)S(1)} %update.2.source.refs_0_), channel_id=1, source_target_pairs={{0,1},{1,0},{2,3},{3,2},{4,5},{5,4},{6,7},{7,6},{8,9},{9,8},{10,11... | collective-permute-start | bytes 417800 | tf_op jit(solution)/shard_map/ppermute | solution.py:676
  40.7 6.8 %collective-permute-start.10 = (f32[128,256]{1,0:T(8,128)S(1)}, f32[128,256]{1,0:T(8,128)S(1)}, u32[]{:S(2)}, u32[]{:S(2)}) collective-permute-start(f32[128,256]{1,0:T(8,128)S(1)} %update.3.refs_1_), channel_id=1, source_target_pairs={{0,1},{1,0},{2,3},{3,2},{4,5},{5,4},{6,7},{7,6},{8,9},{9,8},{10,11... | collective-permute-start | bytes 393224 | tf_op jit(solution)/shard_map/ppermute | solution.py:676

commit v11 on v10

--- a/solution.py
+++ b/solution.py
@@ -173,7 +173,7 @@
 
 
 def fields_kernel(*refs):
-    sets, (far, near, measured, swapped), refs = (refs[:5], refs[5:10]), refs[10:14], refs[14:]
+    sets, (far, near, measured, swapped), refs = (refs[:5], refs[5:10]), refs[10:14], refs[15:]
     fields, sends, (blur_hi, blur_lo, plane_hi, plane_lo) = refs[:2], refs[2:-4], refs[-4:]
     planes = sets[0][3].shape[0]
     radius, rows, across = near.shape
@@ -262,7 +262,7 @@
             sends[2 * part_at + 1][at, inside, lane] = jnp.where(even, up, down)
 
 
-def ratio_fields(own, others, far, near, measured, swapped):
+def ratio_fields(own, others, far, near, measured, swapped, after):
     keep, planes = own[2].shape[0], own[3].shape[0]
     radius, rows, across = near.shape
     field = jax.ShapeDtypeStruct((planes, keep, across), F32)
@@ -270,7 +270,7 @@
     return pl.pallas_call(
         fields_kernel,
         out_shape=(field,) * 2 + (send,) * (2 * PARTS),
-        in_specs=[VMEM] * 14,
+        in_specs=[VMEM] * 14 + [ANY],
         out_specs=(VMEM,) * (2 + 2 * PARTS),
         scratch_shapes=[
             pltpu.VMEM((2, planes * rows, across), BF16),
@@ -280,7 +280,7 @@
         ],
         compiler_params=pltpu.CompilerParams(vmem_limit_bytes=LIMIT),
         name="ratio_fields",
-    )(*own, *others, far, near, measured, swapped)
+    )(*own, *others, far, near, measured, swapped, after)
 
 
 def own_kernel(taps, spread_own, spread_other, field_own, field_other, *inner):
@@ -581,19 +581,21 @@
     return copies
 
 
-def token_kernel(source, token):
+def token_kernel(source, *rest):
+    token = rest[-1]
     token[...] = source[:8, :LANES]
 
 
-def token_of(source):
+def token_of(source, after=(), flops=0):
     return pl.pallas_call(
         token_kernel,
         out_shape=jax.ShapeDtypeStruct((8, LANES), F32),
-        in_specs=[VMEM],
+        in_specs=[VMEM] + [ANY] * len(after),
         out_specs=VMEM,
         compiler_params=pltpu.CompilerParams(vmem_limit_bytes=LIMIT),
+        cost_estimate=pl.CostEstimate(flops=flops, bytes_accessed=flops // 500, transcendentals=0),
         name="token_of",
-    )(source)
+    )(source, *after)
 
 
 def begin_kernel(pieces, *refs):
@@ -656,7 +658,10 @@
     places = slot_places(tiles, views, label_owner, label_index)
     own = prepare(False, taps, lines, estimate, places[1], rows, seen, keep)
     others = prepare(True, taps, swapped, estimate, lines, rows, seen, keep)
-    field_own, field_other, *sends = ratio_fields(own, others, far, near, measured, swapped)
+    came = token_of(far.reshape(radius * rows, across), (others[4],), 8_000_000_000)
+    field_own, field_other, *sends = ratio_fields(
+        own, others, far, near, measured, swapped, came
+    )
     rims = [
         lax.ppermute(send, "tile", pairs) for send, pairs in zip(sends, (far_pairs, near_pairs) * PARTS)
     ]

time: 48.6 us -> 48.2 us (level)
  waiting for transfers between devices: 10.5 us -> 5.96 us
  starting transfers between devices: 26.8 us -> 30.8 us
    ppermute x4, starting transfers between devices: 7.28 us -> 11.7 us  [on_device(): lax.ppermute(send, 'tile', pairs)]
    ppermute x1, waiting for transfers between devices: 7.42 us -> 3.22 us  [on_device(): swapped = lax.ppermute(packed, 'view', partner)]
    ppermute x1, starting transfers between devices: 4.34 us -> 2.43 us  [on_device(): near = lax.ppermute(to_near, 'tile', near_pairs)]
    ppermute x1, starting transfers between devices: 1.64 us -> 3.09 us  [on_device(): swapped = lax.ppermute(packed, 'view', partner)]
where the time goes in v11:
time: 48.2 us; the launch traced here: 47.9 us
  starting transfers between devices  30.8 us (64%)
  Pallas kernels  9.03 us (19%)
  waiting for transfers between devices  5.96 us (12%)
  local copies, waits for them, and re-layouts  1.22 us (3%)
  between operations  0.85 us (2%)
    ppermute x4, starting transfers between devices, on_device(): lax.ppermute(send, 'tile', pairs)  11.7 us
    all_to_all x1, starting transfers between devices, on_device(): lax.all_to_all(sent, ('tile', 'view'), split_axis=0, concat_axis=0, tiled...  4.45 us
    ppermute x2, starting transfers between devices, on_device(): new_other.append(lax.ppermute(new_mine[part], 'view', partner))  4.41 us
    ppermute x2, starting transfers between devices, on_device(): other.append(lax.ppermute(mine[part], 'view', across_pairs))  3.95 us
    ppermute x1, waiting for transfers between devices, on_device(): swapped = lax.ppermute(packed, 'view', partner)  3.22 us
    ppermute x1, starting transfers between devices, on_device(): swapped = lax.ppermute(packed, 'view', partner)  3.09 us
    all_to_all x1, waiting for transfers between devices, on_device(): lax.all_to_all(sent, ('tile', 'view'), split_axis=0, concat_axis=0, tiled...  2.71 us
    pallas_call x2, Pallas kernels, moment_rows(): pl.pallas_call(functools.partial(moments_kernel, views, tiles * planes, p...  2.64 us
  transfers between devices with their start and end apart: 12, of which 2 were waited for; matrix products, arithmetic and copies ran while one was open for 0% of the time, Pallas kernels for 13%

profile of v11, /device:TPU:0, one launch (start us, length us, event | category | flops | bytes accessed | tf_op | source)
XLA Modules:
  0.0 47.9 jit_solution(9204769744544690941)
XLA Ops:
  0.6 0.0 copy-start
  0.6 1.0 %copy-done = f32[8,64,256]{2,1,0:T(8,128)S(1)} copy-done((f32[8,64,256]{2,1,0:T(8,128)S(1)}, f32[8,64,256]{2,1,0:T(8,128)}, u32[]{:S(2)}) %copy-start) | copy-done | bytes 524312
  1.7 0.0 copy-start.1
  1.7 0.8 %collective-permute-start.1 = (f32[7,48,256]{2,1,0:T(8,128)S(1)}, f32[7,48,256]{2,1,0:T(8,128)S(1)}, u32[]{:S(2)}, u32[]{:S(2)}) collective-permute-start(f32[7,48,256]{2,1,0:T(8,128)S(1)} %get-tuple-element.35), channel_id=1, source_target_pairs={{4,8},{12,16},{20,24},{8,4},{16,12},{24,20},{5,9},{13,17},{21,25},... | collective-permute-start | bytes 1032200 | tf_op jit(solution)/shard_map/ppermute | solution.py:656
  2.6 0.2 copy-done.2
  2.7 3.1 %collective-permute-start = (f32[328,256]{1,0:T(8,128)S(1)}, f32[328,256]{1,0:T(8,128)S(1)}, u32[]{:S(2)}, u32[]{:S(2)}) collective-permute-start(f32[328,256]{1,0:T(8,128)S(1)} %view_out.1), channel_id=1, source_target_pairs={{0,1},{1,0},{2,3},{3,2},{4,5},{5,4},{6,7},{7,6},{8,9},{9,8},{10,11... | collective-permute-start | bytes 1007624 | tf_op jit(solution)/shard_map/ppermute | solution.py:654
  5.8 2.4 %collective-permute-start.2 = (f32[7,48,256]{2,1,0:T(8,128)S(1)}, f32[7,48,256]{2,1,0:T(8,128)S(1)}, u32[]{:S(2)}, u32[]{:S(2)}) collective-permute-start(f32[7,48,256]{2,1,0:T(8,128)S(1)} %get-tuple-element.36), channel_id=1, source_target_pairs={{0,4},{4,0},{8,12},{12,8},{16,20},{20,16},{24,28},{28,24},{1,5},{5... | collective-permute-start | bytes 1032200 | tf_op jit(solution)/shard_map/ppermute | solution.py:657
  8.3 0.2 slot_places.1
  8.5 0.6 %prepare.2 = (bf16[2,2,256,256]{3,2,1,0:T(8,128)(2,1)S(1)}, bf16[40,144]{1,0:T(8,128)(2,1)S(1)}, bf16[32,144]{1,0:T(8,128)(2,1)S(1)}, f32[8,48,256]{2,1,0:T(8,128)S(1)}, f32[16,128]{1,0:T(8,128)S(1)}) custom-call(f32[3,1,15]{2,1,0:T(1,128)S(1)} %bitcast.10, f32[8,64,256]{2,1,0:T(8,128)S(1)} %copy-done.1, f32[32,128]{1,0:T(8,128)S(1)} %get-tuple-element.24.after.base), custom_call_target="tpu_custom_call" | custom-call | tf_op jit(solution)/shard_map/prepare/pallas_call | solution.py:155
  9.1 3.2 %collective-permute-done.source.refs_13_ = f32[328,256]{1,0:T(8,128)S(1)} collective-permute-done((f32[328,256]{1,0:T(8,128)S(1)}, f32[328,256]{1,0:T(8,128)S(1)}, u32[]{:S(2)}, u32[]{:S(2)}) %collective-permute-start) | collective-permute-done | bytes 335904 | tf_op jit(solution)/shard_map/ppermute | solution.py:654
  12.3 0.6 %prepare.3 = (bf16[2,2,256,256]{3,2,1,0:T(8,128)(2,1)S(1)}, bf16[40,144]{1,0:T(8,128)(2,1)S(1)}, bf16[32,144]{1,0:T(8,128)(2,1)S(1)}, f32[8,48,256]{2,1,0:T(8,128)S(1)}, f32[16,128]{1,0:T(8,128)S(1)}) custom-call(f32[328,256]{1,0:T(8,128)S(1)} %collective-permute-done.source.refs_13_, f32[8,64,256]{2,1,0:T(8,128)S(1)} %copy-done.1, f32[3,1,15]{2,1,0:T(1,128)S(1)} %bitcast.11), custom_call_target="tpu_custom_call" | custom-call | tf_op jit(solution)/shard_map/prepare/pallas_call | solution.py:155
  12.9 1.8 %ratio_fields.1 = (f32[8,32,256]{2,1,0:T(8,128)S(1)}, f32[8,32,256]{2,1,0:T(8,128)S(1)}, f32[7,16,256]{2,1,0:T(8,128)S(1)}, f32[7,16,256]{2,1,0:T(8,128)S(1)}, f...) custom-call(bf16[2,2,256,256]{3,2,1,0:T(8,128)(2,1)S(1)} %get-tuple-element.27.refs_0_, ...), custom_call_target="tpu_custom_call" | custom-call | tf_op jit(solution)/shard_map/ratio_fields/pallas_call | solution.py:270
  14.8 0.0 copy-start.3
  14.8 0.8 %collective-permute-start.3 = (f32[7,16,256]{2,1,0:T(8,128)S(1)}, f32[7,16,256]{2,1,0:T(8,128)S(1)}, u32[]{:S(2)}, u32[]{:S(2)}) collective-permute-start(f32[7,16,256]{2,1,0:T(8,128)S(1)} %get-tuple-element.40), channel_id=1, source_target_pairs={{4,8},{12,16},{20,24},{8,4},{16,12},{24,20},{5,9},{13,17},{21,25},... | collective-permute-start | bytes 344072 | tf_op jit(solution)/shard_map/ppermute | solution.py:666
  15.6 6.1 %collective-permute-start.4 = (f32[7,16,256]{2,1,0:T(8,128)S(1)}, f32[7,16,256]{2,1,0:T(8,128)S(1)}, u32[]{:S(2)}, u32[]{:S(2)}) collective-permute-start(f32[7,16,256]{2,1,0:T(8,128)S(1)} %get-tuple-element.41), channel_id=1, source_target_pairs={{0,4},{4,0},{8,12},{12,8},{16,20},{20,16},{24,28},{28,24},{1,5},{5... | collective-permute-start | bytes 344072 | tf_op jit(solution)/shard_map/ppermute | solution.py:666
  21.7 0.7 %collective-permute-start.6 = (f32[7,16,256]{2,1,0:T(8,128)S(1)}, f32[7,16,256]{2,1,0:T(8,128)S(1)}, u32[]{:S(2)}, u32[]{:S(2)}) collective-permute-start(f32[7,16,256]{2,1,0:T(8,128)S(1)} %get-tuple-element.44), channel_id=1, source_target_pairs={{4,8},{12,16},{20,24},{8,4},{16,12},{24,20},{5,9},{13,17},{21,25},... | collective-permute-start | bytes 344072 | tf_op jit(solution)/shard_map/ppermute | solution.py:666
  22.4 4.1 %collective-permute-start.7 = (f32[7,16,256]{2,1,0:T(8,128)S(1)}, f32[7,16,256]{2,1,0:T(8,128)S(1)}, u32[]{:S(2)}, u32[]{:S(2)}) collective-permute-start(f32[7,16,256]{2,1,0:T(8,128)S(1)} %get-tuple-element.45), channel_id=1, source_target_pairs={{0,4},{4,0},{8,12},{12,8},{16,20},{20,16},{24,28},{28,24},{1,5},{5... | collective-permute-start | bytes 344072 | tf_op jit(solution)/shard_map/ppermute | solution.py:666
  26.5 0.3 own_planes.1
  26.8 0.0 collective-permute-done.4.near
  26.9 3.7 %collective-permute-start.5 = (f32[8,16,256]{2,1,0:T(8,128)S(1)}, f32[8,16,256]{2,1,0:T(8,128)S(1)}, u32[]{:S(2)}, u32[]{:S(2)}) collective-permute-start(f32[8,16,256]{2,1,0:T(8,128)S(1)} %add_rims.2.correction.mine), channel_id=1, source_target_pairs={{0,3},{1,2},{2,1},{3,0},{4,7},{5,6},{6,5},{7,4},{8,11},{9,10},{10,... | collective-permute-start | bytes 393224 | tf_op jit(solution)/shard_map/ppermute | solution.py:672
  30.6 0.8 %moment_rows.2.rest_0_.refs_0_ = f32[16,128]{1,0:T(8,128)S(1)} custom-call(f32[8,64,256]{2,1,0:T(8,128)S(1)} %copy-done.1, s32[8,64,256]{2,1,0:T(8,128)S(1)} %copy-done.3, f32[160,16]{1,0:T(8,128)S(1)} %get-tuple-element.42.picked, f32[32,128]{1,0:T(8,128)S(1)} %get-tuple-element.24.after.base, f32[8,16,256]{2,1,0:T(8,128)S(1)} %add_rims.2.correction.mine), custom_call_target="tpu_custom_call" | custom-call | tf_op jit(solution)/shard_map/moment_rows/pallas_call | solution.py:512
  31.4 0.0 collective-permute-done.7.near
  31.5 0.3 collective-permute-start.8
  31.7 1.8 %moment_rows.3.rest_0_ = f32[32,128]{1,0:T(8,128)} custom-call(f32[8,64,256]{2,1,0:T(8,128)S(1)} %copy-done.1, s32[8,64,256]{2,1,0:T(8,128)S(1)} %copy-done.3, f32[160,16]{1,0:T(8,128)S(1)} %get-tuple-element.42.picked, f32[32,128]{1,0:T(8,128)S(1)} %get-tuple-element.24.after.base, f32[8,16,256]{2,1,0:T(8,128)S(1)} %add_rims.3.correction.mine, ...), custom_call_target="tpu_custom_call" | custom-call | tf_op jit(solution)/shard_map/moment_rows/pallas_call | solution.py:512
  33.5 4.5 %all-to-all-start = ((f32[32,1,128]{2,1,0:T(1,128)}), f32[32,1,128]{2,1,0:T(1,128)S(1)}, u32[]{:S(2)}, u32[]{:S(2)}) async-start(f32[32,1,128]{2,1,0:T(1,128)} %bitcast.4), calls=%async_computation | async-start | bytes 32768 | tf_op jit(solution)/shard_map/all_to_all | solution.py:675
  38.0 0.0 collective-permute-done.5.other
  38.1 2.5 %collective-permute-start.9 = (f32[136,256]{1,0:T(8,128)S(1)}, f32[136,256]{1,0:T(8,128)S(1)}, u32[]{:S(2)}, u32[]{:S(2)}) collective-permute-start(f32[136,256]{1,0:T(8,128)S(1)} %update.2.source.refs_0_), channel_id=1, source_target_pairs={{0,1},{1,0},{2,3},{3,2},{4,5},{5,4},{6,7},{7,6},{8,9},{9,8},{10,11... | collective-permute-start | bytes 417800 | tf_op jit(solution)/shard_map/ppermute | solution.py:681
  40.6 1.9 %collective-permute-start.10 = (f32[128,256]{1,0:T(8,128)S(1)}, f32[128,256]{1,0:T(8,128)S(1)}, u32[]{:S(2)}, u32[]{:S(2)}) collective-permute-start(f32[128,256]{1,0:T(8,128)S(1)} %update.3.refs_1_), channel_id=1, source_target_pairs={{0,1},{1,0},{2,3},{3,2},{4,5},{5,4},{6,7},{7,6},{8,9},{9,8},{10,11... | collective-permute-start | bytes 393224 | tf_op jit(solution)/shard_map/ppermute | solution.py:681
  42.5 2.7 %all-to-all-done = f32[32,1,128]{2,1,0:T(1,128)S(1)} async-done(((f32[32,1,128]{2,1,0:T(1,128)}), f32[32,1,128]{2,1,0:T(1,128)S(1)}, u32[]{:S(2)}, u32[]{:S(2)}) %all-to-all-start) | async-done | bytes 16416 | tf_op jit(solution)/shard_map/all_to_all | solution.py:675
  45.2 1.0 %nucleus_table.1 = f32[10,128]{1,0:T(8,128)} custom-call(f32[32,128]{1,0:T(8,128)S(1)} %bitcast.8), custom_call_target="tpu_custom_call" | custom-call | flops 10000000000 | bytes 20000000 | tf_op jit(solution)/shard_map/nucleus_table/pallas_call | solution.py:555
  46.2 0.8 %begin_result.1.begun = f32[8,64,256]{2,1,0:T(8,128)} custom-call(f32[136,256]{1,0:T(8,128)S(1)} %update.2.source.refs_0_, f32[128,256]{1,0:T(8,128)S(1)} %update.3.refs_1_), custom_call_target="tpu_custom_call" | custom-call | tf_op jit(solution)/shard_map/begin_result/pallas_call | solution.py:608
  47.1 0.8 %finish.1 = f32[8,64,256]{2,1,0:T(8,128)} custom-call(f32[8,64,256]{2,1,0:T(8,128)} %begin_result.1.begun, f32[136,256]{1,0:T(8,128)S(1)} %collective-permute-done.9.refs_0_, f32[128,256]{1,0:T(8,128)S(1)} %collective-permute-done.10.refs_1_), custom_call_target="tpu_custom_call", output_to_operand_aliasing={{}: (0, {})} | custom-call | tf_op jit(solution)/shard_map/finish/pallas_call | solution.py:626
  (24 shorter events, 0.2 us)
Async XLA Ops:
  0.6 1.0 %copy-start = (f32[8,64,256]{2,1,0:T(8,128)S(1)}, f32[8,64,256]{2,1,0:T(8,128)}, u32[]{:S(2)}) copy-start(f32[8,64,256]{2,1,0:T(8,128)} %estimate.13) | copy-start | bytes 1572868
  1.7 1.0 %copy-start.2 = (f32[1,8,64,256]{3,2,1,0:T(8,128)S(1)}, f32[1,8,64,256]{3,2,1,0:T(8,128)}, u32[]{:S(2)}) copy-start(f32[1,8,64,256]{3,2,1,0:T(8,128)} %refs_12_.1) | copy-start | bytes 1572868
  1.7 1.0 %copy-start.4 = (f32[1,3,15]{2,0,1:T(1,128)S(1)}, f32[1,3,15]{2,0,1:T(1,128)}, u32[]{:S(2)}) copy-start(f32[1,3,15]{2,0,1:T(1,128)} %param.8) | copy-start | bytes 544
  1.7 6.8 %copy-start.1 = (f32[8,64,256]{2,1,0:T(8,128)S(1)}, f32[8,64,256]{2,1,0:T(8,128)}, u32[]{:S(2)}) copy-start(f32[8,64,256]{2,1,0:T(8,128)} %estimate.13) | copy-start | bytes 1572868
  1.7 11.2 %collective-permute-start.1 = (f32[7,48,256]{2,1,0:T(8,128)S(1)}, f32[7,48,256]{2,1,0:T(8,128)S(1)}, u32[]{:S(2)}, u32[]{:S(2)}) collective-permute-start(f32[7,48,256]{2,1,0:T(8,128)S(1)} %get-tuple-element.35), channel_id=1, source_target_pairs={{4,8},{12,16},{20,24},{8,4},{16,12},{24,20},{5,9},{13,17},{21,25},... | collective-permute-start | bytes 1032200 | tf_op jit(solution)/shard_map/ppermute | solution.py:656
  2.7 9.6 %collective-permute-start = (f32[328,256]{1,0:T(8,128)S(1)}, f32[328,256]{1,0:T(8,128)S(1)}, u32[]{:S(2)}, u32[]{:S(2)}) collective-permute-start(f32[328,256]{1,0:T(8,128)S(1)} %view_out.1), channel_id=1, source_target_pairs={{0,1},{1,0},{2,3},{3,2},{4,5},{5,4},{6,7},{7,6},{8,9},{9,8},{10,11... | collective-permute-start | bytes 1007624 | tf_op jit(solution)/shard_map/ppermute | solution.py:654
  5.8 2.4 %copy-start.5 = (s32[1,16,1]{1,2,0:T(1,128)S(1)}, s32[1,16,1]{1,2,0:T(1,128)}, u32[]{:S(2)}) copy-start(s32[1,16,1]{1,2,0:T(1,128)} %param.10) | copy-start | bytes 196
  5.8 2.4 %copy-start.6 = (s32[1,16]{1,0:T(1,128)S(1)}, s32[1,16]{1,0:T(1,128)}, u32[]{:S(2)}) copy-start(s32[1,16]{1,0:T(1,128)} %index_row.1) | copy-start | bytes 196
  5.8 7.1 %collective-permute-start.2 = (f32[7,48,256]{2,1,0:T(8,128)S(1)}, f32[7,48,256]{2,1,0:T(8,128)S(1)}, u32[]{:S(2)}, u32[]{:S(2)}) collective-permute-start(f32[7,48,256]{2,1,0:T(8,128)S(1)} %get-tuple-element.36), channel_id=1, source_target_pairs={{0,4},{4,0},{8,12},{12,8},{16,20},{20,16},{24,28},{28,24},{1,5},{5... | collective-permute-start | bytes 1032200 | tf_op jit(solution)/shard_map/ppermute | solution.py:657
  14.8 15.8 %copy-start.3 = (s32[8,64,256]{2,1,0:T(8,128)S(1)}, s32[8,64,256]{2,1,0:T(8,128)}, u32[]{:S(2)}) copy-start(s32[8,64,256]{2,1,0:T(8,128)} %labels.3) | copy-start | bytes 1572868
  14.8 12.0 %collective-permute-start.3 = (f32[7,16,256]{2,1,0:T(8,128)S(1)}, f32[7,16,256]{2,1,0:T(8,128)S(1)}, u32[]{:S(2)}, u32[]{:S(2)}) collective-permute-start(f32[7,16,256]{2,1,0:T(8,128)S(1)} %get-tuple-element.40), channel_id=1, source_target_pairs={{4,8},{12,16},{20,24},{8,4},{16,12},{24,20},{5,9},{13,17},{21,25},... | collective-permute-start | bytes 344072 | tf_op jit(solution)/shard_map/ppermute | solution.py:666
  15.6 11.2 %collective-permute-start.4 = (f32[7,16,256]{2,1,0:T(8,128)S(1)}, f32[7,16,256]{2,1,0:T(8,128)S(1)}, u32[]{:S(2)}, u32[]{:S(2)}) collective-permute-start(f32[7,16,256]{2,1,0:T(8,128)S(1)} %get-tuple-element.41), channel_id=1, source_target_pairs={{0,4},{4,0},{8,12},{12,8},{16,20},{20,16},{24,28},{28,24},{1,5},{5... | collective-permute-start | bytes 344072 | tf_op jit(solution)/shard_map/ppermute | solution.py:666
  21.7 9.7 %collective-permute-start.6 = (f32[7,16,256]{2,1,0:T(8,128)S(1)}, f32[7,16,256]{2,1,0:T(8,128)S(1)}, u32[]{:S(2)}, u32[]{:S(2)}) collective-permute-start(f32[7,16,256]{2,1,0:T(8,128)S(1)} %get-tuple-element.44), channel_id=1, source_target_pairs={{4,8},{12,16},{20,24},{8,4},{16,12},{24,20},{5,9},{13,17},{21,25},... | collective-permute-start | bytes 344072 | tf_op jit(solution)/shard_map/ppermute | solution.py:666
  22.4 9.0 %collective-permute-start.7 = (f32[7,16,256]{2,1,0:T(8,128)S(1)}, f32[7,16,256]{2,1,0:T(8,128)S(1)}, u32[]{:S(2)}, u32[]{:S(2)}) collective-permute-start(f32[7,16,256]{2,1,0:T(8,128)S(1)} %get-tuple-element.45), channel_id=1, source_target_pairs={{0,4},{4,0},{8,12},{12,8},{16,20},{20,16},{24,28},{28,24},{1,5},{5... | collective-permute-start | bytes 344072 | tf_op jit(solution)/shard_map/ppermute | solution.py:666
  26.9 11.1 %collective-permute-start.5 = (f32[8,16,256]{2,1,0:T(8,128)S(1)}, f32[8,16,256]{2,1,0:T(8,128)S(1)}, u32[]{:S(2)}, u32[]{:S(2)}) collective-permute-start(f32[8,16,256]{2,1,0:T(8,128)S(1)} %add_rims.2.correction.mine), channel_id=1, source_target_pairs={{0,3},{1,2},{2,1},{3,0},{4,7},{5,6},{6,5},{7,4},{8,11},{9,10},{10,... | collective-permute-start | bytes 393224 | tf_op jit(solution)/shard_map/ppermute | solution.py:672
  31.5 9.1 %collective-permute-start.8 = (f32[8,16,256]{2,1,0:T(8,128)S(1)}, f32[8,16,256]{2,1,0:T(8,128)S(1)}, u32[]{:S(2)}, u32[]{:S(2)}) collective-permute-start(f32[8,16,256]{2,1,0:T(8,128)S(1)} %add_rims.3.correction.mine), channel_id=1, source_target_pairs={{0,3},{1,2},{2,1},{3,0},{4,7},{5,6},{6,5},{7,4},{8,11},{9,10},{10,... | collective-permute-start | bytes 393224 | tf_op jit(solution)/shard_map/ppermute | solution.py:672
  33.5 11.7 %all-to-all-start = ((f32[32,1,128]{2,1,0:T(1,128)}), f32[32,1,128]{2,1,0:T(1,128)S(1)}, u32[]{:S(2)}, u32[]{:S(2)}) async-start(f32[32,1,128]{2,1,0:T(1,128)} %bitcast.4), calls=%async_computation | async-start | bytes 32768 | tf_op jit(solution)/shard_map/all_to_all | solution.py:675
  38.1 9.0 %collective-permute-start.9 = (f32[136,256]{1,0:T(8,128)S(1)}, f32[136,256]{1,0:T(8,128)S(1)}, u32[]{:S(2)}, u32[]{:S(2)}) collective-permute-start(f32[136,256]{1,0:T(8,128)S(1)} %update.2.source.refs_0_), channel_id=1, source_target_pairs={{0,1},{1,0},{2,3},{3,2},{4,5},{5,4},{6,7},{7,6},{8,9},{9,8},{10,11... | collective-permute-start | bytes 417800 | tf_op jit(solution)/shard_map/ppermute | solution.py:681
  40.6 6.4 %collective-permute-start.10 = (f32[128,256]{1,0:T(8,128)S(1)}, f32[128,256]{1,0:T(8,128)S(1)}, u32[]{:S(2)}, u32[]{:S(2)}) collective-permute-start(f32[128,256]{1,0:T(8,128)S(1)} %update.3.refs_1_), channel_id=1, source_target_pairs={{0,1},{1,0},{2,3},{3,2},{4,5},{5,4},{6,7},{7,6},{8,9},{9,8},{10,11... | collective-permute-start | bytes 393224 | tf_op jit(solution)/shard_map/ppermute | solution.py:681

commit v12 on v11

--- a/solution.py
+++ b/solution.py
@@ -13,7 +13,7 @@
 NUC_DEV = 128
 LANES = 128
 PARTS = 2
-TAIL = 8
+TAIL = 24
 IDS = 24
 F32 = jnp.float32
 BF16 = jnp.bfloat16
@@ -59,7 +59,7 @@
     return [(slice(row, row + 16), slice(lane, lane + LANES)) for row in range(0, rows, 16) for lane in range(0, across, LANES)]
 
 
-def rims_out_kernel(estimate, to_far, to_near):
+def rims_out_kernel(estimate, after, to_far, to_near):
     planes, radius, rows = estimate.shape[0], to_far.shape[0], to_far.shape[1]
     odd = lax.axis_index("tile") % 2
     half = half_of(lax.axis_index("view"))
@@ -68,40 +68,55 @@
     to_near[...] = estimate[pl.ds(1 - odd, radius), pl.ds(start, rows)]
 
 
-def rims_out(estimate, radius, rows):
+def rims_out(estimate, after, radius, rows):
     shape = jax.ShapeDtypeStruct((radius, rows, estimate.shape[2]), F32)
     return pl.pallas_call(
         rims_out_kernel,
         out_shape=(shape, shape),
-        in_specs=[VMEM],
+        in_specs=[VMEM, ANY],
         out_specs=(VMEM, VMEM),
         compiler_params=pltpu.CompilerParams(vmem_limit_bytes=LIMIT),
         name="rims_out",
-    )(estimate)
-
-
-def view_out_kernel(seen, measured, taps, packed):
+    )(estimate, after)
+
+
+def blank_kernel(rows):
+    rows[...] = jnp.zeros_like(rows)
+
+
+def blank_rows(across):
+    return pl.pallas_call(
+        blank_kernel,
+        out_shape=jax.ShapeDtypeStruct((TAIL, across), F32),
+        out_specs=VMEM,
+        compiler_params=pltpu.CompilerParams(vmem_limit_bytes=LIMIT),
+        cost_estimate=pl.CostEstimate(flops=8_000_000_000, bytes_accessed=16_000_000, transcendentals=0),
+        name="blank_rows",
+    )()
+
+
+def view_out_kernel(seen, measured, taps, blank, packed):
     planes, height = measured.shape[1], measured.shape[2]
     half = half_of(lax.axis_index("view"))
     start = pl.multiple_of((height - seen) * (1 - half), 8)
     for plane in range(planes):
         packed[plane * seen : (plane + 1) * seen] = measured[0, plane, pl.ds(start, seen)]
-    packed[planes * seen :] = jnp.zeros((TAIL, packed.shape[1]), F32)
+    packed[planes * seen :] = blank[...]
     for axis in range(taps.shape[0]):
         at = planes * seen + axis
         packed[at : at + 1, : taps.shape[2]] = taps[axis]
 
 
-def view_out(measured, kernels, seen):
+def view_out(measured, lines, blank, seen):
     _, planes, _, across = measured.shape
     return pl.pallas_call(
         functools.partial(view_out_kernel, seen),
         out_shape=jax.ShapeDtypeStruct((planes * seen + TAIL, across), F32),
-        in_specs=[VMEM, VMEM],
+        in_specs=[VMEM] * 3,
         out_specs=VMEM,
         compiler_params=pltpu.CompilerParams(vmem_limit_bytes=LIMIT),
         name="view_out",
-    )(measured, kernels)
+    )(measured, lines, blank)
 
 
 def prepare_kernel(packed, taps, source, estimate, after, wide, tall, back, part, spread):
@@ -650,15 +665,16 @@
     across_pairs = [(i, i ^ 3) for i in range(views)]
 
     lines = jnp.transpose(kernels, (1, 0, 2))
-    packed = view_out(measured, lines, seen)
+    blank = blank_rows(across)
+    packed = view_out(measured, lines, blank, seen)
     swapped = lax.ppermute(packed, "view", partner)
-    to_far, to_near = rims_out(estimate, radius, rows)
+    to_far, to_near = rims_out(estimate, blank, radius, rows)
     far = lax.ppermute(to_far, "tile", far_pairs)
     near = lax.ppermute(to_near, "tile", near_pairs)
     places = slot_places(tiles, views, label_owner, label_index)
     own = prepare(False, taps, lines, estimate, places[1], rows, seen, keep)
     others = prepare(True, taps, swapped, estimate, lines, rows, seen, keep)
-    came = token_of(far.reshape(radius * rows, across), (others[4],), 8_000_000_000)
+    came = token_of(far.reshape(radius * rows, across), (others[4],), 0)
     field_own, field_other, *sends = ratio_fields(
         own, others, far, near, measured, swapped, came
     )

time: 48.2 us -> 47.1 us (0.977)
  starting transfers between devices: 30.8 us -> 30.1 us
    ppermute x4, starting transfers between devices: 11.7 us -> 10.7 us  [on_device(): lax.ppermute(send, 'tile', pairs)]
    all_to_all x1, starting transfers between devices: 4.45 us -> 3.78 us  [on_device(): lax.all_to_all(sent, ('tile', 'view'), split_axis=0, concat_axis=0, tiled...]
    all_to_all x1, waiting for transfers between devices: 2.71 us -> 2.15 us  [on_device(): lax.all_to_all(sent, ('tile', 'view'), split_axis=0, concat_axis=0, tiled...]
    ppermute x2, starting transfers between devices: 4.41 us -> 4.96 us  [on_device(): new_other.append(lax.ppermute(new_mine[part], 'view', partner))]
    ppermute x1, waiting for transfers between devices: 3.22 us -> 3.75 us  [on_device(): swapped = lax.ppermute(packed, 'view', partner)]
    unnamed x14 -> x12, local copies, waits for them, and re-layouts: 1.22 us -> 1.03 us
  transfers between devices with their start and end apart: 12 -> 12, of which waited for: 2 -> 2; matrix products, arithmetic and copies ran while one was open for 0% -> 0% of each run, Pallas kernels for 13% -> 14%
where the time goes in v12:
time: 47.1 us; the launch traced here: 46.9 us
  starting transfers between devices  30.1 us (64%)
  Pallas kernels  9 us (19%)
  waiting for transfers between devices  5.93 us (13%)
  local copies, waits for them, and re-layouts  1.03 us (2%)
  between operations  0.87 us (2%)
    ppermute x4, starting transfers between devices, on_device(): lax.ppermute(send, 'tile', pairs)  10.7 us
    ppermute x2, starting transfers between devices, on_device(): new_other.append(lax.ppermute(new_mine[part], 'view', partner))  4.96 us
    ppermute x2, starting transfers between devices, on_device(): other.append(lax.ppermute(mine[part], 'view', across_pairs))  3.95 us
    all_to_all x1, starting transfers between devices, on_device(): lax.all_to_all(sent, ('tile', 'view'), split_axis=0, concat_axis=0, tiled...  3.78 us
    ppermute x1, waiting for transfers between devices, on_device(): swapped = lax.ppermute(packed, 'view', partner)  3.75 us
    ppermute x1, starting transfers between devices, on_device(): swapped = lax.ppermute(packed, 'view', partner)  3.09 us
    ppermute x1, starting transfers between devices, on_device(): near = lax.ppermute(to_near, 'tile', near_pairs)  2.9 us
    pallas_call x2, Pallas kernels, moment_rows(): pl.pallas_call(functools.partial(moments_kernel, views, tiles * planes, p...  2.64 us
  transfers between devices with their start and end apart: 12, of which 2 were waited for; matrix products, arithmetic and copies ran while one was open for 0% of the time, Pallas kernels for 14%

profile of v12, /device:TPU:0, one launch (start us, length us, event | category | flops | bytes accessed | tf_op | source)
XLA Modules:
  0.0 46.9 jit_solution(18246708474128713847)
XLA Ops:
  0.7 0.0 copy-start
  0.7 1.0 %copy-done.2 = f32[1,8,64,256]{3,2,1,0:T(8,128)S(1)} copy-done((f32[1,8,64,256]{3,2,1,0:T(8,128)S(1)}, f32[1,8,64,256]{3,2,1,0:T(8,128)}, u32[]{:S(2)}) %copy-start.2) | copy-done | bytes 524312
  1.7 3.1 %collective-permute-start = (f32[344,256]{1,0:T(8,128)S(1)}, f32[344,256]{1,0:T(8,128)S(1)}, u32[]{:S(2)}, u32[]{:S(2)}) collective-permute-start(f32[344,256]{1,0:T(8,128)S(1)} %view_out.1), channel_id=1, source_target_pairs={{0,1},{1,0},{2,3},{3,2},{4,5},{5,4},{6,7},{7,6},{8,9},{9,8},{10,11... | collective-permute-start | bytes 1056776 | tf_op jit(solution)/shard_map/ppermute | solution.py:670
  4.8 0.7 %collective-permute-start.1 = (f32[7,48,256]{2,1,0:T(8,128)S(1)}, f32[7,48,256]{2,1,0:T(8,128)S(1)}, u32[]{:S(2)}, u32[]{:S(2)}) collective-permute-start(f32[7,48,256]{2,1,0:T(8,128)S(1)} %get-tuple-element.35), channel_id=1, source_target_pairs={{4,8},{12,16},{20,24},{8,4},{16,12},{24,20},{5,9},{13,17},{21,25},... | collective-permute-start | bytes 1032200 | tf_op jit(solution)/shard_map/ppermute | solution.py:672
  5.5 0.0 copy-start.4
  5.5 0.0 copy-start.5
  5.6 2.9 %collective-permute-start.2 = (f32[7,48,256]{2,1,0:T(8,128)S(1)}, f32[7,48,256]{2,1,0:T(8,128)S(1)}, u32[]{:S(2)}, u32[]{:S(2)}) collective-permute-start(f32[7,48,256]{2,1,0:T(8,128)S(1)} %get-tuple-element.36), channel_id=1, source_target_pairs={{0,4},{4,0},{8,12},{12,8},{16,20},{20,16},{24,28},{28,24},{1,5},{5... | collective-permute-start | bytes 1032200 | tf_op jit(solution)/shard_map/ppermute | solution.py:673
  8.5 0.2 slot_places.1
  8.7 0.6 %prepare.2 = (bf16[2,2,256,256]{3,2,1,0:T(8,128)(2,1)S(1)}, bf16[40,144]{1,0:T(8,128)(2,1)S(1)}, bf16[32,144]{1,0:T(8,128)(2,1)S(1)}, f32[8,48,256]{2,1,0:T(8,128)S(1)}, f32[16,128]{1,0:T(8,128)S(1)}) custom-call(f32[3,1,15]{2,1,0:T(1,128)S(1)} %bitcast.10, f32[8,64,256]{2,1,0:T(8,128)S(1)} %copy-done, f32[32,128]{1,0:T(8,128)S(1)} %get-tuple-element.24.after.base), custom_call_target="tpu_custom_call" | custom-call | tf_op jit(solution)/shard_map/prepare/pallas_call | solution.py:170
  9.3 3.7 %collective-permute-done.source.refs_13_ = f32[344,256]{1,0:T(8,128)S(1)} collective-permute-done((f32[344,256]{1,0:T(8,128)S(1)}, f32[344,256]{1,0:T(8,128)S(1)}, u32[]{:S(2)}, u32[]{:S(2)}) %collective-permute-start) | collective-permute-done | bytes 352288 | tf_op jit(solution)/shard_map/ppermute | solution.py:670
  13.0 0.6 %prepare.3 = (bf16[2,2,256,256]{3,2,1,0:T(8,128)(2,1)S(1)}, bf16[40,144]{1,0:T(8,128)(2,1)S(1)}, bf16[32,144]{1,0:T(8,128)(2,1)S(1)}, f32[8,48,256]{2,1,0:T(8,128)S(1)}, f32[16,128]{1,0:T(8,128)S(1)}) custom-call(f32[344,256]{1,0:T(8,128)S(1)} %collective-permute-done.source.refs_13_, f32[8,64,256]{2,1,0:T(8,128)S(1)} %copy-done, f32[3,1,15]{2,1,0:T(1,128)S(1)} %bitcast.11), custom_call_target="tpu_custom_call" | custom-call | tf_op jit(solution)/shard_map/prepare/pallas_call | solution.py:170
  13.6 0.0 collective-permute-done.1.refs_10_
  13.6 0.0 collective-permute-done.2.refs_11_
  13.7 1.8 %ratio_fields.1 = (f32[8,32,256]{2,1,0:T(8,128)S(1)}, f32[8,32,256]{2,1,0:T(8,128)S(1)}, f32[7,16,256]{2,1,0:T(8,128)S(1)}, f32[7,16,256]{2,1,0:T(8,128)S(1)}, f...) custom-call(bf16[2,2,256,256]{3,2,1,0:T(8,128)(2,1)S(1)} %get-tuple-element.27.refs_0_, ...), custom_call_target="tpu_custom_call" | custom-call | tf_op jit(solution)/shard_map/ratio_fields/pallas_call | solution.py:285
  15.5 0.0 copy-start.1
  15.5 0.8 %collective-permute-start.3 = (f32[7,16,256]{2,1,0:T(8,128)S(1)}, f32[7,16,256]{2,1,0:T(8,128)S(1)}, u32[]{:S(2)}, u32[]{:S(2)}) collective-permute-start(f32[7,16,256]{2,1,0:T(8,128)S(1)} %get-tuple-element.40), channel_id=1, source_target_pairs={{4,8},{12,16},{20,24},{8,4},{16,12},{24,20},{5,9},{13,17},{21,25},... | collective-permute-start | bytes 344072 | tf_op jit(solution)/shard_map/ppermute | solution.py:682
  16.3 3.8 %collective-permute-start.4 = (f32[7,16,256]{2,1,0:T(8,128)S(1)}, f32[7,16,256]{2,1,0:T(8,128)S(1)}, u32[]{:S(2)}, u32[]{:S(2)}) collective-permute-start(f32[7,16,256]{2,1,0:T(8,128)S(1)} %get-tuple-element.41), channel_id=1, source_target_pairs={{0,4},{4,0},{8,12},{12,8},{16,20},{20,16},{24,28},{28,24},{1,5},{5... | collective-permute-start | bytes 344072 | tf_op jit(solution)/shard_map/ppermute | solution.py:682
  20.0 0.7 %collective-permute-start.6 = (f32[7,16,256]{2,1,0:T(8,128)S(1)}, f32[7,16,256]{2,1,0:T(8,128)S(1)}, u32[]{:S(2)}, u32[]{:S(2)}) collective-permute-start(f32[7,16,256]{2,1,0:T(8,128)S(1)} %get-tuple-element.44), channel_id=1, source_target_pairs={{4,8},{12,16},{20,24},{8,4},{16,12},{24,20},{5,9},{13,17},{21,25},... | collective-permute-start | bytes 344072 | tf_op jit(solution)/shard_map/ppermute | solution.py:682
  20.7 5.5 %collective-permute-start.7 = (f32[7,16,256]{2,1,0:T(8,128)S(1)}, f32[7,16,256]{2,1,0:T(8,128)S(1)}, u32[]{:S(2)}, u32[]{:S(2)}) collective-permute-start(f32[7,16,256]{2,1,0:T(8,128)S(1)} %get-tuple-element.45), channel_id=1, source_target_pairs={{0,4},{4,0},{8,12},{12,8},{16,20},{20,16},{24,28},{28,24},{1,5},{5... | collective-permute-start | bytes 344072 | tf_op jit(solution)/shard_map/ppermute | solution.py:682
  26.2 0.3 own_planes.1
  26.5 0.0 collective-permute-done.4.near
  26.6 2.5 %collective-permute-start.5 = (f32[8,16,256]{2,1,0:T(8,128)S(1)}, f32[8,16,256]{2,1,0:T(8,128)S(1)}, u32[]{:S(2)}, u32[]{:S(2)}) collective-permute-start(f32[8,16,256]{2,1,0:T(8,128)S(1)} %add_rims.2.correction.mine), channel_id=1, source_target_pairs={{0,3},{1,2},{2,1},{3,0},{4,7},{5,6},{6,5},{7,4},{8,11},{9,10},{10,... | collective-permute-start | bytes 393224 | tf_op jit(solution)/shard_map/ppermute | solution.py:688
  29.1 0.8 %moment_rows.2.rest_0_.refs_0_ = f32[16,128]{1,0:T(8,128)S(1)} custom-call(f32[8,64,256]{2,1,0:T(8,128)S(1)} %copy-done, s32[8,64,256]{2,1,0:T(8,128)S(1)} %copy-done.1, f32[160,16]{1,0:T(8,128)S(1)} %get-tuple-element.42.picked, f32[32,128]{1,0:T(8,128)S(1)} %get-tuple-element.24.after.base, f32[8,16,256]{2,1,0:T(8,128)S(1)} %add_rims.2.correction.mine), custom_call_target="tpu_custom_call" | custom-call | tf_op jit(solution)/shard_map/moment_rows/pallas_call | solution.py:527
  30.0 1.4 %collective-permute-start.8 = (f32[8,16,256]{2,1,0:T(8,128)S(1)}, f32[8,16,256]{2,1,0:T(8,128)S(1)}, u32[]{:S(2)}, u32[]{:S(2)}) collective-permute-start(f32[8,16,256]{2,1,0:T(8,128)S(1)} %add_rims.3.correction.mine), channel_id=1, source_target_pairs={{0,3},{1,2},{2,1},{3,0},{4,7},{5,6},{6,5},{7,4},{8,11},{9,10},{10,... | collective-permute-start | bytes 393224 | tf_op jit(solution)/shard_map/ppermute | solution.py:688
  31.4 1.8 %moment_rows.3.rest_0_ = f32[32,128]{1,0:T(8,128)} custom-call(f32[8,64,256]{2,1,0:T(8,128)S(1)} %copy-done, s32[8,64,256]{2,1,0:T(8,128)S(1)} %copy-done.1, f32[160,16]{1,0:T(8,128)S(1)} %get-tuple-element.42.picked, f32[32,128]{1,0:T(8,128)S(1)} %get-tuple-element.24.after.base, f32[8,16,256]{2,1,0:T(8,128)S(1)} %add_rims.3.correction.mine, ...), custom_call_target="tpu_custom_call" | custom-call | tf_op jit(solution)/shard_map/moment_rows/pallas_call | solution.py:527
  33.2 3.8 %all-to-all-start = ((f32[32,1,128]{2,1,0:T(1,128)}), f32[32,1,128]{2,1,0:T(1,128)S(1)}, u32[]{:S(2)}, u32[]{:S(2)}) async-start(f32[32,1,128]{2,1,0:T(1,128)} %bitcast.4), calls=%async_computation | async-start | bytes 32768 | tf_op jit(solution)/shard_map/all_to_all | solution.py:691
  37.1 2.7 %collective-permute-start.9 = (f32[136,256]{1,0:T(8,128)S(1)}, f32[136,256]{1,0:T(8,128)S(1)}, u32[]{:S(2)}, u32[]{:S(2)}) collective-permute-start(f32[136,256]{1,0:T(8,128)S(1)} %update.2.source.refs_0_), channel_id=1, source_target_pairs={{0,1},{1,0},{2,3},{3,2},{4,5},{5,4},{6,7},{7,6},{8,9},{9,8},{10,11... | collective-permute-start | bytes 417800 | tf_op jit(solution)/shard_map/ppermute | solution.py:697
  39.8 2.2 %collective-permute-start.10 = (f32[128,256]{1,0:T(8,128)S(1)}, f32[128,256]{1,0:T(8,128)S(1)}, u32[]{:S(2)}, u32[]{:S(2)}) collective-permute-start(f32[128,256]{1,0:T(8,128)S(1)} %update.3.refs_1_), channel_id=1, source_target_pairs={{0,1},{1,0},{2,3},{3,2},{4,5},{5,4},{6,7},{7,6},{8,9},{9,8},{10,11... | collective-permute-start | bytes 393224 | tf_op jit(solution)/shard_map/ppermute | solution.py:697
  42.1 2.2 %all-to-all-done = f32[32,1,128]{2,1,0:T(1,128)S(1)} async-done(((f32[32,1,128]{2,1,0:T(1,128)}), f32[32,1,128]{2,1,0:T(1,128)S(1)}, u32[]{:S(2)}, u32[]{:S(2)}) %all-to-all-start) | async-done | bytes 16416 | tf_op jit(solution)/shard_map/all_to_all | solution.py:691
  44.2 1.0 %nucleus_table.1 = f32[10,128]{1,0:T(8,128)} custom-call(f32[32,128]{1,0:T(8,128)S(1)} %bitcast.8), custom_call_target="tpu_custom_call" | custom-call | flops 10000000000 | bytes 20000000 | tf_op jit(solution)/shard_map/nucleus_table/pallas_call | solution.py:570
  45.2 0.8 %begin_result.1.begun = f32[8,64,256]{2,1,0:T(8,128)} custom-call(f32[136,256]{1,0:T(8,128)S(1)} %update.2.source.refs_0_, f32[128,256]{1,0:T(8,128)S(1)} %update.3.refs_1_), custom_call_target="tpu_custom_call" | custom-call | tf_op jit(solution)/shard_map/begin_result/pallas_call | solution.py:623
  46.1 0.8 %finish.1 = f32[8,64,256]{2,1,0:T(8,128)} custom-call(f32[8,64,256]{2,1,0:T(8,128)} %begin_result.1.begun, f32[136,256]{1,0:T(8,128)S(1)} %collective-permute-done.9.refs_0_, f32[128,256]{1,0:T(8,128)S(1)} %collective-permute-done.10.refs_1_), custom_call_target="tpu_custom_call", output_to_operand_aliasing={{}: (0, {})} | custom-call | tf_op jit(solution)/shard_map/finish/pallas_call | solution.py:641
  (23 shorter events, 0.2 us)
Async XLA Ops:
  0.6 1.0 %copy-start.2 = (f32[1,8,64,256]{3,2,1,0:T(8,128)S(1)}, f32[1,8,64,256]{3,2,1,0:T(8,128)}, u32[]{:S(2)}) copy-start(f32[1,8,64,256]{3,2,1,0:T(8,128)} %refs_12_.1) | copy-start | bytes 1572868
  0.6 1.0 %copy-start.3 = (f32[1,3,15]{2,0,1:T(1,128)S(1)}, f32[1,3,15]{2,0,1:T(1,128)}, u32[]{:S(2)}) copy-start(f32[1,3,15]{2,0,1:T(1,128)} %param.8) | copy-start | bytes 544
  0.7 4.1 %copy-start = (f32[8,64,256]{2,1,0:T(8,128)S(1)}, f32[8,64,256]{2,1,0:T(8,128)}, u32[]{:S(2)}) copy-start(f32[8,64,256]{2,1,0:T(8,128)} %estimate.13) | copy-start | bytes 1572868
  1.7 11.3 %collective-permute-start = (f32[344,256]{1,0:T(8,128)S(1)}, f32[344,256]{1,0:T(8,128)S(1)}, u32[]{:S(2)}, u32[]{:S(2)}) collective-permute-start(f32[344,256]{1,0:T(8,128)S(1)} %view_out.1), channel_id=1, source_target_pairs={{0,1},{1,0},{2,3},{3,2},{4,5},{5,4},{6,7},{7,6},{8,9},{9,8},{10,11... | collective-permute-start | bytes 1056776 | tf_op jit(solution)/shard_map/ppermute | solution.py:670
  4.8 8.8 %collective-permute-start.1 = (f32[7,48,256]{2,1,0:T(8,128)S(1)}, f32[7,48,256]{2,1,0:T(8,128)S(1)}, u32[]{:S(2)}, u32[]{:S(2)}) collective-permute-start(f32[7,48,256]{2,1,0:T(8,128)S(1)} %get-tuple-element.35), channel_id=1, source_target_pairs={{4,8},{12,16},{20,24},{8,4},{16,12},{24,20},{5,9},{13,17},{21,25},... | collective-permute-start | bytes 1032200 | tf_op jit(solution)/shard_map/ppermute | solution.py:672
  5.5 2.9 %copy-start.4 = (s32[1,16,1]{1,2,0:T(1,128)S(1)}, s32[1,16,1]{1,2,0:T(1,128)}, u32[]{:S(2)}) copy-start(s32[1,16,1]{1,2,0:T(1,128)} %param.10) | copy-start | bytes 196
  5.5 2.9 %copy-start.5 = (s32[1,16]{1,0:T(1,128)S(1)}, s32[1,16]{1,0:T(1,128)}, u32[]{:S(2)}) copy-start(s32[1,16]{1,0:T(1,128)} %index_row.1) | copy-start | bytes 196
  5.6 8.1 %collective-permute-start.2 = (f32[7,48,256]{2,1,0:T(8,128)S(1)}, f32[7,48,256]{2,1,0:T(8,128)S(1)}, u32[]{:S(2)}, u32[]{:S(2)}) collective-permute-start(f32[7,48,256]{2,1,0:T(8,128)S(1)} %get-tuple-element.36), channel_id=1, source_target_pairs={{0,4},{4,0},{8,12},{12,8},{16,20},{20,16},{24,28},{28,24},{1,5},{5... | collective-permute-start | bytes 1032200 | tf_op jit(solution)/shard_map/ppermute | solution.py:673
  15.5 13.6 %copy-start.1 = (s32[8,64,256]{2,1,0:T(8,128)S(1)}, s32[8,64,256]{2,1,0:T(8,128)}, u32[]{:S(2)}) copy-start(s32[8,64,256]{2,1,0:T(8,128)} %labels.3) | copy-start | bytes 1572868
  15.5 11.0 %collective-permute-start.3 = (f32[7,16,256]{2,1,0:T(8,128)S(1)}, f32[7,16,256]{2,1,0:T(8,128)S(1)}, u32[]{:S(2)}, u32[]{:S(2)}) collective-permute-start(f32[7,16,256]{2,1,0:T(8,128)S(1)} %get-tuple-element.40), channel_id=1, source_target_pairs={{4,8},{12,16},{20,24},{8,4},{16,12},{24,20},{5,9},{13,17},{21,25},... | collective-permute-start | bytes 344072 | tf_op jit(solution)/shard_map/ppermute | solution.py:682
  16.3 10.2 %collective-permute-start.4 = (f32[7,16,256]{2,1,0:T(8,128)S(1)}, f32[7,16,256]{2,1,0:T(8,128)S(1)}, u32[]{:S(2)}, u32[]{:S(2)}) collective-permute-start(f32[7,16,256]{2,1,0:T(8,128)S(1)} %get-tuple-element.41), channel_id=1, source_target_pairs={{0,4},{4,0},{8,12},{12,8},{16,20},{20,16},{24,28},{28,24},{1,5},{5... | collective-permute-start | bytes 344072 | tf_op jit(solution)/shard_map/ppermute | solution.py:682
  20.0 9.9 %collective-permute-start.6 = (f32[7,16,256]{2,1,0:T(8,128)S(1)}, f32[7,16,256]{2,1,0:T(8,128)S(1)}, u32[]{:S(2)}, u32[]{:S(2)}) collective-permute-start(f32[7,16,256]{2,1,0:T(8,128)S(1)} %get-tuple-element.44), channel_id=1, source_target_pairs={{4,8},{12,16},{20,24},{8,4},{16,12},{24,20},{5,9},{13,17},{21,25},... | collective-permute-start | bytes 344072 | tf_op jit(solution)/shard_map/ppermute | solution.py:682
  20.7 9.3 %collective-permute-start.7 = (f32[7,16,256]{2,1,0:T(8,128)S(1)}, f32[7,16,256]{2,1,0:T(8,128)S(1)}, u32[]{:S(2)}, u32[]{:S(2)}) collective-permute-start(f32[7,16,256]{2,1,0:T(8,128)S(1)} %get-tuple-element.45), channel_id=1, source_target_pairs={{0,4},{4,0},{8,12},{12,8},{16,20},{20,16},{24,28},{28,24},{1,5},{5... | collective-permute-start | bytes 344072 | tf_op jit(solution)/shard_map/ppermute | solution.py:682
  26.6 10.5 %collective-permute-start.5 = (f32[8,16,256]{2,1,0:T(8,128)S(1)}, f32[8,16,256]{2,1,0:T(8,128)S(1)}, u32[]{:S(2)}, u32[]{:S(2)}) collective-permute-start(f32[8,16,256]{2,1,0:T(8,128)S(1)} %add_rims.2.correction.mine), channel_id=1, source_target_pairs={{0,3},{1,2},{2,1},{3,0},{4,7},{5,6},{6,5},{7,4},{8,11},{9,10},{10,... | collective-permute-start | bytes 393224 | tf_op jit(solution)/shard_map/ppermute | solution.py:688
  30.0 9.8 %collective-permute-start.8 = (f32[8,16,256]{2,1,0:T(8,128)S(1)}, f32[8,16,256]{2,1,0:T(8,128)S(1)}, u32[]{:S(2)}, u32[]{:S(2)}) collective-permute-start(f32[8,16,256]{2,1,0:T(8,128)S(1)} %add_rims.3.correction.mine), channel_id=1, source_target_pairs={{0,3},{1,2},{2,1},{3,0},{4,7},{5,6},{6,5},{7,4},{8,11},{9,10},{10,... | collective-permute-start | bytes 393224 | tf_op jit(solution)/shard_map/ppermute | solution.py:688
  33.2 11.0 %all-to-all-start = ((f32[32,1,128]{2,1,0:T(1,128)}), f32[32,1,128]{2,1,0:T(1,128)S(1)}, u32[]{:S(2)}, u32[]{:S(2)}) async-start(f32[32,1,128]{2,1,0:T(1,128)} %bitcast.4), calls=%async_computation | async-start | bytes 32768 | tf_op jit(solution)/shard_map/all_to_all | solution.py:691
  37.1 9.0 %collective-permute-start.9 = (f32[136,256]{1,0:T(8,128)S(1)}, f32[136,256]{1,0:T(8,128)S(1)}, u32[]{:S(2)}, u32[]{:S(2)}) collective-permute-start(f32[136,256]{1,0:T(8,128)S(1)} %update.2.source.refs_0_), channel_id=1, source_target_pairs={{0,1},{1,0},{2,3},{3,2},{4,5},{5,4},{6,7},{7,6},{8,9},{9,8},{10,11... | collective-permute-start | bytes 417800 | tf_op jit(solution)/shard_map/ppermute | solution.py:697
  39.8 6.2 %collective-permute-start.10 = (f32[128,256]{1,0:T(8,128)S(1)}, f32[128,256]{1,0:T(8,128)S(1)}, u32[]{:S(2)}, u32[]{:S(2)}) collective-permute-start(f32[128,256]{1,0:T(8,128)S(1)} %update.3.refs_1_), channel_id=1, source_target_pairs={{0,1},{1,0},{2,3},{3,2},{4,5},{5,4},{6,7},{7,6},{8,9},{9,8},{10,11... | collective-permute-start | bytes 393224 | tf_op jit(solution)/shard_map/ppermute | solution.py:697

commit v13 on v12

--- a/solution.py
+++ b/solution.py
@@ -359,21 +359,18 @@
     result = rest[-1]
     half = half_of(lax.axis_index("view"))
     start = pl.multiple_of(size * (PARTS * half + part), 8)
-    for plane in range(planes):
-        held = estimate[plane, pl.ds(start, size)]
-        at = slice(plane * size, (plane + 1) * size)
-        result[at] = held * (mine[plane] + other[plane]) * (1.0 / views)
-    spare = result.shape[0] - planes * size
-    if spare:
-        result[planes * size :] = jnp.zeros((spare, across), F32)
+    held = estimate[:, pl.ds(start, size)]
+    result[:planes] = held * (mine[...] + other[...]) * (1.0 / views)
+    if result.shape[0] > planes:
+        result[planes:] = jnp.zeros((result.shape[0] - planes, size, across), F32)
 
 
 def update(views, part, estimate, mine, other, after):
     planes, size, across = mine.shape
-    spare = 8 * (PARTS - 1 - part)
+    count = planes + PARTS - 1 - part
     return pl.pallas_call(
         functools.partial(update_kernel, views, part),
-        out_shape=jax.ShapeDtypeStruct((planes * size + spare, across), F32),
+        out_shape=jax.ShapeDtypeStruct((count, size, across), F32),
         in_specs=[VMEM] * 3 + [ANY] * len(after),
         out_specs=VMEM,
         compiler_params=pltpu.CompilerParams(vmem_limit_bytes=LIMIT),
@@ -578,76 +575,71 @@
     )(rows)
 
 
-def stores(pieces, sources, whole, half, sems):
-    keep = whole.shape[1] // 2
-    copies = []
-    for number, ((first, size), source) in enumerate(zip(pieces, sources)):
-        start = pl.multiple_of(keep * half + first, 8)
-        for plane in range(whole.shape[0]):
-            copies.append(
-                pltpu.make_async_copy(
-                    source.at[pl.ds(plane * size, size)],
-                    whole.at[plane, pl.ds(start, size)],
-                    sems.at[number, plane],
-                )
-            )
-    for copy in copies:
-        copy.start()
-    return copies
+def store_of(source, whole, half, part, sem):
+    planes, size = whole.shape[0], source.shape[1]
+    start = pl.multiple_of(size * (PARTS * half + part), 8)
+    return pltpu.make_async_copy(
+        source.at[pl.ds(0, planes)], whole.at[:, pl.ds(start, size)], sem
+    )
 
 
 def token_kernel(source, *rest):
     token = rest[-1]
-    token[...] = source[:8, :LANES]
-
-
-def token_of(source, after=(), flops=0):
+    token[...] = source[0, :8, :LANES]
+
+
+def token_of(source, after=()):
     return pl.pallas_call(
         token_kernel,
         out_shape=jax.ShapeDtypeStruct((8, LANES), F32),
         in_specs=[VMEM] + [ANY] * len(after),
         out_specs=VMEM,
         compiler_params=pltpu.CompilerParams(vmem_limit_bytes=LIMIT),
-        cost_estimate=pl.CostEstimate(flops=flops, bytes_accessed=flops // 500, transcendentals=0),
         name="token_of",
     )(source, *after)
 
 
-def begin_kernel(pieces, *refs):
+def begin_kernel(*refs):
     sources, (whole, sems) = refs[:-2], refs[-2:]
-    for copy in stores(pieces, sources, whole, half_of(lax.axis_index("view")), sems):
+    half = half_of(lax.axis_index("view"))
+    copies = [
+        store_of(source, whole, half, part, sems.at[part]) for part, source in enumerate(sources)
+    ]
+    for copy in copies:
+        copy.start()
+    for copy in copies:
         copy.wait()
 
 
-def begin_result(pieces, shape, mine):
-    return pl.pallas_call(
-        functools.partial(begin_kernel, pieces),
+def begin_result(shape, mine):
+    return pl.pallas_call(
+        begin_kernel,
         out_shape=jax.ShapeDtypeStruct(shape, F32),
         in_specs=[VMEM] * len(mine),
         out_specs=ANY,
-        scratch_shapes=[pltpu.SemaphoreType.DMA((len(pieces), shape[0]))],
+        scratch_shapes=[pltpu.SemaphoreType.DMA((len(mine),))],
         compiler_params=pltpu.CompilerParams(vmem_limit_bytes=LIMIT),
         name="begin_result",
     )(*mine)
 
 
-def finish_kernel(pieces, begun, *refs):
-    others, (whole, sems) = refs[:-2], refs[-2:]
-    for copy in stores(pieces, others, whole, 1 - half_of(lax.axis_index("view")), sems):
-        copy.wait()
-
-
-def finish(pieces, begun, others):
-    return pl.pallas_call(
-        functools.partial(finish_kernel, pieces),
+def store_kernel(part, begun, other, whole, sem):
+    copy = store_of(other, whole, 1 - half_of(lax.axis_index("view")), part, sem)
+    copy.start()
+    copy.wait()
+
+
+def store_part(part, begun, other):
+    return pl.pallas_call(
+        functools.partial(store_kernel, part),
         out_shape=jax.ShapeDtypeStruct(begun.shape, F32),
-        in_specs=[ANY] + [VMEM] * len(others),
+        in_specs=[ANY, VMEM],
         out_specs=ANY,
         input_output_aliases={0: 0},
-        scratch_shapes=[pltpu.SemaphoreType.DMA((len(pieces), begun.shape[0]))],
-        compiler_params=pltpu.CompilerParams(vmem_limit_bytes=LIMIT),
-        name="finish",
-    )(begun, *others)
+        scratch_shapes=[pltpu.SemaphoreType.DMA],
+        compiler_params=pltpu.CompilerParams(vmem_limit_bytes=LIMIT),
+        name="store_part",
+    )(begun, other)
 
 
 def on_device(estimate, measured, kernels, labels, label_owner, label_index):
@@ -674,7 +666,7 @@
     places = slot_places(tiles, views, label_owner, label_index)
     own = prepare(False, taps, lines, estimate, places[1], rows, seen, keep)
     others = prepare(True, taps, swapped, estimate, lines, rows, seen, keep)
-    came = token_of(far.reshape(radius * rows, across), (others[4],), 0)
+    came = token_of(far, (others[4],))
     field_own, field_other, *sends = ratio_fields(
         own, others, far, near, measured, swapped, came
     )
@@ -689,8 +681,6 @@
         sums = [moment_rows(views, tiles, part, estimate, mine[part], labels, places, sums)]
     sent = sums[0]
     got = lax.all_to_all(sent, ("tile", "view"), split_axis=0, concat_axis=0, tiled=True)
-    size = keep // PARTS
-    pieces = [(part * size, size) for part in range(PARTS)]
     new_mine, new_other, token = [], [], [sent]
     for part in range(PARTS):
         new_mine.append(update(views, part, estimate, mine[part], other[part], token))
@@ -698,8 +688,10 @@
         token = [token_of(new_mine[part])]
     scale = label_index.shape[1] / (planes * height * across)
     moments = nucleus_table(across, scale, got)
-    begun = begin_result(pieces, estimate.shape, new_mine)
-    return finish(pieces, begun, new_other), moments
+    whole = begin_result(estimate.shape, new_mine)
+    for part in range(PARTS):
+        whole = store_part(part, whole, new_other[part])
+    return whole, moments
 
 
 def solution(mesh):

time: 47.1 us -> 47.5 us (level)
    pallas_call x2 -> x3, Pallas kernels: 1.67 us -> 2.07 us  [the longest x2 1.36 us: store_part(): pl.pallas_call(functools.partial(store_kernel, part), out_shape=jax.Shape...]
  transfers between devices with their start and end apart: 12 -> 12, of which waited for: 2 -> 2; matrix products, arithmetic and copies ran while one was open for 0% -> 0% of each run, Pallas kernels for 14% -> 15%
where the time goes in v13:
time: 47.5 us; the launch traced here: 47.3 us
  starting transfers between devices  30.1 us (63%)
  Pallas kernels  9.4 us (20%)
  waiting for transfers between devices  5.92 us (12%)
  local copies, waits for them, and re-layouts  1.03 us (2%)
  between operations  0.88 us (2%)
    ppermute x4, starting transfers between devices, on_device(): lax.ppermute(send, 'tile', pairs)  10.7 us
    ppermute x2, starting transfers between devices, on_device(): new_other.append(lax.ppermute(new_mine[part], 'view', partner))  4.97 us
    ppermute x2, starting transfers between devices, on_device(): other.append(lax.ppermute(mine[part], 'view', across_pairs))  3.95 us
    all_to_all x1, starting transfers between devices, on_device(): lax.all_to_all(sent, ('tile', 'view'), split_axis=0, concat_axis=0, tiled...  3.77 us
    ppermute x1, waiting for transfers between devices, on_device(): swapped = lax.ppermute(packed, 'view', partner)  3.75 us
    ppermute x1, starting transfers between devices, on_device(): swapped = lax.ppermute(packed, 'view', partner)  3.09 us
    ppermute x1, starting transfers between devices, on_device(): near = lax.ppermute(to_near, 'tile', near_pairs)  2.9 us
    pallas_call x2, Pallas kernels, moment_rows(): pl.pallas_call(functools.partial(moments_kernel, views, tiles * planes, p...  2.63 us
  transfers between devices with their start and end apart: 12, of which 2 were waited for; matrix products, arithmetic and copies ran while one was open for 0% of the time, Pallas kernels for 15%

profile of v13, /device:TPU:0, one launch (start us, length us, event | category | flops | bytes accessed | tf_op | source)
XLA Modules:
  0.0 47.3 jit_solution(12410308826318859725)
XLA Ops:
  0.7 0.0 copy-start
  0.7 1.0 %copy-done.2 = f32[1,8,64,256]{3,2,1,0:T(8,128)S(1)} copy-done((f32[1,8,64,256]{3,2,1,0:T(8,128)S(1)}, f32[1,8,64,256]{3,2,1,0:T(8,128)}, u32[]{:S(2)}) %copy-start.2) | copy-done | bytes 524312
  1.7 3.1 %collective-permute-start = (f32[344,256]{1,0:T(8,128)S(1)}, f32[344,256]{1,0:T(8,128)S(1)}, u32[]{:S(2)}, u32[]{:S(2)}) collective-permute-start(f32[344,256]{1,0:T(8,128)S(1)} %view_out.1), channel_id=1, source_target_pairs={{0,1},{1,0},{2,3},{3,2},{4,5},{5,4},{6,7},{7,6},{8,9},{9,8},{10,11... | collective-permute-start | bytes 1056776 | tf_op jit(solution)/shard_map/ppermute | solution.py:662
  4.8 0.7 %collective-permute-start.1 = (f32[7,48,256]{2,1,0:T(8,128)S(1)}, f32[7,48,256]{2,1,0:T(8,128)S(1)}, u32[]{:S(2)}, u32[]{:S(2)}) collective-permute-start(f32[7,48,256]{2,1,0:T(8,128)S(1)} %get-tuple-element.35), channel_id=1, source_target_pairs={{4,8},{12,16},{20,24},{8,4},{16,12},{24,20},{5,9},{13,17},{21,25},... | collective-permute-start | bytes 1032200 | tf_op jit(solution)/shard_map/ppermute | solution.py:664
  5.5 0.0 copy-start.4
  5.5 0.0 copy-start.5
  5.6 2.9 %collective-permute-start.2 = (f32[7,48,256]{2,1,0:T(8,128)S(1)}, f32[7,48,256]{2,1,0:T(8,128)S(1)}, u32[]{:S(2)}, u32[]{:S(2)}) collective-permute-start(f32[7,48,256]{2,1,0:T(8,128)S(1)} %get-tuple-element.36), channel_id=1, source_target_pairs={{0,4},{4,0},{8,12},{12,8},{16,20},{20,16},{24,28},{28,24},{1,5},{5... | collective-permute-start | bytes 1032200 | tf_op jit(solution)/shard_map/ppermute | solution.py:665
  8.5 0.2 slot_places.1
  8.7 0.6 %prepare.2 = (bf16[2,2,256,256]{3,2,1,0:T(8,128)(2,1)S(1)}, bf16[40,144]{1,0:T(8,128)(2,1)S(1)}, bf16[32,144]{1,0:T(8,128)(2,1)S(1)}, f32[8,48,256]{2,1,0:T(8,128)S(1)}, f32[16,128]{1,0:T(8,128)S(1)}) custom-call(f32[3,1,15]{2,1,0:T(1,128)S(1)} %bitcast.8, f32[8,64,256]{2,1,0:T(8,128)S(1)} %copy-done, f32[32,128]{1,0:T(8,128)S(1)} %get-tuple-element.24.after.base), custom_call_target="tpu_custom_call" | custom-call | tf_op jit(solution)/shard_map/prepare/pallas_call | solution.py:170
  9.3 3.7 %collective-permute-done.source.refs_13_ = f32[344,256]{1,0:T(8,128)S(1)} collective-permute-done((f32[344,256]{1,0:T(8,128)S(1)}, f32[344,256]{1,0:T(8,128)S(1)}, u32[]{:S(2)}, u32[]{:S(2)}) %collective-permute-start) | collective-permute-done | bytes 352288 | tf_op jit(solution)/shard_map/ppermute | solution.py:662
  13.0 0.6 %prepare.3 = (bf16[2,2,256,256]{3,2,1,0:T(8,128)(2,1)S(1)}, bf16[40,144]{1,0:T(8,128)(2,1)S(1)}, bf16[32,144]{1,0:T(8,128)(2,1)S(1)}, f32[8,48,256]{2,1,0:T(8,128)S(1)}, f32[16,128]{1,0:T(8,128)S(1)}) custom-call(f32[344,256]{1,0:T(8,128)S(1)} %collective-permute-done.source.refs_13_, f32[8,64,256]{2,1,0:T(8,128)S(1)} %copy-done, f32[3,1,15]{2,1,0:T(1,128)S(1)} %bitcast.9), custom_call_target="tpu_custom_call" | custom-call | tf_op jit(solution)/shard_map/prepare/pallas_call | solution.py:170
  13.7 1.8 %ratio_fields.1 = (f32[8,32,256]{2,1,0:T(8,128)S(1)}, f32[8,32,256]{2,1,0:T(8,128)S(1)}, f32[7,16,256]{2,1,0:T(8,128)S(1)}, f32[7,16,256]{2,1,0:T(8,128)S(1)}, f...) custom-call(bf16[2,2,256,256]{3,2,1,0:T(8,128)(2,1)S(1)} %get-tuple-element.27.refs_0_, ...), custom_call_target="tpu_custom_call" | custom-call | tf_op jit(solution)/shard_map/ratio_fields/pallas_call | solution.py:285
  15.5 0.0 copy-start.1
  15.5 0.8 %collective-permute-start.3 = (f32[7,16,256]{2,1,0:T(8,128)S(1)}, f32[7,16,256]{2,1,0:T(8,128)S(1)}, u32[]{:S(2)}, u32[]{:S(2)}) collective-permute-start(f32[7,16,256]{2,1,0:T(8,128)S(1)} %get-tuple-element.40), channel_id=1, source_target_pairs={{4,8},{12,16},{20,24},{8,4},{16,12},{24,20},{5,9},{13,17},{21,25},... | collective-permute-start | bytes 344072 | tf_op jit(solution)/shard_map/ppermute | solution.py:674
  16.3 3.7 %collective-permute-start.4 = (f32[7,16,256]{2,1,0:T(8,128)S(1)}, f32[7,16,256]{2,1,0:T(8,128)S(1)}, u32[]{:S(2)}, u32[]{:S(2)}) collective-permute-start(f32[7,16,256]{2,1,0:T(8,128)S(1)} %get-tuple-element.41), channel_id=1, source_target_pairs={{0,4},{4,0},{8,12},{12,8},{16,20},{20,16},{24,28},{28,24},{1,5},{5... | collective-permute-start | bytes 344072 | tf_op jit(solution)/shard_map/ppermute | solution.py:674
  20.0 0.7 %collective-permute-start.6 = (f32[7,16,256]{2,1,0:T(8,128)S(1)}, f32[7,16,256]{2,1,0:T(8,128)S(1)}, u32[]{:S(2)}, u32[]{:S(2)}) collective-permute-start(f32[7,16,256]{2,1,0:T(8,128)S(1)} %get-tuple-element.44), channel_id=1, source_target_pairs={{4,8},{12,16},{20,24},{8,4},{16,12},{24,20},{5,9},{13,17},{21,25},... | collective-permute-start | bytes 344072 | tf_op jit(solution)/shard_map/ppermute | solution.py:674
  20.7 5.5 %collective-permute-start.7 = (f32[7,16,256]{2,1,0:T(8,128)S(1)}, f32[7,16,256]{2,1,0:T(8,128)S(1)}, u32[]{:S(2)}, u32[]{:S(2)}) collective-permute-start(f32[7,16,256]{2,1,0:T(8,128)S(1)} %get-tuple-element.45), channel_id=1, source_target_pairs={{0,4},{4,0},{8,12},{12,8},{16,20},{20,16},{24,28},{28,24},{1,5},{5... | collective-permute-start | bytes 344072 | tf_op jit(solution)/shard_map/ppermute | solution.py:674
  26.2 0.3 own_planes.1
  26.6 2.5 %collective-permute-start.5 = (f32[8,16,256]{2,1,0:T(8,128)S(1)}, f32[8,16,256]{2,1,0:T(8,128)S(1)}, u32[]{:S(2)}, u32[]{:S(2)}) collective-permute-start(f32[8,16,256]{2,1,0:T(8,128)S(1)} %add_rims.2.correction.mine), channel_id=1, source_target_pairs={{0,3},{1,2},{2,1},{3,0},{4,7},{5,6},{6,5},{7,4},{8,11},{9,10},{10,... | collective-permute-start | bytes 393224 | tf_op jit(solution)/shard_map/ppermute | solution.py:680
  29.1 0.8 %moment_rows.2.rest_0_.refs_0_ = f32[16,128]{1,0:T(8,128)S(1)} custom-call(f32[8,64,256]{2,1,0:T(8,128)S(1)} %copy-done, s32[8,64,256]{2,1,0:T(8,128)S(1)} %copy-done.1, f32[160,16]{1,0:T(8,128)S(1)} %get-tuple-element.42.picked, f32[32,128]{1,0:T(8,128)S(1)} %get-tuple-element.24.after.base, f32[8,16,256]{2,1,0:T(8,128)S(1)} %add_rims.2.correction.mine), custom_call_target="tpu_custom_call" | custom-call | tf_op jit(solution)/shard_map/moment_rows/pallas_call | solution.py:524
  30.0 0.0 collective-permute-done.7.near
  30.0 1.4 %collective-permute-start.8 = (f32[8,16,256]{2,1,0:T(8,128)S(1)}, f32[8,16,256]{2,1,0:T(8,128)S(1)}, u32[]{:S(2)}, u32[]{:S(2)}) collective-permute-start(f32[8,16,256]{2,1,0:T(8,128)S(1)} %add_rims.3.correction.mine), channel_id=1, source_target_pairs={{0,3},{1,2},{2,1},{3,0},{4,7},{5,6},{6,5},{7,4},{8,11},{9,10},{10,... | collective-permute-start | bytes 393224 | tf_op jit(solution)/shard_map/ppermute | solution.py:680
  31.4 1.8 %moment_rows.3.rest_0_ = f32[32,128]{1,0:T(8,128)} custom-call(f32[8,64,256]{2,1,0:T(8,128)S(1)} %copy-done, s32[8,64,256]{2,1,0:T(8,128)S(1)} %copy-done.1, f32[160,16]{1,0:T(8,128)S(1)} %get-tuple-element.42.picked, f32[32,128]{1,0:T(8,128)S(1)} %get-tuple-element.24.after.base, f32[8,16,256]{2,1,0:T(8,128)S(1)} %add_rims.3.correction.mine, ...), custom_call_target="tpu_custom_call" | custom-call | tf_op jit(solution)/shard_map/moment_rows/pallas_call | solution.py:524
  33.2 3.8 %all-to-all-start = ((f32[32,1,128]{2,1,0:T(1,128)}), f32[32,1,128]{2,1,0:T(1,128)S(1)}, u32[]{:S(2)}, u32[]{:S(2)}) async-start(f32[32,1,128]{2,1,0:T(1,128)} %bitcast.3), calls=%async_computation | async-start | bytes 32768 | tf_op jit(solution)/shard_map/all_to_all | solution.py:683
  37.1 2.7 %collective-permute-start.9 = (f32[9,16,256]{2,1,0:T(8,128)S(1)}, f32[9,16,256]{2,1,0:T(8,128)S(1)}, u32[]{:S(2)}, u32[]{:S(2)}) collective-permute-start(f32[9,16,256]{2,1,0:T(8,128)S(1)} %update.2.source.refs_0_), channel_id=1, source_target_pairs={{0,1},{1,0},{2,3},{3,2},{4,5},{5,4},{6,7},{7,6},{8,9},{9,8},{10,11... | collective-permute-start | bytes 442376 | tf_op jit(solution)/shard_map/ppermute | solution.py:687
  39.8 2.2 %collective-permute-start.10 = (f32[8,16,256]{2,1,0:T(8,128)S(1)}, f32[8,16,256]{2,1,0:T(8,128)S(1)}, u32[]{:S(2)}, u32[]{:S(2)}) collective-permute-start(f32[8,16,256]{2,1,0:T(8,128)S(1)} %update.3.refs_1_), channel_id=1, source_target_pairs={{0,1},{1,0},{2,3},{3,2},{4,5},{5,4},{6,7},{7,6},{8,9},{9,8},{10,11... | collective-permute-start | bytes 393224 | tf_op jit(solution)/shard_map/ppermute | solution.py:687
  42.1 2.1 %all-to-all-done = f32[32,1,128]{2,1,0:T(1,128)S(1)} async-done(((f32[32,1,128]{2,1,0:T(1,128)}), f32[32,1,128]{2,1,0:T(1,128)S(1)}, u32[]{:S(2)}, u32[]{:S(2)}) %all-to-all-start) | async-done | bytes 16416 | tf_op jit(solution)/shard_map/all_to_all | solution.py:683
  44.2 1.0 %nucleus_table.1 = f32[10,128]{1,0:T(8,128)} custom-call(f32[32,128]{1,0:T(8,128)S(1)} %bitcast.6), custom_call_target="tpu_custom_call" | custom-call | flops 10000000000 | bytes 20000000 | tf_op jit(solution)/shard_map/nucleus_table/pallas_call | solution.py:567
  45.2 0.7 %begin_result.1.begun = f32[8,64,256]{2,1,0:T(8,128)} custom-call(f32[9,16,256]{2,1,0:T(8,128)S(1)} %update.2.source.refs_0_, f32[8,16,256]{2,1,0:T(8,128)S(1)} %update.3.refs_1_), custom_call_target="tpu_custom_call" | custom-call | tf_op jit(solution)/shard_map/begin_result/pallas_call | solution.py:615
  45.9 0.0 collective-permute-done.9.other
  46.0 0.7 %store_part.2.begun = f32[8,64,256]{2,1,0:T(8,128)} custom-call(f32[8,64,256]{2,1,0:T(8,128)} %begin_result.1.begun, f32[9,16,256]{2,1,0:T(8,128)S(1)} %collective-permute-done.9.other), custom_call_target="tpu_custom_call", output_to_operand_aliasing={{}: (0, {})} | custom-call | tf_op jit(solution)/shard_map/store_part/pallas_call | solution.py:633
  46.6 0.7 %store_part.3 = f32[8,64,256]{2,1,0:T(8,128)} custom-call(f32[8,64,256]{2,1,0:T(8,128)} %store_part.2.begun, f32[8,16,256]{2,1,0:T(8,128)S(1)} %collective-permute-done.10.other), custom_call_target="tpu_custom_call", output_to_operand_aliasing={{}: (0, {})} | custom-call | tf_op jit(solution)/shard_map/store_part/pallas_call | solution.py:633
  (24 shorter events, 0.2 us)
Async XLA Ops:
  0.6 1.0 %copy-start.2 = (f32[1,8,64,256]{3,2,1,0:T(8,128)S(1)}, f32[1,8,64,256]{3,2,1,0:T(8,128)}, u32[]{:S(2)}) copy-start(f32[1,8,64,256]{3,2,1,0:T(8,128)} %refs_12_.1) | copy-start | bytes 1572868
  0.6 1.0 %copy-start.3 = (f32[1,3,15]{2,0,1:T(1,128)S(1)}, f32[1,3,15]{2,0,1:T(1,128)}, u32[]{:S(2)}) copy-start(f32[1,3,15]{2,0,1:T(1,128)} %param.8) | copy-start | bytes 544
  0.7 4.1 %copy-start = (f32[8,64,256]{2,1,0:T(8,128)S(1)}, f32[8,64,256]{2,1,0:T(8,128)}, u32[]{:S(2)}) copy-start(f32[8,64,256]{2,1,0:T(8,128)} %estimate.13) | copy-start | bytes 1572868
  1.7 11.3 %collective-permute-start = (f32[344,256]{1,0:T(8,128)S(1)}, f32[344,256]{1,0:T(8,128)S(1)}, u32[]{:S(2)}, u32[]{:S(2)}) collective-permute-start(f32[344,256]{1,0:T(8,128)S(1)} %view_out.1), channel_id=1, source_target_pairs={{0,1},{1,0},{2,3},{3,2},{4,5},{5,4},{6,7},{7,6},{8,9},{9,8},{10,11... | collective-permute-start | bytes 1056776 | tf_op jit(solution)/shard_map/ppermute | solution.py:662
  4.8 8.8 %collective-permute-start.1 = (f32[7,48,256]{2,1,0:T(8,128)S(1)}, f32[7,48,256]{2,1,0:T(8,128)S(1)}, u32[]{:S(2)}, u32[]{:S(2)}) collective-permute-start(f32[7,48,256]{2,1,0:T(8,128)S(1)} %get-tuple-element.35), channel_id=1, source_target_pairs={{4,8},{12,16},{20,24},{8,4},{16,12},{24,20},{5,9},{13,17},{21,25},... | collective-permute-start | bytes 1032200 | tf_op jit(solution)/shard_map/ppermute | solution.py:664
  5.5 2.9 %copy-start.4 = (s32[1,16,1]{1,2,0:T(1,128)S(1)}, s32[1,16,1]{1,2,0:T(1,128)}, u32[]{:S(2)}) copy-start(s32[1,16,1]{1,2,0:T(1,128)} %param.10) | copy-start | bytes 196
  5.5 2.9 %copy-start.5 = (s32[1,16]{1,0:T(1,128)S(1)}, s32[1,16]{1,0:T(1,128)}, u32[]{:S(2)}) copy-start(s32[1,16]{1,0:T(1,128)} %index_row.1) | copy-start | bytes 196
  5.6 8.1 %collective-permute-start.2 = (f32[7,48,256]{2,1,0:T(8,128)S(1)}, f32[7,48,256]{2,1,0:T(8,128)S(1)}, u32[]{:S(2)}, u32[]{:S(2)}) collective-permute-start(f32[7,48,256]{2,1,0:T(8,128)S(1)} %get-tuple-element.36), channel_id=1, source_target_pairs={{0,4},{4,0},{8,12},{12,8},{16,20},{20,16},{24,28},{28,24},{1,5},{5... | collective-permute-start | bytes 1032200 | tf_op jit(solution)/shard_map/ppermute | solution.py:665
  15.5 13.6 %copy-start.1 = (s32[8,64,256]{2,1,0:T(8,128)S(1)}, s32[8,64,256]{2,1,0:T(8,128)}, u32[]{:S(2)}) copy-start(s32[8,64,256]{2,1,0:T(8,128)} %labels.3) | copy-start | bytes 1572868
  15.5 11.0 %collective-permute-start.3 = (f32[7,16,256]{2,1,0:T(8,128)S(1)}, f32[7,16,256]{2,1,0:T(8,128)S(1)}, u32[]{:S(2)}, u32[]{:S(2)}) collective-permute-start(f32[7,16,256]{2,1,0:T(8,128)S(1)} %get-tuple-element.40), channel_id=1, source_target_pairs={{4,8},{12,16},{20,24},{8,4},{16,12},{24,20},{5,9},{13,17},{21,25},... | collective-permute-start | bytes 344072 | tf_op jit(solution)/shard_map/ppermute | solution.py:674
  16.3 10.2 %collective-permute-start.4 = (f32[7,16,256]{2,1,0:T(8,128)S(1)}, f32[7,16,256]{2,1,0:T(8,128)S(1)}, u32[]{:S(2)}, u32[]{:S(2)}) collective-permute-start(f32[7,16,256]{2,1,0:T(8,128)S(1)} %get-tuple-element.41), channel_id=1, source_target_pairs={{0,4},{4,0},{8,12},{12,8},{16,20},{20,16},{24,28},{28,24},{1,5},{5... | collective-permute-start | bytes 344072 | tf_op jit(solution)/shard_map/ppermute | solution.py:674
  20.0 9.9 %collective-permute-start.6 = (f32[7,16,256]{2,1,0:T(8,128)S(1)}, f32[7,16,256]{2,1,0:T(8,128)S(1)}, u32[]{:S(2)}, u32[]{:S(2)}) collective-permute-start(f32[7,16,256]{2,1,0:T(8,128)S(1)} %get-tuple-element.44), channel_id=1, source_target_pairs={{4,8},{12,16},{20,24},{8,4},{16,12},{24,20},{5,9},{13,17},{21,25},... | collective-permute-start | bytes 344072 | tf_op jit(solution)/shard_map/ppermute | solution.py:674
  20.7 9.3 %collective-permute-start.7 = (f32[7,16,256]{2,1,0:T(8,128)S(1)}, f32[7,16,256]{2,1,0:T(8,128)S(1)}, u32[]{:S(2)}, u32[]{:S(2)}) collective-permute-start(f32[7,16,256]{2,1,0:T(8,128)S(1)} %get-tuple-element.45), channel_id=1, source_target_pairs={{0,4},{4,0},{8,12},{12,8},{16,20},{20,16},{24,28},{28,24},{1,5},{5... | collective-permute-start | bytes 344072 | tf_op jit(solution)/shard_map/ppermute | solution.py:674
  26.6 10.4 %collective-permute-start.5 = (f32[8,16,256]{2,1,0:T(8,128)S(1)}, f32[8,16,256]{2,1,0:T(8,128)S(1)}, u32[]{:S(2)}, u32[]{:S(2)}) collective-permute-start(f32[8,16,256]{2,1,0:T(8,128)S(1)} %add_rims.2.correction.mine), channel_id=1, source_target_pairs={{0,3},{1,2},{2,1},{3,0},{4,7},{5,6},{6,5},{7,4},{8,11},{9,10},{10,... | collective-permute-start | bytes 393224 | tf_op jit(solution)/shard_map/ppermute | solution.py:680
  30.0 9.8 %collective-permute-start.8 = (f32[8,16,256]{2,1,0:T(8,128)S(1)}, f32[8,16,256]{2,1,0:T(8,128)S(1)}, u32[]{:S(2)}, u32[]{:S(2)}) collective-permute-start(f32[8,16,256]{2,1,0:T(8,128)S(1)} %add_rims.3.correction.mine), channel_id=1, source_target_pairs={{0,3},{1,2},{2,1},{3,0},{4,7},{5,6},{6,5},{7,4},{8,11},{9,10},{10,... | collective-permute-start | bytes 393224 | tf_op jit(solution)/shard_map/ppermute | solution.py:680
  33.2 11.0 %all-to-all-start = ((f32[32,1,128]{2,1,0:T(1,128)}), f32[32,1,128]{2,1,0:T(1,128)S(1)}, u32[]{:S(2)}, u32[]{:S(2)}) async-start(f32[32,1,128]{2,1,0:T(1,128)} %bitcast.3), calls=%async_computation | async-start | bytes 32768 | tf_op jit(solution)/shard_map/all_to_all | solution.py:683
  37.1 8.9 %collective-permute-start.9 = (f32[9,16,256]{2,1,0:T(8,128)S(1)}, f32[9,16,256]{2,1,0:T(8,128)S(1)}, u32[]{:S(2)}, u32[]{:S(2)}) collective-permute-start(f32[9,16,256]{2,1,0:T(8,128)S(1)} %update.2.source.refs_0_), channel_id=1, source_target_pairs={{0,1},{1,0},{2,3},{3,2},{4,5},{5,4},{6,7},{7,6},{8,9},{9,8},{10,11... | collective-permute-start | bytes 442376 | tf_op jit(solution)/shard_map/ppermute | solution.py:687
  39.8 6.8 %collective-permute-start.10 = (f32[8,16,256]{2,1,0:T(8,128)S(1)}, f32[8,16,256]{2,1,0:T(8,128)S(1)}, u32[]{:S(2)}, u32[]{:S(2)}) collective-permute-start(f32[8,16,256]{2,1,0:T(8,128)S(1)} %update.3.refs_1_), channel_id=1, source_target_pairs={{0,1},{1,0},{2,3},{3,2},{4,5},{5,4},{6,7},{7,6},{8,9},{9,8},{10,11... | collective-permute-start | bytes 393224 | tf_op jit(solution)/shard_map/ppermute | solution.py:687

commit v14 on v13

--- a/solution.py
+++ b/solution.py
@@ -22,6 +22,12 @@
 LIMIT = 32 * 1024 * 1024
 
 
+def told(billions):
+    return pl.CostEstimate(
+        flops=billions * 10**9, bytes_accessed=2 * billions * 10**6, transcendentals=0
+    )
+
+
 def half_of(view):
     return (view ^ (view >> 1)) & 1
 
@@ -90,7 +96,7 @@
         out_shape=jax.ShapeDtypeStruct((TAIL, across), F32),
         out_specs=VMEM,
         compiler_params=pltpu.CompilerParams(vmem_limit_bytes=LIMIT),
-        cost_estimate=pl.CostEstimate(flops=8_000_000_000, bytes_accessed=16_000_000, transcendentals=0),
+        cost_estimate=told(8),
         name="blank_rows",
     )()
 
@@ -187,115 +193,110 @@
     return [jnp.broadcast_to(spread[step : step + 1, :], (16, LANES)) for step in range(taps)]
 
 
-def fields_kernel(*refs):
-    sets, (far, near, measured, swapped), refs = (refs[:5], refs[5:10]), refs[10:14], refs[15:]
-    fields, sends, (blur_hi, blur_lo, plane_hi, plane_lo) = refs[:2], refs[2:-4], refs[-4:]
-    planes = sets[0][3].shape[0]
+def view_kernel(first, *refs):
+    wide, tall, back, part, spread, far, near, view = refs[:8]
+    begun = () if first else refs[9 : 9 + 2 * PARTS]
+    refs = refs[9 + len(begun) :]
+    field, *sends = refs[: 1 + 2 * PARTS]
+    blur_hi, blur_lo, plane_hi, plane_lo = refs[1 + 2 * PARTS :]
+    planes = part.shape[0]
     radius, rows, across = near.shape
-    keep, seen = sets[0][2].shape[0], sets[0][1].shape[0]
+    keep, seen = back.shape[0], tall.shape[0]
     taps = 2 * radius + 1
     even = lax.axis_index("tile") % 2 == 0
     half = half_of(lax.axis_index("view"))
     seen_start = pl.multiple_of((2 * keep - seen) * half, 8)
-    factors = [spread_factors(spread, taps) for _, _, _, _, spread in sets]
-    for which, (_, _, _, part, _) in enumerate(sets):
-        for row, lane in chunks(rows, across):
-
-            def rim(place):
-                if place < 0:
-                    at = place + radius
-                    return jnp.where(even, far[at, row, lane], near[at, row, lane])
-                at = place - planes
-                return jnp.where(even, near[at, row, lane], far[at, row, lane])
-
-            below = depth_terms(rim, factors[which], -radius, 0, range(planes), False)
-            above = depth_terms(rim, factors[which], planes, planes + radius, range(planes), False)
-            for plane in range(planes):
-                block = part[plane, row, lane]
-                for term in (below[plane], above[plane]):
-                    block = block if term is None else block + term
-                upper, lower = split(block)
-                at = slice(plane * rows + row.start, plane * rows + row.stop)
-                blur_hi[which, at, lane] = upper
-                blur_lo[which, at, lane] = lower
-    lines = []
-    for which, (wide, _, _, _, _) in enumerate(sets):
-        upper, lower = wide[0, 0], wide[0, 1]
-        lines.append(
-            jnp.dot(blur_hi[which], upper, preferred_element_type=F32)
-            + jnp.dot(blur_lo[which], upper, preferred_element_type=F32)
-            + jnp.dot(blur_hi[which], lower, preferred_element_type=F32)
+    factors = spread_factors(spread, taps)
+    for row, lane in chunks(rows, across):
+
+        def rim(place):
+            if place < 0:
+                at = place + radius
+                return jnp.where(even, far[at, row, lane], near[at, row, lane])
+            at = place - planes
+            return jnp.where(even, near[at, row, lane], far[at, row, lane])
+
+        below = depth_terms(rim, factors, -radius, 0, range(planes), False)
+        above = depth_terms(rim, factors, planes, planes + radius, range(planes), False)
+        for plane in range(planes):
+            block = part[plane, row, lane]
+            for term in (below[plane], above[plane]):
+                block = block if term is None else block + term
+            upper, lower = split(block)
+            at = slice(plane * rows + row.start, plane * rows + row.stop)
+            blur_hi[at, lane] = upper
+            blur_lo[at, lane] = lower
+    upper, lower = wide[0, 0], wide[0, 1]
+    lines = (
+        jnp.dot(blur_hi[...], upper, preferred_element_type=F32)
+        + jnp.dot(blur_lo[...], upper, preferred_element_type=F32)
+        + jnp.dot(blur_hi[...], lower, preferred_element_type=F32)
+    )
+    forwards = []
+    for plane in range(planes):
+        hi, lo = split(lines[plane * rows : (plane + 1) * rows])
+        forwards.append(
+            jnp.dot(tall[...], jnp.concatenate([hi, lo, hi], axis=0), preferred_element_type=F32)
         )
-    both = [(which, plane) for which in range(2) for plane in range(planes)]
-    forwards = {}
-    for which, plane in both:
-        hi, lo = split(lines[which][plane * rows : (plane + 1) * rows])
-        forwards[which, plane] = jnp.dot(
-            sets[which][1][...], jnp.concatenate([hi, lo, hi], axis=0), preferred_element_type=F32
-        )
-    ratios = {}
-    for which, plane in both:
-        if which == 0:
-            recorded = measured[0, plane, pl.ds(seen_start, seen), :]
+    ratios = []
+    for plane in range(planes):
+        if first:
+            recorded = view[0, plane, pl.ds(seen_start, seen), :]
         else:
-            recorded = swapped[plane * seen : (plane + 1) * seen]
-        ratio = recorded / forwards[which, plane]
+            recorded = view[plane * seen : (plane + 1) * seen]
+        ratio = recorded / forwards[plane]
         if rows > seen:
             ratio = jnp.concatenate([ratio, jnp.zeros((rows - seen, across), F32)], axis=0)
-        ratios[which, plane] = split(ratio)
-    turned = {}
-    for which, plane in both:
-        hi, lo = ratios[which, plane]
-        turned[which, plane] = jnp.dot(
-            sets[which][2][...], jnp.concatenate([hi, lo, hi], axis=0), preferred_element_type=F32
-        )
-    for which, plane in both:
-        hi, lo = split(turned[which, plane])
-        plane_hi[which, plane * keep : (plane + 1) * keep] = hi
-        plane_lo[which, plane * keep : (plane + 1) * keep] = lo
-    for which, (wide, _, _, _, _) in enumerate(sets):
-        upper, lower = wide[1, 0], wide[1, 1]
-        result = (
-            jnp.dot(plane_hi[which], upper, preferred_element_type=F32)
-            + jnp.dot(plane_lo[which], upper, preferred_element_type=F32)
-            + jnp.dot(plane_hi[which], lower, preferred_element_type=F32)
-        )
-        fields[which][...] = result.reshape(planes, keep, across)
+        ratios.append(split(ratio))
+    turned = [
+        jnp.dot(back[...], jnp.concatenate([hi, lo, hi], axis=0), preferred_element_type=F32)
+        for hi, lo in ratios
+    ]
+    for plane in range(planes):
+        hi, lo = split(turned[plane])
+        plane_hi[plane * keep : (plane + 1) * keep] = hi
+        plane_lo[plane * keep : (plane + 1) * keep] = lo
+    upper, lower = wide[1, 0], wide[1, 1]
+    result = (
+        jnp.dot(plane_hi[...], upper, preferred_element_type=F32)
+        + jnp.dot(plane_lo[...], upper, preferred_element_type=F32)
+        + jnp.dot(plane_hi[...], lower, preferred_element_type=F32)
+    )
+    field[...] = result.reshape(planes, keep, across)
     for row, lane in chunks(keep, across):
-        below, above = [], []
-        for which in range(2):
-            source = lambda place: fields[which][place, row, lane]
-            outer = range(planes, planes + radius)
-            below.append(depth_terms(source, factors[which], 0, planes, range(-radius, 0), True))
-            above.append(depth_terms(source, factors[which], 0, planes, outer, True))
+        source = lambda place: field[place, row, lane]
+        below = depth_terms(source, factors, 0, planes, range(-radius, 0), True)
+        above = depth_terms(source, factors, 0, planes, range(planes, planes + radius), True)
         part_at, inside = divmod(row.start, keep // PARTS)
         inside = slice(inside, inside + 16)
         for at in range(radius):
-            down = below[0][at - radius] + below[1][at - radius]
-            up = above[0][at + planes] + above[1][at + planes]
-            sends[2 * part_at][at, inside, lane] = jnp.where(even, down, up)
-            sends[2 * part_at + 1][at, inside, lane] = jnp.where(even, up, down)
-
-
-def ratio_fields(own, others, far, near, measured, swapped, after):
-    keep, planes = own[2].shape[0], own[3].shape[0]
+            down, up = below[at - radius], above[at + planes]
+            to_far, to_near = jnp.where(even, down, up), jnp.where(even, up, down)
+            if begun:
+                to_far += begun[2 * part_at][at, inside, lane]
+                to_near += begun[2 * part_at + 1][at, inside, lane]
+            sends[2 * part_at][at, inside, lane] = to_far
+            sends[2 * part_at + 1][at, inside, lane] = to_near
+
+
+def view_field(first, prepared, far, near, view, after, begun):
+    keep, planes = prepared[2].shape[0], prepared[3].shape[0]
     radius, rows, across = near.shape
-    field = jax.ShapeDtypeStruct((planes, keep, across), F32)
     send = jax.ShapeDtypeStruct((radius, keep // PARTS, across), F32)
     return pl.pallas_call(
-        fields_kernel,
-        out_shape=(field,) * 2 + (send,) * (2 * PARTS),
-        in_specs=[VMEM] * 14 + [ANY],
-        out_specs=(VMEM,) * (2 + 2 * PARTS),
+        functools.partial(view_kernel, first),
+        out_shape=(jax.ShapeDtypeStruct((planes, keep, across), F32),) + (send,) * (2 * PARTS),
+        in_specs=[VMEM] * 8 + [ANY] + [VMEM] * len(begun),
+        out_specs=(VMEM,) * (1 + 2 * PARTS),
         scratch_shapes=[
-            pltpu.VMEM((2, planes * rows, across), BF16),
-            pltpu.VMEM((2, planes * rows, across), BF16),
-            pltpu.VMEM((2, planes * keep, across), BF16),
-            pltpu.VMEM((2, planes * keep, across), BF16),
+            pltpu.VMEM((planes * rows, across), BF16),
+            pltpu.VMEM((planes * rows, across), BF16),
+            pltpu.VMEM((planes * keep, across), BF16),
+            pltpu.VMEM((planes * keep, across), BF16),
         ],
         compiler_params=pltpu.CompilerParams(vmem_limit_bytes=LIMIT),
-        name="ratio_fields",
-    )(*own, *others, far, near, measured, swapped, after)
+        name="own_view" if first else "other_view",
+    )(*prepared, far, near, view, after, *begun)
 
 
 def own_kernel(taps, spread_own, spread_other, field_own, field_other, *inner):
@@ -570,7 +571,7 @@
         in_specs=[VMEM],
         out_specs=VMEM,
         compiler_params=pltpu.CompilerParams(vmem_limit_bytes=LIMIT),
-        cost_estimate=pl.CostEstimate(flops=10_000_000_000, bytes_accessed=20_000_000, transcendentals=0),
+        cost_estimate=told(10),
         name="nucleus_table",
     )(rows)
 
@@ -588,13 +589,14 @@
     token[...] = source[0, :8, :LANES]
 
 
-def token_of(source, after=()):
+def token_of(source, after=(), billions=0):
     return pl.pallas_call(
         token_kernel,
         out_shape=jax.ShapeDtypeStruct((8, LANES), F32),
         in_specs=[VMEM] + [ANY] * len(after),
         out_specs=VMEM,
         compiler_params=pltpu.CompilerParams(vmem_limit_bytes=LIMIT),
+        cost_estimate=told(billions),
         name="token_of",
     )(source, *after)
 
@@ -665,11 +667,10 @@
     near = lax.ppermute(to_near, "tile", near_pairs)
     places = slot_places(tiles, views, label_owner, label_index)
     own = prepare(False, taps, lines, estimate, places[1], rows, seen, keep)
-    others = prepare(True, taps, swapped, estimate, lines, rows, seen, keep)
-    came = token_of(far, (others[4],))
-    field_own, field_other, *sends = ratio_fields(
-        own, others, far, near, measured, swapped, came
-    )
+    came = token_of(far, (), 8)
+    field_own, *begun = view_field(True, own, far, near, measured, came, ())
+    others = prepare(True, taps, swapped, estimate, begun[0], rows, seen, keep)
+    field_other, *sends = view_field(False, others, far, near, swapped, came, begun)
     rims = [
         lax.ppermute(send, "tile", pairs) for send, pairs in zip(sends, (far_pairs, near_pairs) * PARTS)
     ]

time: 47.5 us -> 48.6 us (1.023)
  starting transfers between devices: 30.1 us -> 30.8 us
  Pallas kernels: 9.4 us -> 10 us
  waiting for transfers between devices: 5.92 us -> 5.41 us
    ppermute x1, waiting for transfers between devices: 3.75 us -> 1.92 us  [on_device(): swapped = lax.ppermute(packed, 'view', partner)]
    ppermute x4, starting transfers between devices: 10.7 us -> 11.7 us  [on_device(): lax.ppermute(send, 'tile', pairs)]
    all_to_all x1, starting transfers between devices: 3.77 us -> 4.74 us  [on_device(): lax.all_to_all(sent, ('tile', 'view'), split_axis=0, concat_axis=0, tiled...]
    ppermute x2, starting transfers between devices: 4.97 us -> 4.08 us  [on_device(): new_other.append(lax.ppermute(new_mine[part], 'view', partner))]
    all_to_all x1, waiting for transfers between devices: 2.14 us -> 3.03 us  [on_device(): lax.all_to_all(sent, ('tile', 'view'), split_axis=0, concat_axis=0, tiled...]
    pallas_call x1 -> x2, Pallas kernels: 1.81 us -> 2.45 us  [view_field(): pl.pallas_call(functools.partial(view_kernel, first), out_shape=(jax.Shap...]
  transfers between devices with their start and end apart: 12 -> 12, of which waited for: 2 -> 3; matrix products, arithmetic and copies ran while one was open for 0% -> 0% of each run, Pallas kernels for 15% -> 15%
where the time goes in v14:
time: 48.6 us; the launch traced here: 48.3 us
  starting transfers between devices  30.8 us (63%)
  Pallas kernels  10 us (21%)
  waiting for transfers between devices  5.41 us (11%)
  local copies, waits for them, and re-layouts  1.2 us (2%)
  between operations  0.86 us (2%)
    ppermute x4, starting transfers between devices, on_device(): lax.ppermute(send, 'tile', pairs)  11.7 us
    all_to_all x1, starting transfers between devices, on_device(): lax.all_to_all(sent, ('tile', 'view'), split_axis=0, concat_axis=0, tiled...  4.74 us
    ppermute x2, starting transfers between devices, on_device(): new_other.append(lax.ppermute(new_mine[part], 'view', partner))  4.08 us
    ppermute x2, starting transfers between devices, on_device(): other.append(lax.ppermute(mine[part], 'view', across_pairs))  3.95 us
    ppermute x1, starting transfers between devices, on_device(): swapped = lax.ppermute(packed, 'view', partner)  3.09 us
    all_to_all x1, waiting for transfers between devices, on_device(): lax.all_to_all(sent, ('tile', 'view'), split_axis=0, concat_axis=0, tiled...  3.03 us
    pallas_call x2, Pallas kernels, moment_rows(): pl.pallas_call(functools.partial(moments_kernel, views, tiles * planes, p...  2.63 us
    pallas_call x2, Pallas kernels, view_field(): pl.pallas_call(functools.partial(view_kernel, first), out_shape=(jax.Shap...  2.45 us
  transfers between devices with their start and end apart: 12, of which 3 were waited for; matrix products, arithmetic and copies ran while one was open for 0% of the time, Pallas kernels for 15%

profile of v14, /device:TPU:0, one launch (start us, length us, event | category | flops | bytes accessed | tf_op | source)
XLA Modules:
  0.0 48.3 jit_solution(10421516166702309031)
XLA Ops:
  0.6 1.0 %copy-done = f32[8,64,256]{2,1,0:T(8,128)S(1)} copy-done((f32[8,64,256]{2,1,0:T(8,128)S(1)}, f32[8,64,256]{2,1,0:T(8,128)}, u32[]{:S(2)}) %copy-start) | copy-done | bytes 524312
  1.7 0.0 copy-start.3
  1.7 0.8 %collective-permute-start.1 = (f32[7,48,256]{2,1,0:T(8,128)S(1)}, f32[7,48,256]{2,1,0:T(8,128)S(1)}, u32[]{:S(2)}, u32[]{:S(2)}) collective-permute-start(f32[7,48,256]{2,1,0:T(8,128)S(1)} %get-tuple-element.34), channel_id=1, source_target_pairs={{4,8},{12,16},{20,24},{8,4},{16,12},{24,20},{5,9},{13,17},{21,25},... | collective-permute-start | bytes 1032200 | tf_op jit(solution)/shard_map/ppermute | solution.py:666
  2.6 0.2 copy-done.2
  2.7 3.1 %collective-permute-start = (f32[344,256]{1,0:T(8,128)S(1)}, f32[344,256]{1,0:T(8,128)S(1)}, u32[]{:S(2)}, u32[]{:S(2)}) collective-permute-start(f32[344,256]{1,0:T(8,128)S(1)} %view_out.1), channel_id=1, source_target_pairs={{0,1},{1,0},{2,3},{3,2},{4,5},{5,4},{6,7},{7,6},{8,9},{9,8},{10,11... | collective-permute-start | bytes 1056776 | tf_op jit(solution)/shard_map/ppermute | solution.py:664
  5.8 2.4 %collective-permute-start.2 = (f32[7,48,256]{2,1,0:T(8,128)S(1)}, f32[7,48,256]{2,1,0:T(8,128)S(1)}, u32[]{:S(2)}, u32[]{:S(2)}) collective-permute-start(f32[7,48,256]{2,1,0:T(8,128)S(1)} %get-tuple-element.35), channel_id=1, source_target_pairs={{0,4},{4,0},{8,12},{12,8},{16,20},{20,16},{24,28},{28,24},{1,5},{5... | collective-permute-start | bytes 1032200 | tf_op jit(solution)/shard_map/ppermute | solution.py:667
  8.3 0.2 slot_places.1
  8.5 0.6 %prepare.2 = (bf16[2,2,256,256]{3,2,1,0:T(8,128)(2,1)S(1)}, bf16[40,144]{1,0:T(8,128)(2,1)S(1)}, bf16[32,144]{1,0:T(8,128)(2,1)S(1)}, f32[8,48,256]{2,1,0:T(8,128)S(1)}, f32[16,128]{1,0:T(8,128)S(1)}) custom-call(f32[3,1,15]{2,1,0:T(1,128)S(1)} %bitcast.8, f32[8,64,256]{2,1,0:T(8,128)S(1)} %copy-done, f32[32,128]{1,0:T(8,128)S(1)} %get-tuple-element.28.after.base), custom_call_target="tpu_custom_call" | custom-call | tf_op jit(solution)/shard_map/prepare/pallas_call | solution.py:176
  9.1 0.0 collective-permute-done.1.source.refs_5_
  9.1 0.4 collective-permute-done.2.refs_6_
  9.5 1.2 %own_view.1 = (f32[8,32,256]{2,1,0:T(8,128)S(1)}, f32[7,16,256]{2,1,0:T(8,128)S(1)}, f32[7,16,256]{2,1,0:T(8,128)S(1)}, f32[7,16,256]{2,1,0:T(8,128)S(1)}, f32[7,16,256]{2,1,0:T(8,128)S(1)}) custom-call(bf16[2,2,256,256]{3,2,1,0:T(8,128)(2,1)S(1)} %get-tuple-element.30.refs_0_, bf16[40,144]{1,0:T(8,128)(2,1)S(1)} %get-tuple-element.31.refs_1_, ...), custom_call_target="tpu_custom_call" | custom-call | tf_op jit(solution)/shard_map/own_view/pallas_call | solution.py:286
  10.8 1.9 %collective-permute-done.source.refs_7_ = f32[344,256]{1,0:T(8,128)S(1)} collective-permute-done((f32[344,256]{1,0:T(8,128)S(1)}, f32[344,256]{1,0:T(8,128)S(1)}, u32[]{:S(2)}, u32[]{:S(2)}) %collective-permute-start) | collective-permute-done | bytes 352288 | tf_op jit(solution)/shard_map/ppermute | solution.py:664
  12.7 0.6 %prepare.3 = (bf16[2,2,256,256]{3,2,1,0:T(8,128)(2,1)S(1)}, bf16[40,144]{1,0:T(8,128)(2,1)S(1)}, bf16[32,144]{1,0:T(8,128)(2,1)S(1)}, f32[8,48,256]{2,1,0:T(8,128)S(1)}, f32[16,128]{1,0:T(8,128)S(1)}) custom-call(f32[344,256]{1,0:T(8,128)S(1)} %collective-permute-done.source.refs_7_, f32[8,64,256]{2,1,0:T(8,128)S(1)} %copy-done, ...), custom_call_target="tpu_custom_call" | custom-call | tf_op jit(solution)/shard_map/prepare/pallas_call | solution.py:176
  13.3 1.2 %other_view.1 = (f32[8,32,256]{2,1,0:T(8,128)S(1)}, f32[7,16,256]{2,1,0:T(8,128)S(1)}, f32[7,16,256]{2,1,0:T(8,128)S(1)}, f32[7,16,256]{2,1,0:T(8,128)S(1)}, f32[7,16,256]{2,1,0:T(8,128)S(1)}) custom-call(bf16[2,2,256,256]{3,2,1,0:T(8,128)(2,1)S(1)} %get-tuple-element.39.refs_0_, bf16[40,144]{1,0:T(8,128)(2,1)S(1)} %get-tuple-element.40.refs_1_, ...), custom_call_target="tpu_custom_call" | custom-call | tf_op jit(solution)/shard_map/other_view/pallas_call | solution.py:286
  14.5 0.0 copy-start.1
  14.5 0.8 %collective-permute-start.3 = (f32[7,16,256]{2,1,0:T(8,128)S(1)}, f32[7,16,256]{2,1,0:T(8,128)S(1)}, u32[]{:S(2)}, u32[]{:S(2)}) collective-permute-start(f32[7,16,256]{2,1,0:T(8,128)S(1)} %get-tuple-element.48), channel_id=1, source_target_pairs={{4,8},{12,16},{20,24},{8,4},{16,12},{24,20},{5,9},{13,17},{21,25},... | collective-permute-start | bytes 344072 | tf_op jit(solution)/shard_map/ppermute | solution.py:675
  15.3 6.1 %collective-permute-start.4 = (f32[7,16,256]{2,1,0:T(8,128)S(1)}, f32[7,16,256]{2,1,0:T(8,128)S(1)}, u32[]{:S(2)}, u32[]{:S(2)}) collective-permute-start(f32[7,16,256]{2,1,0:T(8,128)S(1)} %get-tuple-element.49), channel_id=1, source_target_pairs={{0,4},{4,0},{8,12},{12,8},{16,20},{20,16},{24,28},{28,24},{1,5},{5... | collective-permute-start | bytes 344072 | tf_op jit(solution)/shard_map/ppermute | solution.py:675
  21.5 0.7 %collective-permute-start.6 = (f32[7,16,256]{2,1,0:T(8,128)S(1)}, f32[7,16,256]{2,1,0:T(8,128)S(1)}, u32[]{:S(2)}, u32[]{:S(2)}) collective-permute-start(f32[7,16,256]{2,1,0:T(8,128)S(1)} %get-tuple-element.52), channel_id=1, source_target_pairs={{4,8},{12,16},{20,24},{8,4},{16,12},{24,20},{5,9},{13,17},{21,25},... | collective-permute-start | bytes 344072 | tf_op jit(solution)/shard_map/ppermute | solution.py:675
  22.1 4.1 %collective-permute-start.7 = (f32[7,16,256]{2,1,0:T(8,128)S(1)}, f32[7,16,256]{2,1,0:T(8,128)S(1)}, u32[]{:S(2)}, u32[]{:S(2)}) collective-permute-start(f32[7,16,256]{2,1,0:T(8,128)S(1)} %get-tuple-element.53), channel_id=1, source_target_pairs={{0,4},{4,0},{8,12},{12,8},{16,20},{20,16},{24,28},{28,24},{1,5},{5... | collective-permute-start | bytes 344072 | tf_op jit(solution)/shard_map/ppermute | solution.py:675
  26.3 0.3 own_planes.1
  26.6 3.7 %collective-permute-start.5 = (f32[8,16,256]{2,1,0:T(8,128)S(1)}, f32[8,16,256]{2,1,0:T(8,128)S(1)}, u32[]{:S(2)}, u32[]{:S(2)}) collective-permute-start(f32[8,16,256]{2,1,0:T(8,128)S(1)} %add_rims.2.correction.mine), channel_id=1, source_target_pairs={{0,3},{1,2},{2,1},{3,0},{4,7},{5,6},{6,5},{7,4},{8,11},{9,10},{10,... | collective-permute-start | bytes 393224 | tf_op jit(solution)/shard_map/ppermute | solution.py:681
  30.3 0.8 %moment_rows.2.rest_0_.refs_0_ = f32[16,128]{1,0:T(8,128)S(1)} custom-call(f32[8,64,256]{2,1,0:T(8,128)S(1)} %copy-done, s32[8,64,256]{2,1,0:T(8,128)S(1)} %copy-done.1, f32[160,16]{1,0:T(8,128)S(1)} %get-tuple-element.50.picked, f32[32,128]{1,0:T(8,128)S(1)} %get-tuple-element.28.after.base, f32[8,16,256]{2,1,0:T(8,128)S(1)} %add_rims.2.correction.mine), custom_call_target="tpu_custom_call" | custom-call | tf_op jit(solution)/shard_map/moment_rows/pallas_call | solution.py:525
  31.2 0.3 collective-permute-start.8
  31.5 1.8 %moment_rows.3.rest_0_ = f32[32,128]{1,0:T(8,128)} custom-call(f32[8,64,256]{2,1,0:T(8,128)S(1)} %copy-done, s32[8,64,256]{2,1,0:T(8,128)S(1)} %copy-done.1, f32[160,16]{1,0:T(8,128)S(1)} %get-tuple-element.50.picked, f32[32,128]{1,0:T(8,128)S(1)} %get-tuple-element.28.after.base, f32[8,16,256]{2,1,0:T(8,128)S(1)} %add_rims.3.correction.mine, ...), custom_call_target="tpu_custom_call" | custom-call | tf_op jit(solution)/shard_map/moment_rows/pallas_call | solution.py:525
  33.3 4.7 %all-to-all-start = ((f32[32,1,128]{2,1,0:T(1,128)}), f32[32,1,128]{2,1,0:T(1,128)S(1)}, u32[]{:S(2)}, u32[]{:S(2)}) async-start(f32[32,1,128]{2,1,0:T(1,128)} %bitcast.3), calls=%async_computation | async-start | bytes 32768 | tf_op jit(solution)/shard_map/all_to_all | solution.py:684
  38.1 2.2 %collective-permute-start.9 = (f32[9,16,256]{2,1,0:T(8,128)S(1)}, f32[9,16,256]{2,1,0:T(8,128)S(1)}, u32[]{:S(2)}, u32[]{:S(2)}) collective-permute-start(f32[9,16,256]{2,1,0:T(8,128)S(1)} %update.2.source.refs_0_), channel_id=1, source_target_pairs={{0,1},{1,0},{2,3},{3,2},{4,5},{5,4},{6,7},{7,6},{8,9},{9,8},{10,11... | collective-permute-start | bytes 442376 | tf_op jit(solution)/shard_map/ppermute | solution.py:688
  40.3 1.8 %collective-permute-start.10 = (f32[8,16,256]{2,1,0:T(8,128)S(1)}, f32[8,16,256]{2,1,0:T(8,128)S(1)}, u32[]{:S(2)}, u32[]{:S(2)}) collective-permute-start(f32[8,16,256]{2,1,0:T(8,128)S(1)} %update.3.refs_1_), channel_id=1, source_target_pairs={{0,1},{1,0},{2,3},{3,2},{4,5},{5,4},{6,7},{7,6},{8,9},{9,8},{10,11... | collective-permute-start | bytes 393224 | tf_op jit(solution)/shard_map/ppermute | solution.py:688
  42.2 3.0 %all-to-all-done = f32[32,1,128]{2,1,0:T(1,128)S(1)} async-done(((f32[32,1,128]{2,1,0:T(1,128)}), f32[32,1,128]{2,1,0:T(1,128)S(1)}, u32[]{:S(2)}, u32[]{:S(2)}) %all-to-all-start) | async-done | bytes 16416 | tf_op jit(solution)/shard_map/all_to_all | solution.py:684
  45.2 1.0 %nucleus_table.1 = f32[10,128]{1,0:T(8,128)} custom-call(f32[32,128]{1,0:T(8,128)S(1)} %bitcast.6), custom_call_target="tpu_custom_call" | custom-call | flops 10000000000 | bytes 20000000 | tf_op jit(solution)/shard_map/nucleus_table/pallas_call | solution.py:568
  46.2 0.7 %begin_result.1.begun = f32[8,64,256]{2,1,0:T(8,128)} custom-call(f32[9,16,256]{2,1,0:T(8,128)S(1)} %update.2.source.refs_0_, f32[8,16,256]{2,1,0:T(8,128)S(1)} %update.3.refs_1_), custom_call_target="tpu_custom_call" | custom-call | tf_op jit(solution)/shard_map/begin_result/pallas_call | solution.py:617
  46.9 0.7 %store_part.2.begun = f32[8,64,256]{2,1,0:T(8,128)} custom-call(f32[8,64,256]{2,1,0:T(8,128)} %begin_result.1.begun, f32[9,16,256]{2,1,0:T(8,128)S(1)} %collective-permute-done.9.other), custom_call_target="tpu_custom_call", output_to_operand_aliasing={{}: (0, {})} | custom-call | tf_op jit(solution)/shard_map/store_part/pallas_call | solution.py:635
  47.6 0.7 %store_part.3 = f32[8,64,256]{2,1,0:T(8,128)} custom-call(f32[8,64,256]{2,1,0:T(8,128)} %store_part.2.begun, f32[8,16,256]{2,1,0:T(8,128)S(1)} %collective-permute-done.10.other), custom_call_target="tpu_custom_call", output_to_operand_aliasing={{}: (0, {})} | custom-call | tf_op jit(solution)/shard_map/store_part/pallas_call | solution.py:635
  (25 shorter events, 0.2 us)
Async XLA Ops:
  0.6 1.0 %copy-start = (f32[8,64,256]{2,1,0:T(8,128)S(1)}, f32[8,64,256]{2,1,0:T(8,128)}, u32[]{:S(2)}) copy-start(f32[8,64,256]{2,1,0:T(8,128)} %estimate.13) | copy-start | bytes 1572868
  1.7 1.0 %copy-start.2 = (f32[1,8,64,256]{3,2,1,0:T(8,128)S(1)}, f32[1,8,64,256]{3,2,1,0:T(8,128)}, u32[]{:S(2)}) copy-start(f32[1,8,64,256]{3,2,1,0:T(8,128)} %refs_7_.1) | copy-start | bytes 1572868
  1.7 1.0 %copy-start.3 = (f32[1,3,15]{2,0,1:T(1,128)S(1)}, f32[1,3,15]{2,0,1:T(1,128)}, u32[]{:S(2)}) copy-start(f32[1,3,15]{2,0,1:T(1,128)} %param.8) | copy-start | bytes 544
  1.7 7.4 %collective-permute-start.1 = (f32[7,48,256]{2,1,0:T(8,128)S(1)}, f32[7,48,256]{2,1,0:T(8,128)S(1)}, u32[]{:S(2)}, u32[]{:S(2)}) collective-permute-start(f32[7,48,256]{2,1,0:T(8,128)S(1)} %get-tuple-element.34), channel_id=1, source_target_pairs={{4,8},{12,16},{20,24},{8,4},{16,12},{24,20},{5,9},{13,17},{21,25},... | collective-permute-start | bytes 1032200 | tf_op jit(solution)/shard_map/ppermute | solution.py:666
  2.7 9.9 %collective-permute-start = (f32[344,256]{1,0:T(8,128)S(1)}, f32[344,256]{1,0:T(8,128)S(1)}, u32[]{:S(2)}, u32[]{:S(2)}) collective-permute-start(f32[344,256]{1,0:T(8,128)S(1)} %view_out.1), channel_id=1, source_target_pairs={{0,1},{1,0},{2,3},{3,2},{4,5},{5,4},{6,7},{7,6},{8,9},{9,8},{10,11... | collective-permute-start | bytes 1056776 | tf_op jit(solution)/shard_map/ppermute | solution.py:664
  5.8 2.4 %copy-start.4 = (s32[1,16,1]{1,2,0:T(1,128)S(1)}, s32[1,16,1]{1,2,0:T(1,128)}, u32[]{:S(2)}) copy-start(s32[1,16,1]{1,2,0:T(1,128)} %param.10) | copy-start | bytes 196
  5.8 2.4 %copy-start.5 = (s32[1,16]{1,0:T(1,128)S(1)}, s32[1,16]{1,0:T(1,128)}, u32[]{:S(2)}) copy-start(s32[1,16]{1,0:T(1,128)} %index_row.1) | copy-start | bytes 196
  5.8 3.7 %collective-permute-start.2 = (f32[7,48,256]{2,1,0:T(8,128)S(1)}, f32[7,48,256]{2,1,0:T(8,128)S(1)}, u32[]{:S(2)}, u32[]{:S(2)}) collective-permute-start(f32[7,48,256]{2,1,0:T(8,128)S(1)} %get-tuple-element.35), channel_id=1, source_target_pairs={{0,4},{4,0},{8,12},{12,8},{16,20},{20,16},{24,28},{28,24},{1,5},{5... | collective-permute-start | bytes 1032200 | tf_op jit(solution)/shard_map/ppermute | solution.py:667
  14.5 15.8 %copy-start.1 = (s32[8,64,256]{2,1,0:T(8,128)S(1)}, s32[8,64,256]{2,1,0:T(8,128)}, u32[]{:S(2)}) copy-start(s32[8,64,256]{2,1,0:T(8,128)} %labels.3) | copy-start | bytes 1572868
  14.5 12.0 %collective-permute-start.3 = (f32[7,16,256]{2,1,0:T(8,128)S(1)}, f32[7,16,256]{2,1,0:T(8,128)S(1)}, u32[]{:S(2)}, u32[]{:S(2)}) collective-permute-start(f32[7,16,256]{2,1,0:T(8,128)S(1)} %get-tuple-element.48), channel_id=1, source_target_pairs={{4,8},{12,16},{20,24},{8,4},{16,12},{24,20},{5,9},{13,17},{21,25},... | collective-permute-start | bytes 344072 | tf_op jit(solution)/shard_map/ppermute | solution.py:675
  15.3 11.2 %collective-permute-start.4 = (f32[7,16,256]{2,1,0:T(8,128)S(1)}, f32[7,16,256]{2,1,0:T(8,128)S(1)}, u32[]{:S(2)}, u32[]{:S(2)}) collective-permute-start(f32[7,16,256]{2,1,0:T(8,128)S(1)} %get-tuple-element.49), channel_id=1, source_target_pairs={{0,4},{4,0},{8,12},{12,8},{16,20},{20,16},{24,28},{28,24},{1,5},{5... | collective-permute-start | bytes 344072 | tf_op jit(solution)/shard_map/ppermute | solution.py:675
  21.5 9.6 %collective-permute-start.6 = (f32[7,16,256]{2,1,0:T(8,128)S(1)}, f32[7,16,256]{2,1,0:T(8,128)S(1)}, u32[]{:S(2)}, u32[]{:S(2)}) collective-permute-start(f32[7,16,256]{2,1,0:T(8,128)S(1)} %get-tuple-element.52), channel_id=1, source_target_pairs={{4,8},{12,16},{20,24},{8,4},{16,12},{24,20},{5,9},{13,17},{21,25},... | collective-permute-start | bytes 344072 | tf_op jit(solution)/shard_map/ppermute | solution.py:675
  22.1 9.0 %collective-permute-start.7 = (f32[7,16,256]{2,1,0:T(8,128)S(1)}, f32[7,16,256]{2,1,0:T(8,128)S(1)}, u32[]{:S(2)}, u32[]{:S(2)}) collective-permute-start(f32[7,16,256]{2,1,0:T(8,128)S(1)} %get-tuple-element.53), channel_id=1, source_target_pairs={{0,4},{4,0},{8,12},{12,8},{16,20},{20,16},{24,28},{28,24},{1,5},{5... | collective-permute-start | bytes 344072 | tf_op jit(solution)/shard_map/ppermute | solution.py:675
  26.6 11.4 %collective-permute-start.5 = (f32[8,16,256]{2,1,0:T(8,128)S(1)}, f32[8,16,256]{2,1,0:T(8,128)S(1)}, u32[]{:S(2)}, u32[]{:S(2)}) collective-permute-start(f32[8,16,256]{2,1,0:T(8,128)S(1)} %add_rims.2.correction.mine), channel_id=1, source_target_pairs={{0,3},{1,2},{2,1},{3,0},{4,7},{5,6},{6,5},{7,4},{8,11},{9,10},{10,... | collective-permute-start | bytes 393224 | tf_op jit(solution)/shard_map/ppermute | solution.py:681
  31.2 9.1 %collective-permute-start.8 = (f32[8,16,256]{2,1,0:T(8,128)S(1)}, f32[8,16,256]{2,1,0:T(8,128)S(1)}, u32[]{:S(2)}, u32[]{:S(2)}) collective-permute-start(f32[8,16,256]{2,1,0:T(8,128)S(1)} %add_rims.3.correction.mine), channel_id=1, source_target_pairs={{0,3},{1,2},{2,1},{3,0},{4,7},{5,6},{6,5},{7,4},{8,11},{9,10},{10,... | collective-permute-start | bytes 393224 | tf_op jit(solution)/shard_map/ppermute | solution.py:681
  33.3 11.9 %all-to-all-start = ((f32[32,1,128]{2,1,0:T(1,128)}), f32[32,1,128]{2,1,0:T(1,128)S(1)}, u32[]{:S(2)}, u32[]{:S(2)}) async-start(f32[32,1,128]{2,1,0:T(1,128)} %bitcast.3), calls=%async_computation | async-start | bytes 32768 | tf_op jit(solution)/shard_map/all_to_all | solution.py:684
  38.1 8.9 %collective-permute-start.9 = (f32[9,16,256]{2,1,0:T(8,128)S(1)}, f32[9,16,256]{2,1,0:T(8,128)S(1)}, u32[]{:S(2)}, u32[]{:S(2)}) collective-permute-start(f32[9,16,256]{2,1,0:T(8,128)S(1)} %update.2.source.refs_0_), channel_id=1, source_target_pairs={{0,1},{1,0},{2,3},{3,2},{4,5},{5,4},{6,7},{7,6},{8,9},{9,8},{10,11... | collective-permute-start | bytes 442376 | tf_op jit(solution)/shard_map/ppermute | solution.py:688
  40.3 7.3 %collective-permute-start.10 = (f32[8,16,256]{2,1,0:T(8,128)S(1)}, f32[8,16,256]{2,1,0:T(8,128)S(1)}, u32[]{:S(2)}, u32[]{:S(2)}) collective-permute-start(f32[8,16,256]{2,1,0:T(8,128)S(1)} %update.3.refs_1_), channel_id=1, source_target_pairs={{0,1},{1,0},{2,3},{3,2},{4,5},{5,4},{6,7},{7,6},{8,9},{9,8},{10,11... | collective-permute-start | bytes 393224 | tf_op jit(solution)/shard_map/ppermute | solution.py:688

commit v15 on v12

--- a/solution.py
+++ b/solution.py
@@ -23,7 +23,7 @@
 
 
 def half_of(view):
-    return (view ^ (view >> 1)) & 1
+    return view & 1
 
 
 def split(value):
@@ -662,7 +662,7 @@
     far_pairs = [(i, i + 1) for i in range(1, tiles - 1, 2)]
     far_pairs = far_pairs + [(b, a) for a, b in far_pairs]
     partner = [(i, i ^ 1) for i in range(views)]
-    across_pairs = [(i, i ^ 3) for i in range(views)]
+    across_pairs = [(i, i ^ 2) for i in range(views)]
 
     lines = jnp.transpose(kernels, (1, 0, 2))
     blank = blank_rows(across)

time: 47.1 us -> 48.4 us (1.028)
  waiting for transfers between devices: 5.93 us -> 12 us
  starting transfers between devices: 30.1 us -> 25.2 us
    ppermute x2, waiting for transfers between devices: 0.01 us -> 4.37 us  [on_device(): other.append(lax.ppermute(mine[part], 'view', across_pairs))]
    ppermute x2, starting transfers between devices: 4.96 us -> 0.77 us  [on_device(): new_other.append(lax.ppermute(new_mine[part], 'view', partner))]
    ppermute x2, waiting for transfers between devices: 0.01 us -> 1.93 us  [on_device(): new_other.append(lax.ppermute(new_mine[part], 'view', partner))]
    ppermute x2, starting transfers between devices: 3.95 us -> 3.06 us  [on_device(): other.append(lax.ppermute(mine[part], 'view', across_pairs))]
  transfers between devices with their start and end apart: 12 -> 12, of which waited for: 2 -> 5; matrix products, arithmetic and copies ran while one was open for 0% -> 0% of each run, Pallas kernels for 14% -> 13%
where the time goes in v15:
time: 48.4 us; the launch traced here: 48.1 us
  starting transfers between devices  25.2 us (52%)
  waiting for transfers between devices  12 us (25%)
  Pallas kernels  8.99 us (19%)
  local copies, waits for them, and re-layouts  1.03 us (2%)
  between operations  0.85 us (2%)
    ppermute x4, starting transfers between devices, on_device(): lax.ppermute(send, 'tile', pairs)  10.7 us
    ppermute x2, waiting for transfers between devices, on_device(): other.append(lax.ppermute(mine[part], 'view', across_pairs))  4.37 us
    all_to_all x1, starting transfers between devices, on_device(): lax.all_to_all(sent, ('tile', 'view'), split_axis=0, concat_axis=0, tiled...  4.01 us
    ppermute x1, waiting for transfers between devices, on_device(): swapped = lax.ppermute(packed, 'view', partner)  3.75 us
    ppermute x1, starting transfers between devices, on_device(): swapped = lax.ppermute(packed, 'view', partner)  3.09 us
    ppermute x2, starting transfers between devices, on_device(): other.append(lax.ppermute(mine[part], 'view', across_pairs))  3.06 us
    ppermute x1, starting transfers between devices, on_device(): near = lax.ppermute(to_near, 'tile', near_pairs)  2.9 us
    pallas_call x2, Pallas kernels, moment_rows(): pl.pallas_call(functools.partial(moments_kernel, views, tiles * planes, p...  2.64 us
  transfers between devices with their start and end apart: 12, of which 5 were waited for; matrix products, arithmetic and copies ran while one was open for 0% of the time, Pallas kernels for 13%

profile of v15, /device:TPU:0, one launch (start us, length us, event | category | flops | bytes accessed | tf_op | source)
XLA Modules:
  0.0 48.1 jit_solution(12137419277438863927)
XLA Ops:
  0.7 0.0 copy-start
  0.7 1.0 %copy-done.2 = f32[1,8,64,256]{3,2,1,0:T(8,128)S(1)} copy-done((f32[1,8,64,256]{3,2,1,0:T(8,128)S(1)}, f32[1,8,64,256]{3,2,1,0:T(8,128)}, u32[]{:S(2)}) %copy-start.2) | copy-done | bytes 524312
  1.7 3.1 %collective-permute-start = (f32[344,256]{1,0:T(8,128)S(1)}, f32[344,256]{1,0:T(8,128)S(1)}, u32[]{:S(2)}, u32[]{:S(2)}) collective-permute-start(f32[344,256]{1,0:T(8,128)S(1)} %view_out.1), channel_id=1, source_target_pairs={{0,1},{1,0},{2,3},{3,2},{4,5},{5,4},{6,7},{7,6},{8,9},{9,8},{10,11... | collective-permute-start | bytes 1056776 | tf_op jit(solution)/shard_map/ppermute | solution.py:670
  4.8 0.7 %collective-permute-start.1 = (f32[7,48,256]{2,1,0:T(8,128)S(1)}, f32[7,48,256]{2,1,0:T(8,128)S(1)}, u32[]{:S(2)}, u32[]{:S(2)}) collective-permute-start(f32[7,48,256]{2,1,0:T(8,128)S(1)} %get-tuple-element.35), channel_id=1, source_target_pairs={{4,8},{12,16},{20,24},{8,4},{16,12},{24,20},{5,9},{13,17},{21,25},... | collective-permute-start | bytes 1032200 | tf_op jit(solution)/shard_map/ppermute | solution.py:672
  5.5 0.0 copy-start.4
  5.5 0.0 copy-start.5
  5.6 2.9 %collective-permute-start.2 = (f32[7,48,256]{2,1,0:T(8,128)S(1)}, f32[7,48,256]{2,1,0:T(8,128)S(1)}, u32[]{:S(2)}, u32[]{:S(2)}) collective-permute-start(f32[7,48,256]{2,1,0:T(8,128)S(1)} %get-tuple-element.36), channel_id=1, source_target_pairs={{0,4},{4,0},{8,12},{12,8},{16,20},{20,16},{24,28},{28,24},{1,5},{5... | collective-permute-start | bytes 1032200 | tf_op jit(solution)/shard_map/ppermute | solution.py:673
  8.5 0.2 slot_places.1
  8.7 0.6 %prepare.2 = (bf16[2,2,256,256]{3,2,1,0:T(8,128)(2,1)S(1)}, bf16[40,144]{1,0:T(8,128)(2,1)S(1)}, bf16[32,144]{1,0:T(8,128)(2,1)S(1)}, f32[8,48,256]{2,1,0:T(8,128)S(1)}, f32[16,128]{1,0:T(8,128)S(1)}) custom-call(f32[3,1,15]{2,1,0:T(1,128)S(1)} %bitcast.10, f32[8,64,256]{2,1,0:T(8,128)S(1)} %copy-done, f32[32,128]{1,0:T(8,128)S(1)} %get-tuple-element.24.after.base), custom_call_target="tpu_custom_call" | custom-call | tf_op jit(solution)/shard_map/prepare/pallas_call | solution.py:170
  9.3 3.7 %collective-permute-done.source.refs_13_ = f32[344,256]{1,0:T(8,128)S(1)} collective-permute-done((f32[344,256]{1,0:T(8,128)S(1)}, f32[344,256]{1,0:T(8,128)S(1)}, u32[]{:S(2)}, u32[]{:S(2)}) %collective-permute-start) | collective-permute-done | bytes 352288 | tf_op jit(solution)/shard_map/ppermute | solution.py:670
  13.0 0.6 %prepare.3 = (bf16[2,2,256,256]{3,2,1,0:T(8,128)(2,1)S(1)}, bf16[40,144]{1,0:T(8,128)(2,1)S(1)}, bf16[32,144]{1,0:T(8,128)(2,1)S(1)}, f32[8,48,256]{2,1,0:T(8,128)S(1)}, f32[16,128]{1,0:T(8,128)S(1)}) custom-call(f32[344,256]{1,0:T(8,128)S(1)} %collective-permute-done.source.refs_13_, f32[8,64,256]{2,1,0:T(8,128)S(1)} %copy-done, f32[3,1,15]{2,1,0:T(1,128)S(1)} %bitcast.11), custom_call_target="tpu_custom_call" | custom-call | tf_op jit(solution)/shard_map/prepare/pallas_call | solution.py:170
  13.7 1.8 %ratio_fields.1 = (f32[8,32,256]{2,1,0:T(8,128)S(1)}, f32[8,32,256]{2,1,0:T(8,128)S(1)}, f32[7,16,256]{2,1,0:T(8,128)S(1)}, f32[7,16,256]{2,1,0:T(8,128)S(1)}, f...) custom-call(bf16[2,2,256,256]{3,2,1,0:T(8,128)(2,1)S(1)} %get-tuple-element.27.refs_0_, ...), custom_call_target="tpu_custom_call" | custom-call | tf_op jit(solution)/shard_map/ratio_fields/pallas_call | solution.py:285
  15.5 0.0 copy-start.1
  15.5 0.8 %collective-permute-start.3 = (f32[7,16,256]{2,1,0:T(8,128)S(1)}, f32[7,16,256]{2,1,0:T(8,128)S(1)}, u32[]{:S(2)}, u32[]{:S(2)}) collective-permute-start(f32[7,16,256]{2,1,0:T(8,128)S(1)} %get-tuple-element.40), channel_id=1, source_target_pairs={{4,8},{12,16},{20,24},{8,4},{16,12},{24,20},{5,9},{13,17},{21,25},... | collective-permute-start | bytes 344072 | tf_op jit(solution)/shard_map/ppermute | solution.py:682
  16.3 3.8 %collective-permute-start.4 = (f32[7,16,256]{2,1,0:T(8,128)S(1)}, f32[7,16,256]{2,1,0:T(8,128)S(1)}, u32[]{:S(2)}, u32[]{:S(2)}) collective-permute-start(f32[7,16,256]{2,1,0:T(8,128)S(1)} %get-tuple-element.41), channel_id=1, source_target_pairs={{0,4},{4,0},{8,12},{12,8},{16,20},{20,16},{24,28},{28,24},{1,5},{5... | collective-permute-start | bytes 344072 | tf_op jit(solution)/shard_map/ppermute | solution.py:682
  20.0 0.7 %collective-permute-start.6 = (f32[7,16,256]{2,1,0:T(8,128)S(1)}, f32[7,16,256]{2,1,0:T(8,128)S(1)}, u32[]{:S(2)}, u32[]{:S(2)}) collective-permute-start(f32[7,16,256]{2,1,0:T(8,128)S(1)} %get-tuple-element.44), channel_id=1, source_target_pairs={{4,8},{12,16},{20,24},{8,4},{16,12},{24,20},{5,9},{13,17},{21,25},... | collective-permute-start | bytes 344072 | tf_op jit(solution)/shard_map/ppermute | solution.py:682
  20.7 5.5 %collective-permute-start.7 = (f32[7,16,256]{2,1,0:T(8,128)S(1)}, f32[7,16,256]{2,1,0:T(8,128)S(1)}, u32[]{:S(2)}, u32[]{:S(2)}) collective-permute-start(f32[7,16,256]{2,1,0:T(8,128)S(1)} %get-tuple-element.45), channel_id=1, source_target_pairs={{0,4},{4,0},{8,12},{12,8},{16,20},{20,16},{24,28},{28,24},{1,5},{5... | collective-permute-start | bytes 344072 | tf_op jit(solution)/shard_map/ppermute | solution.py:682
  26.2 0.3 own_planes.1
  26.6 2.7 %collective-permute-start.5 = (f32[8,16,256]{2,1,0:T(8,128)S(1)}, f32[8,16,256]{2,1,0:T(8,128)S(1)}, u32[]{:S(2)}, u32[]{:S(2)}) collective-permute-start(f32[8,16,256]{2,1,0:T(8,128)S(1)} %add_rims.2.correction.mine), channel_id=1, source_target_pairs={{0,2},{1,3},{2,0},{3,1},{4,6},{5,7},{6,4},{7,5},{8,10},{9,11},{10,... | collective-permute-start | bytes 393224 | tf_op jit(solution)/shard_map/ppermute | solution.py:688
  29.2 0.8 %moment_rows.2.rest_0_.refs_0_ = f32[16,128]{1,0:T(8,128)S(1)} custom-call(f32[8,64,256]{2,1,0:T(8,128)S(1)} %copy-done, s32[8,64,256]{2,1,0:T(8,128)S(1)} %copy-done.1, f32[160,16]{1,0:T(8,128)S(1)} %get-tuple-element.42.picked, f32[32,128]{1,0:T(8,128)S(1)} %get-tuple-element.24.after.base, f32[8,16,256]{2,1,0:T(8,128)S(1)} %add_rims.2.correction.mine), custom_call_target="tpu_custom_call" | custom-call | tf_op jit(solution)/shard_map/moment_rows/pallas_call | solution.py:527
  30.1 0.4 collective-permute-start.8
  30.5 1.8 %moment_rows.3.rest_0_ = f32[32,128]{1,0:T(8,128)} custom-call(f32[8,64,256]{2,1,0:T(8,128)S(1)} %copy-done, s32[8,64,256]{2,1,0:T(8,128)S(1)} %copy-done.1, f32[160,16]{1,0:T(8,128)S(1)} %get-tuple-element.42.picked, f32[32,128]{1,0:T(8,128)S(1)} %get-tuple-element.24.after.base, f32[8,16,256]{2,1,0:T(8,128)S(1)} %add_rims.3.correction.mine, ...), custom_call_target="tpu_custom_call" | custom-call | tf_op jit(solution)/shard_map/moment_rows/pallas_call | solution.py:527
  32.3 4.0 %all-to-all-start = ((f32[32,1,128]{2,1,0:T(1,128)}), f32[32,1,128]{2,1,0:T(1,128)S(1)}, u32[]{:S(2)}, u32[]{:S(2)}) async-start(f32[32,1,128]{2,1,0:T(1,128)} %bitcast.4), calls=%async_computation | async-start | bytes 32768 | tf_op jit(solution)/shard_map/all_to_all | solution.py:691
  36.4 2.2 %collective-permute-done.5.other = f32[8,16,256]{2,1,0:T(8,128)S(1)} collective-permute-done((f32[8,16,256]{2,1,0:T(8,128)S(1)}, f32[8,16,256]{2,1,0:T(8,128)S(1)}, u32[]{:S(2)}, u32[]{:S(2)}) %collective-permute-start.5) | collective-permute-done | bytes 131104 | tf_op jit(solution)/shard_map/ppermute | solution.py:688
  38.6 0.7 %collective-permute-start.9 = (f32[136,256]{1,0:T(8,128)S(1)}, f32[136,256]{1,0:T(8,128)S(1)}, u32[]{:S(2)}, u32[]{:S(2)}) collective-permute-start(f32[136,256]{1,0:T(8,128)S(1)} %update.2.source.refs_0_), channel_id=1, source_target_pairs={{0,1},{1,0},{2,3},{3,2},{4,5},{5,4},{6,7},{7,6},{8,9},{9,8},{10,11... | collective-permute-start | bytes 417800 | tf_op jit(solution)/shard_map/ppermute | solution.py:697
  39.3 2.2 %collective-permute-done.8.other = f32[8,16,256]{2,1,0:T(8,128)S(1)} collective-permute-done((f32[8,16,256]{2,1,0:T(8,128)S(1)}, f32[8,16,256]{2,1,0:T(8,128)S(1)}, u32[]{:S(2)}, u32[]{:S(2)}) %collective-permute-start.8) | collective-permute-done | bytes 131104 | tf_op jit(solution)/shard_map/ppermute | solution.py:688
  41.5 0.1 collective-permute-start.10
  41.6 2.0 %all-to-all-done = f32[32,1,128]{2,1,0:T(1,128)S(1)} async-done(((f32[32,1,128]{2,1,0:T(1,128)}), f32[32,1,128]{2,1,0:T(1,128)S(1)}, u32[]{:S(2)}, u32[]{:S(2)}) %all-to-all-start) | async-done | bytes 16416 | tf_op jit(solution)/shard_map/all_to_all | solution.py:691
  43.5 1.0 %nucleus_table.1 = f32[10,128]{1,0:T(8,128)} custom-call(f32[32,128]{1,0:T(8,128)S(1)} %bitcast.8), custom_call_target="tpu_custom_call" | custom-call | flops 10000000000 | bytes 20000000 | tf_op jit(solution)/shard_map/nucleus_table/pallas_call | solution.py:570
  44.5 0.8 %begin_result.1.begun = f32[8,64,256]{2,1,0:T(8,128)} custom-call(f32[136,256]{1,0:T(8,128)S(1)} %update.2.source.refs_0_, f32[128,256]{1,0:T(8,128)S(1)} %update.3.refs_1_), custom_call_target="tpu_custom_call" | custom-call | tf_op jit(solution)/shard_map/begin_result/pallas_call | solution.py:623
  45.4 1.9 %collective-permute-done.10.refs_1_ = f32[128,256]{1,0:T(8,128)S(1)} collective-permute-done((f32[128,256]{1,0:T(8,128)S(1)}, f32[128,256]{1,0:T(8,128)S(1)}, u32[]{:S(2)}, u32[]{:S(2)}) %collective-permute-start.10) | collective-permute-done | bytes 131104 | tf_op jit(solution)/shard_map/ppermute | solution.py:697
  47.3 0.8 %finish.1 = f32[8,64,256]{2,1,0:T(8,128)} custom-call(f32[8,64,256]{2,1,0:T(8,128)} %begin_result.1.begun, f32[136,256]{1,0:T(8,128)S(1)} %collective-permute-done.9.refs_0_, f32[128,256]{1,0:T(8,128)S(1)} %collective-permute-done.10.refs_1_), custom_call_target="tpu_custom_call", output_to_operand_aliasing={{}: (0, {})} | custom-call | tf_op jit(solution)/shard_map/finish/pallas_call | solution.py:641
  (23 shorter events, 0.2 us)
Async XLA Ops:
  0.6 1.0 %copy-start.2 = (f32[1,8,64,256]{3,2,1,0:T(8,128)S(1)}, f32[1,8,64,256]{3,2,1,0:T(8,128)}, u32[]{:S(2)}) copy-start(f32[1,8,64,256]{3,2,1,0:T(8,128)} %refs_12_.1) | copy-start | bytes 1572868
  0.6 1.0 %copy-start.3 = (f32[1,3,15]{2,0,1:T(1,128)S(1)}, f32[1,3,15]{2,0,1:T(1,128)}, u32[]{:S(2)}) copy-start(f32[1,3,15]{2,0,1:T(1,128)} %param.8) | copy-start | bytes 544
  0.7 4.1 %copy-start = (f32[8,64,256]{2,1,0:T(8,128)S(1)}, f32[8,64,256]{2,1,0:T(8,128)}, u32[]{:S(2)}) copy-start(f32[8,64,256]{2,1,0:T(8,128)} %estimate.13) | copy-start | bytes 1572868
  1.7 11.3 %collective-permute-start = (f32[344,256]{1,0:T(8,128)S(1)}, f32[344,256]{1,0:T(8,128)S(1)}, u32[]{:S(2)}, u32[]{:S(2)}) collective-permute-start(f32[344,256]{1,0:T(8,128)S(1)} %view_out.1), channel_id=1, source_target_pairs={{0,1},{1,0},{2,3},{3,2},{4,5},{5,4},{6,7},{7,6},{8,9},{9,8},{10,11... | collective-permute-start | bytes 1056776 | tf_op jit(solution)/shard_map/ppermute | solution.py:670
  4.8 8.8 %collective-permute-start.1 = (f32[7,48,256]{2,1,0:T(8,128)S(1)}, f32[7,48,256]{2,1,0:T(8,128)S(1)}, u32[]{:S(2)}, u32[]{:S(2)}) collective-permute-start(f32[7,48,256]{2,1,0:T(8,128)S(1)} %get-tuple-element.35), channel_id=1, source_target_pairs={{4,8},{12,16},{20,24},{8,4},{16,12},{24,20},{5,9},{13,17},{21,25},... | collective-permute-start | bytes 1032200 | tf_op jit(solution)/shard_map/ppermute | solution.py:672
  5.5 2.9 %copy-start.4 = (s32[1,16,1]{1,2,0:T(1,128)S(1)}, s32[1,16,1]{1,2,0:T(1,128)}, u32[]{:S(2)}) copy-start(s32[1,16,1]{1,2,0:T(1,128)} %param.10) | copy-start | bytes 196
  5.5 2.9 %copy-start.5 = (s32[1,16]{1,0:T(1,128)S(1)}, s32[1,16]{1,0:T(1,128)}, u32[]{:S(2)}) copy-start(s32[1,16]{1,0:T(1,128)} %index_row.1) | copy-start | bytes 196
  5.6 8.1 %collective-permute-start.2 = (f32[7,48,256]{2,1,0:T(8,128)S(1)}, f32[7,48,256]{2,1,0:T(8,128)S(1)}, u32[]{:S(2)}, u32[]{:S(2)}) collective-permute-start(f32[7,48,256]{2,1,0:T(8,128)S(1)} %get-tuple-element.36), channel_id=1, source_target_pairs={{0,4},{4,0},{8,12},{12,8},{16,20},{20,16},{24,28},{28,24},{1,5},{5... | collective-permute-start | bytes 1032200 | tf_op jit(solution)/shard_map/ppermute | solution.py:673
  15.5 13.8 %copy-start.1 = (s32[8,64,256]{2,1,0:T(8,128)S(1)}, s32[8,64,256]{2,1,0:T(8,128)}, u32[]{:S(2)}) copy-start(s32[8,64,256]{2,1,0:T(8,128)} %labels.3) | copy-start | bytes 1572868
  15.5 11.0 %collective-permute-start.3 = (f32[7,16,256]{2,1,0:T(8,128)S(1)}, f32[7,16,256]{2,1,0:T(8,128)S(1)}, u32[]{:S(2)}, u32[]{:S(2)}) collective-permute-start(f32[7,16,256]{2,1,0:T(8,128)S(1)} %get-tuple-element.40), channel_id=1, source_target_pairs={{4,8},{12,16},{20,24},{8,4},{16,12},{24,20},{5,9},{13,17},{21,25},... | collective-permute-start | bytes 344072 | tf_op jit(solution)/shard_map/ppermute | solution.py:682
  16.3 10.2 %collective-permute-start.4 = (f32[7,16,256]{2,1,0:T(8,128)S(1)}, f32[7,16,256]{2,1,0:T(8,128)S(1)}, u32[]{:S(2)}, u32[]{:S(2)}) collective-permute-start(f32[7,16,256]{2,1,0:T(8,128)S(1)} %get-tuple-element.41), channel_id=1, source_target_pairs={{0,4},{4,0},{8,12},{12,8},{16,20},{20,16},{24,28},{28,24},{1,5},{5... | collective-permute-start | bytes 344072 | tf_op jit(solution)/shard_map/ppermute | solution.py:682
  20.0 10.0 %collective-permute-start.6 = (f32[7,16,256]{2,1,0:T(8,128)S(1)}, f32[7,16,256]{2,1,0:T(8,128)S(1)}, u32[]{:S(2)}, u32[]{:S(2)}) collective-permute-start(f32[7,16,256]{2,1,0:T(8,128)S(1)} %get-tuple-element.44), channel_id=1, source_target_pairs={{4,8},{12,16},{20,24},{8,4},{16,12},{24,20},{5,9},{13,17},{21,25},... | collective-permute-start | bytes 344072 | tf_op jit(solution)/shard_map/ppermute | solution.py:682
  20.7 9.4 %collective-permute-start.7 = (f32[7,16,256]{2,1,0:T(8,128)S(1)}, f32[7,16,256]{2,1,0:T(8,128)S(1)}, u32[]{:S(2)}, u32[]{:S(2)}) collective-permute-start(f32[7,16,256]{2,1,0:T(8,128)S(1)} %get-tuple-element.45), channel_id=1, source_target_pairs={{0,4},{4,0},{8,12},{12,8},{16,20},{20,16},{24,28},{28,24},{1,5},{5... | collective-permute-start | bytes 344072 | tf_op jit(solution)/shard_map/ppermute | solution.py:682
  26.6 12.0 %collective-permute-start.5 = (f32[8,16,256]{2,1,0:T(8,128)S(1)}, f32[8,16,256]{2,1,0:T(8,128)S(1)}, u32[]{:S(2)}, u32[]{:S(2)}) collective-permute-start(f32[8,16,256]{2,1,0:T(8,128)S(1)} %add_rims.2.correction.mine), channel_id=1, source_target_pairs={{0,2},{1,3},{2,0},{3,1},{4,6},{5,7},{6,4},{7,5},{8,10},{9,11},{10,... | collective-permute-start | bytes 393224 | tf_op jit(solution)/shard_map/ppermute | solution.py:688
  30.1 11.3 %collective-permute-start.8 = (f32[8,16,256]{2,1,0:T(8,128)S(1)}, f32[8,16,256]{2,1,0:T(8,128)S(1)}, u32[]{:S(2)}, u32[]{:S(2)}) collective-permute-start(f32[8,16,256]{2,1,0:T(8,128)S(1)} %add_rims.3.correction.mine), channel_id=1, source_target_pairs={{0,2},{1,3},{2,0},{3,1},{4,6},{5,7},{6,4},{7,5},{8,10},{9,11},{10,... | collective-permute-start | bytes 393224 | tf_op jit(solution)/shard_map/ppermute | solution.py:688
  32.3 11.2 %all-to-all-start = ((f32[32,1,128]{2,1,0:T(1,128)}), f32[32,1,128]{2,1,0:T(1,128)S(1)}, u32[]{:S(2)}, u32[]{:S(2)}) async-start(f32[32,1,128]{2,1,0:T(1,128)} %bitcast.4), calls=%async_computation | async-start | bytes 32768 | tf_op jit(solution)/shard_map/all_to_all | solution.py:691
  38.6 8.7 %collective-permute-start.9 = (f32[136,256]{1,0:T(8,128)S(1)}, f32[136,256]{1,0:T(8,128)S(1)}, u32[]{:S(2)}, u32[]{:S(2)}) collective-permute-start(f32[136,256]{1,0:T(8,128)S(1)} %update.2.source.refs_0_), channel_id=1, source_target_pairs={{0,1},{1,0},{2,3},{3,2},{4,5},{5,4},{6,7},{7,6},{8,9},{9,8},{10,11... | collective-permute-start | bytes 417800 | tf_op jit(solution)/shard_map/ppermute | solution.py:697
  41.5 5.8 %collective-permute-start.10 = (f32[128,256]{1,0:T(8,128)S(1)}, f32[128,256]{1,0:T(8,128)S(1)}, u32[]{:S(2)}, u32[]{:S(2)}) collective-permute-start(f32[128,256]{1,0:T(8,128)S(1)} %update.3.refs_1_), channel_id=1, source_target_pairs={{0,1},{1,0},{2,3},{3,2},{4,5},{5,4},{6,7},{7,6},{8,9},{9,8},{10,11... | collective-permute-start | bytes 393224 | tf_op jit(solution)/shard_map/ppermute | solution.py:697

commit v16 on v12

--- a/solution.py
+++ b/solution.py
@@ -684,7 +684,7 @@
     inner = own_planes(taps, own[4], others[4], field_own, field_other)
     mine, other, sums = [], [], []
     for part in range(PARTS):
-        mine.append(add_rims(inner[part], *rims[2 * part : 2 * part + 2], *sums))
+        mine.append(add_rims(inner[part], *rims[2 * part : 2 * part + 2], *mine[-1:]))
         other.append(lax.ppermute(mine[part], "view", across_pairs))
         sums = [moment_rows(views, tiles, part, estimate, mine[part], labels, places, sums)]
     sent = sums[0]

time: 47.1 us -> 47.8 us (1.015)
  waiting for transfers between devices: 5.93 us -> 6.85 us
    ppermute x2, starting transfers between devices: 4.96 us -> 4.03 us  [on_device(): new_other.append(lax.ppermute(new_mine[part], 'view', partner))]
    all_to_all x1, waiting for transfers between devices: 2.15 us -> 3.08 us  [on_device(): lax.all_to_all(sent, ('tile', 'view'), split_axis=0, concat_axis=0, tiled...]
    all_to_all x1, starting transfers between devices: 3.78 us -> 4.64 us  [on_device(): lax.all_to_all(sent, ('tile', 'view'), split_axis=0, concat_axis=0, tiled...]
  transfers between devices with their start and end apart: 12 -> 12, of which waited for: 2 -> 2; matrix products, arithmetic and copies ran while one was open for 0% -> 0% of each run, Pallas kernels for 14% -> 13%
where the time goes in v16:
time: 47.8 us; the launch traced here: 47.6 us
  starting transfers between devices  29.9 us (63%)
  Pallas kernels  8.99 us (19%)
  waiting for transfers between devices  6.85 us (14%)
  local copies, waits for them, and re-layouts  1.03 us (2%)
  between operations  0.86 us (2%)
    ppermute x4, starting transfers between devices, on_device(): lax.ppermute(send, 'tile', pairs)  10.6 us
    all_to_all x1, starting transfers between devices, on_device(): lax.all_to_all(sent, ('tile', 'view'), split_axis=0, concat_axis=0, tiled...  4.64 us
    ppermute x2, starting transfers between devices, on_device(): new_other.append(lax.ppermute(new_mine[part], 'view', partner))  4.03 us
    ppermute x2, starting transfers between devices, on_device(): other.append(lax.ppermute(mine[part], 'view', across_pairs))  3.95 us
    ppermute x1, waiting for transfers between devices, on_device(): swapped = lax.ppermute(packed, 'view', partner)  3.75 us
    ppermute x1, starting transfers between devices, on_device(): swapped = lax.ppermute(packed, 'view', partner)  3.09 us
    all_to_all x1, waiting for transfers between devices, on_device(): lax.all_to_all(sent, ('tile', 'view'), split_axis=0, concat_axis=0, tiled...  3.08 us
    ppermute x1, starting transfers between devices, on_device(): near = lax.ppermute(to_near, 'tile', near_pairs)  2.9 us
  transfers between devices with their start and end apart: 12, of which 2 were waited for; matrix products, arithmetic and copies ran while one was open for 0% of the time, Pallas kernels for 13%

profile of v16, /device:TPU:0, one launch (start us, length us, event | category | flops | bytes accessed | tf_op | source)
XLA Modules:
  0.0 47.6 jit_solution(8155843434049976223)
XLA Ops:
  0.7 0.0 copy-start
  0.7 1.0 %copy-done.2 = f32[1,8,64,256]{3,2,1,0:T(8,128)S(1)} copy-done((f32[1,8,64,256]{3,2,1,0:T(8,128)S(1)}, f32[1,8,64,256]{3,2,1,0:T(8,128)}, u32[]{:S(2)}) %copy-start.2) | copy-done | bytes 524312
  1.7 3.1 %collective-permute-start = (f32[344,256]{1,0:T(8,128)S(1)}, f32[344,256]{1,0:T(8,128)S(1)}, u32[]{:S(2)}, u32[]{:S(2)}) collective-permute-start(f32[344,256]{1,0:T(8,128)S(1)} %view_out.1), channel_id=1, source_target_pairs={{0,1},{1,0},{2,3},{3,2},{4,5},{5,4},{6,7},{7,6},{8,9},{9,8},{10,11... | collective-permute-start | bytes 1056776 | tf_op jit(solution)/shard_map/ppermute | solution.py:670
  4.8 0.7 %collective-permute-start.1 = (f32[7,48,256]{2,1,0:T(8,128)S(1)}, f32[7,48,256]{2,1,0:T(8,128)S(1)}, u32[]{:S(2)}, u32[]{:S(2)}) collective-permute-start(f32[7,48,256]{2,1,0:T(8,128)S(1)} %get-tuple-element.35), channel_id=1, source_target_pairs={{4,8},{12,16},{20,24},{8,4},{16,12},{24,20},{5,9},{13,17},{21,25},... | collective-permute-start | bytes 1032200 | tf_op jit(solution)/shard_map/ppermute | solution.py:672
  5.5 0.0 copy-start.4
  5.5 0.0 copy-start.5
  5.6 2.9 %collective-permute-start.2 = (f32[7,48,256]{2,1,0:T(8,128)S(1)}, f32[7,48,256]{2,1,0:T(8,128)S(1)}, u32[]{:S(2)}, u32[]{:S(2)}) collective-permute-start(f32[7,48,256]{2,1,0:T(8,128)S(1)} %get-tuple-element.36), channel_id=1, source_target_pairs={{0,4},{4,0},{8,12},{12,8},{16,20},{20,16},{24,28},{28,24},{1,5},{5... | collective-permute-start | bytes 1032200 | tf_op jit(solution)/shard_map/ppermute | solution.py:673
  8.5 0.2 slot_places.1
  8.7 0.6 %prepare.2 = (bf16[2,2,256,256]{3,2,1,0:T(8,128)(2,1)S(1)}, bf16[40,144]{1,0:T(8,128)(2,1)S(1)}, bf16[32,144]{1,0:T(8,128)(2,1)S(1)}, f32[8,48,256]{2,1,0:T(8,128)S(1)}, f32[16,128]{1,0:T(8,128)S(1)}) custom-call(f32[3,1,15]{2,1,0:T(1,128)S(1)} %bitcast.10, f32[8,64,256]{2,1,0:T(8,128)S(1)} %copy-done, f32[32,128]{1,0:T(8,128)S(1)} %get-tuple-element.24.after.base), custom_call_target="tpu_custom_call" | custom-call | tf_op jit(solution)/shard_map/prepare/pallas_call | solution.py:170
  9.3 3.7 %collective-permute-done.source.refs_13_ = f32[344,256]{1,0:T(8,128)S(1)} collective-permute-done((f32[344,256]{1,0:T(8,128)S(1)}, f32[344,256]{1,0:T(8,128)S(1)}, u32[]{:S(2)}, u32[]{:S(2)}) %collective-permute-start) | collective-permute-done | bytes 352288 | tf_op jit(solution)/shard_map/ppermute | solution.py:670
  13.0 0.6 %prepare.3 = (bf16[2,2,256,256]{3,2,1,0:T(8,128)(2,1)S(1)}, bf16[40,144]{1,0:T(8,128)(2,1)S(1)}, bf16[32,144]{1,0:T(8,128)(2,1)S(1)}, f32[8,48,256]{2,1,0:T(8,128)S(1)}, f32[16,128]{1,0:T(8,128)S(1)}) custom-call(f32[344,256]{1,0:T(8,128)S(1)} %collective-permute-done.source.refs_13_, f32[8,64,256]{2,1,0:T(8,128)S(1)} %copy-done, f32[3,1,15]{2,1,0:T(1,128)S(1)} %bitcast.11), custom_call_target="tpu_custom_call" | custom-call | tf_op jit(solution)/shard_map/prepare/pallas_call | solution.py:170
  13.6 0.0 collective-permute-done.1.refs_10_
  13.6 0.0 collective-permute-done.2.refs_11_
  13.7 1.8 %ratio_fields.1 = (f32[8,32,256]{2,1,0:T(8,128)S(1)}, f32[8,32,256]{2,1,0:T(8,128)S(1)}, f32[7,16,256]{2,1,0:T(8,128)S(1)}, f32[7,16,256]{2,1,0:T(8,128)S(1)}, f...) custom-call(bf16[2,2,256,256]{3,2,1,0:T(8,128)(2,1)S(1)} %get-tuple-element.27.refs_0_, ...), custom_call_target="tpu_custom_call" | custom-call | tf_op jit(solution)/shard_map/ratio_fields/pallas_call | solution.py:285
  15.5 0.7 %collective-permute-start.3 = (f32[7,16,256]{2,1,0:T(8,128)S(1)}, f32[7,16,256]{2,1,0:T(8,128)S(1)}, u32[]{:S(2)}, u32[]{:S(2)}) collective-permute-start(f32[7,16,256]{2,1,0:T(8,128)S(1)} %get-tuple-element.40), channel_id=1, source_target_pairs={{4,8},{12,16},{20,24},{8,4},{16,12},{24,20},{5,9},{13,17},{21,25},... | collective-permute-start | bytes 344072 | tf_op jit(solution)/shard_map/ppermute | solution.py:682
  16.1 3.8 %collective-permute-start.4 = (f32[7,16,256]{2,1,0:T(8,128)S(1)}, f32[7,16,256]{2,1,0:T(8,128)S(1)}, u32[]{:S(2)}, u32[]{:S(2)}) collective-permute-start(f32[7,16,256]{2,1,0:T(8,128)S(1)} %get-tuple-element.41), channel_id=1, source_target_pairs={{0,4},{4,0},{8,12},{12,8},{16,20},{20,16},{24,28},{28,24},{1,5},{5... | collective-permute-start | bytes 344072 | tf_op jit(solution)/shard_map/ppermute | solution.py:682
  19.9 0.7 %collective-permute-start.6 = (f32[7,16,256]{2,1,0:T(8,128)S(1)}, f32[7,16,256]{2,1,0:T(8,128)S(1)}, u32[]{:S(2)}, u32[]{:S(2)}) collective-permute-start(f32[7,16,256]{2,1,0:T(8,128)S(1)} %get-tuple-element.44), channel_id=1, source_target_pairs={{4,8},{12,16},{20,24},{8,4},{16,12},{24,20},{5,9},{13,17},{21,25},... | collective-permute-start | bytes 344072 | tf_op jit(solution)/shard_map/ppermute | solution.py:682
  20.6 5.5 %collective-permute-start.7 = (f32[7,16,256]{2,1,0:T(8,128)S(1)}, f32[7,16,256]{2,1,0:T(8,128)S(1)}, u32[]{:S(2)}, u32[]{:S(2)}) collective-permute-start(f32[7,16,256]{2,1,0:T(8,128)S(1)} %get-tuple-element.45), channel_id=1, source_target_pairs={{0,4},{4,0},{8,12},{12,8},{16,20},{20,16},{24,28},{28,24},{1,5},{5... | collective-permute-start | bytes 344072 | tf_op jit(solution)/shard_map/ppermute | solution.py:682
  26.1 0.3 own_planes.1
  26.4 0.0 collective-permute-done.4.near
  26.4 0.0 copy-start.1
  26.4 2.5 %collective-permute-start.5 = (f32[8,16,256]{2,1,0:T(8,128)S(1)}, f32[8,16,256]{2,1,0:T(8,128)S(1)}, u32[]{:S(2)}, u32[]{:S(2)}) collective-permute-start(f32[8,16,256]{2,1,0:T(8,128)S(1)} %add_rims.2.rest_0_.correction.mine), channel_id=1, source_target_pairs={{0,3},{1,2},{2,1},{3,0},{4,7},{5,6},{6,5},{7,4},{8,11},{9,10},{10,... | collective-permute-start | bytes 393224 | tf_op jit(solution)/shard_map/ppermute | solution.py:688
  29.0 1.4 %collective-permute-start.8 = (f32[8,16,256]{2,1,0:T(8,128)S(1)}, f32[8,16,256]{2,1,0:T(8,128)S(1)}, u32[]{:S(2)}, u32[]{:S(2)}) collective-permute-start(f32[8,16,256]{2,1,0:T(8,128)S(1)} %add_rims.3.correction.mine), channel_id=1, source_target_pairs={{0,3},{1,2},{2,1},{3,0},{4,7},{5,6},{6,5},{7,4},{8,11},{9,10},{10,... | collective-permute-start | bytes 393224 | tf_op jit(solution)/shard_map/ppermute | solution.py:688
  30.4 0.8 %moment_rows.2.refs_0_ = f32[16,128]{1,0:T(8,128)S(1)} custom-call(f32[8,64,256]{2,1,0:T(8,128)S(1)} %copy-done, s32[8,64,256]{2,1,0:T(8,128)S(1)} %copy-done.1, f32[160,16]{1,0:T(8,128)S(1)} %get-tuple-element.42.picked, f32[32,128]{1,0:T(8,128)S(1)} %get-tuple-element.24.after.base, f32[8,16,256]{2,1,0:T(8,128)S(1)} %add_rims.2.rest_0_.correction.mine), custom_call_target="tpu_custom_call" | custom-call | tf_op jit(solution)/shard_map/moment_rows/pallas_call | solution.py:527
  31.3 1.8 %moment_rows.3.rest_0_ = f32[32,128]{1,0:T(8,128)} custom-call(f32[8,64,256]{2,1,0:T(8,128)S(1)} %copy-done, s32[8,64,256]{2,1,0:T(8,128)S(1)} %copy-done.1, f32[160,16]{1,0:T(8,128)S(1)} %get-tuple-element.42.picked, f32[32,128]{1,0:T(8,128)S(1)} %get-tuple-element.24.after.base, f32[8,16,256]{2,1,0:T(8,128)S(1)} %add_rims.3.correction.mine, ...), custom_call_target="tpu_custom_call" | custom-call | tf_op jit(solution)/shard_map/moment_rows/pallas_call | solution.py:527
  33.1 4.6 %all-to-all-start = ((f32[32,1,128]{2,1,0:T(1,128)}), f32[32,1,128]{2,1,0:T(1,128)S(1)}, u32[]{:S(2)}, u32[]{:S(2)}) async-start(f32[32,1,128]{2,1,0:T(1,128)} %bitcast.4), calls=%async_computation | async-start | bytes 32768 | tf_op jit(solution)/shard_map/all_to_all | solution.py:691
  37.8 1.9 %collective-permute-start.9 = (f32[136,256]{1,0:T(8,128)S(1)}, f32[136,256]{1,0:T(8,128)S(1)}, u32[]{:S(2)}, u32[]{:S(2)}) collective-permute-start(f32[136,256]{1,0:T(8,128)S(1)} %update.2.source.refs_0_), channel_id=1, source_target_pairs={{0,1},{1,0},{2,3},{3,2},{4,5},{5,4},{6,7},{7,6},{8,9},{9,8},{10,11... | collective-permute-start | bytes 417800 | tf_op jit(solution)/shard_map/ppermute | solution.py:697
  39.7 2.1 %collective-permute-start.10 = (f32[128,256]{1,0:T(8,128)S(1)}, f32[128,256]{1,0:T(8,128)S(1)}, u32[]{:S(2)}, u32[]{:S(2)}) collective-permute-start(f32[128,256]{1,0:T(8,128)S(1)} %update.3.refs_1_), channel_id=1, source_target_pairs={{0,1},{1,0},{2,3},{3,2},{4,5},{5,4},{6,7},{7,6},{8,9},{9,8},{10,11... | collective-permute-start | bytes 393224 | tf_op jit(solution)/shard_map/ppermute | solution.py:697
  41.8 3.1 %all-to-all-done = f32[32,1,128]{2,1,0:T(1,128)S(1)} async-done(((f32[32,1,128]{2,1,0:T(1,128)}), f32[32,1,128]{2,1,0:T(1,128)S(1)}, u32[]{:S(2)}, u32[]{:S(2)}) %all-to-all-start) | async-done | bytes 16416 | tf_op jit(solution)/shard_map/all_to_all | solution.py:691
  44.9 1.0 %nucleus_table.1 = f32[10,128]{1,0:T(8,128)} custom-call(f32[32,128]{1,0:T(8,128)S(1)} %bitcast.8), custom_call_target="tpu_custom_call" | custom-call | flops 10000000000 | bytes 20000000 | tf_op jit(solution)/shard_map/nucleus_table/pallas_call | solution.py:570
  45.9 0.8 %begin_result.1.begun = f32[8,64,256]{2,1,0:T(8,128)} custom-call(f32[136,256]{1,0:T(8,128)S(1)} %update.2.source.refs_0_, f32[128,256]{1,0:T(8,128)S(1)} %update.3.refs_1_), custom_call_target="tpu_custom_call" | custom-call | tf_op jit(solution)/shard_map/begin_result/pallas_call | solution.py:623
  46.8 0.8 %finish.1 = f32[8,64,256]{2,1,0:T(8,128)} custom-call(f32[8,64,256]{2,1,0:T(8,128)} %begin_result.1.begun, f32[136,256]{1,0:T(8,128)S(1)} %collective-permute-done.9.refs_0_, f32[128,256]{1,0:T(8,128)S(1)} %collective-permute-done.10.refs_1_), custom_call_target="tpu_custom_call", output_to_operand_aliasing={{}: (0, {})} | custom-call | tf_op jit(solution)/shard_map/finish/pallas_call | solution.py:641
  (23 shorter events, 0.2 us)
Async XLA Ops:
  0.6 1.0 %copy-start.2 = (f32[1,8,64,256]{3,2,1,0:T(8,128)S(1)}, f32[1,8,64,256]{3,2,1,0:T(8,128)}, u32[]{:S(2)}) copy-start(f32[1,8,64,256]{3,2,1,0:T(8,128)} %refs_12_.1) | copy-start | bytes 1572868
  0.6 1.0 %copy-start.3 = (f32[1,3,15]{2,0,1:T(1,128)S(1)}, f32[1,3,15]{2,0,1:T(1,128)}, u32[]{:S(2)}) copy-start(f32[1,3,15]{2,0,1:T(1,128)} %param.8) | copy-start | bytes 544
  0.7 4.1 %copy-start = (f32[8,64,256]{2,1,0:T(8,128)S(1)}, f32[8,64,256]{2,1,0:T(8,128)}, u32[]{:S(2)}) copy-start(f32[8,64,256]{2,1,0:T(8,128)} %estimate.13) | copy-start | bytes 1572868
  1.7 11.3 %collective-permute-start = (f32[344,256]{1,0:T(8,128)S(1)}, f32[344,256]{1,0:T(8,128)S(1)}, u32[]{:S(2)}, u32[]{:S(2)}) collective-permute-start(f32[344,256]{1,0:T(8,128)S(1)} %view_out.1), channel_id=1, source_target_pairs={{0,1},{1,0},{2,3},{3,2},{4,5},{5,4},{6,7},{7,6},{8,9},{9,8},{10,11... | collective-permute-start | bytes 1056776 | tf_op jit(solution)/shard_map/ppermute | solution.py:670
  4.8 8.8 %collective-permute-start.1 = (f32[7,48,256]{2,1,0:T(8,128)S(1)}, f32[7,48,256]{2,1,0:T(8,128)S(1)}, u32[]{:S(2)}, u32[]{:S(2)}) collective-permute-start(f32[7,48,256]{2,1,0:T(8,128)S(1)} %get-tuple-element.35), channel_id=1, source_target_pairs={{4,8},{12,16},{20,24},{8,4},{16,12},{24,20},{5,9},{13,17},{21,25},... | collective-permute-start | bytes 1032200 | tf_op jit(solution)/shard_map/ppermute | solution.py:672
  5.5 2.9 %copy-start.4 = (s32[1,16,1]{1,2,0:T(1,128)S(1)}, s32[1,16,1]{1,2,0:T(1,128)}, u32[]{:S(2)}) copy-start(s32[1,16,1]{1,2,0:T(1,128)} %param.10) | copy-start | bytes 196
  5.5 2.9 %copy-start.5 = (s32[1,16]{1,0:T(1,128)S(1)}, s32[1,16]{1,0:T(1,128)}, u32[]{:S(2)}) copy-start(s32[1,16]{1,0:T(1,128)} %index_row.1) | copy-start | bytes 196
  5.6 8.1 %collective-permute-start.2 = (f32[7,48,256]{2,1,0:T(8,128)S(1)}, f32[7,48,256]{2,1,0:T(8,128)S(1)}, u32[]{:S(2)}, u32[]{:S(2)}) collective-permute-start(f32[7,48,256]{2,1,0:T(8,128)S(1)} %get-tuple-element.36), channel_id=1, source_target_pairs={{0,4},{4,0},{8,12},{12,8},{16,20},{20,16},{24,28},{28,24},{1,5},{5... | collective-permute-start | bytes 1032200 | tf_op jit(solution)/shard_map/ppermute | solution.py:673
  15.5 10.9 %collective-permute-start.3 = (f32[7,16,256]{2,1,0:T(8,128)S(1)}, f32[7,16,256]{2,1,0:T(8,128)S(1)}, u32[]{:S(2)}, u32[]{:S(2)}) collective-permute-start(f32[7,16,256]{2,1,0:T(8,128)S(1)} %get-tuple-element.40), channel_id=1, source_target_pairs={{4,8},{12,16},{20,24},{8,4},{16,12},{24,20},{5,9},{13,17},{21,25},... | collective-permute-start | bytes 344072 | tf_op jit(solution)/shard_map/ppermute | solution.py:682
  16.1 10.2 %collective-permute-start.4 = (f32[7,16,256]{2,1,0:T(8,128)S(1)}, f32[7,16,256]{2,1,0:T(8,128)S(1)}, u32[]{:S(2)}, u32[]{:S(2)}) collective-permute-start(f32[7,16,256]{2,1,0:T(8,128)S(1)} %get-tuple-element.41), channel_id=1, source_target_pairs={{0,4},{4,0},{8,12},{12,8},{16,20},{20,16},{24,28},{28,24},{1,5},{5... | collective-permute-start | bytes 344072 | tf_op jit(solution)/shard_map/ppermute | solution.py:682
  19.9 9.1 %collective-permute-start.6 = (f32[7,16,256]{2,1,0:T(8,128)S(1)}, f32[7,16,256]{2,1,0:T(8,128)S(1)}, u32[]{:S(2)}, u32[]{:S(2)}) collective-permute-start(f32[7,16,256]{2,1,0:T(8,128)S(1)} %get-tuple-element.44), channel_id=1, source_target_pairs={{4,8},{12,16},{20,24},{8,4},{16,12},{24,20},{5,9},{13,17},{21,25},... | collective-permute-start | bytes 344072 | tf_op jit(solution)/shard_map/ppermute | solution.py:682
  20.6 8.4 %collective-permute-start.7 = (f32[7,16,256]{2,1,0:T(8,128)S(1)}, f32[7,16,256]{2,1,0:T(8,128)S(1)}, u32[]{:S(2)}, u32[]{:S(2)}) collective-permute-start(f32[7,16,256]{2,1,0:T(8,128)S(1)} %get-tuple-element.45), channel_id=1, source_target_pairs={{0,4},{4,0},{8,12},{12,8},{16,20},{20,16},{24,28},{28,24},{1,5},{5... | collective-permute-start | bytes 344072 | tf_op jit(solution)/shard_map/ppermute | solution.py:682
  26.4 4.1 %copy-start.1 = (s32[8,64,256]{2,1,0:T(8,128)S(1)}, s32[8,64,256]{2,1,0:T(8,128)}, u32[]{:S(2)}) copy-start(s32[8,64,256]{2,1,0:T(8,128)} %labels.3) | copy-start | bytes 1572868
  26.4 11.3 %collective-permute-start.5 = (f32[8,16,256]{2,1,0:T(8,128)S(1)}, f32[8,16,256]{2,1,0:T(8,128)S(1)}, u32[]{:S(2)}, u32[]{:S(2)}) collective-permute-start(f32[8,16,256]{2,1,0:T(8,128)S(1)} %add_rims.2.rest_0_.correction.mine), channel_id=1, source_target_pairs={{0,3},{1,2},{2,1},{3,0},{4,7},{5,6},{6,5},{7,4},{8,11},{9,10},{10,... | collective-permute-start | bytes 393224 | tf_op jit(solution)/shard_map/ppermute | solution.py:688
  29.0 10.7 %collective-permute-start.8 = (f32[8,16,256]{2,1,0:T(8,128)S(1)}, f32[8,16,256]{2,1,0:T(8,128)S(1)}, u32[]{:S(2)}, u32[]{:S(2)}) collective-permute-start(f32[8,16,256]{2,1,0:T(8,128)S(1)} %add_rims.3.correction.mine), channel_id=1, source_target_pairs={{0,3},{1,2},{2,1},{3,0},{4,7},{5,6},{6,5},{7,4},{8,11},{9,10},{10,... | collective-permute-start | bytes 393224 | tf_op jit(solution)/shard_map/ppermute | solution.py:688
  33.1 11.8 %all-to-all-start = ((f32[32,1,128]{2,1,0:T(1,128)}), f32[32,1,128]{2,1,0:T(1,128)S(1)}, u32[]{:S(2)}, u32[]{:S(2)}) async-start(f32[32,1,128]{2,1,0:T(1,128)} %bitcast.4), calls=%async_computation | async-start | bytes 32768 | tf_op jit(solution)/shard_map/all_to_all | solution.py:691
  37.8 9.0 %collective-permute-start.9 = (f32[136,256]{1,0:T(8,128)S(1)}, f32[136,256]{1,0:T(8,128)S(1)}, u32[]{:S(2)}, u32[]{:S(2)}) collective-permute-start(f32[136,256]{1,0:T(8,128)S(1)} %update.2.source.refs_0_), channel_id=1, source_target_pairs={{0,1},{1,0},{2,3},{3,2},{4,5},{5,4},{6,7},{7,6},{8,9},{9,8},{10,11... | collective-permute-start | bytes 417800 | tf_op jit(solution)/shard_map/ppermute | solution.py:697
  39.7 7.1 %collective-permute-start.10 = (f32[128,256]{1,0:T(8,128)S(1)}, f32[128,256]{1,0:T(8,128)S(1)}, u32[]{:S(2)}, u32[]{:S(2)}) collective-permute-start(f32[128,256]{1,0:T(8,128)S(1)} %update.3.refs_1_), channel_id=1, source_target_pairs={{0,1},{1,0},{2,3},{3,2},{4,5},{5,4},{6,7},{7,6},{8,9},{9,8},{10,11... | collective-permute-start | bytes 393224 | tf_op jit(solution)/shard_map/ppermute | solution.py:697

commit v17 on v12

--- a/solution.py
+++ b/solution.py
@@ -398,7 +398,7 @@
     result = jnp.zeros((count, LANES), F32)
     for place in range(CAP):
         chosen = named & (rank == place)
-        picked[place * count : (place + 1) * count] = chosen.astype(F32)
+        picked[place * count : (place + 1) * count] = chosen.astype(F32).astype(BF16)
         ids = jnp.sum(jnp.where(chosen, index, 0.0), axis=1, keepdims=True)
         result = jnp.where(lanes == place * WIDTH + IDS, ids, result)
     base[...] = result
@@ -410,7 +410,7 @@
     return pl.pallas_call(
         functools.partial(slots_kernel, views),
         out_shape=(
-            jax.ShapeDtypeStruct((CAP * count, slots), F32),
+            jax.ShapeDtypeStruct((CAP * count, slots), BF16),
             jax.ShapeDtypeStruct((count, LANES), F32),
         ),
         in_specs=[VMEM, VMEM],
@@ -510,9 +510,13 @@
     lax.fori_loop(0, slots // group, one_group, 0)
     if part < PARTS - 1:
         return
+    whole = table[...]
+    upper, _ = split(whole)
+    middle, lower = split(whole - upper.astype(F32))
     rows = jnp.dot(
-        picked[...], table[...], precision=lax.Precision.HIGHEST, preferred_element_type=F32
+        picked[...], jnp.concatenate([upper, middle, lower], axis=1), preferred_element_type=F32
     )
+    rows = rows[:, :LANES] + rows[:, LANES : 2 * LANES] + rows[:, 2 * LANES :]
     total = base[...]
     count = total.shape[0]
     for place in range(CAP):

time: 47.1 us -> 47.1 us (level)
  transfers between devices with their start and end apart: 12 -> 12, of which waited for: 2 -> 2; matrix products, arithmetic and copies ran while one was open for 0% -> 0% of each run, Pallas kernels for 14% -> 13%
where the time goes in v17:
time: 47.1 us; the launch traced here: 46.9 us
  starting transfers between devices  30.1 us (64%)
  Pallas kernels  8.95 us (19%)
  waiting for transfers between devices  5.87 us (12%)
  local copies, waits for them, and re-layouts  1.03 us (2%)
  between operations  0.88 us (2%)
    ppermute x4, starting transfers between devices, on_device(): lax.ppermute(send, 'tile', pairs)  10.7 us
    ppermute x2, starting transfers between devices, on_device(): new_other.append(lax.ppermute(new_mine[part], 'view', partner))  5.02 us
    ppermute x2, starting transfers between devices, on_device(): other.append(lax.ppermute(mine[part], 'view', across_pairs))  3.95 us
    all_to_all x1, starting transfers between devices, on_device(): lax.all_to_all(sent, ('tile', 'view'), split_axis=0, concat_axis=0, tiled...  3.77 us
    ppermute x1, waiting for transfers between devices, on_device(): swapped = lax.ppermute(packed, 'view', partner)  3.75 us
    ppermute x1, starting transfers between devices, on_device(): swapped = lax.ppermute(packed, 'view', partner)  3.09 us
    ppermute x1, starting transfers between devices, on_device(): near = lax.ppermute(to_near, 'tile', near_pairs)  2.9 us
    pallas_call x2, Pallas kernels, moment_rows(): pl.pallas_call(functools.partial(moments_kernel, views, tiles * planes, p...  2.59 us
  transfers between devices with their start and end apart: 12, of which 2 were waited for; matrix products, arithmetic and copies ran while one was open for 0% of the time, Pallas kernels for 13%

profile of v17, /device:TPU:0, one launch (start us, length us, event | category | flops | bytes accessed | tf_op | source)
XLA Modules:
  0.0 46.9 jit_solution(14539727665801604401)
XLA Ops:
  0.7 0.0 copy-start
  0.7 1.0 %copy-done.2 = f32[1,8,64,256]{3,2,1,0:T(8,128)S(1)} copy-done((f32[1,8,64,256]{3,2,1,0:T(8,128)S(1)}, f32[1,8,64,256]{3,2,1,0:T(8,128)}, u32[]{:S(2)}) %copy-start.2) | copy-done | bytes 524312
  1.7 3.1 %collective-permute-start = (f32[344,256]{1,0:T(8,128)S(1)}, f32[344,256]{1,0:T(8,128)S(1)}, u32[]{:S(2)}, u32[]{:S(2)}) collective-permute-start(f32[344,256]{1,0:T(8,128)S(1)} %view_out.1), channel_id=1, source_target_pairs={{0,1},{1,0},{2,3},{3,2},{4,5},{5,4},{6,7},{7,6},{8,9},{9,8},{10,11... | collective-permute-start | bytes 1056776 | tf_op jit(solution)/shard_map/ppermute | solution.py:674
  4.8 0.7 %collective-permute-start.1 = (f32[7,48,256]{2,1,0:T(8,128)S(1)}, f32[7,48,256]{2,1,0:T(8,128)S(1)}, u32[]{:S(2)}, u32[]{:S(2)}) collective-permute-start(f32[7,48,256]{2,1,0:T(8,128)S(1)} %get-tuple-element.35), channel_id=1, source_target_pairs={{4,8},{12,16},{20,24},{8,4},{16,12},{24,20},{5,9},{13,17},{21,25},... | collective-permute-start | bytes 1032200 | tf_op jit(solution)/shard_map/ppermute | solution.py:676
  5.5 0.0 copy-start.4
  5.5 0.0 copy-start.5
  5.6 2.9 %collective-permute-start.2 = (f32[7,48,256]{2,1,0:T(8,128)S(1)}, f32[7,48,256]{2,1,0:T(8,128)S(1)}, u32[]{:S(2)}, u32[]{:S(2)}) collective-permute-start(f32[7,48,256]{2,1,0:T(8,128)S(1)} %get-tuple-element.36), channel_id=1, source_target_pairs={{0,4},{4,0},{8,12},{12,8},{16,20},{20,16},{24,28},{28,24},{1,5},{5... | collective-permute-start | bytes 1032200 | tf_op jit(solution)/shard_map/ppermute | solution.py:677
  8.5 0.2 slot_places.1
  8.7 0.6 %prepare.2 = (bf16[2,2,256,256]{3,2,1,0:T(8,128)(2,1)S(1)}, bf16[40,144]{1,0:T(8,128)(2,1)S(1)}, bf16[32,144]{1,0:T(8,128)(2,1)S(1)}, f32[8,48,256]{2,1,0:T(8,128)S(1)}, f32[16,128]{1,0:T(8,128)S(1)}) custom-call(f32[3,1,15]{2,1,0:T(1,128)S(1)} %bitcast.10, f32[8,64,256]{2,1,0:T(8,128)S(1)} %copy-done, f32[32,128]{1,0:T(8,128)S(1)} %get-tuple-element.24.after.base), custom_call_target="tpu_custom_call" | custom-call | tf_op jit(solution)/shard_map/prepare/pallas_call | solution.py:170
  9.3 3.7 %collective-permute-done.source.refs_13_ = f32[344,256]{1,0:T(8,128)S(1)} collective-permute-done((f32[344,256]{1,0:T(8,128)S(1)}, f32[344,256]{1,0:T(8,128)S(1)}, u32[]{:S(2)}, u32[]{:S(2)}) %collective-permute-start) | collective-permute-done | bytes 352288 | tf_op jit(solution)/shard_map/ppermute | solution.py:674
  13.0 0.6 %prepare.3 = (bf16[2,2,256,256]{3,2,1,0:T(8,128)(2,1)S(1)}, bf16[40,144]{1,0:T(8,128)(2,1)S(1)}, bf16[32,144]{1,0:T(8,128)(2,1)S(1)}, f32[8,48,256]{2,1,0:T(8,128)S(1)}, f32[16,128]{1,0:T(8,128)S(1)}) custom-call(f32[344,256]{1,0:T(8,128)S(1)} %collective-permute-done.source.refs_13_, f32[8,64,256]{2,1,0:T(8,128)S(1)} %copy-done, f32[3,1,15]{2,1,0:T(1,128)S(1)} %bitcast.11), custom_call_target="tpu_custom_call" | custom-call | tf_op jit(solution)/shard_map/prepare/pallas_call | solution.py:170
  13.6 0.0 collective-permute-done.2.refs_11_
  13.7 1.8 %ratio_fields.1 = (f32[8,32,256]{2,1,0:T(8,128)S(1)}, f32[8,32,256]{2,1,0:T(8,128)S(1)}, f32[7,16,256]{2,1,0:T(8,128)S(1)}, f32[7,16,256]{2,1,0:T(8,128)S(1)}, f...) custom-call(bf16[2,2,256,256]{3,2,1,0:T(8,128)(2,1)S(1)} %get-tuple-element.27.refs_0_, ...), custom_call_target="tpu_custom_call" | custom-call | tf_op jit(solution)/shard_map/ratio_fields/pallas_call | solution.py:285
  15.5 0.0 copy-start.1
  15.5 0.8 %collective-permute-start.3 = (f32[7,16,256]{2,1,0:T(8,128)S(1)}, f32[7,16,256]{2,1,0:T(8,128)S(1)}, u32[]{:S(2)}, u32[]{:S(2)}) collective-permute-start(f32[7,16,256]{2,1,0:T(8,128)S(1)} %get-tuple-element.40), channel_id=1, source_target_pairs={{4,8},{12,16},{20,24},{8,4},{16,12},{24,20},{5,9},{13,17},{21,25},... | collective-permute-start | bytes 344072 | tf_op jit(solution)/shard_map/ppermute | solution.py:686
  16.3 3.7 %collective-permute-start.4 = (f32[7,16,256]{2,1,0:T(8,128)S(1)}, f32[7,16,256]{2,1,0:T(8,128)S(1)}, u32[]{:S(2)}, u32[]{:S(2)}) collective-permute-start(f32[7,16,256]{2,1,0:T(8,128)S(1)} %get-tuple-element.41), channel_id=1, source_target_pairs={{0,4},{4,0},{8,12},{12,8},{16,20},{20,16},{24,28},{28,24},{1,5},{5... | collective-permute-start | bytes 344072 | tf_op jit(solution)/shard_map/ppermute | solution.py:686
  20.0 0.7 %collective-permute-start.6 = (f32[7,16,256]{2,1,0:T(8,128)S(1)}, f32[7,16,256]{2,1,0:T(8,128)S(1)}, u32[]{:S(2)}, u32[]{:S(2)}) collective-permute-start(f32[7,16,256]{2,1,0:T(8,128)S(1)} %get-tuple-element.44), channel_id=1, source_target_pairs={{4,8},{12,16},{20,24},{8,4},{16,12},{24,20},{5,9},{13,17},{21,25},... | collective-permute-start | bytes 344072 | tf_op jit(solution)/shard_map/ppermute | solution.py:686
  20.7 5.5 %collective-permute-start.7 = (f32[7,16,256]{2,1,0:T(8,128)S(1)}, f32[7,16,256]{2,1,0:T(8,128)S(1)}, u32[]{:S(2)}, u32[]{:S(2)}) collective-permute-start(f32[7,16,256]{2,1,0:T(8,128)S(1)} %get-tuple-element.45), channel_id=1, source_target_pairs={{0,4},{4,0},{8,12},{12,8},{16,20},{20,16},{24,28},{28,24},{1,5},{5... | collective-permute-start | bytes 344072 | tf_op jit(solution)/shard_map/ppermute | solution.py:686
  26.2 0.3 own_planes.1
  26.5 0.0 collective-permute-done.4.near
  26.6 2.5 %collective-permute-start.5 = (f32[8,16,256]{2,1,0:T(8,128)S(1)}, f32[8,16,256]{2,1,0:T(8,128)S(1)}, u32[]{:S(2)}, u32[]{:S(2)}) collective-permute-start(f32[8,16,256]{2,1,0:T(8,128)S(1)} %add_rims.2.correction.mine), channel_id=1, source_target_pairs={{0,3},{1,2},{2,1},{3,0},{4,7},{5,6},{6,5},{7,4},{8,11},{9,10},{10,... | collective-permute-start | bytes 393224 | tf_op jit(solution)/shard_map/ppermute | solution.py:692
  29.1 0.8 %moment_rows.2.rest_0_.refs_0_ = f32[16,128]{1,0:T(8,128)S(1)} custom-call(f32[8,64,256]{2,1,0:T(8,128)S(1)} %copy-done, s32[8,64,256]{2,1,0:T(8,128)S(1)} %copy-done.1, bf16[160,16]{1,0:T(8,128)(2,1)S(1)} %get-tuple-element.42.picked, f32[32,128]{1,0:T(8,128)S(1)} %get-tuple-element.24.after.base, f32[8,16,256]{2,1,0:T(8,128)S(1)} %add_rims.2.correction.mine), custom_call_target="tpu_custom_call" | custom-call | tf_op jit(solution)/shard_map/moment_rows/pallas_call | solution.py:531
  30.0 0.0 collective-permute-done.6.far
  30.0 1.4 %collective-permute-start.8 = (f32[8,16,256]{2,1,0:T(8,128)S(1)}, f32[8,16,256]{2,1,0:T(8,128)S(1)}, u32[]{:S(2)}, u32[]{:S(2)}) collective-permute-start(f32[8,16,256]{2,1,0:T(8,128)S(1)} %add_rims.3.correction.mine), channel_id=1, source_target_pairs={{0,3},{1,2},{2,1},{3,0},{4,7},{5,6},{6,5},{7,4},{8,11},{9,10},{10,... | collective-permute-start | bytes 393224 | tf_op jit(solution)/shard_map/ppermute | solution.py:692
  31.4 1.7 %moment_rows.3.rest_0_ = f32[32,128]{1,0:T(8,128)} custom-call(f32[8,64,256]{2,1,0:T(8,128)S(1)} %copy-done, s32[8,64,256]{2,1,0:T(8,128)S(1)} %copy-done.1, bf16[160,16]{1,0:T(8,128)(2,1)S(1)} %get-tuple-element.42.picked, f32[32,128]{1,0:T(8,128)S(1)} %get-tuple-element.24.after.base, f32[8,16,256]{2,1,0:T(8,128)S(1)} %add_rims.3.correction.mine, ...), custom_call_target="tpu_custom_call" | custom-call | tf_op jit(solution)/shard_map/moment_rows/pallas_call | solution.py:531
  33.2 3.8 %all-to-all-start = ((f32[32,1,128]{2,1,0:T(1,128)}), f32[32,1,128]{2,1,0:T(1,128)S(1)}, u32[]{:S(2)}, u32[]{:S(2)}) async-start(f32[32,1,128]{2,1,0:T(1,128)} %bitcast.4), calls=%async_computation | async-start | bytes 32768 | tf_op jit(solution)/shard_map/all_to_all | solution.py:695
  37.0 2.8 %collective-permute-start.9 = (f32[136,256]{1,0:T(8,128)S(1)}, f32[136,256]{1,0:T(8,128)S(1)}, u32[]{:S(2)}, u32[]{:S(2)}) collective-permute-start(f32[136,256]{1,0:T(8,128)S(1)} %update.2.source.refs_0_), channel_id=1, source_target_pairs={{0,1},{1,0},{2,3},{3,2},{4,5},{5,4},{6,7},{7,6},{8,9},{9,8},{10,11... | collective-permute-start | bytes 417800 | tf_op jit(solution)/shard_map/ppermute | solution.py:701
  39.8 2.2 %collective-permute-start.10 = (f32[128,256]{1,0:T(8,128)S(1)}, f32[128,256]{1,0:T(8,128)S(1)}, u32[]{:S(2)}, u32[]{:S(2)}) collective-permute-start(f32[128,256]{1,0:T(8,128)S(1)} %update.3.refs_1_), channel_id=1, source_target_pairs={{0,1},{1,0},{2,3},{3,2},{4,5},{5,4},{6,7},{7,6},{8,9},{9,8},{10,11... | collective-permute-start | bytes 393224 | tf_op jit(solution)/shard_map/ppermute | solution.py:701
  42.1 2.1 %all-to-all-done = f32[32,1,128]{2,1,0:T(1,128)S(1)} async-done(((f32[32,1,128]{2,1,0:T(1,128)}), f32[32,1,128]{2,1,0:T(1,128)S(1)}, u32[]{:S(2)}, u32[]{:S(2)}) %all-to-all-start) | async-done | bytes 16416 | tf_op jit(solution)/shard_map/all_to_all | solution.py:695
  44.2 1.0 %nucleus_table.1 = f32[10,128]{1,0:T(8,128)} custom-call(f32[32,128]{1,0:T(8,128)S(1)} %bitcast.8), custom_call_target="tpu_custom_call" | custom-call | flops 10000000000 | bytes 20000000 | tf_op jit(solution)/shard_map/nucleus_table/pallas_call | solution.py:574
  45.2 0.8 %begin_result.1.begun = f32[8,64,256]{2,1,0:T(8,128)} custom-call(f32[136,256]{1,0:T(8,128)S(1)} %update.2.source.refs_0_, f32[128,256]{1,0:T(8,128)S(1)} %update.3.refs_1_), custom_call_target="tpu_custom_call" | custom-call | tf_op jit(solution)/shard_map/begin_result/pallas_call | solution.py:627
  46.0 0.8 %finish.1 = f32[8,64,256]{2,1,0:T(8,128)} custom-call(f32[8,64,256]{2,1,0:T(8,128)} %begin_result.1.begun, f32[136,256]{1,0:T(8,128)S(1)} %collective-permute-done.9.refs_0_, f32[128,256]{1,0:T(8,128)S(1)} %collective-permute-done.10.refs_1_), custom_call_target="tpu_custom_call", output_to_operand_aliasing={{}: (0, {})} | custom-call | tf_op jit(solution)/shard_map/finish/pallas_call | solution.py:645
  (23 shorter events, 0.2 us)
Async XLA Ops:
  0.6 1.0 %copy-start.2 = (f32[1,8,64,256]{3,2,1,0:T(8,128)S(1)}, f32[1,8,64,256]{3,2,1,0:T(8,128)}, u32[]{:S(2)}) copy-start(f32[1,8,64,256]{3,2,1,0:T(8,128)} %refs_12_.1) | copy-start | bytes 1572868
  0.6 1.0 %copy-start.3 = (f32[1,3,15]{2,0,1:T(1,128)S(1)}, f32[1,3,15]{2,0,1:T(1,128)}, u32[]{:S(2)}) copy-start(f32[1,3,15]{2,0,1:T(1,128)} %param.8) | copy-start | bytes 544
  0.7 4.1 %copy-start = (f32[8,64,256]{2,1,0:T(8,128)S(1)}, f32[8,64,256]{2,1,0:T(8,128)}, u32[]{:S(2)}) copy-start(f32[8,64,256]{2,1,0:T(8,128)} %estimate.13) | copy-start | bytes 1572868
  1.7 11.3 %collective-permute-start = (f32[344,256]{1,0:T(8,128)S(1)}, f32[344,256]{1,0:T(8,128)S(1)}, u32[]{:S(2)}, u32[]{:S(2)}) collective-permute-start(f32[344,256]{1,0:T(8,128)S(1)} %view_out.1), channel_id=1, source_target_pairs={{0,1},{1,0},{2,3},{3,2},{4,5},{5,4},{6,7},{7,6},{8,9},{9,8},{10,11... | collective-permute-start | bytes 1056776 | tf_op jit(solution)/shard_map/ppermute | solution.py:674
  4.8 8.8 %collective-permute-start.1 = (f32[7,48,256]{2,1,0:T(8,128)S(1)}, f32[7,48,256]{2,1,0:T(8,128)S(1)}, u32[]{:S(2)}, u32[]{:S(2)}) collective-permute-start(f32[7,48,256]{2,1,0:T(8,128)S(1)} %get-tuple-element.35), channel_id=1, source_target_pairs={{4,8},{12,16},{20,24},{8,4},{16,12},{24,20},{5,9},{13,17},{21,25},... | collective-permute-start | bytes 1032200 | tf_op jit(solution)/shard_map/ppermute | solution.py:676
  5.5 2.9 %copy-start.4 = (s32[1,16,1]{1,2,0:T(1,128)S(1)}, s32[1,16,1]{1,2,0:T(1,128)}, u32[]{:S(2)}) copy-start(s32[1,16,1]{1,2,0:T(1,128)} %param.10) | copy-start | bytes 196
  5.5 2.9 %copy-start.5 = (s32[1,16]{1,0:T(1,128)S(1)}, s32[1,16]{1,0:T(1,128)}, u32[]{:S(2)}) copy-start(s32[1,16]{1,0:T(1,128)} %index_row.1) | copy-start | bytes 196
  5.6 8.1 %collective-permute-start.2 = (f32[7,48,256]{2,1,0:T(8,128)S(1)}, f32[7,48,256]{2,1,0:T(8,128)S(1)}, u32[]{:S(2)}, u32[]{:S(2)}) collective-permute-start(f32[7,48,256]{2,1,0:T(8,128)S(1)} %get-tuple-element.36), channel_id=1, source_target_pairs={{0,4},{4,0},{8,12},{12,8},{16,20},{20,16},{24,28},{28,24},{1,5},{5... | collective-permute-start | bytes 1032200 | tf_op jit(solution)/shard_map/ppermute | solution.py:677
  15.5 13.6 %copy-start.1 = (s32[8,64,256]{2,1,0:T(8,128)S(1)}, s32[8,64,256]{2,1,0:T(8,128)}, u32[]{:S(2)}) copy-start(s32[8,64,256]{2,1,0:T(8,128)} %labels.3) | copy-start | bytes 1572868
  15.5 11.0 %collective-permute-start.3 = (f32[7,16,256]{2,1,0:T(8,128)S(1)}, f32[7,16,256]{2,1,0:T(8,128)S(1)}, u32[]{:S(2)}, u32[]{:S(2)}) collective-permute-start(f32[7,16,256]{2,1,0:T(8,128)S(1)} %get-tuple-element.40), channel_id=1, source_target_pairs={{4,8},{12,16},{20,24},{8,4},{16,12},{24,20},{5,9},{13,17},{21,25},... | collective-permute-start | bytes 344072 | tf_op jit(solution)/shard_map/ppermute | solution.py:686
  16.3 10.2 %collective-permute-start.4 = (f32[7,16,256]{2,1,0:T(8,128)S(1)}, f32[7,16,256]{2,1,0:T(8,128)S(1)}, u32[]{:S(2)}, u32[]{:S(2)}) collective-permute-start(f32[7,16,256]{2,1,0:T(8,128)S(1)} %get-tuple-element.41), channel_id=1, source_target_pairs={{0,4},{4,0},{8,12},{12,8},{16,20},{20,16},{24,28},{28,24},{1,5},{5... | collective-permute-start | bytes 344072 | tf_op jit(solution)/shard_map/ppermute | solution.py:686
  20.0 9.9 %collective-permute-start.6 = (f32[7,16,256]{2,1,0:T(8,128)S(1)}, f32[7,16,256]{2,1,0:T(8,128)S(1)}, u32[]{:S(2)}, u32[]{:S(2)}) collective-permute-start(f32[7,16,256]{2,1,0:T(8,128)S(1)} %get-tuple-element.44), channel_id=1, source_target_pairs={{4,8},{12,16},{20,24},{8,4},{16,12},{24,20},{5,9},{13,17},{21,25},... | collective-permute-start | bytes 344072 | tf_op jit(solution)/shard_map/ppermute | solution.py:686
  20.7 9.3 %collective-permute-start.7 = (f32[7,16,256]{2,1,0:T(8,128)S(1)}, f32[7,16,256]{2,1,0:T(8,128)S(1)}, u32[]{:S(2)}, u32[]{:S(2)}) collective-permute-start(f32[7,16,256]{2,1,0:T(8,128)S(1)} %get-tuple-element.45), channel_id=1, source_target_pairs={{0,4},{4,0},{8,12},{12,8},{16,20},{20,16},{24,28},{28,24},{1,5},{5... | collective-permute-start | bytes 344072 | tf_op jit(solution)/shard_map/ppermute | solution.py:686
  26.6 10.4 %collective-permute-start.5 = (f32[8,16,256]{2,1,0:T(8,128)S(1)}, f32[8,16,256]{2,1,0:T(8,128)S(1)}, u32[]{:S(2)}, u32[]{:S(2)}) collective-permute-start(f32[8,16,256]{2,1,0:T(8,128)S(1)} %add_rims.2.correction.mine), channel_id=1, source_target_pairs={{0,3},{1,2},{2,1},{3,0},{4,7},{5,6},{6,5},{7,4},{8,11},{9,10},{10,... | collective-permute-start | bytes 393224 | tf_op jit(solution)/shard_map/ppermute | solution.py:692
  30.0 9.8 %collective-permute-start.8 = (f32[8,16,256]{2,1,0:T(8,128)S(1)}, f32[8,16,256]{2,1,0:T(8,128)S(1)}, u32[]{:S(2)}, u32[]{:S(2)}) collective-permute-start(f32[8,16,256]{2,1,0:T(8,128)S(1)} %add_rims.3.correction.mine), channel_id=1, source_target_pairs={{0,3},{1,2},{2,1},{3,0},{4,7},{5,6},{6,5},{7,4},{8,11},{9,10},{10,... | collective-permute-start | bytes 393224 | tf_op jit(solution)/shard_map/ppermute | solution.py:692
  33.2 11.0 %all-to-all-start = ((f32[32,1,128]{2,1,0:T(1,128)}), f32[32,1,128]{2,1,0:T(1,128)S(1)}, u32[]{:S(2)}, u32[]{:S(2)}) async-start(f32[32,1,128]{2,1,0:T(1,128)} %bitcast.4), calls=%async_computation | async-start | bytes 32768 | tf_op jit(solution)/shard_map/all_to_all | solution.py:695
  37.0 9.0 %collective-permute-start.9 = (f32[136,256]{1,0:T(8,128)S(1)}, f32[136,256]{1,0:T(8,128)S(1)}, u32[]{:S(2)}, u32[]{:S(2)}) collective-permute-start(f32[136,256]{1,0:T(8,128)S(1)} %update.2.source.refs_0_), channel_id=1, source_target_pairs={{0,1},{1,0},{2,3},{3,2},{4,5},{5,4},{6,7},{7,6},{8,9},{9,8},{10,11... | collective-permute-start | bytes 417800 | tf_op jit(solution)/shard_map/ppermute | solution.py:701
  39.8 6.2 %collective-permute-start.10 = (f32[128,256]{1,0:T(8,128)S(1)}, f32[128,256]{1,0:T(8,128)S(1)}, u32[]{:S(2)}, u32[]{:S(2)}) collective-permute-start(f32[128,256]{1,0:T(8,128)S(1)} %update.3.refs_1_), channel_id=1, source_target_pairs={{0,1},{1,0},{2,3},{3,2},{4,5},{5,4},{6,7},{7,6},{8,9},{9,8},{10,11... | collective-permute-start | bytes 393224 | tf_op jit(solution)/shard_map/ppermute | solution.py:701

commit v18 on v17

--- a/solution.py
+++ b/solution.py
@@ -13,7 +13,7 @@
 NUC_DEV = 128
 LANES = 128
 PARTS = 2
-TAIL = 24
+TAIL = 16
 IDS = 24
 F32 = jnp.float32
 BF16 = jnp.bfloat16

time: 47.1 us -> 47.1 us (level)
  no operation moved by 1% of the time
where the time goes in v18:
time: 47.1 us; the launch traced here: 46.9 us
  starting transfers between devices  30.3 us (64%)
  Pallas kernels  8.96 us (19%)
  waiting for transfers between devices  5.7 us (12%)
  local copies, waits for them, and re-layouts  1.03 us (2%)
  between operations  0.87 us (2%)
    ppermute x4, starting transfers between devices, on_device(): lax.ppermute(send, 'tile', pairs)  10.9 us
    ppermute x2, starting transfers between devices, on_device(): new_other.append(lax.ppermute(new_mine[part], 'view', partner))  5.02 us
    ppermute x2, starting transfers between devices, on_device(): other.append(lax.ppermute(mine[part], 'view', across_pairs))  3.95 us
    all_to_all x1, starting transfers between devices, on_device(): lax.all_to_all(sent, ('tile', 'view'), split_axis=0, concat_axis=0, tiled...  3.78 us
    ppermute x1, waiting for transfers between devices, on_device(): swapped = lax.ppermute(packed, 'view', partner)  3.57 us
    ppermute x1, starting transfers between devices, on_device(): swapped = lax.ppermute(packed, 'view', partner)  3.09 us
    ppermute x1, starting transfers between devices, on_device(): near = lax.ppermute(to_near, 'tile', near_pairs)  2.9 us
    pallas_call x2, Pallas kernels, moment_rows(): pl.pallas_call(functools.partial(moments_kernel, views, tiles * planes, p...  2.59 us
  transfers between devices with their start and end apart: 12, of which 2 were waited for; matrix products, arithmetic and copies ran while one was open for 0% of the time, Pallas kernels for 13%

profile of v18, /device:TPU:0, one launch (start us, length us, event | category | flops | bytes accessed | tf_op | source)
XLA Modules:
  0.0 46.9 jit_solution(14325895356073785899)
XLA Ops:
  0.7 0.0 copy-start
  0.7 1.0 %copy-done.2 = f32[1,8,64,256]{3,2,1,0:T(8,128)S(1)} copy-done((f32[1,8,64,256]{3,2,1,0:T(8,128)S(1)}, f32[1,8,64,256]{3,2,1,0:T(8,128)}, u32[]{:S(2)}) %copy-start.2) | copy-done | bytes 524312
  1.7 3.1 %collective-permute-start = (f32[336,256]{1,0:T(8,128)S(1)}, f32[336,256]{1,0:T(8,128)S(1)}, u32[]{:S(2)}, u32[]{:S(2)}) collective-permute-start(f32[336,256]{1,0:T(8,128)S(1)} %view_out.1), channel_id=1, source_target_pairs={{0,1},{1,0},{2,3},{3,2},{4,5},{5,4},{6,7},{7,6},{8,9},{9,8},{10,11... | collective-permute-start | bytes 1032200 | tf_op jit(solution)/shard_map/ppermute | solution.py:674
  4.8 0.7 %collective-permute-start.1 = (f32[7,48,256]{2,1,0:T(8,128)S(1)}, f32[7,48,256]{2,1,0:T(8,128)S(1)}, u32[]{:S(2)}, u32[]{:S(2)}) collective-permute-start(f32[7,48,256]{2,1,0:T(8,128)S(1)} %get-tuple-element.35), channel_id=1, source_target_pairs={{4,8},{12,16},{20,24},{8,4},{16,12},{24,20},{5,9},{13,17},{21,25},... | collective-permute-start | bytes 1032200 | tf_op jit(solution)/shard_map/ppermute | solution.py:676
  5.5 0.0 copy-start.4
  5.5 0.0 copy-start.5
  5.6 2.9 %collective-permute-start.2 = (f32[7,48,256]{2,1,0:T(8,128)S(1)}, f32[7,48,256]{2,1,0:T(8,128)S(1)}, u32[]{:S(2)}, u32[]{:S(2)}) collective-permute-start(f32[7,48,256]{2,1,0:T(8,128)S(1)} %get-tuple-element.36), channel_id=1, source_target_pairs={{0,4},{4,0},{8,12},{12,8},{16,20},{20,16},{24,28},{28,24},{1,5},{5... | collective-permute-start | bytes 1032200 | tf_op jit(solution)/shard_map/ppermute | solution.py:677
  8.5 0.2 slot_places.1
  8.7 0.6 %prepare.2 = (bf16[2,2,256,256]{3,2,1,0:T(8,128)(2,1)S(1)}, bf16[40,144]{1,0:T(8,128)(2,1)S(1)}, bf16[32,144]{1,0:T(8,128)(2,1)S(1)}, f32[8,48,256]{2,1,0:T(8,128)S(1)}, f32[16,128]{1,0:T(8,128)S(1)}) custom-call(f32[3,1,15]{2,1,0:T(1,128)S(1)} %bitcast.10, f32[8,64,256]{2,1,0:T(8,128)S(1)} %copy-done, f32[32,128]{1,0:T(8,128)S(1)} %get-tuple-element.24.after.base), custom_call_target="tpu_custom_call" | custom-call | tf_op jit(solution)/shard_map/prepare/pallas_call | solution.py:170
  9.3 3.6 %collective-permute-done.source.refs_13_ = f32[336,256]{1,0:T(8,128)S(1)} collective-permute-done((f32[336,256]{1,0:T(8,128)S(1)}, f32[336,256]{1,0:T(8,128)S(1)}, u32[]{:S(2)}, u32[]{:S(2)}) %collective-permute-start) | collective-permute-done | bytes 344096 | tf_op jit(solution)/shard_map/ppermute | solution.py:674
  12.9 0.6 %prepare.3 = (bf16[2,2,256,256]{3,2,1,0:T(8,128)(2,1)S(1)}, bf16[40,144]{1,0:T(8,128)(2,1)S(1)}, bf16[32,144]{1,0:T(8,128)(2,1)S(1)}, f32[8,48,256]{2,1,0:T(8,128)S(1)}, f32[16,128]{1,0:T(8,128)S(1)}) custom-call(f32[336,256]{1,0:T(8,128)S(1)} %collective-permute-done.source.refs_13_, f32[8,64,256]{2,1,0:T(8,128)S(1)} %copy-done, f32[3,1,15]{2,1,0:T(1,128)S(1)} %bitcast.11), custom_call_target="tpu_custom_call" | custom-call | tf_op jit(solution)/shard_map/prepare/pallas_call | solution.py:170
  13.4 0.0 collective-permute-done.1.refs_10_
  13.5 0.0 collective-permute-done.2.refs_11_
  13.5 1.8 %ratio_fields.1 = (f32[8,32,256]{2,1,0:T(8,128)S(1)}, f32[8,32,256]{2,1,0:T(8,128)S(1)}, f32[7,16,256]{2,1,0:T(8,128)S(1)}, f32[7,16,256]{2,1,0:T(8,128)S(1)}, f...) custom-call(bf16[2,2,256,256]{3,2,1,0:T(8,128)(2,1)S(1)} %get-tuple-element.27.refs_0_, ...), custom_call_target="tpu_custom_call" | custom-call | tf_op jit(solution)/shard_map/ratio_fields/pallas_call | solution.py:285
  15.3 0.0 copy-start.1
  15.3 0.8 %collective-permute-start.3 = (f32[7,16,256]{2,1,0:T(8,128)S(1)}, f32[7,16,256]{2,1,0:T(8,128)S(1)}, u32[]{:S(2)}, u32[]{:S(2)}) collective-permute-start(f32[7,16,256]{2,1,0:T(8,128)S(1)} %get-tuple-element.40), channel_id=1, source_target_pairs={{4,8},{12,16},{20,24},{8,4},{16,12},{24,20},{5,9},{13,17},{21,25},... | collective-permute-start | bytes 344072 | tf_op jit(solution)/shard_map/ppermute | solution.py:686
  16.1 3.9 %collective-permute-start.4 = (f32[7,16,256]{2,1,0:T(8,128)S(1)}, f32[7,16,256]{2,1,0:T(8,128)S(1)}, u32[]{:S(2)}, u32[]{:S(2)}) collective-permute-start(f32[7,16,256]{2,1,0:T(8,128)S(1)} %get-tuple-element.41), channel_id=1, source_target_pairs={{0,4},{4,0},{8,12},{12,8},{16,20},{20,16},{24,28},{28,24},{1,5},{5... | collective-permute-start | bytes 344072 | tf_op jit(solution)/shard_map/ppermute | solution.py:686
  20.1 0.7 %collective-permute-start.6 = (f32[7,16,256]{2,1,0:T(8,128)S(1)}, f32[7,16,256]{2,1,0:T(8,128)S(1)}, u32[]{:S(2)}, u32[]{:S(2)}) collective-permute-start(f32[7,16,256]{2,1,0:T(8,128)S(1)} %get-tuple-element.44), channel_id=1, source_target_pairs={{4,8},{12,16},{20,24},{8,4},{16,12},{24,20},{5,9},{13,17},{21,25},... | collective-permute-start | bytes 344072 | tf_op jit(solution)/shard_map/ppermute | solution.py:686
  20.7 5.5 %collective-permute-start.7 = (f32[7,16,256]{2,1,0:T(8,128)S(1)}, f32[7,16,256]{2,1,0:T(8,128)S(1)}, u32[]{:S(2)}, u32[]{:S(2)}) collective-permute-start(f32[7,16,256]{2,1,0:T(8,128)S(1)} %get-tuple-element.45), channel_id=1, source_target_pairs={{0,4},{4,0},{8,12},{12,8},{16,20},{20,16},{24,28},{28,24},{1,5},{5... | collective-permute-start | bytes 344072 | tf_op jit(solution)/shard_map/ppermute | solution.py:686
  26.2 0.3 own_planes.1
  26.5 0.0 collective-permute-done.3.far
  26.6 2.5 %collective-permute-start.5 = (f32[8,16,256]{2,1,0:T(8,128)S(1)}, f32[8,16,256]{2,1,0:T(8,128)S(1)}, u32[]{:S(2)}, u32[]{:S(2)}) collective-permute-start(f32[8,16,256]{2,1,0:T(8,128)S(1)} %add_rims.2.correction.mine), channel_id=1, source_target_pairs={{0,3},{1,2},{2,1},{3,0},{4,7},{5,6},{6,5},{7,4},{8,11},{9,10},{10,... | collective-permute-start | bytes 393224 | tf_op jit(solution)/shard_map/ppermute | solution.py:692
  29.1 0.8 %moment_rows.2.rest_0_.refs_0_ = f32[16,128]{1,0:T(8,128)S(1)} custom-call(f32[8,64,256]{2,1,0:T(8,128)S(1)} %copy-done, s32[8,64,256]{2,1,0:T(8,128)S(1)} %copy-done.1, bf16[160,16]{1,0:T(8,128)(2,1)S(1)} %get-tuple-element.42.picked, f32[32,128]{1,0:T(8,128)S(1)} %get-tuple-element.24.after.base, f32[8,16,256]{2,1,0:T(8,128)S(1)} %add_rims.2.correction.mine), custom_call_target="tpu_custom_call" | custom-call | tf_op jit(solution)/shard_map/moment_rows/pallas_call | solution.py:531
  30.0 1.4 %collective-permute-start.8 = (f32[8,16,256]{2,1,0:T(8,128)S(1)}, f32[8,16,256]{2,1,0:T(8,128)S(1)}, u32[]{:S(2)}, u32[]{:S(2)}) collective-permute-start(f32[8,16,256]{2,1,0:T(8,128)S(1)} %add_rims.3.correction.mine), channel_id=1, source_target_pairs={{0,3},{1,2},{2,1},{3,0},{4,7},{5,6},{6,5},{7,4},{8,11},{9,10},{10,... | collective-permute-start | bytes 393224 | tf_op jit(solution)/shard_map/ppermute | solution.py:692
  31.5 1.7 %moment_rows.3.rest_0_ = f32[32,128]{1,0:T(8,128)} custom-call(f32[8,64,256]{2,1,0:T(8,128)S(1)} %copy-done, s32[8,64,256]{2,1,0:T(8,128)S(1)} %copy-done.1, bf16[160,16]{1,0:T(8,128)(2,1)S(1)} %get-tuple-element.42.picked, f32[32,128]{1,0:T(8,128)S(1)} %get-tuple-element.24.after.base, f32[8,16,256]{2,1,0:T(8,128)S(1)} %add_rims.3.correction.mine, ...), custom_call_target="tpu_custom_call" | custom-call | tf_op jit(solution)/shard_map/moment_rows/pallas_call | solution.py:531
  33.2 3.8 %all-to-all-start = ((f32[32,1,128]{2,1,0:T(1,128)}), f32[32,1,128]{2,1,0:T(1,128)S(1)}, u32[]{:S(2)}, u32[]{:S(2)}) async-start(f32[32,1,128]{2,1,0:T(1,128)} %bitcast.4), calls=%async_computation | async-start | bytes 32768 | tf_op jit(solution)/shard_map/all_to_all | solution.py:695
  37.0 2.8 %collective-permute-start.9 = (f32[136,256]{1,0:T(8,128)S(1)}, f32[136,256]{1,0:T(8,128)S(1)}, u32[]{:S(2)}, u32[]{:S(2)}) collective-permute-start(f32[136,256]{1,0:T(8,128)S(1)} %update.2.source.refs_0_), channel_id=1, source_target_pairs={{0,1},{1,0},{2,3},{3,2},{4,5},{5,4},{6,7},{7,6},{8,9},{9,8},{10,11... | collective-permute-start | bytes 417800 | tf_op jit(solution)/shard_map/ppermute | solution.py:701
  39.9 2.2 %collective-permute-start.10 = (f32[128,256]{1,0:T(8,128)S(1)}, f32[128,256]{1,0:T(8,128)S(1)}, u32[]{:S(2)}, u32[]{:S(2)}) collective-permute-start(f32[128,256]{1,0:T(8,128)S(1)} %update.3.refs_1_), channel_id=1, source_target_pairs={{0,1},{1,0},{2,3},{3,2},{4,5},{5,4},{6,7},{7,6},{8,9},{9,8},{10,11... | collective-permute-start | bytes 393224 | tf_op jit(solution)/shard_map/ppermute | solution.py:701
  42.1 2.1 %all-to-all-done = f32[32,1,128]{2,1,0:T(1,128)S(1)} async-done(((f32[32,1,128]{2,1,0:T(1,128)}), f32[32,1,128]{2,1,0:T(1,128)S(1)}, u32[]{:S(2)}, u32[]{:S(2)}) %all-to-all-start) | async-done | bytes 16416 | tf_op jit(solution)/shard_map/all_to_all | solution.py:695
  44.2 1.0 %nucleus_table.1 = f32[10,128]{1,0:T(8,128)} custom-call(f32[32,128]{1,0:T(8,128)S(1)} %bitcast.8), custom_call_target="tpu_custom_call" | custom-call | flops 10000000000 | bytes 20000000 | tf_op jit(solution)/shard_map/nucleus_table/pallas_call | solution.py:574
  45.2 0.8 %begin_result.1.begun = f32[8,64,256]{2,1,0:T(8,128)} custom-call(f32[136,256]{1,0:T(8,128)S(1)} %update.2.source.refs_0_, f32[128,256]{1,0:T(8,128)S(1)} %update.3.refs_1_), custom_call_target="tpu_custom_call" | custom-call | tf_op jit(solution)/shard_map/begin_result/pallas_call | solution.py:627
  46.0 0.8 %finish.1 = f32[8,64,256]{2,1,0:T(8,128)} custom-call(f32[8,64,256]{2,1,0:T(8,128)} %begin_result.1.begun, f32[136,256]{1,0:T(8,128)S(1)} %collective-permute-done.9.refs_0_, f32[128,256]{1,0:T(8,128)S(1)} %collective-permute-done.10.refs_1_), custom_call_target="tpu_custom_call", output_to_operand_aliasing={{}: (0, {})} | custom-call | tf_op jit(solution)/shard_map/finish/pallas_call | solution.py:645
  (23 shorter events, 0.2 us)
Async XLA Ops:
  0.6 1.0 %copy-start.2 = (f32[1,8,64,256]{3,2,1,0:T(8,128)S(1)}, f32[1,8,64,256]{3,2,1,0:T(8,128)}, u32[]{:S(2)}) copy-start(f32[1,8,64,256]{3,2,1,0:T(8,128)} %refs_12_.1) | copy-start | bytes 1572868
  0.6 1.0 %copy-start.3 = (f32[1,3,15]{2,0,1:T(1,128)S(1)}, f32[1,3,15]{2,0,1:T(1,128)}, u32[]{:S(2)}) copy-start(f32[1,3,15]{2,0,1:T(1,128)} %param.8) | copy-start | bytes 544
  0.7 4.1 %copy-start = (f32[8,64,256]{2,1,0:T(8,128)S(1)}, f32[8,64,256]{2,1,0:T(8,128)}, u32[]{:S(2)}) copy-start(f32[8,64,256]{2,1,0:T(8,128)} %estimate.13) | copy-start | bytes 1572868
  1.7 11.2 %collective-permute-start = (f32[336,256]{1,0:T(8,128)S(1)}, f32[336,256]{1,0:T(8,128)S(1)}, u32[]{:S(2)}, u32[]{:S(2)}) collective-permute-start(f32[336,256]{1,0:T(8,128)S(1)} %view_out.1), channel_id=1, source_target_pairs={{0,1},{1,0},{2,3},{3,2},{4,5},{5,4},{6,7},{7,6},{8,9},{9,8},{10,11... | collective-permute-start | bytes 1032200 | tf_op jit(solution)/shard_map/ppermute | solution.py:674
  4.8 8.6 %collective-permute-start.1 = (f32[7,48,256]{2,1,0:T(8,128)S(1)}, f32[7,48,256]{2,1,0:T(8,128)S(1)}, u32[]{:S(2)}, u32[]{:S(2)}) collective-permute-start(f32[7,48,256]{2,1,0:T(8,128)S(1)} %get-tuple-element.35), channel_id=1, source_target_pairs={{4,8},{12,16},{20,24},{8,4},{16,12},{24,20},{5,9},{13,17},{21,25},... | collective-permute-start | bytes 1032200 | tf_op jit(solution)/shard_map/ppermute | solution.py:676
  5.5 2.9 %copy-start.4 = (s32[1,16,1]{1,2,0:T(1,128)S(1)}, s32[1,16,1]{1,2,0:T(1,128)}, u32[]{:S(2)}) copy-start(s32[1,16,1]{1,2,0:T(1,128)} %param.10) | copy-start | bytes 196
  5.5 2.9 %copy-start.5 = (s32[1,16]{1,0:T(1,128)S(1)}, s32[1,16]{1,0:T(1,128)}, u32[]{:S(2)}) copy-start(s32[1,16]{1,0:T(1,128)} %index_row.1) | copy-start | bytes 196
  5.6 7.9 %collective-permute-start.2 = (f32[7,48,256]{2,1,0:T(8,128)S(1)}, f32[7,48,256]{2,1,0:T(8,128)S(1)}, u32[]{:S(2)}, u32[]{:S(2)}) collective-permute-start(f32[7,48,256]{2,1,0:T(8,128)S(1)} %get-tuple-element.36), channel_id=1, source_target_pairs={{0,4},{4,0},{8,12},{12,8},{16,20},{20,16},{24,28},{28,24},{1,5},{5... | collective-permute-start | bytes 1032200 | tf_op jit(solution)/shard_map/ppermute | solution.py:677
  15.3 13.8 %copy-start.1 = (s32[8,64,256]{2,1,0:T(8,128)S(1)}, s32[8,64,256]{2,1,0:T(8,128)}, u32[]{:S(2)}) copy-start(s32[8,64,256]{2,1,0:T(8,128)} %labels.3) | copy-start | bytes 1572868
  15.3 11.2 %collective-permute-start.3 = (f32[7,16,256]{2,1,0:T(8,128)S(1)}, f32[7,16,256]{2,1,0:T(8,128)S(1)}, u32[]{:S(2)}, u32[]{:S(2)}) collective-permute-start(f32[7,16,256]{2,1,0:T(8,128)S(1)} %get-tuple-element.40), channel_id=1, source_target_pairs={{4,8},{12,16},{20,24},{8,4},{16,12},{24,20},{5,9},{13,17},{21,25},... | collective-permute-start | bytes 344072 | tf_op jit(solution)/shard_map/ppermute | solution.py:686
  16.1 10.4 %collective-permute-start.4 = (f32[7,16,256]{2,1,0:T(8,128)S(1)}, f32[7,16,256]{2,1,0:T(8,128)S(1)}, u32[]{:S(2)}, u32[]{:S(2)}) collective-permute-start(f32[7,16,256]{2,1,0:T(8,128)S(1)} %get-tuple-element.41), channel_id=1, source_target_pairs={{0,4},{4,0},{8,12},{12,8},{16,20},{20,16},{24,28},{28,24},{1,5},{5... | collective-permute-start | bytes 344072 | tf_op jit(solution)/shard_map/ppermute | solution.py:686
  20.1 9.9 %collective-permute-start.6 = (f32[7,16,256]{2,1,0:T(8,128)S(1)}, f32[7,16,256]{2,1,0:T(8,128)S(1)}, u32[]{:S(2)}, u32[]{:S(2)}) collective-permute-start(f32[7,16,256]{2,1,0:T(8,128)S(1)} %get-tuple-element.44), channel_id=1, source_target_pairs={{4,8},{12,16},{20,24},{8,4},{16,12},{24,20},{5,9},{13,17},{21,25},... | collective-permute-start | bytes 344072 | tf_op jit(solution)/shard_map/ppermute | solution.py:686
  20.7 9.3 %collective-permute-start.7 = (f32[7,16,256]{2,1,0:T(8,128)S(1)}, f32[7,16,256]{2,1,0:T(8,128)S(1)}, u32[]{:S(2)}, u32[]{:S(2)}) collective-permute-start(f32[7,16,256]{2,1,0:T(8,128)S(1)} %get-tuple-element.45), channel_id=1, source_target_pairs={{0,4},{4,0},{8,12},{12,8},{16,20},{20,16},{24,28},{28,24},{1,5},{5... | collective-permute-start | bytes 344072 | tf_op jit(solution)/shard_map/ppermute | solution.py:686
  26.6 10.4 %collective-permute-start.5 = (f32[8,16,256]{2,1,0:T(8,128)S(1)}, f32[8,16,256]{2,1,0:T(8,128)S(1)}, u32[]{:S(2)}, u32[]{:S(2)}) collective-permute-start(f32[8,16,256]{2,1,0:T(8,128)S(1)} %add_rims.2.correction.mine), channel_id=1, source_target_pairs={{0,3},{1,2},{2,1},{3,0},{4,7},{5,6},{6,5},{7,4},{8,11},{9,10},{10,... | collective-permute-start | bytes 393224 | tf_op jit(solution)/shard_map/ppermute | solution.py:692
  30.0 9.8 %collective-permute-start.8 = (f32[8,16,256]{2,1,0:T(8,128)S(1)}, f32[8,16,256]{2,1,0:T(8,128)S(1)}, u32[]{:S(2)}, u32[]{:S(2)}) collective-permute-start(f32[8,16,256]{2,1,0:T(8,128)S(1)} %add_rims.3.correction.mine), channel_id=1, source_target_pairs={{0,3},{1,2},{2,1},{3,0},{4,7},{5,6},{6,5},{7,4},{8,11},{9,10},{10,... | collective-permute-start | bytes 393224 | tf_op jit(solution)/shard_map/ppermute | solution.py:692
  33.2 11.0 %all-to-all-start = ((f32[32,1,128]{2,1,0:T(1,128)}), f32[32,1,128]{2,1,0:T(1,128)S(1)}, u32[]{:S(2)}, u32[]{:S(2)}) async-start(f32[32,1,128]{2,1,0:T(1,128)} %bitcast.4), calls=%async_computation | async-start | bytes 32768 | tf_op jit(solution)/shard_map/all_to_all | solution.py:695
  37.0 9.0 %collective-permute-start.9 = (f32[136,256]{1,0:T(8,128)S(1)}, f32[136,256]{1,0:T(8,128)S(1)}, u32[]{:S(2)}, u32[]{:S(2)}) collective-permute-start(f32[136,256]{1,0:T(8,128)S(1)} %update.2.source.refs_0_), channel_id=1, source_target_pairs={{0,1},{1,0},{2,3},{3,2},{4,5},{5,4},{6,7},{7,6},{8,9},{9,8},{10,11... | collective-permute-start | bytes 417800 | tf_op jit(solution)/shard_map/ppermute | solution.py:701
  39.9 6.2 %collective-permute-start.10 = (f32[128,256]{1,0:T(8,128)S(1)}, f32[128,256]{1,0:T(8,128)S(1)}, u32[]{:S(2)}, u32[]{:S(2)}) collective-permute-start(f32[128,256]{1,0:T(8,128)S(1)} %update.3.refs_1_), channel_id=1, source_target_pairs={{0,1},{1,0},{2,3},{3,2},{4,5},{5,4},{6,7},{7,6},{8,9},{9,8},{10,11... | collective-permute-start | bytes 393224 | tf_op jit(solution)/shard_map/ppermute | solution.py:701
